TPU v7x, 256 devices: a whole 4x4x8 slice. The times are simulated.
256 devices in a mesh: loss: 32 (over y, z_hi, core), dp: 8 (over z_lo, x).
Axes of the slice: x: 4, y: 4, z: 8 (z_hi: 4, z_lo: 2; z = z_hi * 2 + z_lo), core: 2. Of those that a mesh axis runs over, the one named last changes fastest.
Arguments:
- picture_pooled_features: bfloat16 [8, 4096, 1152], P('dp', 'loss'), may hold values from -6 to 6
- sentence_pooled_features: bfloat16 [8, 4096, 1152], P('dp', 'loss'), may hold values from -6 to 6
- description_keys: int32 [8, 4096], P('dp', 'loss'), may hold values from 0 to 8191
- picture_projection_weights: bfloat16 [1152, 1152], replicated, may hold values from -0.1875 to 0.1875
- sentence_projection_weights: bfloat16 [1152, 1152], replicated, may hold values from -0.1875 to 0.1875
- learned_inverse_heat_exponent: float32 [1], replicated, may hold values from 1.5 to 2.3
- learned_shift_amount: float32 [1], replicated, may hold values from -3 to -1
Outputs:
- grad_w_img: float32 [1152, 1152], P('loss', 'dp')
- grad_w_txt: float32 [1152, 1152], P('loss', 'dp')
- statistics: float32 [3], replicated
All inputs are finite; a program needn't handle non-finite values.
Results may differ from a plain program's by a relative error of at most 0.0048.
Values may be sent and summed in bfloat16 or wider, within the bound.
No kernel may reach another device: no remote copies, remote signals or barrier semaphores. Data moves between devices by JAX's collectives and lax.ppermute only.
A program may use at most 128 MiB of HBM per device.

v0:
```python
import jax
import jax.numpy as jnp
from jax import lax
from jax.sharding import PartitionSpec as P

epsilon = 1e-06


def partner(array, axis, apart):
    return lax.ppermute(array, axis, [(i, i ^ 1 << apart) for i in range(lax.axis_size(axis))])


def project_rows(features, weight):
    projected = jnp.dot(features, weight, preferred_element_type=jnp.float32)
    lengths = jnp.sqrt(jnp.sum(projected * projected, axis=1, keepdims=True) + epsilon)
    return (projected / lengths, lengths)


def peer_block_routine(
    picture_vector_entries,
    sentence_vector_entries,
    picture_description_keys,
    sentence_description_keys,
    heat_multiplier,
    start_position,
):
    similarity_entries = lax.dot_general(
        picture_vector_entries,
        sentence_vector_entries,
        (((1,), (1,)), ((), ())),
        preferred_element_type=jnp.float32,
    )
    similarity_grid = heat_multiplier * similarity_entries + start_position
    labels = jnp.where(
        picture_description_keys[:, None] == sentence_description_keys[None, :], 1.0, -1.0
    ).astype(jnp.float32)
    margins = -labels * similarity_grid
    row_count = picture_vector_entries.shape[0]
    objective_accumulated_sum = jnp.sum(jax.nn.softplus(margins)) / row_count
    derivative_collection = -labels * jax.nn.sigmoid(margins) / row_count
    return (
        objective_accumulated_sum,
        derivative_collection,
        jnp.sum(derivative_collection * heat_multiplier * similarity_entries),
        jnp.sum(derivative_collection),
    )


def first_factor_contraction(derivative_collection, embed):
    return lax.dot_general(
        derivative_collection.astype(jnp.bfloat16),
        embed,
        (((0,), (0,)), ((), ())),
        preferred_element_type=jnp.float32,
    )


def body(
    picture_pooled_features,
    sentence_pooled_features,
    description_keys,
    picture_projection_weights,
    sentence_projection_weights,
    learned_inverse_heat_exponent,
    learned_shift_amount,
):
    img_rows = picture_pooled_features[0]
    txt_rows = sentence_pooled_features[0]
    own_description_keys = description_keys[0]
    heat_multiplier = jnp.exp(learned_inverse_heat_exponent[0])
    start_position = learned_shift_amount[0]
    img_full, img_len = project_rows(img_rows, picture_projection_weights)
    txt_full, txt_len = project_rows(txt_rows, sentence_projection_weights)
    own_picture_vectors = img_full.astype(jnp.bfloat16)
    own_sentence_vectors = txt_full.astype(jnp.bfloat16)
    objective_accumulated_sum, derivative_collection, heat_derivative, shift_derivative = (
        peer_block_routine(
            own_picture_vectors,
            own_sentence_vectors,
            own_description_keys,
            own_description_keys,
            heat_multiplier,
            start_position,
        )
    )
    picture_derivative = heat_multiplier * jnp.dot(
        derivative_collection.astype(jnp.bfloat16),
        own_sentence_vectors,
        preferred_element_type=jnp.float32,
    )
    sentence_derivative = heat_multiplier * first_factor_contraction(
        derivative_collection, own_picture_vectors
    )
    bit_count = lax.axis_size("loss").bit_length() - 1
    for bit_number in range(bit_count):
        peer_sentence_vectors, peer_description_keys = partner(
            (own_sentence_vectors, own_description_keys), "loss", bit_number
        )
        (
            block_objective_amount,
            block_derivative_collection,
            block_heat_derivative,
            block_shift_derivative,
        ) = peer_block_routine(
            own_picture_vectors,
            peer_sentence_vectors,
            own_description_keys,
            peer_description_keys,
            heat_multiplier,
            start_position,
        )
        objective_piece = (
            heat_multiplier
            * first_factor_contraction(block_derivative_collection, own_picture_vectors)
        ).astype(jnp.bfloat16)
        returned = partner(objective_piece, "loss", bit_number)
        picture_derivative = picture_derivative + heat_multiplier * jnp.dot(
            block_derivative_collection.astype(jnp.bfloat16),
            peer_sentence_vectors,
            preferred_element_type=jnp.float32,
        )
        sentence_derivative = sentence_derivative + returned.astype(jnp.float32)
        objective_accumulated_sum = objective_accumulated_sum + block_objective_amount
        heat_derivative = heat_derivative + block_heat_derivative
        shift_derivative = shift_derivative + block_shift_derivative
    img_dir = (
        (
            picture_derivative
            - img_full * jnp.sum(img_full * picture_derivative, axis=1, keepdims=True)
        )
        / img_len
    ).astype(jnp.bfloat16)
    txt_dir = (
        (
            sentence_derivative
            - txt_full * jnp.sum(txt_full * sentence_derivative, axis=1, keepdims=True)
        )
        / txt_len
    ).astype(jnp.bfloat16)
    head_img = lax.dot_general(
        img_rows, img_dir, (((0,), (0,)), ((), ())), preferred_element_type=jnp.float32
    )
    head_txt = lax.dot_general(
        txt_rows, txt_dir, (((0,), (0,)), ((), ())), preferred_element_type=jnp.float32
    )
    loss_ways = lax.axis_size("loss")
    data_ways = lax.axis_size("dp")
    first = (
        lax.psum_scatter(head_img, "loss", scatter_dimension=0, tiled=True),
        lax.psum_scatter(head_txt, "loss", scatter_dimension=0, tiled=True),
    )
    final = (
        lax.psum_scatter(first[0], "dp", scatter_dimension=1, tiled=True),
        lax.psum_scatter(first[1], "dp", scatter_dimension=1, tiled=True),
    )
    grad_img, grad_txt = (final[0], final[1])
    running_counts = jnp.stack([objective_accumulated_sum, heat_derivative, shift_derivative])
    totals = lax.psum(running_counts, ("loss", "dp"))
    statistics = totals / (loss_ways * data_ways)
    return (grad_img, grad_txt, statistics)


def solution(mesh):
    return jax.shard_map(
        body,
        mesh=mesh,
        in_specs=(
            P("dp", "loss", None),
            P("dp", "loss", None),
            P("dp", "loss"),
            P(),
            P(),
            P(),
            P(),
        ),
        out_specs=(P("loss", "dp"), P("loss", "dp"), P()),
        check_vma=False,
    )
```

profile of v0, /device:TPU:32, one launch (start us, length us, event | category | flops | bytes accessed | tf_op | source)
XLA Modules:
  0.0 545.7 jit_solution(6788083842768784595)
XLA Ops:
  7.2 1.7 copy-done
  8.9 1.6 multiply_reduce_fusion.2
  11.5 1.6 collective-permute-start.7
  13.1 6.3 %collective-permute-start.5 = (bf16[128,1152]{1,0:T(8,128)(2,1)}, bf16[128,1152]{1,0:T(8,128)(2,1)}, u32[]{:S(2)}, u32[]{:S(2)}) collective-permute-start(bf16[128,1152]{1,0:T(8,128)(2,1)} %fusion.42), channel_id=1, source_target_pairs={{0,32},{8,40},{16,48},{24,56},{32,0},{40,8},{48,16},{56,24},{64,96... | collective-permute-start | bytes 884744 | tf_op jit(solution)/shard_map/ppermute | solution.py:10
  21.4 2.5 multiply_reduce_fusion.3
  26.6 2.1 fusion.25
  31.3 2.1 collective-permute-done.5
  33.4 4.7 collective-permute-start.4
  39.3 5.1 collective-permute-done.3
  44.4 2.9 collective-permute-start.9
  48.8 1.5 collective-permute-start.8
  51.5 3.0 collective-permute-done.6
  55.1 2.2 fusion.24
  57.7 3.0 collective-permute-start.14
  63.2 3.5 collective-permute-start.11
  72.9 3.3 convolution_bitcast_fusion.1
  76.3 12.7 %collective-permute-done.11 = bf16[128,1152]{1,0:T(8,128)(2,1)S(1)} collective-permute-done((bf16[128,1152]{1,0:T(8,128)(2,1)S(1)}, bf16[128,1152]{1,0:T(8,128)(2,1)S(1)}, u32[]{:S(2)}, u32[]{:S(2)}) %collective-permute-start.11) | collective-permute-done | bytes 294944 | tf_op jit(solution)/shard_map/ppermute | solution.py:10
  89.6 3.3 convolution_bitcast_fusion
  94.8 344.8 %all-reduce.5.cloned.1.call-done = (f32[1152,1152]{0,1:T(8,128)}, f32[1152,1152]{0,1:T(8,128)}) async-done(((f32[1152,1152]{0,1:T(8,128)}, f32[1152,1152]{0,1:T(8,128)}), (f32[1152,1152]{0,1:T(8,128)}, f32[1152,1152]{0,1:T(8,128)})) %all-reduce.5.cloned.1.call-update) | async-done | bytes 10616848
  439.6 2.3 constant_dynamic-slice_fusion.1
  453.1 2.3 constant_dynamic-slice_fusion
  455.6 79.9 %psum.7 = f32[3]{0:T(128)S(1)} all-reduce(f32[3]{0:T(128)S(1)} %pad_maximum_fusion), channel_id=1, replica_groups=mesh['loss'=32,'dp'=8] {'loss','dp'}, use_global_device_ids=true, to_apply=%region_26.27 | all-reduce | flops 3 | bytes 24 | tf_op jit(solution)/shard_map/psum | solution.py:158
  536.0 1.6 copy.12
  537.6 1.6 copy.13
  (69 shorter events, 22.9 us)
Async XLA Ops:
  7.2 19.4 %copy-start.8 = (s32[1,128]{1,0:T(1,128)S(1)}, s32[1,128]{1,0:T(1,128)}, u32[]{:S(2)}) copy-start(s32[1,128]{1,0:T(1,128)} %param.9) | copy-start | bytes 1540
  7.2 432.4 %all-reduce.5.cloned.1.call-start = ((), (), s32[]{:S(2)}) async-start(), calls=%async_computation.4 | async-start | bytes 21233664
  10.6 13.4 %copy-start.1 = (f32[128,1152]{1,0:T(8,128)}, f32[128,1152]{1,0:T(8,128)S(1)}, u32[]{:S(2)}) copy-start(f32[128,1152]{1,0:T(8,128)S(1)} %get-tuple-element.45) | copy-start | bytes 1769476
  11.5 17.2 %collective-permute-start.7 = (bf16[128,1152]{1,0:T(8,128)(2,1)}, bf16[128,1152]{1,0:T(8,128)(2,1)}, u32[]{:S(2)}, u32[]{:S(2)}) collective-permute-start(bf16[128,1152]{1,0:T(8,128)(2,1)} %fusion.42), channel_id=1, source_target_pairs={{0,64},{8,72},{16,80},{24,88},{32,96},{40,104},{48,112},{56,120},{... | collective-permute-start | bytes 884744 | tf_op jit(solution)/shard_map/ppermute | solution.py:10
  13.1 20.3 %collective-permute-start.5 = (bf16[128,1152]{1,0:T(8,128)(2,1)}, bf16[128,1152]{1,0:T(8,128)(2,1)}, u32[]{:S(2)}, u32[]{:S(2)}) collective-permute-start(bf16[128,1152]{1,0:T(8,128)(2,1)} %fusion.42), channel_id=1, source_target_pairs={{0,32},{8,40},{16,48},{24,56},{32,0},{40,8},{48,16},{56,24},{64,96... | collective-permute-start | bytes 884744 | tf_op jit(solution)/shard_map/ppermute | solution.py:10
  19.4 25.0 %collective-permute-start.3 = (bf16[128,1152]{1,0:T(8,128)(2,1)}, bf16[128,1152]{1,0:T(8,128)(2,1)}, u32[]{:S(2)}, u32[]{:S(2)}) collective-permute-start(bf16[128,1152]{1,0:T(8,128)(2,1)} %fusion.42), channel_id=1, source_target_pairs={{0,16},{8,24},{16,0},{24,8},{32,48},{40,56},{48,32},{56,40},{64,80... | collective-permute-start | bytes 884744 | tf_op jit(solution)/shard_map/ppermute | solution.py:10
  20.8 27.9 %collective-permute-start.1 = (bf16[128,1152]{1,0:T(8,128)(2,1)}, bf16[128,1152]{1,0:T(8,128)(2,1)}, u32[]{:S(2)}, u32[]{:S(2)}) collective-permute-start(bf16[128,1152]{1,0:T(8,128)(2,1)} %fusion.42), channel_id=1, source_target_pairs={{0,8},{8,0},{16,24},{24,16},{32,40},{40,32},{48,56},{56,48},{64,72... | collective-permute-start | bytes 884744 | tf_op jit(solution)/shard_map/ppermute | solution.py:10
  20.9 27.7 %collective-permute-start = (s32[128]{0:T(128)}, s32[128]{0:T(128)S(1)}, u32[]{:S(2)}, u32[]{:S(2)}) collective-permute-start(s32[128]{0:T(128)} %bitcast.68), channel_id=1, source_target_pairs={{0,8},{8,0},{16,24},{24,16},{32,40},{40,32},{48,56},{56,48},{64,72... | collective-permute-start | bytes 1544 | tf_op jit(solution)/shard_map/ppermute | solution.py:10
  28.7 22.8 %collective-permute-start.2 = (s32[128]{0:T(128)S(1)}, s32[128]{0:T(128)S(1)}, u32[]{:S(2)}, u32[]{:S(2)}) collective-permute-start(s32[128]{0:T(128)S(1)} %bitcast.70), channel_id=1, source_target_pairs={{0,16},{8,24},{16,0},{24,8},{32,48},{40,56},{48,32},{56,40},{64,80... | collective-permute-start | bytes 1544 | tf_op jit(solution)/shard_map/ppermute | solution.py:10
  33.4 18.1 %collective-permute-start.4 = (s32[128]{0:T(128)S(1)}, s32[128]{0:T(128)S(1)}, u32[]{:S(2)}, u32[]{:S(2)}) collective-permute-start(s32[128]{0:T(128)S(1)} %bitcast.71), channel_id=1, source_target_pairs={{0,32},{8,40},{16,48},{24,56},{32,0},{40,8},{48,16},{56,24},{64,96... | collective-permute-start | bytes 1544 | tf_op jit(solution)/shard_map/ppermute | solution.py:10
  44.4 10.7 %collective-permute-start.9 = (bf16[128,1152]{1,0:T(8,128)(2,1)}, bf16[128,1152]{1,0:T(8,128)(2,1)S(1)}, u32[]{:S(2)}, u32[]{:S(2)}) collective-permute-start(bf16[128,1152]{1,0:T(8,128)(2,1)} %fusion.42), channel_id=1, source_target_pairs={{0,128},{8,136},{16,144},{24,152},{32,160},{40,168},{48,176},{56,1... | collective-permute-start | bytes 884744 | tf_op jit(solution)/shard_map/ppermute | solution.py:10
  48.5 6.0 %collective-permute-start.6 = (s32[128]{0:T(128)S(1)}, s32[128]{0:T(128)S(1)}, u32[]{:S(2)}, u32[]{:S(2)}) collective-permute-start(s32[128]{0:T(128)S(1)} %bitcast.72), channel_id=1, source_target_pairs={{0,64},{8,72},{16,80},{24,88},{32,96},{40,104},{48,112},{56,120},{... | collective-permute-start | bytes 1544 | tf_op jit(solution)/shard_map/ppermute | solution.py:10
  48.8 6.4 %collective-permute-start.8 = (s32[128]{0:T(128)S(1)}, s32[128]{0:T(128)S(1)}, u32[]{:S(2)}, u32[]{:S(2)}) collective-permute-start(s32[128]{0:T(128)S(1)} %bitcast.73), channel_id=1, source_target_pairs={{0,128},{8,136},{16,144},{24,152},{32,160},{40,168},{48,176},{56,1... | collective-permute-start | bytes 1544 | tf_op jit(solution)/shard_map/ppermute | solution.py:10
  51.5 18.6 %copy-start.3 = (f32[128,1152]{1,0:T(8,128)S(1)}, f32[128,1152]{1,0:T(8,128)}, u32[]{:S(2)}) copy-start(f32[128,1152]{1,0:T(8,128)} %fusion.25) | copy-start | bytes 1769476
  57.7 18.6 %collective-permute-start.14 = (bf16[128,1152]{1,0:T(8,128)(2,1)S(1)}, bf16[128,1152]{1,0:T(8,128)(2,1)S(1)}, u32[]{:S(2)}, u32[]{:S(2)}) collective-permute-start(bf16[128,1152]{1,0:T(8,128)(2,1)S(1)} %fusion.8), channel_id=1, source_target_pairs={{0,128},{8,136},{16,144},{24,152},{32,160},{40,168},{48,176},{56,1... | collective-permute-start | bytes 884744 | tf_op jit(solution)/shard_map/ppermute | solution.py:10
  61.1 15.2 %collective-permute-start.13 = (bf16[128,1152]{1,0:T(8,128)(2,1)S(1)}, bf16[128,1152]{1,0:T(8,128)(2,1)S(1)}, u32[]{:S(2)}, u32[]{:S(2)}) collective-permute-start(bf16[128,1152]{1,0:T(8,128)(2,1)S(1)} %fusion.7), channel_id=1, source_target_pairs={{0,64},{8,72},{16,80},{24,88},{32,96},{40,104},{48,112},{56,120},{... | collective-permute-start | bytes 884744 | tf_op jit(solution)/shard_map/ppermute | solution.py:10
  61.6 14.6 %collective-permute-start.12 = (bf16[128,1152]{1,0:T(8,128)(2,1)S(1)}, bf16[128,1152]{1,0:T(8,128)(2,1)S(1)}, u32[]{:S(2)}, u32[]{:S(2)}) collective-permute-start(bf16[128,1152]{1,0:T(8,128)(2,1)S(1)} %fusion.6), channel_id=1, source_target_pairs={{0,32},{8,40},{16,48},{24,56},{32,0},{40,8},{48,16},{56,24},{64,96... | collective-permute-start | bytes 884744 | tf_op jit(solution)/shard_map/ppermute | solution.py:10
  63.2 25.7 %collective-permute-start.11 = (bf16[128,1152]{1,0:T(8,128)(2,1)S(1)}, bf16[128,1152]{1,0:T(8,128)(2,1)S(1)}, u32[]{:S(2)}, u32[]{:S(2)}) collective-permute-start(bf16[128,1152]{1,0:T(8,128)(2,1)S(1)} %fusion.5), channel_id=1, source_target_pairs={{0,16},{8,24},{16,0},{24,8},{32,48},{40,56},{48,32},{56,40},{64,80... | collective-permute-start | bytes 884744 | tf_op jit(solution)/shard_map/ppermute | solution.py:10
  67.0 21.9 %collective-permute-start.10 = (bf16[128,1152]{1,0:T(8,128)(2,1)S(1)}, bf16[128,1152]{1,0:T(8,128)(2,1)S(1)}, u32[]{:S(2)}, u32[]{:S(2)}) collective-permute-start(bf16[128,1152]{1,0:T(8,128)(2,1)S(1)} %fusion.4), channel_id=1, source_target_pairs={{0,8},{8,0},{16,24},{24,16},{32,40},{40,32},{48,56},{56,48},{64,72... | collective-permute-start | bytes 884744 | tf_op jit(solution)/shard_map/ppermute | solution.py:10
  71.4 17.5 %copy-start.2 = (f32[128,1152]{1,0:T(8,128)S(1)}, f32[128,1152]{1,0:T(8,128)}, u32[]{:S(2)}) copy-start(f32[128,1152]{1,0:T(8,128)} %copy-done.1) | copy-start | bytes 1769476
  71.4 17.5 %copy-start.7 = (f32[128,128]{1,0:T(8,128)S(1)}, f32[128,128]{1,0:T(8,128)}, u32[]{:S(2)}) copy-start(f32[128,128]{1,0:T(8,128)} %copy-done.6) | copy-start | bytes 196612
  72.9 16.7 %copy-start.5 = (bf16[1,128,1152]{2,1,0:T(8,128)(2,1)S(1)}, bf16[1,128,1152]{2,1,0:T(8,128)(2,1)}, u32[]{:S(2)}) copy-start(bf16[1,128,1152]{2,1,0:T(8,128)(2,1)} %param.8) | copy-start | bytes 884740
  92.9 443.1 %reduce-scatter.5.cloned.1.call-start = ((), (), s32[]{:S(2)}) async-start(), calls=%async_computation.2 | async-start | bytes 663552 | tf_op jit(solution)/shard_map/reduce_scatter | solution.py:153
  441.9 95.6 %reduce-scatter.7.cloned.1.call-start = ((), (), s32[]{:S(2)}) async-start(), calls=%async_computation.3 | async-start | bytes 663552 | tf_op jit(solution)/shard_map/reduce_scatter | solution.py:154
  (4 other events, 15.7 us)
Sparse Core Ops, SparseCore 0:
  93.0 346.5 all-reduce.4
  442.1 39.8 reduce-scatter.4
  484.6 39.4 reduce-scatter.6
where the time goes:
time: 548 us; the launch traced here: 546 us
  waiting for transfers between devices  368 us (67%)
  blocking collectives  79.9 us (15%)
  starting transfers between devices  29 us (5%)
  matrix products  29 us (5%)
  between operations  27.2 us (5%)
  local copies, waits for them, and re-layouts  10.8 us (2%)
    unnamed x4, waiting for transfers between devices  345 us
    psum x1, blocking collectives, body(): totals = lax.psum(running_counts, ('loss', 'dp'))  79.9 us
    ppermute x15, starting transfers between devices, partner(): lax.ppermute(array, axis, [(i, i ^ 1 << apart) for i in range(lax.axis_si...  28.9 us
    ppermute x15, waiting for transfers between devices, partner(): lax.ppermute(array, axis, [(i, i ^ 1 << apart) for i in range(lax.axis_si...  23.4 us
  transfers between devices with their start and end apart: 18, of which 6 were waited for; matrix products, arithmetic and copies ran while one was open for 5% of the time, Pallas kernels for 0%

commit v1 on v0

v1 whole, which is shorter than its diff:
```python
import jax
import jax.numpy as jnp
from jax import lax
from jax.sharding import Mesh, PartitionSpec as P

epsilon = 1e-06
LOSS = ("ly", "lz", "lc")


def exchange(array, axis, apart):
    return lax.ppermute(array, axis, [(i, i ^ apart) for i in range(lax.axis_size(axis))])


def project_rows(features, weight):
    projected = jnp.dot(features, weight, preferred_element_type=jnp.float32)
    lengths = jnp.sqrt(jnp.sum(projected * projected, axis=1, keepdims=True) + epsilon)
    return projected / lengths, lengths


def three_parts(values):
    high = values.astype(jnp.bfloat16)
    rest = values - high.astype(jnp.float32)
    middle = rest.astype(jnp.bfloat16)
    low = (rest - middle.astype(jnp.float32)).astype(jnp.bfloat16)
    return jnp.concatenate([high, middle, low])


def tile_terms(similarity, same, heat, shift, rows):
    logits = heat * similarity + shift
    labels = jnp.where(same, 1.0, -1.0).astype(jnp.float32)
    margins = -labels * logits
    gradient = -labels * jax.nn.sigmoid(margins) / rows
    return margins, gradient


def nt(a, b):
    return lax.dot_general(a, b, (((1,), (1,)), ((), ())), preferred_element_type=jnp.float32)


def tn(a, b):
    return lax.dot_general(a, b, (((0,), (0,)), ((), ())), preferred_element_type=jnp.float32)


def tangent(total, unit, length):
    inner = jnp.sum(unit * total, axis=1, keepdims=True)
    return ((total - unit * inner) / length).astype(jnp.bfloat16)


def body(pictures, sentences, keys, picture_weights, sentence_weights, heat_log, shift_value):
    rows, width = pictures.shape[1:]
    ways = lax.axis_size("dp")
    heat = jnp.exp(heat_log[0])
    shift = shift_value[0]
    own_keys = keys[0]
    own = jnp.concatenate([pictures[0], sentences[0]], axis=0)

    bits = [("lz", 2), ("lz", 1), ("ly", 2), ("ly", 1), ("lc", 1)]
    near_keys = [exchange(own_keys, axis, apart) for axis, apart in bits]
    near = [exchange(own, axis, apart) for axis, apart in bits]
    gathered = lax.all_gather(own, "dp", axis=0)

    img_unit, img_len = project_rows(own[:rows], picture_weights)
    txt_unit, txt_len = project_rows(own[rows:], sentence_weights)
    img_vec = [img_unit.astype(jnp.bfloat16)]
    txt_vec = [txt_unit.astype(jnp.bfloat16)]
    for block in reversed(near):
        img_vec.append(project_rows(block[:rows], picture_weights)[0].astype(jnp.bfloat16))
        txt_vec.append(project_rows(block[rows:], sentence_weights)[0].astype(jnp.bfloat16))
    all_keys = jnp.concatenate([own_keys] + near_keys[::-1])
    all_img = jnp.concatenate(img_vec, axis=0)
    all_txt = jnp.concatenate(txt_vec, axis=0)
    same = own_keys[:, None] == all_keys[None, :]

    similarity = nt(img_vec[0], all_txt)
    margins, gradient = tile_terms(similarity, same, heat, shift, rows)
    numbers = jnp.stack(
        [
            jnp.sum(jax.nn.softplus(margins)) / rows,
            jnp.sum(gradient * heat * similarity),
            jnp.sum(gradient),
        ]
    )
    img_total = heat * jnp.dot(
        gradient.astype(jnp.bfloat16), all_txt, preferred_element_type=jnp.float32
    )
    back_similarity = nt(txt_vec[0], all_img)
    _, back_gradient = tile_terms(back_similarity, same, heat, shift, rows)
    txt_total = heat * jnp.dot(
        back_gradient.astype(jnp.bfloat16), all_img, preferred_element_type=jnp.float32
    )
    img_dir = tangent(img_total, img_unit, img_len)
    txt_dir = tangent(txt_total, txt_unit, txt_len)

    cols = width // ways
    spread = jnp.concatenate(
        [img_dir.T.reshape(ways, cols, rows), txt_dir.T.reshape(ways, cols, rows)], axis=1
    )
    extra = jnp.zeros((16, rows), jnp.bfloat16).at[0, :9].set(three_parts(numbers))
    spread = jnp.concatenate([spread, jnp.broadcast_to(extra, (ways, 16, rows))], axis=1)
    spread = lax.all_to_all(spread, "dp", 0, 0, tiled=True)
    numbers = jnp.sum(
        jnp.sum(spread[:, 2 * cols, :9].astype(jnp.float32), axis=0).reshape(3, 3), axis=0
    )

    def head(features, directions):
        return lax.dot_general(
            features,
            directions,
            (((0, 1), (0, 2)), ((), ())),
            preferred_element_type=jnp.float32,
        )

    heads = jnp.concatenate(
        [
            head(gathered[:, :rows], spread[:, :cols]),
            head(gathered[:, rows:], spread[:, cols : 2 * cols]),
        ],
        axis=1,
    )
    quads = lax.axis_size("ly") * lax.axis_size("lz")
    part = width // (2 * quads)
    heads = heads.reshape(quads, 2, part, 2 * cols)
    core = lax.axis_index("lc")
    kept = jnp.where(core == 0, heads[:, 0], heads[:, 1])
    given = jnp.where(core == 0, heads[:, 1], heads[:, 0]).astype(jnp.bfloat16)
    number_row = jnp.zeros((1, 1, 2 * cols), jnp.bfloat16)
    mine = number_row.at[0, 0, :9].set(three_parts(numbers))
    given = jnp.concatenate([given, jnp.broadcast_to(mine, (quads, 1, 2 * cols))], axis=1)
    taken = exchange(given, "lc", 1).astype(jnp.float32)
    numbers = numbers + jnp.sum(taken[0, part, :9].reshape(3, 3), axis=0)
    both = number_row.at[0, 0, :9].set(three_parts(numbers))
    kept = (kept + taken[:, :part]).astype(jnp.bfloat16)
    kept = jnp.concatenate([kept, jnp.broadcast_to(both, (quads, 1, 2 * cols))], axis=1)
    kept = lax.all_to_all(kept, ("ly", "lz"), 0, 0, tiled=True)
    sums = jnp.sum(kept.astype(jnp.float32), axis=0)
    statistics = jnp.sum(sums[part, :9].reshape(3, 3), axis=0) / (2 * quads * ways)
    return sums[:part, :cols], sums[:part, cols:], statistics


def solution(mesh):
    split = Mesh(mesh.devices.reshape(4, 4, 2, 8), ("ly", "lz", "lc", "dp"))
    return jax.shard_map(
        body,
        mesh=split,
        in_specs=(P("dp", LOSS, None), P("dp", LOSS, None), P("dp", LOSS), P(), P(), P(), P()),
        out_specs=(P(LOSS, "dp"), P(LOSS, "dp"), P()),
        check_vma=False,
    )
```

time: 548 us -> 193 us (0.35)
  waiting for transfers between devices: 368 us -> 60.1 us
  blocking collectives: 79.9 us -> 28.2 us
  other arithmetic: 1.63 us -> 14.4 us
  between operations: 27.2 us -> 16.5 us
    unnamed x4 -> x1, waiting for transfers between devices: 345 us -> 0.02 us
    psum x1 -> x0, blocking collectives: 79.9 us -> none  [body(): totals = lax.psum(running_counts, ('loss', 'dp'))]
    ppermute x15 -> x11, waiting for transfers between devices: 23.4 us -> 52.3 us  [exchange(): lax.ppermute(array, axis, [(i, i ^ apart) for i in range(lax.axis_size(ax...]
    all_to_all x0 -> x1, blocking collectives: none -> 28.2 us  [body(): kept = lax.all_to_all(kept, ('ly', 'lz'), 0, 0, tiled=True)]
    dot_general x20 -> x5, matrix products: 24.8 us -> 10.9 us  [the longest x2 4.46 us: head(): lax.dot_general(features, directions, (((0, 1), (0, 2)), ((), ())), prefe...]
    dot_general x2 -> x12, matrix products: 4.18 us -> 17 us  [project_rows(): projected = jnp.dot(features, weight, preferred_element_type=jnp.float32)]
    all_to_all x0 -> x1, waiting for transfers between devices: none -> 7.76 us  [body(): spread = lax.all_to_all(spread, 'dp', 0, 0, tiled=True)]
    unnamed x25 -> x33, local copies, waits for them, and re-layouts: 10.8 us -> 3.79 us
  transfers between devices with their start and end apart: 18 -> 13, of which waited for: 6 -> 7; matrix products, arithmetic and copies ran while one was open for 5% -> 18% of each run, Pallas kernels for 0% -> 0%
where the time goes in v1:
time: 193 us; the launch traced here: 192 us
  waiting for transfers between devices  60.1 us (31%)
  starting transfers between devices  32 us (17%)
  blocking collectives  28.2 us (15%)
  matrix products  28 us (15%)
  between operations  16.5 us (9%)
  other arithmetic  14.4 us (7%)
  local copies, waits for them, and re-layouts  12.9 us (7%)
    ppermute x11, waiting for transfers between devices, exchange(): lax.ppermute(array, axis, [(i, i ^ apart) for i in range(lax.axis_size(ax...  52.3 us
    all_to_all x1, blocking collectives, body(): kept = lax.all_to_all(kept, ('ly', 'lz'), 0, 0, tiled=True)  28.2 us
    ppermute x11, starting transfers between devices, exchange(): lax.ppermute(array, axis, [(i, i ^ apart) for i in range(lax.axis_size(ax...  26.5 us
    dot_general x12, matrix products, project_rows(): projected = jnp.dot(features, weight, preferred_element_type=jnp.float32)  17 us
    all_to_all x1, waiting for transfers between devices, body(): spread = lax.all_to_all(spread, 'dp', 0, 0, tiled=True)  7.76 us
    all_to_all x1, starting transfers between devices, body(): spread = lax.all_to_all(spread, 'dp', 0, 0, tiled=True)  5.47 us
    dot_general x2, matrix products, head(): lax.dot_general(features, directions, (((0, 1), (0, 2)), ((), ())), prefe...  4.46 us
    dot_general x1, matrix products, body(): jnp.dot(back_gradient.astype(jnp.bfloat16), all_img, preferred_element_ty...  4.19 us
  transfers between devices with their start and end apart: 13, of which 7 were waited for; matrix products, arithmetic and copies ran while one was open for 18% of the time, Pallas kernels for 0%

profile of v1, /device:TPU:32, one launch (start us, length us, event | category | flops | bytes accessed | tf_op | source)
XLA Modules:
  0.0 192.1 jit_solution(134021820851045151)
XLA Ops:
  7.2 2.1 %pad_maximum_fusion.2 = bf16[256,1152]{1,0:T(8,128)(2,1)} fusion(bf16[128,1152]{1,0:T(8,128)(2,1)} %bitcast.75, bf16[128,1152]{1,0:T(8,128)(2,1)} %bitcast.76), kind=kLoop, calls=%fused_computation.25 | loop fusion | flops 1179648 | bytes 1179648 | tf_op jit(solution)/shard_map/concatenate | solution.py:55
  11.0 2.9 %collective-permute-start.7 = (bf16[256,1152]{1,0:T(8,128)(2,1)}, bf16[256,1152]{1,0:T(8,128)(2,1)}, u32[]{:S(2)}, u32[]{:S(2)}) collective-permute-start(bf16[256,1152]{1,0:T(8,128)(2,1)} %pad_maximum_fusion.2), channel_id=1, source_target_pairs={{0,128},{64,192},{128,0},{192,64},{1,129},{65,193},{129,1},{193,65... | collective-permute-start | bytes 1769480 | tf_op jit(solution)/shard_map/ppermute | solution.py:11
  13.9 3.3 %collective-permute-start.8 = (bf16[256,1152]{1,0:T(8,128)(2,1)}, bf16[256,1152]{1,0:T(8,128)(2,1)}, u32[]{:S(2)}, u32[]{:S(2)}) collective-permute-start(bf16[256,1152]{1,0:T(8,128)(2,1)} %pad_maximum_fusion.2), channel_id=1, source_target_pairs={{0,16},{16,0},{32,48},{48,32},{1,17},{17,1},{33,49},{49,33},{2,18}... | collective-permute-start | bytes 1769480 | tf_op jit(solution)/shard_map/ppermute | solution.py:11
  23.1 14.9 %collective-permute-done.1 = s32[128]{0:T(128)S(1)} collective-permute-done((s32[128]{0:T(128)S(1)}, s32[128]{0:T(128)S(1)}, u32[]{:S(2)}, u32[]{:S(2)}) %collective-permute-start.1) | collective-permute-done | bytes 544 | tf_op jit(solution)/shard_map/ppermute | solution.py:11
  37.9 3.2 %collective-permute-start.2 = (s32[128]{0:T(128)S(1)}, s32[128]{0:T(128)S(1)}, u32[]{:S(2)}, u32[]{:S(2)}) collective-permute-start(s32[128]{0:T(128)S(1)} %bitcast.81), channel_id=1, source_target_pairs={{0,128},{64,192},{128,0},{192,64},{1,129},{65,193},{129,1},{193,65... | collective-permute-start | bytes 1544 | tf_op jit(solution)/shard_map/ppermute | solution.py:11
  41.1 1.8 collective-permute-done.2
  43.0 3.3 %collective-permute-start.3 = (s32[128]{0:T(128)S(1)}, s32[128]{0:T(128)S(1)}, u32[]{:S(2)}, u32[]{:S(2)}) collective-permute-start(s32[128]{0:T(128)S(1)} %bitcast.82), channel_id=1, source_target_pairs={{0,16},{16,0},{32,48},{48,32},{1,17},{17,1},{33,49},{49,33},{2,18}... | collective-permute-start | bytes 1544 | tf_op jit(solution)/shard_map/ppermute | solution.py:11
  47.8 5.9 %collective-permute-start.4 = (s32[128]{0:T(128)S(1)}, s32[128]{0:T(128)S(1)}, u32[]{:S(2)}, u32[]{:S(2)}) collective-permute-start(s32[128]{0:T(128)S(1)} %bitcast.83), channel_id=1, source_target_pairs={{0,32},{16,48},{32,0},{48,16},{1,33},{17,49},{33,1},{49,17},{2,34}... | collective-permute-start | bytes 1544 | tf_op jit(solution)/shard_map/ppermute | solution.py:11
  55.3 5.9 %collective-permute-start.9 = (bf16[256,1152]{1,0:T(8,128)(2,1)}, bf16[256,1152]{1,0:T(8,128)(2,1)S(1)}, u32[]{:S(2)}, u32[]{:S(2)}) collective-permute-start(bf16[256,1152]{1,0:T(8,128)(2,1)} %pad_maximum_fusion.2), channel_id=1, source_target_pairs={{0,32},{16,48},{32,0},{48,16},{1,33},{17,49},{33,1},{49,17},{2,34}... | collective-permute-start | bytes 1769480 | tf_op jit(solution)/shard_map/ppermute | solution.py:11
  66.2 1.7 multiply_reduce_fusion.8
  67.9 30.7 %collective-permute-done.9 = bf16[256,1152]{1,0:T(8,128)(2,1)S(1)} collective-permute-done((bf16[256,1152]{1,0:T(8,128)(2,1)}, bf16[256,1152]{1,0:T(8,128)(2,1)S(1)}, u32[]{:S(2)}, u32[]{:S(2)}) %collective-permute-start.9) | collective-permute-done | bytes 589856 | tf_op jit(solution)/shard_map/ppermute | solution.py:11
  105.0 2.7 %multiply_reduce_fusion.5 = (f32[128]{0:T(128)S(1)}, f32[128,1152]{1,0:T(8,128)S(1)}) fusion(bf16[1152,1152]{1,0:T(8,128)(2,1)} %param.16, bf16[256,1152]{1,0:T(8,128)(2,1)} %collective-permute-done.5), kind=kOutput, calls=%fused_computation.37 | convolution fusion | flops 340033408 | bytes 3539456 | tf_op jit(solution)/shard_map/dot_general | solution.py:15
  111.1 1.7 multiply_reduce_fusion.2
  116.1 4.2 %multiply_reduce_fusion = (f32[128]{0:T(128)S(1)}, f32[128,1152]{1,0:T(8,128)}) fusion(f32[128,1152]{1,0:T(8,128)S(1)} %get-tuple-element.55, f32[128]{0:T(128)S(1)} %add_sqrt_fusion.10, bf16[768,1152]{1,0:T(8,128)(2,1)} %copy-done.11, f32[]{:T(128)} %bitcast.72, f32[]{:T(128)} %bitcast.3, s32[768]{0:T(1024)S(1)} %constant_dynamic-update-slice_fusion.1, ...), kind=kOutput, calls=%fused_computation.27 | convolution fusion | flops 455049088 | bytes 2953736 | tf_op jit(solution)/shard_map/dot_general | solution.py:88
  120.3 2.0 %fusion.49 = bf16[1152,128]{0,1:T(8,128)(2,1)} fusion(f32[128]{0:T(128)S(1)} %add_sqrt_fusion.10, f32[128,1152]{1,0:T(8,128)} %get-tuple-element.80, f32[128]{0:T(128)S(1)} %get-tuple-element.79, f32[128,1152]{1,0:T(8,128)S(1)} %get-tuple-element.55), kind=kLoop, calls=%fused_computation.98 | loop fusion | flops 737280 | bytes 1475584 | tf_op jit(solution)/shard_map/div | solution.py:46
  126.4 5.5 %all-to-all-start = ((bf16[8,304,128]{2,1,0:T(8,128)(2,1)}), bf16[8,304,128]{2,1,0:T(8,128)(2,1)S(1)}, u32[]{:S(2)}, u32[]{:S(2)}) async-start(bf16[8,304,128]{2,1,0:T(8,128)(2,1)} %pad_maximum_fusion.1), calls=%async_computation | async-start | bytes 1245184 | tf_op jit(solution)/shard_map/all_to_all | solution.py:100
  131.9 7.8 %all-to-all-done = bf16[8,304,128]{2,1,0:T(8,128)(2,1)S(1)} async-done(((bf16[8,304,128]{2,1,0:T(8,128)(2,1)}), bf16[8,304,128]{2,1,0:T(8,128)(2,1)S(1)}, u32[]{:S(2)}, u32[]{:S(2)}) %all-to-all-start) | async-done | bytes 622624 | tf_op jit(solution)/shard_map/all_to_all | solution.py:100
  139.9 2.2 %convolution_bitcast_fusion.1 = f32[1152,144]{0,1:T(8,128)S(1)} fusion(bf16[8,256,1152]{2,1,0:T(8,128)(2,1)} %bitcast.77, bf16[8,304,128]{2,1,0:T(8,128)(2,1)S(1)} %all-to-all-done), kind=kOutput, calls=%fused_computation.3 | convolution fusion | flops 339738624 | bytes 3317760 | tf_op jit(solution)/shard_map/dot_general | solution.py:106
  142.2 2.2 %convolution_bitcast_fusion = f32[1152,144]{0,1:T(8,128)S(1)} fusion(bf16[8,256,1152]{2,1,0:T(8,128)(2,1)} %bitcast.78, bf16[8,304,128]{2,1,0:T(8,128)(2,1)S(1)} %all-to-all-done), kind=kOutput, calls=%fused_computation.2 | convolution fusion | flops 339738624 | bytes 3317760 | tf_op jit(solution)/shard_map/dot_general | solution.py:106
  145.6 3.1 %copy.16 = f32[1152,288]{1,0:T(8,128)} copy(f32[1152,288]{0,1:T(8,128)} %pad_maximum_fusion) | data formatting | bytes 2654208 | tf_op jit(solution)/shard_map/concatenate | solution.py:113
  148.6 2.6 %reshape.199 = f32[16,2,36,288]{3,2,1,0:T(8,128)} reshape(f32[1152,288]{1,0:T(8,128)} %copy.16) | data formatting | bytes 2654208 | tf_op jit(solution)/shard_map/reshape | solution.py:122
  151.2 1.7 fusion.13
  153.2 1.9 collective-permute-done.10
  155.7 28.2 %all_to_all.10 = bf16[16,37,288]{2,1,0:T(8,128)(2,1)S(1)} all-to-all(bf16[16,37,288]{2,1,0:T(8,128)(2,1)S(1)} %pad_maximum_fusion.4), channel_id=1, replica_groups=mesh['ly'=4,'lz'=4,'lc'=2,'dp'=8] {'ly','lz'}, dimensions={0} | all-to-all | bytes 681984 | tf_op jit(solution)/shard_map/all_to_all | solution.py:134
  (119 shorter events, 34.2 us)
Async XLA Ops:
  7.2 10.1 %copy-start = (bf16[1152,1152]{1,0:T(8,128)(2,1)S(1)}, bf16[1152,1152]{1,0:T(8,128)(2,1)}, u32[]{:S(2)}) copy-start(bf16[1152,1152]{1,0:T(8,128)(2,1)} %param.17) | copy-start | bytes 7962628
  7.2 10.1 %copy-start.6 = (bf16[1,128,1152]{2,1,0:T(8,128)(2,1)S(1)}, bf16[1,128,1152]{2,1,0:T(8,128)(2,1)}, u32[]{:S(2)}) copy-start(bf16[1,128,1152]{2,1,0:T(8,128)(2,1)} %param.14) | copy-start | bytes 884740
  7.2 10.0 %copy-start.13 = (s32[1,128]{1,0:T(1,128)S(1)}, s32[1,128]{1,0:T(1,128)}, u32[]{:S(2)}) copy-start(s32[1,128]{1,0:T(1,128)} %param.15) | copy-start | bytes 1540
  7.2 132.7 %all-gather.3.cloned.1.call-start = ((), (), s32[]{:S(2)}) async-start(), calls=%async_computation.2 | async-start | bytes 5308416 | tf_op jit(solution)/shard_map/all_gather | solution.py:60
  9.4 51.8 %collective-permute-start.5 = (bf16[256,1152]{1,0:T(8,128)(2,1)}, bf16[256,1152]{1,0:T(8,128)(2,1)}, u32[]{:S(2)}, u32[]{:S(2)}) collective-permute-start(bf16[256,1152]{1,0:T(8,128)(2,1)} %pad_maximum_fusion.2), channel_id=1, source_target_pairs={{0,8},{8,0},{1,9},{9,1},{2,10},{10,2},{3,11},{11,3},{4,12},{12,4},... | collective-permute-start | bytes 1769480 | tf_op jit(solution)/shard_map/ppermute | solution.py:11
  9.4 53.5 %collective-permute-start.6 = (bf16[256,1152]{1,0:T(8,128)(2,1)}, bf16[256,1152]{1,0:T(8,128)(2,1)}, u32[]{:S(2)}, u32[]{:S(2)}) collective-permute-start(bf16[256,1152]{1,0:T(8,128)(2,1)} %pad_maximum_fusion.2), channel_id=1, source_target_pairs={{0,64},{64,0},{128,192},{192,128},{1,65},{65,1},{129,193},{193,129... | collective-permute-start | bytes 1769480 | tf_op jit(solution)/shard_map/ppermute | solution.py:11
  11.0 53.6 %collective-permute-start.7 = (bf16[256,1152]{1,0:T(8,128)(2,1)}, bf16[256,1152]{1,0:T(8,128)(2,1)}, u32[]{:S(2)}, u32[]{:S(2)}) collective-permute-start(bf16[256,1152]{1,0:T(8,128)(2,1)} %pad_maximum_fusion.2), channel_id=1, source_target_pairs={{0,128},{64,192},{128,0},{192,64},{1,129},{65,193},{129,1},{193,65... | collective-permute-start | bytes 1769480 | tf_op jit(solution)/shard_map/ppermute | solution.py:11
  13.9 52.4 %collective-permute-start.8 = (bf16[256,1152]{1,0:T(8,128)(2,1)}, bf16[256,1152]{1,0:T(8,128)(2,1)}, u32[]{:S(2)}, u32[]{:S(2)}) collective-permute-start(bf16[256,1152]{1,0:T(8,128)(2,1)} %pad_maximum_fusion.2), channel_id=1, source_target_pairs={{0,16},{16,0},{32,48},{48,32},{1,17},{17,1},{33,49},{49,33},{2,18}... | collective-permute-start | bytes 1769480 | tf_op jit(solution)/shard_map/ppermute | solution.py:11
  17.2 5.7 %collective-permute-start = (s32[128]{0:T(128)S(1)}, s32[128]{0:T(128)S(1)}, u32[]{:S(2)}, u32[]{:S(2)}) collective-permute-start(s32[128]{0:T(128)S(1)} %bitcast.79), channel_id=1, source_target_pairs={{0,8},{8,0},{1,9},{9,1},{2,10},{10,2},{3,11},{11,3},{4,12},{12,4},... | collective-permute-start | bytes 1544 | tf_op jit(solution)/shard_map/ppermute | solution.py:11
  17.3 1.8 copy-start.1
  17.3 1.8 copy-start.7
  22.8 15.1 %collective-permute-start.1 = (s32[128]{0:T(128)S(1)}, s32[128]{0:T(128)S(1)}, u32[]{:S(2)}, u32[]{:S(2)}) collective-permute-start(s32[128]{0:T(128)S(1)} %bitcast.80), channel_id=1, source_target_pairs={{0,64},{64,0},{128,192},{192,128},{1,65},{65,1},{129,193},{193,129... | collective-permute-start | bytes 1544 | tf_op jit(solution)/shard_map/ppermute | solution.py:11
  37.9 5.0 %collective-permute-start.2 = (s32[128]{0:T(128)S(1)}, s32[128]{0:T(128)S(1)}, u32[]{:S(2)}, u32[]{:S(2)}) collective-permute-start(s32[128]{0:T(128)S(1)} %bitcast.81), channel_id=1, source_target_pairs={{0,128},{64,192},{128,0},{192,64},{1,129},{65,193},{129,1},{193,65... | collective-permute-start | bytes 1544 | tf_op jit(solution)/shard_map/ppermute | solution.py:11
  43.0 4.8 %collective-permute-start.3 = (s32[128]{0:T(128)S(1)}, s32[128]{0:T(128)S(1)}, u32[]{:S(2)}, u32[]{:S(2)}) collective-permute-start(s32[128]{0:T(128)S(1)} %bitcast.82), channel_id=1, source_target_pairs={{0,16},{16,0},{32,48},{48,32},{1,17},{17,1},{33,49},{49,33},{2,18}... | collective-permute-start | bytes 1544 | tf_op jit(solution)/shard_map/ppermute | solution.py:11
  47.8 7.5 %collective-permute-start.4 = (s32[128]{0:T(128)S(1)}, s32[128]{0:T(128)S(1)}, u32[]{:S(2)}, u32[]{:S(2)}) collective-permute-start(s32[128]{0:T(128)S(1)} %bitcast.83), channel_id=1, source_target_pairs={{0,32},{16,48},{32,0},{48,16},{1,33},{17,49},{33,1},{49,17},{2,34}... | collective-permute-start | bytes 1544 | tf_op jit(solution)/shard_map/ppermute | solution.py:11
  55.3 43.4 %collective-permute-start.9 = (bf16[256,1152]{1,0:T(8,128)(2,1)}, bf16[256,1152]{1,0:T(8,128)(2,1)S(1)}, u32[]{:S(2)}, u32[]{:S(2)}) collective-permute-start(bf16[256,1152]{1,0:T(8,128)(2,1)} %pad_maximum_fusion.2), channel_id=1, source_target_pairs={{0,32},{16,48},{32,0},{48,16},{1,33},{17,49},{33,1},{49,17},{2,34}... | collective-permute-start | bytes 1769480 | tf_op jit(solution)/shard_map/ppermute | solution.py:11
  67.9 31.6 %copy-start.12 = (bf16[768,1152]{1,0:T(8,128)(2,1)S(1)}, bf16[768,1152]{1,0:T(8,128)(2,1)}, u32[]{:S(2)}) copy-start(bf16[768,1152]{1,0:T(8,128)(2,1)} %convert_dynamic-update-slice_fusion) | copy-start | bytes 5308420
  105.0 2.7 %copy-start.2 = (bf16[1152,1152]{1,0:T(8,128)(2,1)S(1)}, bf16[1152,1152]{1,0:T(8,128)(2,1)}, u32[]{:S(2)}) copy-start(bf16[1152,1152]{1,0:T(8,128)(2,1)} %param.16) | copy-start | bytes 7962628
  111.1 1.7 copy-start.9
  112.8 1.5 copy-start.10
  114.9 1.2 copy-start.11
  126.4 13.2 %all-to-all-start = ((bf16[8,304,128]{2,1,0:T(8,128)(2,1)}), bf16[8,304,128]{2,1,0:T(8,128)(2,1)S(1)}, u32[]{:S(2)}, u32[]{:S(2)}) async-start(bf16[8,304,128]{2,1,0:T(8,128)(2,1)} %pad_maximum_fusion.1), calls=%async_computation | async-start | bytes 1245184 | tf_op jit(solution)/shard_map/all_to_all | solution.py:100
  151.2 3.9 %copy-start.3 = (f32[16,2,36,288]{3,2,1,0:T(8,128)S(1)}, f32[16,2,36,288]{3,2,1,0:T(8,128)}, u32[]{:S(2)}) copy-start(f32[16,2,36,288]{3,2,1,0:T(8,128)} %reshape.199) | copy-start | bytes 3981316
  153.1 2.0 %collective-permute-start.10 = (bf16[16,37,288]{2,1,0:T(8,128)(2,1)S(1)}, bf16[16,37,288]{2,1,0:T(8,128)(2,1)S(1)}, u32[]{:S(2)}, u32[]{:S(2)}) collective-permute-start(bf16[16,37,288]{2,1,0:T(8,128)(2,1)S(1)} %pad_maximum_fusion.3), channel_id=1, source_target_pairs={{0,8},{8,0},{1,9},{9,1},{2,10},{10,2},{3,11},{11,3},{4,12},{12,4},... | collective-permute-start | bytes 1022984 | tf_op jit(solution)/shard_map/ppermute | solution.py:11
  (3 other events, 2.8 us)
Sparse Core Ops, SparseCore 0:
  17.3 90.3 all-gather.2

commit v2 on v1

v2 whole, which is shorter than its diff:
```python
import functools

import jax
import jax.numpy as jnp
from jax import lax
from jax.experimental import pallas as pl
from jax.experimental.pallas import tpu as pltpu
from jax.sharding import Mesh, PartitionSpec as P

EPSILON = 1e-06
LOSS = ("ly", "lz", "lc")
ROWS = 128
WIDTH = 1152
KEY_ROWS = 16
CHUNK = 36
SLOT = 40
COLS = 144
LANES = 128
TAIL = COLS - LANES
QUADS = 16
F32 = jnp.float32
BF16 = jnp.bfloat16

VMEM = pl.BlockSpec(memory_space=pltpu.VMEM)
SMEM = pl.BlockSpec(memory_space=pltpu.SMEM)


def params():
    return pltpu.CompilerParams(vmem_limit_bytes=40 * 2**20)


def cost(flops, moved):
    return pl.CostEstimate(flops=flops, bytes_accessed=moved, transcendentals=0)


def exchange(array, axis, apart):
    return lax.ppermute(array, axis, [(i, i ^ apart) for i in range(lax.axis_size(axis))])


def after(array, *others):
    return lax.optimization_barrier((array, *others))[0]


def nt(a, b):
    return lax.dot_general(a, b, (((1,), (1,)), ((), ())), preferred_element_type=F32)


def mm(a, b):
    return jnp.dot(a, b, preferred_element_type=F32)


def project_kernel(x_ref, w_ref, key_ref, out_ref, unit_ref, len_ref, acc):
    step = pl.program_id(0)

    @pl.when(step == 0)
    def _():
        acc[...] = jnp.zeros_like(acc)

    acc[...] += mm(x_ref[...], w_ref[...])

    @pl.when(step == pl.num_programs(0) - 1)
    def _():
        u = acc[...]
        length = jnp.sqrt(jnp.sum(u * u, axis=1, keepdims=True) + EPSILON)
        unit = u / length
        unit_ref[...] = unit
        out_ref[:ROWS, :] = unit.astype(BF16)
        out_ref[ROWS:, :] = key_ref[...]
        len_ref[...] = jnp.broadcast_to(length, len_ref.shape)


def project(x, w, keys):
    depth = 384
    return pl.pallas_call(
        project_kernel,
        grid=(WIDTH // depth,),
        in_specs=[
            pl.BlockSpec((ROWS, depth), lambda k: (0, k)),
            pl.BlockSpec((depth, WIDTH), lambda k: (k, 0)),
            pl.BlockSpec((KEY_ROWS, WIDTH), lambda k: (0, 0)),
        ],
        out_specs=[
            pl.BlockSpec((ROWS + KEY_ROWS, WIDTH), lambda k: (0, 0)),
            pl.BlockSpec((ROWS, WIDTH), lambda k: (0, 0)),
            pl.BlockSpec((ROWS, LANES), lambda k: (0, 0)),
        ],
        out_shape=[
            jax.ShapeDtypeStruct((ROWS + KEY_ROWS, WIDTH), BF16),
            jax.ShapeDtypeStruct((ROWS, WIDTH), F32),
            jax.ShapeDtypeStruct((ROWS, LANES), F32),
        ],
        scratch_shapes=[pltpu.VMEM((ROWS, WIDTH), F32)],
        compiler_params=params(),
        cost_estimate=cost(2 * ROWS * WIDTH * WIDTH, 4 * 2**20),
    )(x, w, keys)


def tile_kernel(with_stats, ways, scal, own, unit, length, own_key, *refs):
    blocks, out = refs[:-1], refs[-1]
    heat, shift = scal[0], scal[1]
    mine = own[:ROWS, :]
    key_col = own_key[:, :1]
    total = jnp.zeros((ROWS, WIDTH), F32)
    loss_acc = jnp.zeros((ROWS, ROWS), F32)
    heat_acc = jnp.zeros((ROWS, ROWS), F32)
    grad_acc = jnp.zeros((ROWS, ROWS), F32)
    for block in blocks:
        vec = block[:ROWS, :]
        keys = block[ROWS:, :LANES].astype(F32)
        key_row = keys[0:1] * 128.0 + keys[1:2]
        same = key_col == key_row
        sim = nt(mine, vec)
        logits = heat * sim + shift
        z = jnp.where(same, -logits, logits)
        t = jnp.exp(-jnp.abs(z))
        q = 1.0 / (1.0 + t)
        sig = jnp.where(z >= 0, q, t * q)
        g = jnp.where(same, -sig, sig) * (1.0 / ROWS)
        total += mm(g.astype(BF16), vec)
        if with_stats:
            loss_acc += jnp.maximum(z, 0.0) + jnp.log1p(t)
            heat_acc += g * sim
            grad_acc += g
    total = total * heat
    u = unit[...]
    inner = jnp.sum(u * total, axis=1, keepdims=True)
    du = (total - u * inner) / length[:, :1]
    flipped = du.T.astype(BF16)
    for w in range(ways):
        for h in range(2):
            start = h * ways * COLS + w * COLS
            out[w, h * COLS : (h + 1) * COLS, :] = flipped[start : start + COLS]
    if with_stats:
        def full(x):
            return jnp.sum(jnp.sum(x, axis=1, keepdims=True), axis=0, keepdims=True)

        lane = lax.broadcasted_iota(jnp.int32, (KEY_ROWS, LANES), 1)
        row = lax.broadcasted_iota(jnp.int32, (KEY_ROWS, LANES), 0)
        kind = lane % 3
        value = jnp.where(
            kind == 0,
            full(loss_acc) * (1.0 / ROWS),
            jnp.where(kind == 1, full(heat_acc) * heat, full(grad_acc)),
        )
        value = jnp.where((row == 0) & (lane < 9), value, 0.0)
        high = value.astype(BF16).astype(F32)
        middle = (value - high).astype(BF16).astype(F32)
        low = value - high - middle
        parts = jnp.where(lane < 3, high, jnp.where(lane < 6, middle, low)).astype(BF16)
        for w in range(ways):
            out[w, 2 * COLS :, :] = parts


def tiles(with_stats, ways, scal, own, unit, length, own_key, blocks):
    rows = 2 * COLS + (KEY_ROWS if with_stats else 0)
    return pl.pallas_call(
        functools.partial(tile_kernel, with_stats, ways),
        in_specs=[SMEM] + [VMEM] * (4 + len(blocks)),
        out_specs=VMEM,
        out_shape=jax.ShapeDtypeStruct((ways, rows, ROWS), BF16),
        compiler_params=params(),
        cost_estimate=cost(4 * 6 * ROWS * ROWS * WIDTH, 8 * 2**20),
    )(scal, own, unit, length, own_key, *blocks)


def head_kernel(with_stats, core, feat, spread, kept, given):
    ways = feat.shape[0]
    total = jnp.zeros((2 * COLS, feat.shape[2]), F32)
    for w in range(ways):
        total += mm(spread[w, : 2 * COLS, :], feat[w])
    half = QUADS * SLOT
    kept[...] = jnp.zeros_like(kept)
    given[...] = jnp.zeros_like(given)
    for h in range(2):
        main = total[h * COLS : h * COLS + LANES, :].T
        rest = total[h * COLS + LANES : (h + 1) * COLS, :]
        for side, out in enumerate((kept, given)):
            for m in range(QUADS):
                start = side * half + m * SLOT
                out[2 * m + h, :SLOT, :] = main[start : start + SLOT].astype(BF16)
                out[2 * m + h, 48:, :SLOT] = rest[:, start : start + SLOT].astype(BF16)
    if with_stats:
        parts = jnp.zeros((KEY_ROWS, LANES), F32)
        for w in range(ways):
            parts += spread[w, 2 * COLS :, :].astype(F32)
        lane = lax.broadcasted_iota(jnp.int32, (8, LANES), 1)
        row = lax.broadcasted_iota(jnp.int32, (8, LANES), 0)
        sums = parts[0:1]
        summed = jnp.zeros((8, LANES), F32)
        for k in range(3):
            number = jnp.sum(
                jnp.where((lane[:1] % 3 == k) & (lane[:1] < 9), sums, 0.0), axis=1, keepdims=True
            )
            summed = jnp.where(lane % 3 == k, number, summed)
        value = jnp.where((row == core[0]) & (lane < 9), summed, 0.0)
        high = value.astype(BF16).astype(F32)
        middle = (value - high).astype(BF16).astype(F32)
        low = value - high - middle
        spare = jnp.where(lane < 3, high, jnp.where(lane < 6, middle, low)).astype(BF16)
        for m in range(2 * QUADS):
            kept[m, SLOT:48, :] = spare
            given[m, SLOT:48, :] = spare


def heads(with_stats, core, feat, spread):
    shape = jax.ShapeDtypeStruct((2 * QUADS, 64, LANES), BF16)
    return pl.pallas_call(
        functools.partial(head_kernel, with_stats),
        in_specs=[SMEM, VMEM, VMEM],
        out_specs=[VMEM, VMEM],
        out_shape=[shape, shape],
        compiler_params=params(),
        cost_estimate=cost(2 * feat.shape[0] * ROWS * 2 * COLS * feat.shape[2], 4 * 2**20),
    )(core, feat, spread)


def final_kernel(count, parts, out, stats):
    total = jnp.sum(parts[...].astype(F32), axis=0)
    out[:, :LANES] = total[:CHUNK]
    rest = total[48:, :].T
    out[:, LANES:] = rest[:CHUNK, :]
    lane = lax.broadcasted_iota(jnp.int32, (1, LANES), 1)
    row = total[SLOT : SLOT + 1] + total[SLOT + 1 : SLOT + 2]
    answer = jnp.zeros((1, LANES), F32)
    for k in range(3):
        number = jnp.sum(jnp.where((lane % 3 == k) & (lane < 9), row, 0.0), axis=1, keepdims=True)
        answer = jnp.where(lane == k, number, answer)
    stats[...] = answer * (1.0 / count)


def final(count, parts):
    return pl.pallas_call(
        functools.partial(final_kernel, count),
        in_specs=[VMEM],
        out_specs=[VMEM, VMEM],
        out_shape=[
            jax.ShapeDtypeStruct((CHUNK, COLS), F32),
            jax.ShapeDtypeStruct((1, LANES), F32),
        ],
        compiler_params=params(),
        cost_estimate=cost(2 * QUADS * 64 * LANES, 2**20),
    )(parts)


def body(pictures, sentences, keys, picture_weights, sentence_weights, heat_log, shift_value):
    ways = lax.axis_size("dx")
    core = lax.axis_index("lc")
    scal = jnp.stack([jnp.exp(heat_log[0]), shift_value[0]])
    key = keys[0]
    key_rows = jnp.zeros((KEY_ROWS, WIDTH), BF16)
    key_rows = key_rows.at[0, :ROWS].set((key >> 7).astype(BF16))
    key_rows = key_rows.at[1, :ROWS].set((key & 127).astype(BF16))
    key_col = jnp.broadcast_to(key.astype(F32)[:, None], (ROWS, LANES))

    txt, txt_unit, txt_len = project(sentences[0], sentence_weights, key_rows)
    txt_a = exchange(txt, "lz", 1)
    txt_y2 = exchange(txt, "ly", 2)
    txt_y1 = exchange(txt, "ly", 1)
    txt_c = exchange(txt, "lc", 1)
    txt_b = exchange(txt_a, "lz", 3)

    img, img_unit, img_len = project(pictures[0], picture_weights, key_rows)
    img_a = exchange(after(img, txt_a), "lz", 1)
    img_n = after(img, txt_y1, txt_y2)
    img_y2 = exchange(img_n, "ly", 2)
    img_y1 = exchange(img_n, "ly", 1)
    img_c = exchange(img_n, "lc", 1)
    img_b = exchange(img_a, "lz", 3)

    slot = lax.broadcasted_iota(jnp.int32, (1, 2 * QUADS * SLOT), 1)
    side, place = slot // (QUADS * SLOT), slot % (QUADS * SLOT)
    chunk = 2 * (place // SLOT) + jnp.where(core == 0, side, 1 - side)
    within = place % SLOT
    source = jnp.where(within < CHUNK, chunk * CHUNK + within, -1)
    order = (lax.broadcasted_iota(jnp.int32, (WIDTH, 1), 0) == source).astype(BF16)
    img_feat = lax.all_gather(mm(pictures[0], order).astype(BF16), "dx", axis=0)
    txt_feat = lax.all_gather(mm(sentences[0], order).astype(BF16), "dx", axis=0)

    count = 2 * QUADS * lax.axis_size("dz") * ways
    core_ref = core.astype(jnp.int32)[None]

    def tail(with_stats, own, unit, length, blocks, feat):
        spread = tiles(with_stats, ways, scal, own, unit, length, key_col, blocks)
        spread = lax.all_to_all(spread, "dx", 0, 0, tiled=True)
        kept, given = heads(with_stats, core_ref, feat, spread)
        taken = exchange(given, "lc", 1)
        sums = (kept.astype(F32) + taken.astype(F32)).astype(BF16)
        sums = lax.all_to_all(sums, ("ly", "lz", "dz"), 0, 0, tiled=True)
        return final(count, sums)

    grad_img, stats = tail(
        True, img, img_unit, img_len, [txt, txt_c, txt_y1, txt_y2, txt_a, txt_b], img_feat
    )
    grad_txt, _ = tail(
        False, txt, txt_unit, txt_len, [img, img_c, img_y1, img_y2, img_a, img_b], txt_feat
    )
    return grad_img, grad_txt, stats[0, :3]


def solution(mesh):
    split = Mesh(mesh.devices.reshape(4, 4, 2, 2, 4), ("ly", "lz", "lc", "dz", "dx"))
    dp = ("dz", "dx")
    return jax.shard_map(
        body,
        mesh=split,
        in_specs=(P(dp, LOSS, None), P(dp, LOSS, None), P(dp, LOSS), P(), P(), P(), P()),
        out_specs=(P(LOSS, dp), P(LOSS, dp), P()),
        check_vma=False,
    )
```

time: 193 us -> 161 us (0.83)
  blocking collectives: 28.2 us -> 0 us
  matrix products: 28 us -> 4.46 us
  waiting for transfers between devices: 60.1 us -> 77.6 us
  Pallas kernels: 0 us -> 15.2 us
  other arithmetic: 14.4 us -> 2.08 us
  starting transfers between devices: 32 us -> 38.7 us
  local copies, waits for them, and re-layouts: 12.9 us -> 6.42 us
    all_to_all x1 -> x4, waiting for transfers between devices: 7.76 us -> 39.9 us  [the longest x2 24.9 us: tail(): sums = lax.all_to_all(sums, ('ly', 'lz', 'dz'), 0, 0, tiled=True)]
    all_to_all x1 -> x0, blocking collectives: 28.2 us -> none  [body(): kept = lax.all_to_all(kept, ('ly', 'lz'), 0, 0, tiled=True)]
    dot_general x17 -> x2, matrix products: 28 us -> 4.46 us  [mm(): return jnp.dot(a, b, preferred_element_type=F32)]
    pallas_call x0 -> x8, Pallas kernels: none -> 15.2 us  [the longest x2 7.72 us: tiles(): pl.pallas_call(functools.partial(tile_kernel, with_stats, ways), in_specs...]
    ppermute x11 -> x12, waiting for transfers between devices: 52.3 us -> 37.7 us  [exchange(): lax.ppermute(array, axis, [(i, i ^ apart) for i in range(lax.axis_size(ax...]
    all_to_all x1 -> x4, starting transfers between devices: 5.47 us -> 19.2 us  [the longest x2 11.1 us: tail(): sums = lax.all_to_all(sums, ('ly', 'lz', 'dz'), 0, 0, tiled=True)]
    ppermute x11 -> x12, starting transfers between devices: 26.5 us -> 19.4 us  [exchange(): lax.ppermute(array, axis, [(i, i ^ apart) for i in range(lax.axis_size(ax...]
    concatenate x7 -> x0, other arithmetic: 4.59 us -> none  [the longest x1 2.13 us: body(): own = jnp.concatenate([pictures[0], sentences[0]], axis=0)]
  transfers between devices with their start and end apart: 13 -> 18, of which waited for: 7 -> 10; matrix products, arithmetic and copies ran while one was open for 18% -> 5% of each run, Pallas kernels for 0% -> 9%
where the time goes in v2:
time: 161 us; the launch traced here: 160 us
  waiting for transfers between devices  77.6 us (48%)
  starting transfers between devices  38.7 us (24%)
  between operations  15.6 us (10%)
  Pallas kernels  15.2 us (9%)
  local copies, waits for them, and re-layouts  6.42 us (4%)
  matrix products  4.46 us (3%)
  other arithmetic  2.08 us (1%)
    ppermute x12, waiting for transfers between devices, exchange(): lax.ppermute(array, axis, [(i, i ^ apart) for i in range(lax.axis_size(ax...  37.7 us
    all_to_all x2, waiting for transfers between devices, tail(): sums = lax.all_to_all(sums, ('ly', 'lz', 'dz'), 0, 0, tiled=True)  24.9 us
    ppermute x12, starting transfers between devices, exchange(): lax.ppermute(array, axis, [(i, i ^ apart) for i in range(lax.axis_size(ax...  19.4 us
    all_to_all x2, waiting for transfers between devices, tail(): spread = lax.all_to_all(spread, 'dx', 0, 0, tiled=True)  15 us
    all_to_all x2, starting transfers between devices, tail(): sums = lax.all_to_all(sums, ('ly', 'lz', 'dz'), 0, 0, tiled=True)  11.1 us
    all_to_all x2, starting transfers between devices, tail(): spread = lax.all_to_all(spread, 'dx', 0, 0, tiled=True)  8.12 us
    pallas_call x2, Pallas kernels, tiles(): pl.pallas_call(functools.partial(tile_kernel, with_stats, ways), in_specs...  7.72 us
    dot_general x2, matrix products, mm(): return jnp.dot(a, b, preferred_element_type=F32)  4.46 us
  transfers between devices with their start and end apart: 18, of which 10 were waited for; matrix products, arithmetic and copies ran while one was open for 5% of the time, Pallas kernels for 9%

profile of v2, /device:TPU:32, one launch (start us, length us, event | category | flops | bytes accessed | tf_op | source)
XLA Modules:
  0.0 160.1 jit_solution(15223689469440165035)
XLA Ops:
  7.3 2.7 %fusion.16 = bf16[128,1280]{0,1:T(8,128)(2,1)} fusion(s32[1280]{0:T(1024)S(1)} %fusion.22, bf16[1,128,1152]{2,1,0:T(8,128)(2,1)} %param.11), kind=kOutput, calls=%fused_computation.9 | convolution fusion | flops 380600320 | bytes 627712 | tf_op jit(solution)/shard_map/dot_general | solution.py:49
  10.1 1.7 %fusion.13 = bf16[128,1280]{0,1:T(8,128)(2,1)} fusion(s32[1280]{0:T(1024)S(1)} %fusion.22, bf16[1,128,1152]{2,1,0:T(8,128)(2,1)S(1)} %copy-done.4), kind=kOutput, calls=%fused_computation.8 | convolution fusion | flops 380600320 | bytes 627712 | tf_op jit(solution)/shard_map/dot_general | solution.py:49
  14.1 3.3 %collective-permute-start.3 = (bf16[144,1152]{1,0:T(8,128)(2,1)S(1)}, bf16[144,1152]{1,0:T(8,128)(2,1)S(1)}, u32[]{:S(2)}, u32[]{:S(2)}) collective-permute-start(bf16[144,1152]{1,0:T(8,128)(2,1)S(1)} %get-tuple-element.45.refs_0_.own), channel_id=1, source_target_pairs={{0,16},{16,0},{32,48},{48,32},{1,17},{17,1},{33,49},{49,33},{2,18}... | collective-permute-start | bytes 995336 | tf_op jit(solution)/shard_map/ppermute | solution.py:37
  18.9 2.9 %collective-permute-start.2 = (bf16[144,1152]{1,0:T(8,128)(2,1)S(1)}, bf16[144,1152]{1,0:T(8,128)(2,1)S(1)}, u32[]{:S(2)}, u32[]{:S(2)}) collective-permute-start(bf16[144,1152]{1,0:T(8,128)(2,1)S(1)} %get-tuple-element.45.refs_0_.own), channel_id=1, source_target_pairs={{0,128},{64,192},{128,0},{192,64},{1,129},{65,193},{129,1},{193,65... | collective-permute-start | bytes 995336 | tf_op jit(solution)/shard_map/ppermute | solution.py:37
  21.8 9.2 %collective-permute-done.3.refs_4_ = bf16[144,1152]{1,0:T(8,128)(2,1)S(1)} collective-permute-done((bf16[144,1152]{1,0:T(8,128)(2,1)S(1)}, bf16[144,1152]{1,0:T(8,128)(2,1)S(1)}, u32[]{:S(2)}, u32[]{:S(2)}) %collective-permute-start.3) | collective-permute-done | bytes 331808 | tf_op jit(solution)/shard_map/ppermute | solution.py:37
  31.1 6.0 %collective-permute-start.4 = (bf16[144,1152]{1,0:T(8,128)(2,1)S(1)}, bf16[144,1152]{1,0:T(8,128)(2,1)S(1)}, u32[]{:S(2)}, u32[]{:S(2)}) collective-permute-start(bf16[144,1152]{1,0:T(8,128)(2,1)S(1)} %collective-permute-done.3.refs_4_), channel_id=1, source_target_pairs={{0,48},{16,32},{32,16},{48,0},{1,49},{17,33},{33,17},{49,1},{2,50}... | collective-permute-start | bytes 995336 | tf_op jit(solution)/shard_map/ppermute | solution.py:37
  40.8 9.8 %collective-permute-done.4.refs_5_ = bf16[144,1152]{1,0:T(8,128)(2,1)S(1)} collective-permute-done((bf16[144,1152]{1,0:T(8,128)(2,1)S(1)}, bf16[144,1152]{1,0:T(8,128)(2,1)S(1)}, u32[]{:S(2)}, u32[]{:S(2)}) %collective-permute-start.4) | collective-permute-done | bytes 331808 | tf_op jit(solution)/shard_map/ppermute | solution.py:37
  50.7 3.7 %shard_map.96 = bf16[4,304,128]{2,1,0:T(8,128)(2,1)} custom-call(f32[2]{0:T(128)S(1)} %pad_maximum_fusion.scal, bf16[144,1152]{1,0:T(8,128)(2,1)S(1)} %get-tuple-element.52.own.refs_0_, f32[128,1152]{1,0:T(8,128)S(1)} %get-tuple-element.43.unit, f32[128,128]{1,0:T(8,128)S(1)} %get-tuple-element.44.length, f32[128,128]{1,0:T(8,128)S(1)} %broadcast_in_dim.7.own_key, ...), custom_call_target="tpu_custom_call" | custom-call | flops 452984832 | bytes 8388608 | tf_op jit(solution)/shard_map/pallas_call | solution.py:156
  54.5 4.4 %all-to-all-start = ((bf16[4,304,128]{2,1,0:T(8,128)(2,1)}), bf16[4,304,128]{2,1,0:T(8,128)(2,1)S(1)}, u32[]{:S(2)}, u32[]{:S(2)}) async-start(bf16[4,304,128]{2,1,0:T(8,128)(2,1)} %shard_map.96), calls=%async_computation | async-start | bytes 622592 | tf_op jit(solution)/shard_map/all_to_all | solution.py:284
  58.9 1.6 %copy.10 = bf16[512,1280]{1,0:T(8,128)(2,1)S(1)} copy(bf16[512,1280]{0,1:T(8,128)(2,1)} %all-gather.5.cloned.1.call-done) | data formatting | bytes 2621440 | tf_op jit(solution)/shard_map/all_gather | solution.py:276
  60.5 8.7 %all-to-all-done.spread = bf16[4,304,128]{2,1,0:T(8,128)(2,1)S(1)} async-done(((bf16[4,304,128]{2,1,0:T(8,128)(2,1)}), bf16[4,304,128]{2,1,0:T(8,128)(2,1)S(1)}, u32[]{:S(2)}, u32[]{:S(2)}) %all-to-all-start) | async-done | bytes 311328 | tf_op jit(solution)/shard_map/all_to_all | solution.py:284
  69.3 2.1 %shard_map.97 = (bf16[32,64,128]{2,1,0:T(8,128)(2,1)S(1)}, bf16[32,64,128]{2,1,0:T(8,128)(2,1)}) custom-call(s32[1]{0:T(128)} %bitcast.core, bf16[4,128,1280]{2,1,0:T(8,128)(2,1)S(1)} %bitcast.17, bf16[4,304,128]{2,1,0:T(8,128)(2,1)S(1)} %all-to-all-done.spread), custom_call_target="tpu_custom_call" | custom-call | flops 377487360 | bytes 4194304 | tf_op jit(solution)/shard_map/pallas_call | solution.py:207
  73.4 2.7 %collective-permute-start.8 = (bf16[144,1152]{1,0:T(8,128)(2,1)S(1)}, bf16[144,1152]{1,0:T(8,128)(2,1)S(1)}, u32[]{:S(2)}, u32[]{:S(2)}) collective-permute-start(bf16[144,1152]{1,0:T(8,128)(2,1)S(1)} %get-tuple-element.52.own.refs_0_), channel_id=1, source_target_pairs={{0,128},{64,192},{128,0},{192,64},{1,129},{65,193},{129,1},{193,65... | collective-permute-start | bytes 995336 | tf_op jit(solution)/shard_map/ppermute | solution.py:37
  76.9 5.7 %collective-permute-done.7.refs_2_ = bf16[144,1152]{1,0:T(8,128)(2,1)S(1)} collective-permute-done((bf16[144,1152]{1,0:T(8,128)(2,1)S(1)}, bf16[144,1152]{1,0:T(8,128)(2,1)S(1)}, u32[]{:S(2)}, u32[]{:S(2)}) %collective-permute-start.7) | collective-permute-done | bytes 331808 | tf_op jit(solution)/shard_map/ppermute | solution.py:37
  82.5 8.3 %collective-permute-done.8.refs_3_ = bf16[144,1152]{1,0:T(8,128)(2,1)S(1)} collective-permute-done((bf16[144,1152]{1,0:T(8,128)(2,1)S(1)}, bf16[144,1152]{1,0:T(8,128)(2,1)S(1)}, u32[]{:S(2)}, u32[]{:S(2)}) %collective-permute-start.8) | collective-permute-done | bytes 331808 | tf_op jit(solution)/shard_map/ppermute | solution.py:37
  90.9 2.7 %collective-permute-done.10.refs_5_ = bf16[144,1152]{1,0:T(8,128)(2,1)S(1)} collective-permute-done((bf16[144,1152]{1,0:T(8,128)(2,1)}, bf16[144,1152]{1,0:T(8,128)(2,1)S(1)}, u32[]{:S(2)}, u32[]{:S(2)}) %collective-permute-start.10) | collective-permute-done | bytes 331808 | tf_op jit(solution)/shard_map/ppermute | solution.py:37
  94.4 4.0 %shard_map.99 = bf16[4,288,128]{2,1,0:T(8,128)(2,1)} custom-call(f32[2]{0:T(128)S(1)} %pad_maximum_fusion.scal, bf16[144,1152]{1,0:T(8,128)(2,1)S(1)} %get-tuple-element.45.refs_0_.own, f32[128,1152]{1,0:T(8,128)S(1)} %copy-done.3, f32[128,128]{1,0:T(8,128)S(1)} %copy-done.7, f32[128,128]{1,0:T(8,128)S(1)} %broadcast_in_dim.7.own_key, ...), custom_call_target="tpu_custom_call" | custom-call | flops 452984832 | bytes 8388608 | tf_op jit(solution)/shard_map/pallas_call | solution.py:156
  98.4 3.7 %all-to-all-start.2 = ((bf16[4,288,128]{2,1,0:T(8,128)(2,1)}), bf16[4,288,128]{2,1,0:T(8,128)(2,1)S(1)}, u32[]{:S(2)}, u32[]{:S(2)}) async-start(bf16[4,288,128]{2,1,0:T(8,128)(2,1)} %shard_map.99), calls=%async_computation.2 | async-start | bytes 589824 | tf_op jit(solution)/shard_map/all_to_all | solution.py:284
  103.1 6.2 %all-to-all-done.2.spread = bf16[4,288,128]{2,1,0:T(8,128)(2,1)S(1)} async-done(((bf16[4,288,128]{2,1,0:T(8,128)(2,1)}), bf16[4,288,128]{2,1,0:T(8,128)(2,1)S(1)}, u32[]{:S(2)}, u32[]{:S(2)}) %all-to-all-start.2) | async-done | bytes 294944 | tf_op jit(solution)/shard_map/all_to_all | solution.py:284
  109.3 6.3 %all-to-all-start.1 = ((bf16[32,64,128]{2,1,0:T(8,128)(2,1)}), bf16[32,64,128]{2,1,0:T(8,128)(2,1)S(1)}, u32[]{:S(2)}, u32[]{:S(2)}) async-start(bf16[32,64,128]{2,1,0:T(8,128)(2,1)} %add_convert_fusion.1), calls=%async_computation.1 | async-start | bytes 1048576 | tf_op jit(solution)/shard_map/all_to_all | solution.py:288
  118.6 1.9 %collective-permute-done.11 = bf16[32,64,128]{2,1,0:T(8,128)(2,1)S(1)} collective-permute-done((bf16[32,64,128]{2,1,0:T(8,128)(2,1)S(1)}, bf16[32,64,128]{2,1,0:T(8,128)(2,1)S(1)}, u32[]{:S(2)}, u32[]{:S(2)}) %collective-permute-start.11) | collective-permute-done | bytes 524320 | tf_op jit(solution)/shard_map/ppermute | solution.py:37
  121.4 10.5 %all-to-all-done.1.parts = bf16[32,64,128]{2,1,0:T(8,128)(2,1)S(1)} async-done(((bf16[32,64,128]{2,1,0:T(8,128)(2,1)}), bf16[32,64,128]{2,1,0:T(8,128)(2,1)S(1)}, u32[]{:S(2)}, u32[]{:S(2)}) %all-to-all-start.1) | async-done | bytes 524320 | tf_op jit(solution)/shard_map/all_to_all | solution.py:288
  131.9 4.8 %all-to-all-start.3 = ((bf16[32,64,128]{2,1,0:T(8,128)(2,1)}), bf16[32,64,128]{2,1,0:T(8,128)(2,1)S(1)}, u32[]{:S(2)}, u32[]{:S(2)}) async-start(bf16[32,64,128]{2,1,0:T(8,128)(2,1)} %add_convert_fusion), calls=%async_computation.3 | async-start | bytes 1048576 | tf_op jit(solution)/shard_map/all_to_all | solution.py:288
  138.1 14.4 %all-to-all-done.3.parts = bf16[32,64,128]{2,1,0:T(8,128)(2,1)S(1)} async-done(((bf16[32,64,128]{2,1,0:T(8,128)(2,1)}), bf16[32,64,128]{2,1,0:T(8,128)(2,1)S(1)}, u32[]{:S(2)}, u32[]{:S(2)}) %all-to-all-start.3) | async-done | bytes 524320 | tf_op jit(solution)/shard_map/all_to_all | solution.py:288
  (53 shorter events, 16.9 us)
Async XLA Ops:
  7.2 51.8 %all-gather.5.cloned.1.call-start = ((), (), s32[]{:S(2)}) async-start(), calls=%async_computation.4 | async-start | bytes 1638400 | tf_op jit(solution)/shard_map/all_gather | solution.py:276
  7.2 2.9 %copy-start.4 = (bf16[1,128,1152]{2,1,0:T(8,128)(2,1)S(1)}, bf16[1,128,1152]{2,1,0:T(8,128)(2,1)}, u32[]{:S(2)}) copy-start(bf16[1,128,1152]{2,1,0:T(8,128)(2,1)} %param.12) | copy-start | bytes 884740
  10.0 1.8 %copy-start.8 = (s32[1,128]{1,0:T(1,128)S(1)}, s32[1,128]{1,0:T(1,128)}, u32[]{:S(2)}) copy-start(s32[1,128]{1,0:T(1,128)} %param.13) | copy-start | bytes 1540
  10.0 2.0 %copy-start = (bf16[1152,1152]{1,0:T(8,128)(2,1)S(1)}, bf16[1152,1152]{1,0:T(8,128)(2,1)}, u32[]{:S(2)}) copy-start(bf16[1152,1152]{1,0:T(8,128)(2,1)} %w_ref.3) | copy-start | bytes 7962628
  10.0 105.6 %all-gather.7.cloned.1.call-start = ((), (), s32[]{:S(2)}) async-start(), calls=%async_computation.5 | async-start | bytes 1638400 | tf_op jit(solution)/shard_map/all_gather | solution.py:277
  12.1 26.3 %copy-start.1 = (bf16[1152,1152]{1,0:T(8,128)(2,1)S(1)}, bf16[1152,1152]{1,0:T(8,128)(2,1)}, u32[]{:S(2)}) copy-start(bf16[1152,1152]{1,0:T(8,128)(2,1)} %w_ref.2) | copy-start | bytes 7962628
  14.1 36.6 %copy-start.2 = (f32[128,1152]{1,0:T(8,128)}, f32[128,1152]{1,0:T(8,128)S(1)}, u32[]{:S(2)}) copy-start(f32[128,1152]{1,0:T(8,128)S(1)} %get-tuple-element.49.unit) | copy-start | bytes 1769476
  14.1 17.0 %collective-permute-start.3 = (bf16[144,1152]{1,0:T(8,128)(2,1)S(1)}, bf16[144,1152]{1,0:T(8,128)(2,1)S(1)}, u32[]{:S(2)}, u32[]{:S(2)}) collective-permute-start(bf16[144,1152]{1,0:T(8,128)(2,1)S(1)} %get-tuple-element.45.refs_0_.own), channel_id=1, source_target_pairs={{0,16},{16,0},{32,48},{48,32},{1,17},{17,1},{33,49},{49,33},{2,18}... | collective-permute-start | bytes 995336 | tf_op jit(solution)/shard_map/ppermute | solution.py:37
  17.3 23.5 %collective-permute-start.1 = (bf16[144,1152]{1,0:T(8,128)(2,1)S(1)}, bf16[144,1152]{1,0:T(8,128)(2,1)S(1)}, u32[]{:S(2)}, u32[]{:S(2)}) collective-permute-start(bf16[144,1152]{1,0:T(8,128)(2,1)S(1)} %get-tuple-element.45.refs_0_.own), channel_id=1, source_target_pairs={{0,64},{64,0},{128,192},{192,128},{1,65},{65,1},{129,193},{193,129... | collective-permute-start | bytes 995336 | tf_op jit(solution)/shard_map/ppermute | solution.py:37
  18.9 21.9 %collective-permute-start.2 = (bf16[144,1152]{1,0:T(8,128)(2,1)S(1)}, bf16[144,1152]{1,0:T(8,128)(2,1)S(1)}, u32[]{:S(2)}, u32[]{:S(2)}) collective-permute-start(bf16[144,1152]{1,0:T(8,128)(2,1)S(1)} %get-tuple-element.45.refs_0_.own), channel_id=1, source_target_pairs={{0,128},{64,192},{128,0},{192,64},{1,129},{65,193},{129,1},{193,65... | collective-permute-start | bytes 995336 | tf_op jit(solution)/shard_map/ppermute | solution.py:37
  21.8 19.0 %collective-permute-start = (bf16[144,1152]{1,0:T(8,128)(2,1)S(1)}, bf16[144,1152]{1,0:T(8,128)(2,1)S(1)}, u32[]{:S(2)}, u32[]{:S(2)}) collective-permute-start(bf16[144,1152]{1,0:T(8,128)(2,1)S(1)} %get-tuple-element.45.refs_0_.own), channel_id=1, source_target_pairs={{0,8},{8,0},{1,9},{9,1},{2,10},{10,2},{3,11},{11,3},{4,12},{12,4},... | collective-permute-start | bytes 995336 | tf_op jit(solution)/shard_map/ppermute | solution.py:37
  31.1 19.6 %collective-permute-start.4 = (bf16[144,1152]{1,0:T(8,128)(2,1)S(1)}, bf16[144,1152]{1,0:T(8,128)(2,1)S(1)}, u32[]{:S(2)}, u32[]{:S(2)}) collective-permute-start(bf16[144,1152]{1,0:T(8,128)(2,1)S(1)} %collective-permute-done.3.refs_4_), channel_id=1, source_target_pairs={{0,48},{16,32},{32,16},{48,0},{1,49},{17,33},{33,17},{49,1},{2,50}... | collective-permute-start | bytes 995336 | tf_op jit(solution)/shard_map/ppermute | solution.py:37
  54.5 39.1 %copy-start.3 = (f32[128,1152]{1,0:T(8,128)S(1)}, f32[128,1152]{1,0:T(8,128)}, u32[]{:S(2)}) copy-start(f32[128,1152]{1,0:T(8,128)} %copy-done.2) | copy-start | bytes 1769476
  54.5 14.8 %all-to-all-start = ((bf16[4,304,128]{2,1,0:T(8,128)(2,1)}), bf16[4,304,128]{2,1,0:T(8,128)(2,1)S(1)}, u32[]{:S(2)}, u32[]{:S(2)}) async-start(bf16[4,304,128]{2,1,0:T(8,128)(2,1)} %shard_map.96), calls=%async_computation | async-start | bytes 622592 | tf_op jit(solution)/shard_map/all_to_all | solution.py:284
  58.9 17.2 %collective-permute-start.9 = (bf16[144,1152]{1,0:T(8,128)(2,1)S(1)}, bf16[144,1152]{1,0:T(8,128)(2,1)}, u32[]{:S(2)}, u32[]{:S(2)}) collective-permute-start(bf16[144,1152]{1,0:T(8,128)(2,1)S(1)} %get-tuple-element.52.own.refs_0_), channel_id=1, source_target_pairs={{0,16},{16,0},{32,48},{48,32},{1,17},{17,1},{33,49},{49,33},{2,18}... | collective-permute-start | bytes 995336 | tf_op jit(solution)/shard_map/ppermute | solution.py:37
  71.4 30.7 %collective-permute-start.5 = (bf16[32,64,128]{2,1,0:T(8,128)(2,1)}, bf16[32,64,128]{2,1,0:T(8,128)(2,1)S(1)}, u32[]{:S(2)}, u32[]{:S(2)}) collective-permute-start(bf16[32,64,128]{2,1,0:T(8,128)(2,1)} %get-tuple-element.47), channel_id=1, source_target_pairs={{0,8},{8,0},{1,9},{9,1},{2,10},{10,2},{3,11},{11,3},{4,12},{12,4},... | collective-permute-start | bytes 1572872 | tf_op jit(solution)/shard_map/ppermute | solution.py:37
  71.4 5.5 %collective-permute-start.6 = (bf16[144,1152]{1,0:T(8,128)(2,1)S(1)}, bf16[144,1152]{1,0:T(8,128)(2,1)S(1)}, u32[]{:S(2)}, u32[]{:S(2)}) collective-permute-start(bf16[144,1152]{1,0:T(8,128)(2,1)S(1)} %get-tuple-element.52.own.refs_0_), channel_id=1, source_target_pairs={{0,8},{8,0},{1,9},{9,1},{2,10},{10,2},{3,11},{11,3},{4,12},{12,4},... | collective-permute-start | bytes 995336 | tf_op jit(solution)/shard_map/ppermute | solution.py:37
  71.9 10.7 %collective-permute-start.7 = (bf16[144,1152]{1,0:T(8,128)(2,1)S(1)}, bf16[144,1152]{1,0:T(8,128)(2,1)S(1)}, u32[]{:S(2)}, u32[]{:S(2)}) collective-permute-start(bf16[144,1152]{1,0:T(8,128)(2,1)S(1)} %get-tuple-element.52.own.refs_0_), channel_id=1, source_target_pairs={{0,64},{64,0},{128,192},{192,128},{1,65},{65,1},{129,193},{193,129... | collective-permute-start | bytes 995336 | tf_op jit(solution)/shard_map/ppermute | solution.py:37
  73.4 17.5 %collective-permute-start.8 = (bf16[144,1152]{1,0:T(8,128)(2,1)S(1)}, bf16[144,1152]{1,0:T(8,128)(2,1)S(1)}, u32[]{:S(2)}, u32[]{:S(2)}) collective-permute-start(bf16[144,1152]{1,0:T(8,128)(2,1)S(1)} %get-tuple-element.52.own.refs_0_), channel_id=1, source_target_pairs={{0,128},{64,192},{128,0},{192,64},{1,129},{65,193},{129,1},{193,65... | collective-permute-start | bytes 995336 | tf_op jit(solution)/shard_map/ppermute | solution.py:37
  76.1 17.5 %collective-permute-start.10 = (bf16[144,1152]{1,0:T(8,128)(2,1)}, bf16[144,1152]{1,0:T(8,128)(2,1)S(1)}, u32[]{:S(2)}, u32[]{:S(2)}) collective-permute-start(bf16[144,1152]{1,0:T(8,128)(2,1)} %collective-permute-done.9.refs_4_), channel_id=1, source_target_pairs={{0,48},{16,32},{32,16},{48,0},{1,49},{17,33},{33,17},{49,1},{2,50}... | collective-permute-start | bytes 995336 | tf_op jit(solution)/shard_map/ppermute | solution.py:37
  98.4 10.9 %all-to-all-start.2 = ((bf16[4,288,128]{2,1,0:T(8,128)(2,1)}), bf16[4,288,128]{2,1,0:T(8,128)(2,1)S(1)}, u32[]{:S(2)}, u32[]{:S(2)}) async-start(bf16[4,288,128]{2,1,0:T(8,128)(2,1)} %shard_map.99), calls=%async_computation.2 | async-start | bytes 589824 | tf_op jit(solution)/shard_map/all_to_all | solution.py:284
  109.3 22.6 %all-to-all-start.1 = ((bf16[32,64,128]{2,1,0:T(8,128)(2,1)}), bf16[32,64,128]{2,1,0:T(8,128)(2,1)S(1)}, u32[]{:S(2)}, u32[]{:S(2)}) async-start(bf16[32,64,128]{2,1,0:T(8,128)(2,1)} %add_convert_fusion.1), calls=%async_computation.1 | async-start | bytes 1048576 | tf_op jit(solution)/shard_map/all_to_all | solution.py:288
  118.5 2.0 %collective-permute-start.11 = (bf16[32,64,128]{2,1,0:T(8,128)(2,1)S(1)}, bf16[32,64,128]{2,1,0:T(8,128)(2,1)S(1)}, u32[]{:S(2)}, u32[]{:S(2)}) collective-permute-start(bf16[32,64,128]{2,1,0:T(8,128)(2,1)S(1)} %get-tuple-element.54), channel_id=1, source_target_pairs={{0,8},{8,0},{1,9},{9,1},{2,10},{10,2},{3,11},{11,3},{4,12},{12,4},... | collective-permute-start | bytes 1572872 | tf_op jit(solution)/shard_map/ppermute | solution.py:37
  131.9 20.5 %all-to-all-start.3 = ((bf16[32,64,128]{2,1,0:T(8,128)(2,1)}), bf16[32,64,128]{2,1,0:T(8,128)(2,1)S(1)}, u32[]{:S(2)}, u32[]{:S(2)}) async-start(bf16[32,64,128]{2,1,0:T(8,128)(2,1)} %add_convert_fusion), calls=%async_computation.3 | async-start | bytes 1048576 | tf_op jit(solution)/shard_map/all_to_all | solution.py:288
  (3 other events, 2.4 us)
Sparse Core Ops, SparseCore 0:
  10.1 33.1 all-gather.4
  45.1 33.8 all-gather.6

commit v3 on v2

v3 whole, which is shorter than its diff:
```python
import functools

import jax
import jax.numpy as jnp
from jax import lax
from jax.experimental import pallas as pl
from jax.experimental.pallas import tpu as pltpu
from jax.sharding import Mesh, PartitionSpec as P

EPSILON = 1e-06
LOSS = ("ly", "lz", "lc")
ROWS = 128
WIDTH = 1152
KEY_ROWS = 16
CHUNK = 36
SLOT = 40
COLS = 144
LANES = 128
TAIL = COLS - LANES
QUADS = 16
STATS = 112
F32 = jnp.float32
BF16 = jnp.bfloat16

VMEM = pl.BlockSpec(memory_space=pltpu.VMEM)
SMEM = pl.BlockSpec(memory_space=pltpu.SMEM)


def params():
    return pltpu.CompilerParams(vmem_limit_bytes=40 * 2**20)


def cost(flops, moved):
    return pl.CostEstimate(flops=flops, bytes_accessed=moved, transcendentals=0)


def exchange(array, axis, apart):
    return lax.ppermute(array, axis, [(i, i ^ apart) for i in range(lax.axis_size(axis))])


def after(array, *others):
    return lax.optimization_barrier((array, *others))[0]


def nt(a, b):
    return lax.dot_general(a, b, (((1,), (1,)), ((), ())), preferred_element_type=F32)


def mm(a, b):
    return jnp.dot(a, b, preferred_element_type=F32)


def project_kernel(x_ref, w_ref, key_ref, out_ref, unit_ref, len_ref, acc):
    step = pl.program_id(0)

    @pl.when(step == 0)
    def _():
        acc[...] = jnp.zeros_like(acc)

    acc[...] += mm(x_ref[...], w_ref[...])

    @pl.when(step == pl.num_programs(0) - 1)
    def _():
        u = acc[...]
        length = jnp.sqrt(jnp.sum(u * u, axis=1, keepdims=True) + EPSILON)
        unit = u / length
        unit_ref[...] = unit
        out_ref[:ROWS, :] = unit.astype(BF16)
        key = jnp.broadcast_to(key_ref[...], (KEY_ROWS, ROWS))
        row = lax.broadcasted_iota(jnp.int32, (KEY_ROWS, ROWS), 0)
        digits = jnp.where(row == 0, key >> 7, jnp.where(row == 1, key & 127, 0))
        out_ref[ROWS:, :] = jnp.zeros((KEY_ROWS, WIDTH), BF16)
        out_ref[ROWS:, :ROWS] = digits.astype(F32).astype(BF16)
        len_ref[...] = jnp.broadcast_to(length, len_ref.shape)


def project(x, w, keys):
    depth = 384
    return pl.pallas_call(
        project_kernel,
        grid=(WIDTH // depth,),
        in_specs=[
            pl.BlockSpec((ROWS, depth), lambda k: (0, k)),
            pl.BlockSpec((depth, WIDTH), lambda k: (k, 0)),
            pl.BlockSpec((1, ROWS), lambda k: (0, 0)),
        ],
        out_specs=[
            pl.BlockSpec((ROWS + KEY_ROWS, WIDTH), lambda k: (0, 0)),
            pl.BlockSpec((ROWS, WIDTH), lambda k: (0, 0)),
            pl.BlockSpec((ROWS, LANES), lambda k: (0, 0)),
        ],
        out_shape=[
            jax.ShapeDtypeStruct((ROWS + KEY_ROWS, WIDTH), BF16),
            jax.ShapeDtypeStruct((ROWS, WIDTH), F32),
            jax.ShapeDtypeStruct((ROWS, LANES), F32),
        ],
        scratch_shapes=[pltpu.VMEM((ROWS, WIDTH), F32)],
        compiler_params=params(),
        cost_estimate=cost(2 * ROWS * WIDTH * WIDTH, 4 * 2**20),
    )(x, w, keys)


def tile_kernel(with_stats, ways, spot, scal, own, unit, length, own_key, *refs):
    blocks, outs, held = refs[: -ways - 1], refs[-ways - 1 : -1], refs[-1]
    heat, shift = scal[0], scal[1]
    mine = own[:ROWS, :]
    key_col = own_key[:, :1]
    total = jnp.zeros((ROWS, WIDTH), F32)
    loss_acc = jnp.zeros((ROWS, ROWS), F32)
    heat_acc = jnp.zeros((ROWS, ROWS), F32)
    grad_acc = jnp.zeros((ROWS, ROWS), F32)
    for block in blocks:
        vec = block[:ROWS, :]
        keys = block[ROWS:, :LANES].astype(F32)
        key_row = keys[0:1] * 128.0 + keys[1:2]
        same = key_col == key_row
        sim = nt(mine, vec)
        logits = heat * sim + shift
        z = jnp.where(same, -logits, logits)
        t = jnp.exp(-jnp.abs(z))
        q = 1.0 / (1.0 + t)
        sig = jnp.where(z >= 0, q, t * q)
        g = jnp.where(same, -sig, sig) * (1.0 / ROWS)
        total += mm(g.astype(BF16), vec)
        if with_stats:
            loss_acc += jnp.maximum(z, 0.0) + jnp.log1p(t)
            heat_acc += g * sim
            grad_acc += g
    total = total * heat
    u = unit[...]
    inner = jnp.sum(u * total, axis=1, keepdims=True)
    du = (total - u * inner) / length[:, :1]
    held[...] = du.T.astype(BF16).reshape(held.shape)
    for step, out in enumerate(outs):
        w = lax.rem(spot[0] + step, ways)
        for h in range(2):
            out[h * COLS : (h + 1) * COLS, :] = held[h * ways + w]
    if with_stats:
        def full(x):
            return jnp.sum(jnp.sum(x, axis=1, keepdims=True), axis=0, keepdims=True)

        lane = lax.broadcasted_iota(jnp.int32, (KEY_ROWS, LANES), 1)
        row = lax.broadcasted_iota(jnp.int32, (KEY_ROWS, LANES), 0)
        kind = lane % 3
        value = jnp.where(
            kind == 0,
            full(loss_acc) * (1.0 / ROWS),
            jnp.where(kind == 1, full(heat_acc) * heat, full(grad_acc)),
        )
        value = jnp.where((row == 0) & (lane < 9), value, 0.0)
        high = value.astype(BF16).astype(F32)
        middle = (value - high).astype(BF16).astype(F32)
        low = value - high - middle
        parts = jnp.where(lane < 3, high, jnp.where(lane < 6, middle, low)).astype(BF16)
        for out in outs:
            out[2 * COLS :, :] = parts


def tiles(with_stats, ways, spot, scal, own, unit, length, own_key, blocks):
    rows = 2 * COLS + (KEY_ROWS if with_stats else 0)
    return pl.pallas_call(
        functools.partial(tile_kernel, with_stats, ways),
        in_specs=[SMEM] * 2 + [VMEM] * (4 + len(blocks)),
        out_specs=[VMEM] * ways,
        out_shape=[jax.ShapeDtypeStruct((rows, ROWS), BF16)] * ways,
        scratch_shapes=[pltpu.VMEM((2 * ways, COLS, ROWS), BF16)],
        compiler_params=params(),
        cost_estimate=cost(4 * 6 * ROWS * ROWS * WIDTH, 8 * 2**20),
    )(spot, scal, own, unit, length, own_key, *blocks)


def head_kernel(with_stats, spot, feat, *refs):
    spreads, (kept, given, held) = refs[:-3], refs[-3:]
    ways = len(spreads)
    total = jnp.zeros((2 * COLS, feat.shape[1]), F32)
    for step, spread in enumerate(spreads):
        source = lax.rem(spot[0] + ways - step, ways)
        rows = feat[pl.ds(pl.multiple_of(source * ROWS, ROWS), ROWS), :]
        total += mm(spread[: 2 * COLS, :], rows)
    spare = None
    if with_stats:
        parts = jnp.zeros((KEY_ROWS, LANES), F32)
        for spread in spreads:
            parts += spread[2 * COLS :, :].astype(F32)
        lane = lax.broadcasted_iota(jnp.int32, (8, LANES), 1)
        row = lax.broadcasted_iota(jnp.int32, (8, LANES), 0)
        place = lane - STATS
        summed = jnp.zeros((8, LANES), F32)
        for k in range(3):
            number = jnp.sum(
                jnp.where((lane[:1] % 3 == k) & (lane[:1] < 9), parts[0:1], 0.0),
                axis=1,
                keepdims=True,
            )
            summed = jnp.where(place % 3 == k, number, summed)
        value = jnp.where((row == spot[1]) & (place >= 0) & (place < 9), summed, 0.0)
        high = value.astype(BF16).astype(F32)
        middle = (value - high).astype(BF16).astype(F32)
        low = value - high - middle
        spare = jnp.where(place < 3, high, jnp.where(place < 6, middle, low))
    for h in range(2):
        main = total[h * COLS : h * COLS + LANES, :].T
        rest = total[h * COLS + LANES : (h + 1) * COLS, :]
        for m in range(QUADS):
            for side in range(2):
                start = (2 * m + side) * CHUNK
                target = held.at[side, 2 * m + h]
                target[:CHUNK, :] = main[start : start + CHUNK]
                target[CHUNK:SLOT, :] = jnp.zeros((SLOT - CHUNK, LANES), F32)
                target[SLOT:, :] = jnp.zeros((8, LANES), F32) if spare is None else spare
                for k in range(2):
                    target[SLOT:, 64 * k : 64 * k + CHUNK] = rest[
                        8 * k : 8 * k + 8, start : start + CHUNK
                    ]
    kept[...] = held[spot[1]]
    given[...] = held[1 - spot[1]].astype(BF16)


def heads(with_stats, spot, feat, spreads):
    shape = (2 * QUADS, SLOT + 8, LANES)
    return pl.pallas_call(
        functools.partial(head_kernel, with_stats),
        in_specs=[SMEM] + [VMEM] * (1 + len(spreads)),
        out_specs=[VMEM, VMEM],
        out_shape=[jax.ShapeDtypeStruct(shape, F32), jax.ShapeDtypeStruct(shape, BF16)],
        scratch_shapes=[pltpu.VMEM((2, *shape), F32)],
        compiler_params=params(),
        cost_estimate=cost(2 * 4 * ROWS * 2 * COLS * feat.shape[1], 4 * 2**20),
    )(spot, feat, *spreads)


def final_kernel(count, parts, out, stats):
    total = jnp.sum(parts[...].astype(F32), axis=0)
    out[:, :LANES] = total[:CHUNK]
    rest = total[SLOT:, :].T
    out[:, LANES : LANES + 8] = rest[:CHUNK]
    out[:, LANES + 8 :] = rest[64 : 64 + CHUNK]
    lane = lax.broadcasted_iota(jnp.int32, (1, LANES), 1)
    place = lane - STATS
    row = total[SLOT : SLOT + 1] + total[SLOT + 1 : SLOT + 2]
    answer = jnp.zeros((1, LANES), F32)
    for k in range(3):
        number = jnp.sum(
            jnp.where((place % 3 == k) & (place >= 0) & (place < 9), row, 0.0),
            axis=1,
            keepdims=True,
        )
        answer = jnp.where(lane == k, number, answer)
    stats[...] = answer * (1.0 / count)


def final(count, parts):
    return pl.pallas_call(
        functools.partial(final_kernel, count),
        in_specs=[VMEM],
        out_specs=[VMEM, VMEM],
        out_shape=[
            jax.ShapeDtypeStruct((CHUNK, COLS), F32),
            jax.ShapeDtypeStruct((1, LANES), F32),
        ],
        compiler_params=params(),
        cost_estimate=cost(2 * QUADS * 48 * LANES, 2**20),
    )(parts)


def body(pictures, sentences, keys, picture_weights, sentence_weights, heat_log, shift_value):
    ways = lax.axis_size("dx")
    core = lax.axis_index("lc")
    spot = jnp.stack([lax.axis_index("dx"), core]).astype(jnp.int32)
    scal = jnp.stack([jnp.exp(heat_log[0]), shift_value[0]])
    key_col = jnp.broadcast_to(keys[0].astype(F32)[:, None], (ROWS, LANES))

    txt, txt_unit, txt_len = project(sentences[0], sentence_weights, keys)
    txt_a = exchange(txt, "lz", 1)
    txt_y2 = exchange(txt, "ly", 2)
    txt_y1 = exchange(txt, "ly", 1)
    txt_c = exchange(txt, "lc", 1)
    txt_b = exchange(txt_a, "lz", 3)

    img_feat = lax.all_gather(pictures[0], "dx", axis=0, tiled=True)
    txt_feat = lax.all_gather(sentences[0], "dx", axis=0, tiled=True)
    img, img_unit, img_len = project(after(pictures[0], txt_c), picture_weights, keys)

    img_a = exchange(after(img, txt_a), "lz", 1)
    img_n = after(img, txt_y1, txt_y2)
    img_y2 = exchange(img_n, "ly", 2)
    img_y1 = exchange(img_n, "ly", 1)
    img_c = exchange(img_n, "lc", 1)
    img_b = exchange(img_a, "lz", 3)

    count = 2 * QUADS * lax.axis_size("dz") * ways

    def turn(array, step):
        return lax.ppermute(array, "dx", [(i, (i + step) % ways) for i in range(ways)])

    def columns(with_stats, own, unit, length, blocks):
        outs = tiles(with_stats, ways, spot, scal, own, unit, length, key_col, blocks)
        return [outs[0]] + [turn(out, step) for step, out in enumerate(outs) if step]

    def share(with_stats, feat, spreads):
        kept, given = heads(with_stats, spot, feat, spreads)
        taken = exchange(given, "lc", 1)
        return (kept + taken.astype(F32)).astype(BF16)

    def collect(sums):
        return final(count, lax.all_to_all(sums, ("ly", "lz", "dz"), 0, 0, tiled=True))

    img_blocks = list(
        lax.optimization_barrier(
            (txt, txt_c, txt_y1, txt_y2, txt_a, txt_b, img_a, img_c, img_y1, img_y2)
        )
    )[:6]
    img_cols = columns(True, img, img_unit, img_len, img_blocks)
    img_feat = after(img_feat, img_b)
    img_sums = share(True, img_feat, img_cols)
    txt_cols = columns(
        False, txt, txt_unit, txt_len, [img, img_c, img_y1, img_y2, img_a, img_b]
    )
    txt_sums = share(False, txt_feat, txt_cols)
    grad_img, stats = collect(img_sums)
    grad_txt, _ = collect(txt_sums)
    return grad_img, grad_txt, stats[0, :3]


def solution(mesh):
    split = Mesh(mesh.devices.reshape(4, 4, 2, 2, 4), ("ly", "lz", "lc", "dz", "dx"))
    dp = ("dz", "dx")
    return jax.shard_map(
        body,
        mesh=split,
        in_specs=(P(dp, LOSS, None), P(dp, LOSS, None), P(dp, LOSS), P(), P(), P(), P()),
        out_specs=(P(LOSS, dp), P(LOSS, dp), P()),
        check_vma=False,
    )
```

time: 161 us -> 144 us (0.89)
  waiting for transfers between devices: 77.6 us -> 43.3 us
  starting transfers between devices: 38.7 us -> 55.3 us
  local copies, waits for them, and re-layouts: 6.42 us -> 11.8 us
  matrix products: 4.46 us -> 0 us
    all_to_all x4 -> x2, waiting for transfers between devices: 39.9 us -> 21.9 us  [collect(): lax.all_to_all(sums, ('ly', 'lz', 'dz'), 0, 0, tiled=True)]
    ppermute x12, waiting for transfers between devices: 37.7 us -> 20.7 us  [exchange(): lax.ppermute(array, axis, [(i, i ^ apart) for i in range(lax.axis_size(ax...]
    ppermute x0 -> x6, starting transfers between devices: none -> 11.3 us  [turn(): lax.ppermute(array, 'dx', [(i, (i + step) % ways) for i in range(ways)])]
    unnamed x18 -> x28, local copies, waits for them, and re-layouts: 2.44 us -> 11.3 us
    ppermute x12, starting transfers between devices: 19.4 us -> 25 us  [exchange(): lax.ppermute(array, axis, [(i, i ^ apart) for i in range(lax.axis_size(ax...]
    dot_general x2 -> x0, matrix products: 4.46 us -> none  [mm(): return jnp.dot(a, b, preferred_element_type=F32)]
    all_gather x2 -> x0, local copies, waits for them, and re-layouts: 3.21 us -> none  [the longest x1 1.61 us: body(): img_feat = lax.all_gather(mm(pictures[0], order).astype(BF16), 'dx', axis=0)]
    all_to_all x4 -> x2, starting transfers between devices: 19.2 us -> 19 us  [collect(): lax.all_to_all(sums, ('ly', 'lz', 'dz'), 0, 0, tiled=True)]
  transfers between devices with their start and end apart: 18 -> 22, of which waited for: 10 -> 8; matrix products, arithmetic and copies ran while one was open for 5% -> 2% of each run, Pallas kernels for 9% -> 10%
where the time goes in v3:
time: 144 us; the launch traced here: 143 us
  starting transfers between devices  55.3 us (38%)
  waiting for transfers between devices  43.3 us (30%)
  between operations  15.6 us (11%)
  Pallas kernels  15.4 us (11%)
  local copies, waits for them, and re-layouts  11.8 us (8%)
  other arithmetic  1.82 us (1%)
    ppermute x12, starting transfers between devices, exchange(): lax.ppermute(array, axis, [(i, i ^ apart) for i in range(lax.axis_size(ax...  25 us
    all_to_all x2, waiting for transfers between devices, collect(): lax.all_to_all(sums, ('ly', 'lz', 'dz'), 0, 0, tiled=True)  21.9 us
    ppermute x12, waiting for transfers between devices, exchange(): lax.ppermute(array, axis, [(i, i ^ apart) for i in range(lax.axis_size(ax...  20.7 us
    all_to_all x2, starting transfers between devices, collect(): lax.all_to_all(sums, ('ly', 'lz', 'dz'), 0, 0, tiled=True)  19 us
    ppermute x6, starting transfers between devices, turn(): lax.ppermute(array, 'dx', [(i, (i + step) % ways) for i in range(ways)])  11.3 us
    unnamed x28, local copies, waits for them, and re-layouts  11.3 us
    pallas_call x2, Pallas kernels, tiles(): pl.pallas_call(functools.partial(tile_kernel, with_stats, ways), in_specs...  7.11 us
    pallas_call x2, Pallas kernels, heads(): pl.pallas_call(functools.partial(head_kernel, with_stats), in_specs=[SMEM...  4.02 us
  transfers between devices with their start and end apart: 22, of which 8 were waited for; matrix products, arithmetic and copies ran while one was open for 2% of the time, Pallas kernels for 10%

profile of v3, /device:TPU:32, one launch (start us, length us, event | category | flops | bytes accessed | tf_op | source)
XLA Modules:
  0.0 143.3 jit_solution(4597534775387556442)
XLA Ops:
  8.0 1.7 %copy-done = bf16[1152,1152]{1,0:T(8,128)(2,1)S(1)} copy-done((bf16[1152,1152]{1,0:T(8,128)(2,1)S(1)}, bf16[1152,1152]{1,0:T(8,128)(2,1)}, u32[]{:S(2)}) %copy-start) | copy-done | bytes 2654232
  13.5 3.3 %collective-permute-start.1 = (bf16[144,1152]{1,0:T(8,128)(2,1)S(1)}, bf16[144,1152]{1,0:T(8,128)(2,1)}, u32[]{:S(2)}, u32[]{:S(2)}) collective-permute-start(bf16[144,1152]{1,0:T(8,128)(2,1)S(1)} %get-tuple-element.42.refs_0_.own), channel_id=1, source_target_pairs={{0,16},{16,0},{32,48},{48,32},{1,17},{17,1},{33,49},{49,33},{2,18}... | collective-permute-start | bytes 995336 | tf_op jit(solution)/shard_map/ppermute | solution.py:38
  16.8 1.7 %collective-permute-start.4 = (bf16[144,1152]{1,0:T(8,128)(2,1)S(1)}, bf16[144,1152]{1,0:T(8,128)(2,1)}, u32[]{:S(2)}, u32[]{:S(2)}) collective-permute-start(bf16[144,1152]{1,0:T(8,128)(2,1)S(1)} %get-tuple-element.42.refs_0_.own), channel_id=1, source_target_pairs={{0,64},{64,0},{128,192},{192,128},{1,65},{65,1},{129,193},{193,129... | collective-permute-start | bytes 995336 | tf_op jit(solution)/shard_map/ppermute | solution.py:38
  18.5 2.9 %collective-permute-start.5 = (bf16[144,1152]{1,0:T(8,128)(2,1)S(1)}, bf16[144,1152]{1,0:T(8,128)(2,1)}, u32[]{:S(2)}, u32[]{:S(2)}) collective-permute-start(bf16[144,1152]{1,0:T(8,128)(2,1)S(1)} %get-tuple-element.42.refs_0_.own), channel_id=1, source_target_pairs={{0,128},{64,192},{128,0},{192,64},{1,129},{65,193},{129,1},{193,65... | collective-permute-start | bytes 995336 | tf_op jit(solution)/shard_map/ppermute | solution.py:38
  25.2 6.0 %collective-permute-done.1.refs_4_ = bf16[144,1152]{1,0:T(8,128)(2,1)} collective-permute-done((bf16[144,1152]{1,0:T(8,128)(2,1)S(1)}, bf16[144,1152]{1,0:T(8,128)(2,1)}, u32[]{:S(2)}, u32[]{:S(2)}) %collective-permute-start.1) | collective-permute-done | bytes 331808 | tf_op jit(solution)/shard_map/ppermute | solution.py:38
  31.2 3.5 %collective-permute-start.2 = (bf16[144,1152]{1,0:T(8,128)(2,1)S(1)}, bf16[144,1152]{1,0:T(8,128)(2,1)S(1)}, u32[]{:S(2)}, u32[]{:S(2)}) collective-permute-start(bf16[144,1152]{1,0:T(8,128)(2,1)S(1)} %get-tuple-element.41.own.refs_0_), channel_id=1, source_target_pairs={{0,16},{16,0},{32,48},{48,32},{1,17},{17,1},{33,49},{49,33},{2,18}... | collective-permute-start | bytes 995336 | tf_op jit(solution)/shard_map/ppermute | solution.py:38
  37.8 2.9 %collective-permute-start.9 = (bf16[144,1152]{1,0:T(8,128)(2,1)S(1)}, bf16[144,1152]{1,0:T(8,128)(2,1)S(1)}, u32[]{:S(2)}, u32[]{:S(2)}) collective-permute-start(bf16[144,1152]{1,0:T(8,128)(2,1)S(1)} %get-tuple-element.41.own.refs_0_), channel_id=1, source_target_pairs={{0,128},{64,192},{128,0},{192,64},{1,129},{65,193},{129,1},{193,65... | collective-permute-start | bytes 995336 | tf_op jit(solution)/shard_map/ppermute | solution.py:38
  40.7 2.6 %collective-permute-start.6 = (bf16[144,1152]{1,0:T(8,128)(2,1)}, bf16[144,1152]{1,0:T(8,128)(2,1)S(1)}, u32[]{:S(2)}, u32[]{:S(2)}) collective-permute-start(bf16[144,1152]{1,0:T(8,128)(2,1)} %collective-permute-done.1.refs_4_), channel_id=1, source_target_pairs={{0,48},{16,32},{32,16},{48,0},{1,49},{17,33},{33,17},{49,1},{2,50}... | collective-permute-start | bytes 995336 | tf_op jit(solution)/shard_map/ppermute | solution.py:38
  43.4 4.2 %collective-permute-done.2.refs_4_ = bf16[144,1152]{1,0:T(8,128)(2,1)S(1)} collective-permute-done((bf16[144,1152]{1,0:T(8,128)(2,1)S(1)}, bf16[144,1152]{1,0:T(8,128)(2,1)S(1)}, u32[]{:S(2)}, u32[]{:S(2)}) %collective-permute-start.2) | collective-permute-done | bytes 331808 | tf_op jit(solution)/shard_map/ppermute | solution.py:38
  47.5 6.5 %collective-permute-start.3 = (bf16[144,1152]{1,0:T(8,128)(2,1)S(1)}, bf16[144,1152]{1,0:T(8,128)(2,1)S(1)}, u32[]{:S(2)}, u32[]{:S(2)}) collective-permute-start(bf16[144,1152]{1,0:T(8,128)(2,1)S(1)} %collective-permute-done.2.refs_4_), channel_id=1, source_target_pairs={{0,48},{16,32},{32,16},{48,0},{1,49},{17,33},{33,17},{49,1},{2,50}... | collective-permute-start | bytes 995336 | tf_op jit(solution)/shard_map/ppermute | solution.py:38
  54.0 2.0 %collective-permute-done.6.refs_5_ = bf16[144,1152]{1,0:T(8,128)(2,1)S(1)} collective-permute-done((bf16[144,1152]{1,0:T(8,128)(2,1)}, bf16[144,1152]{1,0:T(8,128)(2,1)S(1)}, u32[]{:S(2)}, u32[]{:S(2)}) %collective-permute-start.6) | collective-permute-done | bytes 331808 | tf_op jit(solution)/shard_map/ppermute | solution.py:38
  58.2 4.3 %shard_map.96 = (bf16[304,128]{1,0:T(8,128)(2,1)S(1)}, bf16[304,128]{1,0:T(8,128)(2,1)}, bf16[304,128]{1,0:T(8,128)(2,1)}, bf16[304,128]{1,0:T(8,128)(2,1)S(1)}) custom-call(s32[2]{0:T(128)S(1)} %pad_add_fusion.spot, f32[2]{0:T(128)S(1)} %pad_maximum_fusion.scal, bf16[144,1152]{1,0:T(8,128)(2,1)S(1)} %get-tuple-element.41.own.refs_0_, ...), custom_call_target="tpu_custom_call" | custom-call | flops 452984832 | bytes 8388608 | tf_op jit(solution)/shard_map/pallas_call | solution.py:161
  63.8 2.8 %collective-permute-start.11 = (bf16[304,128]{1,0:T(8,128)(2,1)}, bf16[304,128]{1,0:T(8,128)(2,1)S(1)}, u32[]{:S(2)}, u32[]{:S(2)}) collective-permute-start(bf16[304,128]{1,0:T(8,128)(2,1)} %get-tuple-element.50), channel_id=1, source_target_pairs={{0,2},{1,3},{2,0},{3,1},{4,6},{5,7},{6,4},{7,5},{8,10},{9,11},{10,... | collective-permute-start | bytes 233480 | tf_op jit(solution)/shard_map/ppermute | solution.py:294
  68.0 6.4 %collective-permute-done.3.refs_5_ = bf16[144,1152]{1,0:T(8,128)(2,1)S(1)} collective-permute-done((bf16[144,1152]{1,0:T(8,128)(2,1)S(1)}, bf16[144,1152]{1,0:T(8,128)(2,1)S(1)}, u32[]{:S(2)}, u32[]{:S(2)}) %collective-permute-start.3) | collective-permute-done | bytes 331808 | tf_op jit(solution)/shard_map/ppermute | solution.py:38
  75.7 2.0 %shard_map.97 = (f32[32,48,128]{2,1,0:T(8,128)S(1)}, bf16[32,48,128]{2,1,0:T(8,128)(2,1)S(1)}) custom-call(s32[2]{0:T(128)S(1)} %pad_add_fusion.spot, bf16[512,1152]{1,0:T(8,128)(2,1)S(1)} %bitcast.13, bf16[304,128]{1,0:T(8,128)(2,1)S(1)} %get-tuple-element.48.refs_0_, bf16[304,128]{1,0:T(8,128)(2,1)S(1)} %collective-permute-done.10.refs_1_, ...), custom_call_target="tpu_custom_call" | custom-call | flops 339738624 | bytes 4194304 | tf_op jit(solution)/shard_map/pallas_call | solution.py:221
  78.1 2.8 %shard_map.99 = (bf16[288,128]{1,0:T(8,128)(2,1)S(1)}, bf16[288,128]{1,0:T(8,128)(2,1)S(1)}, bf16[288,128]{1,0:T(8,128)(2,1)S(1)}, bf16[288,128]{1,0:T(8,128)(2,1)S(1)}) custom-call(s32[2]{0:T(128)S(1)} %pad_add_fusion.spot, f32[2]{0:T(128)S(1)} %pad_maximum_fusion.scal, bf16[144,1152]{1,0:T(8,128)(2,1)S(1)} %get-tuple-element.42.refs_0_.own, ...), custom_call_target="tpu_custom_call" | custom-call | flops 452984832 | bytes 8388608 | tf_op jit(solution)/shard_map/pallas_call | solution.py:161
  80.9 1.6 %collective-permute-start.14 = (bf16[288,128]{1,0:T(8,128)(2,1)S(1)}, bf16[288,128]{1,0:T(8,128)(2,1)S(1)}, u32[]{:S(2)}, u32[]{:S(2)}) collective-permute-start(bf16[288,128]{1,0:T(8,128)(2,1)S(1)} %get-tuple-element.58), channel_id=1, source_target_pairs={{0,1},{1,2},{2,3},{3,0},{4,5},{5,6},{6,7},{7,4},{8,9},{9,10},{10,1... | collective-permute-start | bytes 221192 | tf_op jit(solution)/shard_map/ppermute | solution.py:294
  82.5 2.8 %collective-permute-start.15 = (bf16[288,128]{1,0:T(8,128)(2,1)S(1)}, bf16[288,128]{1,0:T(8,128)(2,1)S(1)}, u32[]{:S(2)}, u32[]{:S(2)}) collective-permute-start(bf16[288,128]{1,0:T(8,128)(2,1)S(1)} %get-tuple-element.59), channel_id=1, source_target_pairs={{0,2},{1,3},{2,0},{3,1},{4,6},{5,7},{6,4},{7,5},{8,10},{9,11},{10,... | collective-permute-start | bytes 221192 | tf_op jit(solution)/shard_map/ppermute | solution.py:294
  87.5 14.3 %all-to-all-start = ((bf16[32,48,128]{2,1,0:T(8,128)(2,1)}), bf16[32,48,128]{2,1,0:T(8,128)(2,1)S(1)}, u32[]{:S(2)}, u32[]{:S(2)}) async-start(bf16[32,48,128]{2,1,0:T(8,128)(2,1)} %add_convert_fusion.1), calls=%async_computation | async-start | bytes 786432 | tf_op jit(solution)/shard_map/all_to_all | solution.py:306
  103.1 2.0 %shard_map.100 = (f32[32,48,128]{2,1,0:T(8,128)S(1)}, bf16[32,48,128]{2,1,0:T(8,128)(2,1)S(1)}) custom-call(s32[2]{0:T(128)S(1)} %pad_add_fusion.spot, bf16[512,1152]{1,0:T(8,128)(2,1)S(1)} %bitcast.12, bf16[288,128]{1,0:T(8,128)(2,1)S(1)} %get-tuple-element.57.refs_0_, bf16[288,128]{1,0:T(8,128)(2,1)S(1)} %collective-permute-done.14.refs_1_, ...), custom_call_target="tpu_custom_call" | custom-call | flops 339738624 | bytes 4194304 | tf_op jit(solution)/shard_map/pallas_call | solution.py:221
  105.2 1.7 %collective-permute-done.17 = bf16[32,48,128]{2,1,0:T(8,128)(2,1)S(1)} collective-permute-done((bf16[32,48,128]{2,1,0:T(8,128)(2,1)S(1)}, bf16[32,48,128]{2,1,0:T(8,128)(2,1)S(1)}, u32[]{:S(2)}, u32[]{:S(2)}) %collective-permute-start.17) | collective-permute-done | bytes 393248 | tf_op jit(solution)/shard_map/ppermute | solution.py:38
  107.8 8.8 %all-to-all-done.parts = bf16[32,48,128]{2,1,0:T(8,128)(2,1)S(1)} async-done(((bf16[32,48,128]{2,1,0:T(8,128)(2,1)}), bf16[32,48,128]{2,1,0:T(8,128)(2,1)S(1)}, u32[]{:S(2)}, u32[]{:S(2)}) %all-to-all-start) | async-done | bytes 393248 | tf_op jit(solution)/shard_map/all_to_all | solution.py:306
  116.6 4.7 %all-to-all-start.1 = ((bf16[32,48,128]{2,1,0:T(8,128)(2,1)}), bf16[32,48,128]{2,1,0:T(8,128)(2,1)S(1)}, u32[]{:S(2)}, u32[]{:S(2)}) async-start(bf16[32,48,128]{2,1,0:T(8,128)(2,1)} %add_convert_fusion), calls=%async_computation.1 | async-start | bytes 786432 | tf_op jit(solution)/shard_map/all_to_all | solution.py:306
  122.6 13.1 %all-to-all-done.1.parts = bf16[32,48,128]{2,1,0:T(8,128)(2,1)S(1)} async-done(((bf16[32,48,128]{2,1,0:T(8,128)(2,1)}), bf16[32,48,128]{2,1,0:T(8,128)(2,1)S(1)}, u32[]{:S(2)}, u32[]{:S(2)}) %all-to-all-start.1) | async-done | bytes 393248 | tf_op jit(solution)/shard_map/all_to_all | solution.py:306
  (65 shorter events, 23.4 us)
Async XLA Ops:
  7.2 14.9 %copy-start.13 = (s32[1,128]{1,0:T(1,128)S(1)}, s32[1,128]{1,0:T(1,128)}, u32[]{:S(2)}) copy-start(s32[1,128]{1,0:T(1,128)} %key_ref.3) | copy-start | bytes 1540
  7.2 67.3 %all-gather.5.cloned.1.call-start = ((), (), s32[]{:S(2)}) async-start(), calls=%async_computation.2 | async-start | bytes 1474560 | tf_op jit(solution)/shard_map/all_gather | solution.py:280
  7.9 93.9 %all-gather.7.cloned.1.call-start = ((), (), s32[]{:S(2)}) async-start(), calls=%async_computation.3 | async-start | bytes 1474560 | tf_op jit(solution)/shard_map/all_gather | solution.py:281
  13.5 7.9 %collective-permute-start = (bf16[144,1152]{1,0:T(8,128)(2,1)S(1)}, bf16[144,1152]{1,0:T(8,128)(2,1)S(1)}, u32[]{:S(2)}, u32[]{:S(2)}) collective-permute-start(bf16[144,1152]{1,0:T(8,128)(2,1)S(1)} %get-tuple-element.42.refs_0_.own), channel_id=1, source_target_pairs={{0,8},{8,0},{1,9},{9,1},{2,10},{10,2},{3,11},{11,3},{4,12},{12,4},... | collective-permute-start | bytes 995336 | tf_op jit(solution)/shard_map/ppermute | solution.py:38
  13.5 17.7 %collective-permute-start.1 = (bf16[144,1152]{1,0:T(8,128)(2,1)S(1)}, bf16[144,1152]{1,0:T(8,128)(2,1)}, u32[]{:S(2)}, u32[]{:S(2)}) collective-permute-start(bf16[144,1152]{1,0:T(8,128)(2,1)S(1)} %get-tuple-element.42.refs_0_.own), channel_id=1, source_target_pairs={{0,16},{16,0},{32,48},{48,32},{1,17},{17,1},{33,49},{49,33},{2,18}... | collective-permute-start | bytes 995336 | tf_op jit(solution)/shard_map/ppermute | solution.py:38
  16.8 19.3 %collective-permute-start.4 = (bf16[144,1152]{1,0:T(8,128)(2,1)S(1)}, bf16[144,1152]{1,0:T(8,128)(2,1)}, u32[]{:S(2)}, u32[]{:S(2)}) collective-permute-start(bf16[144,1152]{1,0:T(8,128)(2,1)S(1)} %get-tuple-element.42.refs_0_.own), channel_id=1, source_target_pairs={{0,64},{64,0},{128,192},{192,128},{1,65},{65,1},{129,193},{193,129... | collective-permute-start | bytes 995336 | tf_op jit(solution)/shard_map/ppermute | solution.py:38
  18.5 18.0 %collective-permute-start.5 = (bf16[144,1152]{1,0:T(8,128)(2,1)S(1)}, bf16[144,1152]{1,0:T(8,128)(2,1)}, u32[]{:S(2)}, u32[]{:S(2)}) collective-permute-start(bf16[144,1152]{1,0:T(8,128)(2,1)S(1)} %get-tuple-element.42.refs_0_.own), channel_id=1, source_target_pairs={{0,128},{64,192},{128,0},{192,64},{1,129},{65,193},{129,1},{193,65... | collective-permute-start | bytes 995336 | tf_op jit(solution)/shard_map/ppermute | solution.py:38
  25.2 52.9 %copy-start.7 = (f32[128,1152]{1,0:T(8,128)S(1)}, f32[128,1152]{1,0:T(8,128)}, u32[]{:S(2)}) copy-start(f32[128,1152]{1,0:T(8,128)} %copy-done.6) | copy-start | bytes 1769476
  31.2 16.4 %collective-permute-start.2 = (bf16[144,1152]{1,0:T(8,128)(2,1)S(1)}, bf16[144,1152]{1,0:T(8,128)(2,1)S(1)}, u32[]{:S(2)}, u32[]{:S(2)}) collective-permute-start(bf16[144,1152]{1,0:T(8,128)(2,1)S(1)} %get-tuple-element.41.own.refs_0_), channel_id=1, source_target_pairs={{0,16},{16,0},{32,48},{48,32},{1,17},{17,1},{33,49},{49,33},{2,18}... | collective-permute-start | bytes 995336 | tf_op jit(solution)/shard_map/ppermute | solution.py:38
  36.5 19.5 %collective-permute-start.7 = (bf16[144,1152]{1,0:T(8,128)(2,1)S(1)}, bf16[144,1152]{1,0:T(8,128)(2,1)S(1)}, u32[]{:S(2)}, u32[]{:S(2)}) collective-permute-start(bf16[144,1152]{1,0:T(8,128)(2,1)S(1)} %get-tuple-element.41.own.refs_0_), channel_id=1, source_target_pairs={{0,8},{8,0},{1,9},{9,1},{2,10},{10,2},{3,11},{11,3},{4,12},{12,4},... | collective-permute-start | bytes 995336 | tf_op jit(solution)/shard_map/ppermute | solution.py:38
  36.5 19.5 %collective-permute-start.8 = (bf16[144,1152]{1,0:T(8,128)(2,1)S(1)}, bf16[144,1152]{1,0:T(8,128)(2,1)S(1)}, u32[]{:S(2)}, u32[]{:S(2)}) collective-permute-start(bf16[144,1152]{1,0:T(8,128)(2,1)S(1)} %get-tuple-element.41.own.refs_0_), channel_id=1, source_target_pairs={{0,64},{64,0},{128,192},{192,128},{1,65},{65,1},{129,193},{193,129... | collective-permute-start | bytes 995336 | tf_op jit(solution)/shard_map/ppermute | solution.py:38
  37.8 18.2 %collective-permute-start.9 = (bf16[144,1152]{1,0:T(8,128)(2,1)S(1)}, bf16[144,1152]{1,0:T(8,128)(2,1)S(1)}, u32[]{:S(2)}, u32[]{:S(2)}) collective-permute-start(bf16[144,1152]{1,0:T(8,128)(2,1)S(1)} %get-tuple-element.41.own.refs_0_), channel_id=1, source_target_pairs={{0,128},{64,192},{128,0},{192,64},{1,129},{65,193},{129,1},{193,65... | collective-permute-start | bytes 995336 | tf_op jit(solution)/shard_map/ppermute | solution.py:38
  40.7 15.3 %collective-permute-start.6 = (bf16[144,1152]{1,0:T(8,128)(2,1)}, bf16[144,1152]{1,0:T(8,128)(2,1)S(1)}, u32[]{:S(2)}, u32[]{:S(2)}) collective-permute-start(bf16[144,1152]{1,0:T(8,128)(2,1)} %collective-permute-done.1.refs_4_), channel_id=1, source_target_pairs={{0,48},{16,32},{32,16},{48,0},{1,49},{17,33},{33,17},{49,1},{2,50}... | collective-permute-start | bytes 995336 | tf_op jit(solution)/shard_map/ppermute | solution.py:38
  47.5 26.9 %collective-permute-start.3 = (bf16[144,1152]{1,0:T(8,128)(2,1)S(1)}, bf16[144,1152]{1,0:T(8,128)(2,1)S(1)}, u32[]{:S(2)}, u32[]{:S(2)}) collective-permute-start(bf16[144,1152]{1,0:T(8,128)(2,1)S(1)} %collective-permute-done.2.refs_4_), channel_id=1, source_target_pairs={{0,48},{16,32},{32,16},{48,0},{1,49},{17,33},{33,17},{49,1},{2,50}... | collective-permute-start | bytes 995336 | tf_op jit(solution)/shard_map/ppermute | solution.py:38
  62.4 12.0 %collective-permute-start.10 = (bf16[304,128]{1,0:T(8,128)(2,1)}, bf16[304,128]{1,0:T(8,128)(2,1)S(1)}, u32[]{:S(2)}, u32[]{:S(2)}) collective-permute-start(bf16[304,128]{1,0:T(8,128)(2,1)} %get-tuple-element.49), channel_id=1, source_target_pairs={{0,1},{1,2},{2,3},{3,0},{4,5},{5,6},{6,7},{7,4},{8,9},{9,10},{10,1... | collective-permute-start | bytes 233480 | tf_op jit(solution)/shard_map/ppermute | solution.py:294
  63.8 10.6 %collective-permute-start.11 = (bf16[304,128]{1,0:T(8,128)(2,1)}, bf16[304,128]{1,0:T(8,128)(2,1)S(1)}, u32[]{:S(2)}, u32[]{:S(2)}) collective-permute-start(bf16[304,128]{1,0:T(8,128)(2,1)} %get-tuple-element.50), channel_id=1, source_target_pairs={{0,2},{1,3},{2,0},{3,1},{4,6},{5,7},{6,4},{7,5},{8,10},{9,11},{10,... | collective-permute-start | bytes 233480 | tf_op jit(solution)/shard_map/ppermute | solution.py:294
  66.6 7.9 %collective-permute-start.12 = (bf16[304,128]{1,0:T(8,128)(2,1)S(1)}, bf16[304,128]{1,0:T(8,128)(2,1)S(1)}, u32[]{:S(2)}, u32[]{:S(2)}) collective-permute-start(bf16[304,128]{1,0:T(8,128)(2,1)S(1)} %get-tuple-element.51), channel_id=1, source_target_pairs={{0,3},{1,0},{2,1},{3,2},{4,7},{5,4},{6,5},{7,6},{8,11},{9,8},{10,9... | collective-permute-start | bytes 233480 | tf_op jit(solution)/shard_map/ppermute | solution.py:294
  77.8 8.9 %collective-permute-start.13 = (bf16[32,48,128]{2,1,0:T(8,128)(2,1)S(1)}, bf16[32,48,128]{2,1,0:T(8,128)(2,1)S(1)}, u32[]{:S(2)}, u32[]{:S(2)}) collective-permute-start(bf16[32,48,128]{2,1,0:T(8,128)(2,1)S(1)} %get-tuple-element.53), channel_id=1, source_target_pairs={{0,8},{8,0},{1,9},{9,1},{2,10},{10,2},{3,11},{11,3},{4,12},{12,4},... | collective-permute-start | bytes 1179656 | tf_op jit(solution)/shard_map/ppermute | solution.py:38
  80.9 20.9 %collective-permute-start.14 = (bf16[288,128]{1,0:T(8,128)(2,1)S(1)}, bf16[288,128]{1,0:T(8,128)(2,1)S(1)}, u32[]{:S(2)}, u32[]{:S(2)}) collective-permute-start(bf16[288,128]{1,0:T(8,128)(2,1)S(1)} %get-tuple-element.58), channel_id=1, source_target_pairs={{0,1},{1,2},{2,3},{3,0},{4,5},{5,6},{6,7},{7,4},{8,9},{9,10},{10,1... | collective-permute-start | bytes 221192 | tf_op jit(solution)/shard_map/ppermute | solution.py:294
  82.5 19.3 %collective-permute-start.15 = (bf16[288,128]{1,0:T(8,128)(2,1)S(1)}, bf16[288,128]{1,0:T(8,128)(2,1)S(1)}, u32[]{:S(2)}, u32[]{:S(2)}) collective-permute-start(bf16[288,128]{1,0:T(8,128)(2,1)S(1)} %get-tuple-element.59), channel_id=1, source_target_pairs={{0,2},{1,3},{2,0},{3,1},{4,6},{5,7},{6,4},{7,5},{8,10},{9,11},{10,... | collective-permute-start | bytes 221192 | tf_op jit(solution)/shard_map/ppermute | solution.py:294
  85.2 16.6 %collective-permute-start.16 = (bf16[288,128]{1,0:T(8,128)(2,1)S(1)}, bf16[288,128]{1,0:T(8,128)(2,1)S(1)}, u32[]{:S(2)}, u32[]{:S(2)}) collective-permute-start(bf16[288,128]{1,0:T(8,128)(2,1)S(1)} %get-tuple-element.60), channel_id=1, source_target_pairs={{0,3},{1,0},{2,1},{3,2},{4,7},{5,4},{6,5},{7,6},{8,11},{9,8},{10,9... | collective-permute-start | bytes 221192 | tf_op jit(solution)/shard_map/ppermute | solution.py:294
  87.5 29.1 %all-to-all-start = ((bf16[32,48,128]{2,1,0:T(8,128)(2,1)}), bf16[32,48,128]{2,1,0:T(8,128)(2,1)S(1)}, u32[]{:S(2)}, u32[]{:S(2)}) async-start(bf16[32,48,128]{2,1,0:T(8,128)(2,1)} %add_convert_fusion.1), calls=%async_computation | async-start | bytes 786432 | tf_op jit(solution)/shard_map/all_to_all | solution.py:306
  105.1 1.8 %collective-permute-start.17 = (bf16[32,48,128]{2,1,0:T(8,128)(2,1)S(1)}, bf16[32,48,128]{2,1,0:T(8,128)(2,1)S(1)}, u32[]{:S(2)}, u32[]{:S(2)}) collective-permute-start(bf16[32,48,128]{2,1,0:T(8,128)(2,1)S(1)} %get-tuple-element.62), channel_id=1, source_target_pairs={{0,8},{8,0},{1,9},{9,1},{2,10},{10,2},{3,11},{11,3},{4,12},{12,4},... | collective-permute-start | bytes 1179656 | tf_op jit(solution)/shard_map/ppermute | solution.py:38
  116.6 19.1 %all-to-all-start.1 = ((bf16[32,48,128]{2,1,0:T(8,128)(2,1)}), bf16[32,48,128]{2,1,0:T(8,128)(2,1)S(1)}, u32[]{:S(2)}, u32[]{:S(2)}) async-start(bf16[32,48,128]{2,1,0:T(8,128)(2,1)} %add_convert_fusion), calls=%async_computation.1 | async-start | bytes 786432 | tf_op jit(solution)/shard_map/all_to_all | solution.py:306
  (12 other events, 22.1 us)
Sparse Core Ops, SparseCore 0:
  9.8 29.5 all-gather.4
  41.2 30.4 all-gather.6

commit v4 on v3

v4 whole, which is shorter than its diff:
```python
import functools

import jax
import jax.numpy as jnp
from jax import lax
from jax.experimental import pallas as pl
from jax.experimental.pallas import tpu as pltpu
from jax.sharding import Mesh, PartitionSpec as P

EPSILON = 1e-06
LOSS = ("ly", "lz", "lc")
ROWS = 128
WIDTH = 1152
KEY_ROWS = 16
CHUNK = 36
SLOT = 40
COLS = 144
LANES = 128
TAIL = COLS - LANES
QUADS = 16
STATS = 112
DEPTH = 384
PIECES = WIDTH // DEPTH
F32 = jnp.float32
BF16 = jnp.bfloat16

VMEM = pl.BlockSpec(memory_space=pltpu.VMEM)
SMEM = pl.BlockSpec(memory_space=pltpu.SMEM)


def params(megabytes):
    return pltpu.CompilerParams(vmem_limit_bytes=megabytes * 2**20)


def cost(flops, moved):
    return pl.CostEstimate(flops=flops, bytes_accessed=moved, transcendentals=0)


def exchange(array, axis, apart):
    return lax.ppermute(array, axis, [(i, i ^ apart) for i in range(lax.axis_size(axis))])


def after(array, *others):
    return lax.optimization_barrier((array, *others))[0]


def nt(a, b):
    return lax.dot_general(a, b, (((1,), (1,)), ((), ())), preferred_element_type=F32)


def mm(a, b):
    return jnp.dot(a, b, preferred_element_type=F32)


def project_kernel(x_hbm, w_hbm, key_hbm, out_ref, x, w, key, sems):
    copies = [
        pltpu.make_async_copy(x_hbm, x, sems.at[0]),
        pltpu.make_async_copy(key_hbm, key, sems.at[1]),
    ]
    for k in range(PIECES):
        span = pl.ds(k * DEPTH, DEPTH)
        copies.append(pltpu.make_async_copy(w_hbm.at[span], w.at[span], sems.at[2 + k]))
    for copy in copies:
        copy.start()
    copies[0].wait()
    u = jnp.zeros((ROWS, WIDTH), F32)
    for k in range(PIECES):
        copies[2 + k].wait()
        span = slice(k * DEPTH, (k + 1) * DEPTH)
        u += mm(x[:, span], w[span])
    out_ref[:ROWS, :] = (u / lengths(u)).astype(BF16)
    copies[1].wait()
    digit = jnp.broadcast_to(key[...], (KEY_ROWS, ROWS))
    row = lax.broadcasted_iota(jnp.int32, (KEY_ROWS, ROWS), 0)
    digit = jnp.where(row == 0, digit >> 7, jnp.where(row == 1, digit & 127, 0))
    out_ref[ROWS:, :] = jnp.zeros((KEY_ROWS, WIDTH), BF16)
    out_ref[ROWS:, :ROWS] = digit.astype(F32).astype(BF16)


def lengths(u):
    return jnp.sqrt(jnp.sum(u * u, axis=1, keepdims=True) + EPSILON)


def project(x, w, keys):
    return pl.pallas_call(
        project_kernel,
        in_specs=[pl.BlockSpec(memory_space=pltpu.HBM)] * 3,
        out_specs=VMEM,
        out_shape=jax.ShapeDtypeStruct((ROWS + KEY_ROWS, WIDTH), BF16),
        scratch_shapes=[
            pltpu.VMEM((ROWS, WIDTH), BF16),
            pltpu.VMEM((WIDTH, WIDTH), BF16),
            pltpu.VMEM((1, ROWS), jnp.int32),
            pltpu.SemaphoreType.DMA((2 + PIECES,)),
        ],
        compiler_params=params(56),
        cost_estimate=cost(2 * ROWS * WIDTH * WIDTH, 4 * 2**20),
    )(x, w, keys)


def add_tiles(with_stats, scal, mine, key_col, blocks, total, sums):
    heat, shift = scal[0], scal[1]
    for block in blocks:
        vec = block[:ROWS, :]
        keys = block[ROWS:, :LANES].astype(F32)
        same = key_col == keys[0:1] * 128.0 + keys[1:2]
        sim = nt(mine, vec)
        logits = heat * sim + shift
        z = jnp.where(same, -logits, logits)
        t = jnp.exp(-jnp.abs(z))
        q = 1.0 / (1.0 + t)
        sig = jnp.where(z >= 0, q, t * q)
        g = jnp.where(same, -sig, sig) * (1.0 / ROWS)
        total += mm(g.astype(BF16), vec)
        if with_stats:
            new = (jnp.maximum(z, 0.0) + jnp.log1p(t), g * sim, g)
            sums = [old + add for old, add in zip(sums, new)]
    return total, sums


def early_kernel(with_stats, scal, x, w, key, own, *refs):
    blocks, (total_ref, unit_ref, len_ref, key_ref, sum_ref) = refs[:-5], refs[-5:]
    u = mm(x[...], w[...])
    length = lengths(u)
    unit_ref[...] = u / length
    len_ref[...] = jnp.broadcast_to(length, len_ref.shape)
    key_col = jnp.broadcast_to(key[...].astype(F32), (ROWS, ROWS)).T
    key_ref[...] = key_col
    zero = jnp.zeros((ROWS, ROWS), F32)
    total, sums = add_tiles(
        with_stats,
        scal,
        own[:ROWS, :],
        key_col,
        blocks,
        jnp.zeros((ROWS, WIDTH), F32),
        [zero] * 3,
    )
    total_ref[...] = total
    for k in range(3):
        sum_ref[k] = sums[k]


def early(with_stats, scal, x, w, keys, own, blocks):
    shapes = [(ROWS, WIDTH), (ROWS, WIDTH), (ROWS, LANES), (ROWS, ROWS), (3, ROWS, ROWS)]
    return pl.pallas_call(
        functools.partial(early_kernel, with_stats),
        in_specs=[SMEM] + [VMEM] * (4 + len(blocks)),
        out_specs=[VMEM] * len(shapes),
        out_shape=[jax.ShapeDtypeStruct(shape, F32) for shape in shapes],
        compiler_params=params(56),
        cost_estimate=cost(4 * 5 * ROWS * ROWS * WIDTH, 8 * 2**20),
    )(scal, x, w, keys, own, *blocks)


def late_kernel(with_stats, ways, count, spot, scal, own, total_ref, unit, length, key, acc, *refs):
    blocks, outs, held = refs[:count], refs[count:-1], refs[-1]
    heat = scal[0]
    total, sums = add_tiles(
        with_stats,
        scal,
        own[:ROWS, :],
        key[...],
        blocks,
        total_ref[...],
        [acc[k] for k in range(3)],
    )
    total = total * heat
    u = unit[...]
    inner = jnp.sum(u * total, axis=1, keepdims=True)
    du = (total - u * inner) / length[:, :1]
    held[...] = du.T.astype(BF16).reshape(held.shape)
    if with_stats:
        def full(x):
            return jnp.sum(jnp.sum(x, axis=1, keepdims=True), axis=0, keepdims=True)

        lane = lax.broadcasted_iota(jnp.int32, (KEY_ROWS, LANES), 1)
        row = lax.broadcasted_iota(jnp.int32, (KEY_ROWS, LANES), 0)
        kind = lane % 3
        value = jnp.where(
            kind == 0,
            full(sums[0]) * (1.0 / ROWS),
            jnp.where(kind == 1, full(sums[1]) * heat, full(sums[2])),
        )
        value = jnp.where((row == 0) & (lane < 9), value, 0.0)
        high = value.astype(BF16).astype(F32)
        middle = (value - high).astype(BF16).astype(F32)
        low = value - high - middle
        parts = jnp.where(lane < 3, high, jnp.where(lane < 6, middle, low)).astype(BF16)
        out = outs[0]
        for w in range(ways):
            for h in range(2):
                out[w, h * COLS : (h + 1) * COLS, :] = held[h * ways + w]
            out[w, 2 * COLS :, :] = parts
    else:
        for step, out in enumerate(outs):
            w = lax.rem(spot[0] + step, ways)
            for h in range(2):
                out[h * COLS : (h + 1) * COLS, :] = held[h * ways + w]


def late(with_stats, ways, spot, scal, own, partial, blocks):
    if with_stats:
        shapes = [(ways, 2 * COLS + KEY_ROWS, ROWS)]
    else:
        shapes = [(2 * COLS, ROWS)] * ways
    return pl.pallas_call(
        functools.partial(late_kernel, with_stats, ways, len(blocks)),
        in_specs=[SMEM] * 2 + [VMEM] * (6 + len(blocks)),
        out_specs=[VMEM] * len(shapes),
        out_shape=[jax.ShapeDtypeStruct(shape, BF16) for shape in shapes],
        scratch_shapes=[pltpu.VMEM((2 * ways, COLS, ROWS), BF16)],
        compiler_params=params(56),
        cost_estimate=cost(4 * 2 * ROWS * ROWS * WIDTH, 4 * 2**20),
    )(spot, scal, own, *partial, *blocks)


def head_kernel(with_stats, spot, feat, *refs):
    spreads, (kept, given, held) = refs[:-3], refs[-3:]
    if with_stats:
        spreads = [spreads[0].at[w] for w in range(spreads[0].shape[0])]
    ways = len(spreads)
    total = jnp.zeros((2 * COLS, feat.shape[1]), F32)
    for step, spread in enumerate(spreads):
        source = step if with_stats else lax.rem(spot[0] + ways - step, ways)
        start = source * ROWS if with_stats else pl.multiple_of(source * ROWS, ROWS)
        rows = feat[pl.ds(start, ROWS), :]
        total += mm(spread[: 2 * COLS, :], rows)
    spare = None
    if with_stats:
        parts = jnp.zeros((KEY_ROWS, LANES), F32)
        for spread in spreads:
            parts += spread[2 * COLS :, :].astype(F32)
        lane = lax.broadcasted_iota(jnp.int32, (8, LANES), 1)
        row = lax.broadcasted_iota(jnp.int32, (8, LANES), 0)
        place = lane - STATS
        summed = jnp.zeros((8, LANES), F32)
        for k in range(3):
            number = jnp.sum(
                jnp.where((lane[:1] % 3 == k) & (lane[:1] < 9), parts[0:1], 0.0),
                axis=1,
                keepdims=True,
            )
            summed = jnp.where(place % 3 == k, number, summed)
        value = jnp.where((row == spot[1]) & (place >= 0) & (place < 9), summed, 0.0)
        high = value.astype(BF16).astype(F32)
        middle = (value - high).astype(BF16).astype(F32)
        low = value - high - middle
        spare = jnp.where(place < 3, high, jnp.where(place < 6, middle, low))
    for h in range(2):
        main = total[h * COLS : h * COLS + LANES, :].T
        rest = total[h * COLS + LANES : (h + 1) * COLS, :]
        for m in range(QUADS):
            for side in range(2):
                start = (2 * m + side) * CHUNK
                target = held.at[side, 2 * m + h]
                target[:CHUNK, :] = main[start : start + CHUNK]
                target[CHUNK:SLOT, :] = jnp.zeros((SLOT - CHUNK, LANES), F32)
                target[SLOT:, :] = jnp.zeros((8, LANES), F32) if spare is None else spare
                for k in range(2):
                    target[SLOT:, 64 * k : 64 * k + CHUNK] = rest[
                        8 * k : 8 * k + 8, start : start + CHUNK
                    ]
    kept[...] = held[spot[1]]
    given[...] = held[1 - spot[1]].astype(BF16)


def heads(with_stats, spot, feat, spreads):
    shape = (2 * QUADS, SLOT + 8, LANES)
    return pl.pallas_call(
        functools.partial(head_kernel, with_stats),
        in_specs=[SMEM] + [VMEM] * (1 + len(spreads)),
        out_specs=[VMEM, VMEM],
        out_shape=[jax.ShapeDtypeStruct(shape, F32), jax.ShapeDtypeStruct(shape, BF16)],
        scratch_shapes=[pltpu.VMEM((2, *shape), F32)],
        compiler_params=params(24),
        cost_estimate=cost(2 * 4 * ROWS * 2 * COLS * feat.shape[1], 4 * 2**20),
    )(spot, feat, *spreads)


def final_kernel(count, parts, out, stats):
    total = jnp.sum(parts[...].astype(F32), axis=0)
    out[:, :LANES] = total[:CHUNK]
    rest = total[SLOT:, :].T
    out[:, LANES : LANES + 8] = rest[:CHUNK]
    out[:, LANES + 8 :] = rest[64 : 64 + CHUNK]
    lane = lax.broadcasted_iota(jnp.int32, (1, LANES), 1)
    place = lane - STATS
    row = total[SLOT : SLOT + 1] + total[SLOT + 1 : SLOT + 2]
    answer = jnp.zeros((1, LANES), F32)
    for k in range(3):
        number = jnp.sum(
            jnp.where((place % 3 == k) & (place >= 0) & (place < 9), row, 0.0),
            axis=1,
            keepdims=True,
        )
        answer = jnp.where(lane == k, number, answer)
    stats[...] = answer * (1.0 / count)


def final(count, parts):
    return pl.pallas_call(
        functools.partial(final_kernel, count),
        in_specs=[VMEM],
        out_specs=[VMEM, VMEM],
        out_shape=[
            jax.ShapeDtypeStruct((CHUNK, COLS), F32),
            jax.ShapeDtypeStruct((1, LANES), F32),
        ],
        compiler_params=params(8),
        cost_estimate=cost(2 * QUADS * 48 * LANES, 2**20),
    )(parts)


def body(pictures, sentences, keys, picture_weights, sentence_weights, heat_log, shift_value):
    ways = lax.axis_size("dx")
    spot = jnp.stack([lax.axis_index("dx"), lax.axis_index("lc")]).astype(jnp.int32)
    scal = jnp.stack([jnp.exp(heat_log[0]), shift_value[0]])
    img_feat = lax.all_gather(pictures[0], "dx", axis=0, tiled=True)
    txt_feat = lax.all_gather(sentences[0], "dx", axis=0, tiled=True)

    txt = project(sentences[0], sentence_weights, keys)
    txt_a = exchange(txt, "lz", 1)
    txt_y2 = exchange(txt, "ly", 2)
    txt_y1 = exchange(txt, "ly", 1)
    txt_c = exchange(txt, "lc", 1)
    img = project(after(pictures[0], txt_c), picture_weights, keys)
    txt_b = exchange(after(txt_a, txt_y1, txt_y2), "lz", 3)

    img_a = exchange(after(img, txt_a), "lz", 1)
    img_c = exchange(img, "lc", 1)
    img_b = exchange(img_a, "lz", 3)
    img_n = after(img, img_a)
    img_y2 = exchange(img_n, "ly", 2)
    img_y1 = exchange(img_n, "ly", 1)

    count = 2 * QUADS * lax.axis_size("dz") * ways

    def turn(array, step):
        return lax.ppermute(array, "dx", [(i, (i + step) % ways) for i in range(ways)])

    def share(with_stats, feat, spreads):
        kept, given = heads(with_stats, spot, feat, spreads)
        taken = exchange(given, "lc", 1)
        return (kept + taken.astype(F32)).astype(BF16)

    def collect(sums):
        return final(count, lax.all_to_all(sums, ("ly", "lz", "dz"), 0, 0, tiled=True))

    img_part = early(
        True, scal, pictures[0], picture_weights, keys, img, [txt, txt_c, txt_y1, txt_y2, txt_a]
    )
    last, img_feat = lax.optimization_barrier((txt_b, img_feat, img_a, img_c))[:2]
    img_outs = late(True, ways, spot, scal, img, img_part, [last])[0]
    img_cols = lax.all_to_all(img_outs, "dx", 0, 0, tiled=True)
    txt_part = early(
        False, scal, sentences[0], sentence_weights, keys, txt, [img, img_c, img_a]
    )
    img_feat = after(img_feat, img_b, img_y1, img_y2, *txt_part)
    img_sums = share(True, img_feat, [img_cols])
    lasts = list(lax.optimization_barrier((img_y1, img_y2, img_b, img_cols))[:3])
    outs = late(False, ways, spot, scal, txt, txt_part, lasts)
    *outs, txt_feat = lax.optimization_barrier((*outs, txt_feat))
    txt_cols = [outs[0]] + [turn(out, step) for step, out in enumerate(outs) if step]
    txt_sums = share(False, txt_feat, txt_cols)
    grad_img, stats = collect(img_sums)
    grad_txt, _ = collect(txt_sums)
    return grad_img, grad_txt, stats[0, :3]


def solution(mesh):
    split = Mesh(mesh.devices.reshape(4, 4, 2, 2, 4), ("ly", "lz", "lc", "dz", "dx"))
    dp = ("dz", "dx")
    return jax.shard_map(
        body,
        mesh=split,
        in_specs=(P(dp, LOSS, None), P(dp, LOSS, None), P(dp, LOSS), P(), P(), P(), P()),
        out_specs=(P(LOSS, dp), P(LOSS, dp), P()),
        check_vma=False,
    )
```

time: 144 us -> 137 us (0.951)
  Pallas kernels: 15.4 us -> 29.3 us
  starting transfers between devices: 55.3 us -> 43.7 us
  local copies, waits for them, and re-layouts: 11.8 us -> 5.03 us
  waiting for transfers between devices: 43.3 us -> 40.2 us
    pallas_call x4 -> x6, Pallas kernels: 9.75 us -> 23.7 us  [the longest x2 9.9 us: early(): pl.pallas_call(functools.partial(early_kernel, with_stats), in_specs=[SME...]
    all_to_all x2, starting transfers between devices: 19 us -> 9.75 us  [collect(): lax.all_to_all(sums, ('ly', 'lz', 'dz'), 0, 0, tiled=True)]
    unnamed x28 -> x30, local copies, waits for them, and re-layouts: 11.3 us -> 4.52 us
    ppermute x6 -> x3, starting transfers between devices: 11.3 us -> 4.57 us  [turn(): lax.ppermute(array, 'dx', [(i, (i + step) % ways) for i in range(ways)])]
    ppermute x12, waiting for transfers between devices: 20.7 us -> 15.5 us  [exchange(): lax.ppermute(array, axis, [(i, i ^ apart) for i in range(lax.axis_size(ax...]
    all_to_all x0 -> x1, starting transfers between devices: none -> 4.38 us  [body(): img_cols = lax.all_to_all(img_outs, 'dx', 0, 0, tiled=True)]
    all_to_all x0 -> x1, waiting for transfers between devices: none -> 1.66 us  [body(): img_cols = lax.all_to_all(img_outs, 'dx', 0, 0, tiled=True)]
  transfers between devices with their start and end apart: 22 -> 20, of which waited for: 8 -> 7; matrix products, arithmetic and copies ran while one was open for 2% -> 2% of each run, Pallas kernels for 10% -> 21%
where the time goes in v4:
time: 137 us
  starting transfers between devices  43.7 us (32%)
  waiting for transfers between devices  40.2 us (29%)
  Pallas kernels  29.3 us (21%)
  between operations  15.6 us (11%)
  local copies, waits for them, and re-layouts  5.03 us (4%)
  other arithmetic  2.9 us (2%)
    ppermute x12, starting transfers between devices, exchange(): lax.ppermute(array, axis, [(i, i ^ apart) for i in range(lax.axis_size(ax...  25 us
    all_to_all x2, waiting for transfers between devices, collect(): lax.all_to_all(sums, ('ly', 'lz', 'dz'), 0, 0, tiled=True)  21.6 us
    ppermute x12, waiting for transfers between devices, exchange(): lax.ppermute(array, axis, [(i, i ^ apart) for i in range(lax.axis_size(ax...  15.5 us
    pallas_call x2, Pallas kernels, early(): pl.pallas_call(functools.partial(early_kernel, with_stats), in_specs=[SME...  9.9 us
    all_to_all x2, starting transfers between devices, collect(): lax.all_to_all(sums, ('ly', 'lz', 'dz'), 0, 0, tiled=True)  9.75 us
    pallas_call x2, Pallas kernels, late(): pl.pallas_call(functools.partial(late_kernel, with_stats, ways, len(block...  7.12 us
    pallas_call x2, Pallas kernels, project(): pl.pallas_call(project_kernel, in_specs=[pl.BlockSpec(memory_space=pltpu....  6.64 us
    ppermute x3, starting transfers between devices, turn(): lax.ppermute(array, 'dx', [(i, (i + step) % ways) for i in range(ways)])  4.57 us
  transfers between devices with their start and end apart: 20, of which 7 were waited for; matrix products, arithmetic and copies ran while one was open for 2% of the time, Pallas kernels for 21%

profile of v4, /device:TPU:32, one launch (start us, length us, event | category | flops | bytes accessed | tf_op | source)
XLA Modules:
  0.0 136.8 jit_solution(14219421689438776853)
XLA Ops:
  8.6 3.3 %shard_map.94.own.refs_0_ = bf16[144,1152]{1,0:T(8,128)(2,1)} custom-call(bf16[128,1152]{1,0:T(8,128)(2,1)} %bitcast.10, bf16[1152,1152]{1,0:T(8,128)(2,1)} %w.2, s32[1,128]{1,0:T(1,128)} %key.3), custom_call_target="tpu_custom_call" | custom-call | flops 339738624 | bytes 4194304 | tf_op jit(solution)/shard_map/pallas_call | solution.py:85
  12.0 3.4 %collective-permute-start = (bf16[144,1152]{1,0:T(8,128)(2,1)}, bf16[144,1152]{1,0:T(8,128)(2,1)S(1)}, u32[]{:S(2)}, u32[]{:S(2)}) collective-permute-start(bf16[144,1152]{1,0:T(8,128)(2,1)} %shard_map.94.own.refs_0_), channel_id=1, source_target_pairs={{0,16},{16,0},{32,48},{48,32},{1,17},{17,1},{33,49},{49,33},{2,18}... | collective-permute-start | bytes 995336 | tf_op jit(solution)/shard_map/ppermute | solution.py:40
  17.0 2.9 %collective-permute-start.2 = (bf16[144,1152]{1,0:T(8,128)(2,1)}, bf16[144,1152]{1,0:T(8,128)(2,1)S(1)}, u32[]{:S(2)}, u32[]{:S(2)}) collective-permute-start(bf16[144,1152]{1,0:T(8,128)(2,1)} %shard_map.94.own.refs_0_), channel_id=1, source_target_pairs={{0,128},{64,192},{128,0},{192,64},{1,129},{65,193},{129,1},{193,65... | collective-permute-start | bytes 995336 | tf_op jit(solution)/shard_map/ppermute | solution.py:40
  19.9 3.4 %shard_map.95.refs_0_.own = bf16[144,1152]{1,0:T(8,128)(2,1)} custom-call(bf16[128,1152]{1,0:T(8,128)(2,1)} %bitcast.12, bf16[1152,1152]{1,0:T(8,128)(2,1)} %w.3, s32[1,128]{1,0:T(1,128)} %key.3), custom_call_target="tpu_custom_call" | custom-call | flops 339738624 | bytes 4194304 | tf_op jit(solution)/shard_map/pallas_call | solution.py:85
  23.3 6.8 %collective-permute-done.refs_4_ = bf16[144,1152]{1,0:T(8,128)(2,1)S(1)} collective-permute-done((bf16[144,1152]{1,0:T(8,128)(2,1)}, bf16[144,1152]{1,0:T(8,128)(2,1)S(1)}, u32[]{:S(2)}, u32[]{:S(2)}) %collective-permute-start) | collective-permute-done | bytes 331808 | tf_op jit(solution)/shard_map/ppermute | solution.py:40
  30.0 3.3 %collective-permute-start.5 = (bf16[144,1152]{1,0:T(8,128)(2,1)}, bf16[144,1152]{1,0:T(8,128)(2,1)S(1)}, u32[]{:S(2)}, u32[]{:S(2)}) collective-permute-start(bf16[144,1152]{1,0:T(8,128)(2,1)} %shard_map.95.refs_0_.own), channel_id=1, source_target_pairs={{0,16},{16,0},{32,48},{48,32},{1,17},{17,1},{33,49},{49,33},{2,18}... | collective-permute-start | bytes 995336 | tf_op jit(solution)/shard_map/ppermute | solution.py:40
  33.3 1.7 %collective-permute-done.2.refs_3_ = bf16[144,1152]{1,0:T(8,128)(2,1)S(1)} collective-permute-done((bf16[144,1152]{1,0:T(8,128)(2,1)}, bf16[144,1152]{1,0:T(8,128)(2,1)S(1)}, u32[]{:S(2)}, u32[]{:S(2)}) %collective-permute-start.2) | collective-permute-done | bytes 331808 | tf_op jit(solution)/shard_map/ppermute | solution.py:40
  35.7 3.6 %collective-permute-start.3 = (bf16[144,1152]{1,0:T(8,128)(2,1)S(1)}, bf16[144,1152]{1,0:T(8,128)(2,1)S(1)}, u32[]{:S(2)}, u32[]{:S(2)}) collective-permute-start(bf16[144,1152]{1,0:T(8,128)(2,1)S(1)} %collective-permute-done.refs_4_), channel_id=1, source_target_pairs={{0,48},{16,32},{32,16},{48,0},{1,49},{17,33},{33,17},{49,1},{2,50}... | collective-permute-start | bytes 995336 | tf_op jit(solution)/shard_map/ppermute | solution.py:40
  41.3 5.3 %collective-permute-done.5.refs_2_ = bf16[144,1152]{1,0:T(8,128)(2,1)S(1)} collective-permute-done((bf16[144,1152]{1,0:T(8,128)(2,1)}, bf16[144,1152]{1,0:T(8,128)(2,1)S(1)}, u32[]{:S(2)}, u32[]{:S(2)}) %collective-permute-start.5) | collective-permute-done | bytes 331808 | tf_op jit(solution)/shard_map/ppermute | solution.py:40
  47.1 2.9 %collective-permute-start.9 = (bf16[144,1152]{1,0:T(8,128)(2,1)}, bf16[144,1152]{1,0:T(8,128)(2,1)S(1)}, u32[]{:S(2)}, u32[]{:S(2)}) collective-permute-start(bf16[144,1152]{1,0:T(8,128)(2,1)} %shard_map.95.refs_0_.own), channel_id=1, source_target_pairs={{0,128},{64,192},{128,0},{192,64},{1,129},{65,193},{129,1},{193,65... | collective-permute-start | bytes 995336 | tf_op jit(solution)/shard_map/ppermute | solution.py:40
  50.0 6.4 %collective-permute-start.7 = (bf16[144,1152]{1,0:T(8,128)(2,1)S(1)}, bf16[144,1152]{1,0:T(8,128)(2,1)S(1)}, u32[]{:S(2)}, u32[]{:S(2)}) collective-permute-start(bf16[144,1152]{1,0:T(8,128)(2,1)S(1)} %collective-permute-done.5.refs_2_), channel_id=1, source_target_pairs={{0,48},{16,32},{32,16},{48,0},{1,49},{17,33},{33,17},{49,1},{2,50}... | collective-permute-start | bytes 995336 | tf_op jit(solution)/shard_map/ppermute | solution.py:40
  57.0 5.5 %shard_map.97 = (f32[128,1152]{1,0:T(8,128)}, f32[128,1152]{1,0:T(8,128)}, f32[128,128]{1,0:T(8,128)}, f32[128,128]{1,0:T(8,128)}, f32[3,128,128]{2,1,0:T(8,128)}) custom-call(f32[2]{0:T(128)} %pad_maximum_fusion.scal, bf16[128,1152]{1,0:T(8,128)(2,1)} %bitcast.13, bf16[1152,1152]{1,0:T(8,128)(2,1)} %w.3, s32[1,128]{1,0:T(1,128)} %key.3, ...), custom_call_target="tpu_custom_call" | custom-call | flops 377487360 | bytes 8388608 | tf_op jit(solution)/shard_map/pallas_call | solution.py:146
  63.3 3.1 %shard_map.98 = bf16[4,304,128]{2,1,0:T(8,128)(2,1)} custom-call(s32[2]{0:T(128)} %pad_add_fusion.spot, f32[2]{0:T(128)} %pad_maximum_fusion.scal, bf16[144,1152]{1,0:T(8,128)(2,1)} %shard_map.95.refs_0_.own, f32[128,1152]{1,0:T(8,128)} %get-tuple-element.50.total_ref, f32[128,1152]{1,0:T(8,128)} %get-tuple-element.51.unit, ...), custom_call_target="tpu_custom_call" | custom-call | flops 150994944 | bytes 4194304 | tf_op jit(solution)/shard_map/pallas_call | solution.py:207
  66.5 4.4 %all-to-all-start = ((bf16[4,304,128]{2,1,0:T(8,128)(2,1)}), bf16[4,304,128]{2,1,0:T(8,128)(2,1)S(1)}, u32[]{:S(2)}, u32[]{:S(2)}) async-start(bf16[4,304,128]{2,1,0:T(8,128)(2,1)} %shard_map.98), calls=%async_computation | async-start | bytes 622592 | tf_op jit(solution)/shard_map/all_to_all | solution.py:355
  70.9 4.4 %shard_map.96 = (f32[128,1152]{1,0:T(8,128)}, f32[128,1152]{1,0:T(8,128)}, f32[128,128]{1,0:T(8,128)}, f32[128,128]{1,0:T(8,128)}, f32[3,128,128]{2,1,0:T(8,128)}) custom-call(f32[2]{0:T(128)} %pad_maximum_fusion.scal, bf16[128,1152]{1,0:T(8,128)(2,1)} %bitcast.11, bf16[1152,1152]{1,0:T(8,128)(2,1)} %w.2, s32[1,128]{1,0:T(1,128)} %key.3, ...), custom_call_target="tpu_custom_call" | custom-call | flops 377487360 | bytes 8388608 | tf_op jit(solution)/shard_map/pallas_call | solution.py:146
  77.8 2.0 %shard_map.99 = (f32[32,48,128]{2,1,0:T(8,128)S(1)}, bf16[32,48,128]{2,1,0:T(8,128)(2,1)S(1)}) custom-call(s32[2]{0:T(128)S(1)} %copy-done.3, bf16[512,1152]{1,0:T(8,128)(2,1)S(1)} %bitcast.9, bf16[4,304,128]{2,1,0:T(8,128)(2,1)S(1)} %all-to-all-done.refs_0_), custom_call_target="tpu_custom_call" | custom-call | flops 339738624 | bytes 4194304 | tf_op jit(solution)/shard_map/pallas_call | solution.py:270
  80.2 4.0 %shard_map.101 = (bf16[288,128]{1,0:T(8,128)(2,1)}, bf16[288,128]{1,0:T(8,128)(2,1)}, bf16[288,128]{1,0:T(8,128)(2,1)}, bf16[288,128]{1,0:T(8,128)(2,1)}) custom-call(s32[2]{0:T(128)} %pad_add_fusion.spot, f32[2]{0:T(128)} %pad_maximum_fusion.scal, bf16[144,1152]{1,0:T(8,128)(2,1)} %shard_map.94.own.refs_0_, f32[128,1152]{1,0:T(8,128)} %get-tuple-element.44.total_ref, ...), custom_call_target="tpu_custom_call" | custom-call | flops 150994944 | bytes 4194304 | tf_op jit(solution)/shard_map/pallas_call | solution.py:207
  84.8 2.5 %collective-permute-start.12 = (bf16[288,128]{1,0:T(8,128)(2,1)}, bf16[288,128]{1,0:T(8,128)(2,1)S(1)}, u32[]{:S(2)}, u32[]{:S(2)}) collective-permute-start(bf16[288,128]{1,0:T(8,128)(2,1)} %get-tuple-element.69), channel_id=1, source_target_pairs={{0,2},{1,3},{2,0},{3,1},{4,6},{5,7},{6,4},{7,5},{8,10},{9,11},{10,... | collective-permute-start | bytes 221192 | tf_op jit(solution)/shard_map/ppermute | solution.py:340
  89.6 5.0 %all-to-all-start.1 = ((bf16[32,48,128]{2,1,0:T(8,128)(2,1)}), bf16[32,48,128]{2,1,0:T(8,128)(2,1)S(1)}, u32[]{:S(2)}, u32[]{:S(2)}) async-start(bf16[32,48,128]{2,1,0:T(8,128)(2,1)} %add_convert_fusion.1), calls=%async_computation.1 | async-start | bytes 786432 | tf_op jit(solution)/shard_map/all_to_all | solution.py:348
  96.8 2.0 %shard_map.102 = (f32[32,48,128]{2,1,0:T(8,128)S(1)}, bf16[32,48,128]{2,1,0:T(8,128)(2,1)S(1)}) custom-call(s32[2]{0:T(128)S(1)} %copy-done.4, bf16[512,1152]{1,0:T(8,128)(2,1)S(1)} %bitcast.8, bf16[288,128]{1,0:T(8,128)(2,1)S(1)} %copy-done.2, bf16[288,128]{1,0:T(8,128)(2,1)S(1)} %collective-permute-done.11.refs_1_, ...), custom_call_target="tpu_custom_call" | custom-call | flops 339738624 | bytes 4194304 | tf_op jit(solution)/shard_map/pallas_call | solution.py:270
  98.9 1.7 %collective-permute-done.14 = bf16[32,48,128]{2,1,0:T(8,128)(2,1)S(1)} collective-permute-done((bf16[32,48,128]{2,1,0:T(8,128)(2,1)S(1)}, bf16[32,48,128]{2,1,0:T(8,128)(2,1)S(1)}, u32[]{:S(2)}, u32[]{:S(2)}) %collective-permute-start.14) | collective-permute-done | bytes 393248 | tf_op jit(solution)/shard_map/ppermute | solution.py:40
  101.4 8.2 %all-to-all-done.1.parts = bf16[32,48,128]{2,1,0:T(8,128)(2,1)S(1)} async-done(((bf16[32,48,128]{2,1,0:T(8,128)(2,1)}), bf16[32,48,128]{2,1,0:T(8,128)(2,1)S(1)}, u32[]{:S(2)}, u32[]{:S(2)}) %all-to-all-start.1) | async-done | bytes 393248 | tf_op jit(solution)/shard_map/all_to_all | solution.py:348
  109.7 4.8 %all-to-all-start.2 = ((bf16[32,48,128]{2,1,0:T(8,128)(2,1)}), bf16[32,48,128]{2,1,0:T(8,128)(2,1)S(1)}, u32[]{:S(2)}, u32[]{:S(2)}) async-start(bf16[32,48,128]{2,1,0:T(8,128)(2,1)} %add_convert_fusion), calls=%async_computation.2 | async-start | bytes 786432 | tf_op jit(solution)/shard_map/all_to_all | solution.py:348
  115.8 13.3 %all-to-all-done.2.parts = bf16[32,48,128]{2,1,0:T(8,128)(2,1)S(1)} async-done(((bf16[32,48,128]{2,1,0:T(8,128)(2,1)}), bf16[32,48,128]{2,1,0:T(8,128)(2,1)S(1)}, u32[]{:S(2)}, u32[]{:S(2)}) %all-to-all-start.2) | async-done | bytes 393248 | tf_op jit(solution)/shard_map/all_to_all | solution.py:348
  (63 shorter events, 17.3 us)
Async XLA Ops:
  7.2 55.4 %all-gather.5.cloned.1.call-start = ((), (), s32[]{:S(2)}) async-start(), calls=%async_computation.3 | async-start | bytes 1474560 | tf_op jit(solution)/shard_map/all_gather | solution.py:319
  7.9 76.3 %all-gather.7.cloned.1.call-start = ((), (), s32[]{:S(2)}) async-start(), calls=%async_computation.4 | async-start | bytes 1474560 | tf_op jit(solution)/shard_map/all_gather | solution.py:320
  11.9 7.9 %collective-permute-start.4 = (bf16[144,1152]{1,0:T(8,128)(2,1)}, bf16[144,1152]{1,0:T(8,128)(2,1)S(1)}, u32[]{:S(2)}, u32[]{:S(2)}) collective-permute-start(bf16[144,1152]{1,0:T(8,128)(2,1)} %shard_map.94.own.refs_0_), channel_id=1, source_target_pairs={{0,8},{8,0},{1,9},{9,1},{2,10},{10,2},{3,11},{11,3},{4,12},{12,4},... | collective-permute-start | bytes 995336 | tf_op jit(solution)/shard_map/ppermute | solution.py:40
  12.0 18.0 %collective-permute-start = (bf16[144,1152]{1,0:T(8,128)(2,1)}, bf16[144,1152]{1,0:T(8,128)(2,1)S(1)}, u32[]{:S(2)}, u32[]{:S(2)}) collective-permute-start(bf16[144,1152]{1,0:T(8,128)(2,1)} %shard_map.94.own.refs_0_), channel_id=1, source_target_pairs={{0,16},{16,0},{32,48},{48,32},{1,17},{17,1},{33,49},{49,33},{2,18}... | collective-permute-start | bytes 995336 | tf_op jit(solution)/shard_map/ppermute | solution.py:40
  15.4 17.9 %collective-permute-start.1 = (bf16[144,1152]{1,0:T(8,128)(2,1)}, bf16[144,1152]{1,0:T(8,128)(2,1)S(1)}, u32[]{:S(2)}, u32[]{:S(2)}) collective-permute-start(bf16[144,1152]{1,0:T(8,128)(2,1)} %shard_map.94.own.refs_0_), channel_id=1, source_target_pairs={{0,64},{64,0},{128,192},{192,128},{1,65},{65,1},{129,193},{193,129... | collective-permute-start | bytes 995336 | tf_op jit(solution)/shard_map/ppermute | solution.py:40
  17.0 18.0 %collective-permute-start.2 = (bf16[144,1152]{1,0:T(8,128)(2,1)}, bf16[144,1152]{1,0:T(8,128)(2,1)S(1)}, u32[]{:S(2)}, u32[]{:S(2)}) collective-permute-start(bf16[144,1152]{1,0:T(8,128)(2,1)} %shard_map.94.own.refs_0_), channel_id=1, source_target_pairs={{0,128},{64,192},{128,0},{192,64},{1,129},{65,193},{129,1},{193,65... | collective-permute-start | bytes 995336 | tf_op jit(solution)/shard_map/ppermute | solution.py:40
  19.9 37.1 %copy-start.10 = (bf16[144,1152]{1,0:T(8,128)(2,1)}, bf16[144,1152]{1,0:T(8,128)(2,1)S(1)}, u32[]{:S(2)}) copy-start(bf16[144,1152]{1,0:T(8,128)(2,1)S(1)} %collective-permute-done.4.refs_1_) | copy-start | bytes 995332
  30.0 27.0 %copy-start.11 = (bf16[144,1152]{1,0:T(8,128)(2,1)}, bf16[144,1152]{1,0:T(8,128)(2,1)S(1)}, u32[]{:S(2)}) copy-start(bf16[144,1152]{1,0:T(8,128)(2,1)S(1)} %collective-permute-done.refs_4_) | copy-start | bytes 995332
  30.0 16.6 %collective-permute-start.5 = (bf16[144,1152]{1,0:T(8,128)(2,1)}, bf16[144,1152]{1,0:T(8,128)(2,1)S(1)}, u32[]{:S(2)}, u32[]{:S(2)}) collective-permute-start(bf16[144,1152]{1,0:T(8,128)(2,1)} %shard_map.95.refs_0_.own), channel_id=1, source_target_pairs={{0,16},{16,0},{32,48},{48,32},{1,17},{17,1},{33,49},{49,33},{2,18}... | collective-permute-start | bytes 995336 | tf_op jit(solution)/shard_map/ppermute | solution.py:40
  33.3 23.7 %copy-start.13 = (bf16[144,1152]{1,0:T(8,128)(2,1)}, bf16[144,1152]{1,0:T(8,128)(2,1)S(1)}, u32[]{:S(2)}) copy-start(bf16[144,1152]{1,0:T(8,128)(2,1)S(1)} %collective-permute-done.1.refs_2_) | copy-start | bytes 995332
  35.7 26.7 %collective-permute-start.3 = (bf16[144,1152]{1,0:T(8,128)(2,1)S(1)}, bf16[144,1152]{1,0:T(8,128)(2,1)S(1)}, u32[]{:S(2)}, u32[]{:S(2)}) collective-permute-start(bf16[144,1152]{1,0:T(8,128)(2,1)S(1)} %collective-permute-done.refs_4_), channel_id=1, source_target_pairs={{0,48},{16,32},{32,16},{48,0},{1,49},{17,33},{33,17},{49,1},{2,50}... | collective-permute-start | bytes 995336 | tf_op jit(solution)/shard_map/ppermute | solution.py:40
  39.3 23.2 %collective-permute-start.6 = (bf16[144,1152]{1,0:T(8,128)(2,1)}, bf16[144,1152]{1,0:T(8,128)(2,1)S(1)}, u32[]{:S(2)}, u32[]{:S(2)}) collective-permute-start(bf16[144,1152]{1,0:T(8,128)(2,1)} %shard_map.95.refs_0_.own), channel_id=1, source_target_pairs={{0,8},{8,0},{1,9},{9,1},{2,10},{10,2},{3,11},{11,3},{4,12},{12,4},... | collective-permute-start | bytes 995336 | tf_op jit(solution)/shard_map/ppermute | solution.py:40
  46.6 19.9 %copy-start.9 = (bf16[144,1152]{1,0:T(8,128)(2,1)}, bf16[144,1152]{1,0:T(8,128)(2,1)S(1)}, u32[]{:S(2)}) copy-start(bf16[144,1152]{1,0:T(8,128)(2,1)S(1)} %collective-permute-done.5.refs_2_) | copy-start | bytes 995332
  46.6 28.7 %collective-permute-start.8 = (bf16[144,1152]{1,0:T(8,128)(2,1)}, bf16[144,1152]{1,0:T(8,128)(2,1)S(1)}, u32[]{:S(2)}, u32[]{:S(2)}) collective-permute-start(bf16[144,1152]{1,0:T(8,128)(2,1)} %shard_map.95.refs_0_.own), channel_id=1, source_target_pairs={{0,64},{64,0},{128,192},{192,128},{1,65},{65,1},{129,193},{193,129... | collective-permute-start | bytes 995336 | tf_op jit(solution)/shard_map/ppermute | solution.py:40
  47.1 28.2 %collective-permute-start.9 = (bf16[144,1152]{1,0:T(8,128)(2,1)}, bf16[144,1152]{1,0:T(8,128)(2,1)S(1)}, u32[]{:S(2)}, u32[]{:S(2)}) collective-permute-start(bf16[144,1152]{1,0:T(8,128)(2,1)} %shard_map.95.refs_0_.own), channel_id=1, source_target_pairs={{0,128},{64,192},{128,0},{192,64},{1,129},{65,193},{129,1},{193,65... | collective-permute-start | bytes 995336 | tf_op jit(solution)/shard_map/ppermute | solution.py:40
  50.0 25.3 %collective-permute-start.7 = (bf16[144,1152]{1,0:T(8,128)(2,1)S(1)}, bf16[144,1152]{1,0:T(8,128)(2,1)S(1)}, u32[]{:S(2)}, u32[]{:S(2)}) collective-permute-start(bf16[144,1152]{1,0:T(8,128)(2,1)S(1)} %collective-permute-done.5.refs_2_), channel_id=1, source_target_pairs={{0,48},{16,32},{32,16},{48,0},{1,49},{17,33},{33,17},{49,1},{2,50}... | collective-permute-start | bytes 995336 | tf_op jit(solution)/shard_map/ppermute | solution.py:40
  66.5 11.3 %all-to-all-start = ((bf16[4,304,128]{2,1,0:T(8,128)(2,1)}), bf16[4,304,128]{2,1,0:T(8,128)(2,1)S(1)}, u32[]{:S(2)}, u32[]{:S(2)}) async-start(bf16[4,304,128]{2,1,0:T(8,128)(2,1)} %shard_map.98), calls=%async_computation | async-start | bytes 622592 | tf_op jit(solution)/shard_map/all_to_all | solution.py:355
  79.9 8.9 %collective-permute-start.10 = (bf16[32,48,128]{2,1,0:T(8,128)(2,1)S(1)}, bf16[32,48,128]{2,1,0:T(8,128)(2,1)S(1)}, u32[]{:S(2)}, u32[]{:S(2)}) collective-permute-start(bf16[32,48,128]{2,1,0:T(8,128)(2,1)S(1)} %get-tuple-element.57), channel_id=1, source_target_pairs={{0,8},{8,0},{1,9},{9,1},{2,10},{10,2},{3,11},{11,3},{4,12},{12,4},... | collective-permute-start | bytes 1179656 | tf_op jit(solution)/shard_map/ppermute | solution.py:40
  84.2 10.4 %collective-permute-start.11 = (bf16[288,128]{1,0:T(8,128)(2,1)}, bf16[288,128]{1,0:T(8,128)(2,1)S(1)}, u32[]{:S(2)}, u32[]{:S(2)}) collective-permute-start(bf16[288,128]{1,0:T(8,128)(2,1)} %get-tuple-element.68), channel_id=1, source_target_pairs={{0,1},{1,2},{2,3},{3,0},{4,5},{5,6},{6,7},{7,4},{8,9},{9,10},{10,1... | collective-permute-start | bytes 221192 | tf_op jit(solution)/shard_map/ppermute | solution.py:340
  84.8 9.8 %collective-permute-start.12 = (bf16[288,128]{1,0:T(8,128)(2,1)}, bf16[288,128]{1,0:T(8,128)(2,1)S(1)}, u32[]{:S(2)}, u32[]{:S(2)}) collective-permute-start(bf16[288,128]{1,0:T(8,128)(2,1)} %get-tuple-element.69), channel_id=1, source_target_pairs={{0,2},{1,3},{2,0},{3,1},{4,6},{5,7},{6,4},{7,5},{8,10},{9,11},{10,... | collective-permute-start | bytes 221192 | tf_op jit(solution)/shard_map/ppermute | solution.py:340
  87.3 7.3 %collective-permute-start.13 = (bf16[288,128]{1,0:T(8,128)(2,1)}, bf16[288,128]{1,0:T(8,128)(2,1)S(1)}, u32[]{:S(2)}, u32[]{:S(2)}) collective-permute-start(bf16[288,128]{1,0:T(8,128)(2,1)} %get-tuple-element.70), channel_id=1, source_target_pairs={{0,3},{1,0},{2,1},{3,2},{4,7},{5,4},{6,5},{7,6},{8,11},{9,8},{10,9... | collective-permute-start | bytes 221192 | tf_op jit(solution)/shard_map/ppermute | solution.py:340
  89.6 20.1 %all-to-all-start.1 = ((bf16[32,48,128]{2,1,0:T(8,128)(2,1)}), bf16[32,48,128]{2,1,0:T(8,128)(2,1)S(1)}, u32[]{:S(2)}, u32[]{:S(2)}) async-start(bf16[32,48,128]{2,1,0:T(8,128)(2,1)} %add_convert_fusion.1), calls=%async_computation.1 | async-start | bytes 786432 | tf_op jit(solution)/shard_map/all_to_all | solution.py:348
  98.8 1.8 %collective-permute-start.14 = (bf16[32,48,128]{2,1,0:T(8,128)(2,1)S(1)}, bf16[32,48,128]{2,1,0:T(8,128)(2,1)S(1)}, u32[]{:S(2)}, u32[]{:S(2)}) collective-permute-start(bf16[32,48,128]{2,1,0:T(8,128)(2,1)S(1)} %get-tuple-element.72), channel_id=1, source_target_pairs={{0,8},{8,0},{1,9},{9,1},{2,10},{10,2},{3,11},{11,3},{4,12},{12,4},... | collective-permute-start | bytes 1179656 | tf_op jit(solution)/shard_map/ppermute | solution.py:40
  109.7 19.4 %all-to-all-start.2 = ((bf16[32,48,128]{2,1,0:T(8,128)(2,1)}), bf16[32,48,128]{2,1,0:T(8,128)(2,1)S(1)}, u32[]{:S(2)}, u32[]{:S(2)}) async-start(bf16[32,48,128]{2,1,0:T(8,128)(2,1)} %add_convert_fusion), calls=%async_computation.2 | async-start | bytes 786432 | tf_op jit(solution)/shard_map/all_to_all | solution.py:348
  (11 other events, 52.4 us)
Sparse Core Ops, SparseCore 0:
  9.8 29.5 all-gather.4
  41.2 27.6 all-gather.6

commit v5 on v4

--- a/solution.py
+++ b/solution.py
@@ -316,32 +316,31 @@
     ways = lax.axis_size("dx")
     spot = jnp.stack([lax.axis_index("dx"), lax.axis_index("lc")]).astype(jnp.int32)
     scal = jnp.stack([jnp.exp(heat_log[0]), shift_value[0]])
-    img_feat = lax.all_gather(pictures[0], "dx", axis=0, tiled=True)
-    txt_feat = lax.all_gather(sentences[0], "dx", axis=0, tiled=True)
-
     txt = project(sentences[0], sentence_weights, keys)
     txt_a = exchange(txt, "lz", 1)
+    txt_b = exchange(txt, "lz", 2)
     txt_y2 = exchange(txt, "ly", 2)
     txt_y1 = exchange(txt, "ly", 1)
     txt_c = exchange(txt, "lc", 1)
+    img_feat = lax.all_gather(after(pictures[0], txt), "dx", axis=0, tiled=True)
+    txt_feat = lax.all_gather(after(sentences[0], txt), "dx", axis=0, tiled=True)
+
     img = project(after(pictures[0], txt_c), picture_weights, keys)
-    txt_b = exchange(after(txt_a, txt_y1, txt_y2), "lz", 3)
-
-    img_a = exchange(after(img, txt_a), "lz", 1)
+    img_a = exchange(img, "lz", 1)
     img_c = exchange(img, "lc", 1)
-    img_b = exchange(img_a, "lz", 3)
-    img_n = after(img, img_a)
+    img_n = after(img, txt_y1, txt_y2)
     img_y2 = exchange(img_n, "ly", 2)
     img_y1 = exchange(img_n, "ly", 1)
+    img_b = exchange(img_a, "lz", 3)
 
     count = 2 * QUADS * lax.axis_size("dz") * ways
 
     def turn(array, step):
         return lax.ppermute(array, "dx", [(i, (i + step) % ways) for i in range(ways)])
 
-    def share(with_stats, feat, spreads):
+    def share(with_stats, feat, spreads, *others):
         kept, given = heads(with_stats, spot, feat, spreads)
-        taken = exchange(given, "lc", 1)
+        taken = after(exchange(given, "lc", 1), *others)
         return (kept + taken.astype(F32)).astype(BF16)
 
     def collect(sums):
@@ -350,16 +349,15 @@
     img_part = early(
         True, scal, pictures[0], picture_weights, keys, img, [txt, txt_c, txt_y1, txt_y2, txt_a]
     )
-    last, img_feat = lax.optimization_barrier((txt_b, img_feat, img_a, img_c))[:2]
+    last = after(txt_b, img_feat, img_a, img_c, img_y1, img_y2)
     img_outs = late(True, ways, spot, scal, img, img_part, [last])[0]
     img_cols = lax.all_to_all(img_outs, "dx", 0, 0, tiled=True)
     txt_part = early(
-        False, scal, sentences[0], sentence_weights, keys, txt, [img, img_c, img_a]
-    )
-    img_feat = after(img_feat, img_b, img_y1, img_y2, *txt_part)
-    img_sums = share(True, img_feat, [img_cols])
-    lasts = list(lax.optimization_barrier((img_y1, img_y2, img_b, img_cols))[:3])
-    outs = late(False, ways, spot, scal, txt, txt_part, lasts)
+        False, scal, sentences[0], sentence_weights, keys, txt, [img, img_c, img_y1, img_y2, img_a]
+    )
+    img_sums = share(True, after(img_feat, img_b, *txt_part), [img_cols])
+    last = after(img_b, img_cols)
+    outs = late(False, ways, spot, scal, txt, txt_part, [last])
     *outs, txt_feat = lax.optimization_barrier((*outs, txt_feat))
     txt_cols = [outs[0]] + [turn(out, step) for step, out in enumerate(outs) if step]
     txt_sums = share(False, txt_feat, txt_cols)

time: 137 us -> 146 us (1.066)
  waiting for transfers between devices: 40.2 us -> 54.4 us
  starting transfers between devices: 43.7 us -> 39.5 us
  local copies, waits for them, and re-layouts: 5.03 us -> 3.46 us
    ppermute x12, waiting for transfers between devices: 15.5 us -> 31.1 us  [exchange(): lax.ppermute(array, axis, [(i, i ^ apart) for i in range(lax.axis_size(ax...]
    ppermute x12, starting transfers between devices: 25 us -> 21.7 us  [exchange(): lax.ppermute(array, axis, [(i, i ^ apart) for i in range(lax.axis_size(ax...]
    unnamed x30, local copies, waits for them, and re-layouts: 4.52 us -> 2.95 us
  transfers between devices with their start and end apart: 20 -> 20, of which waited for: 7 -> 7; matrix products, arithmetic and copies ran while one was open for 2% -> 2% of each run, Pallas kernels for 21% -> 17%
where the time goes in v5:
time: 146 us; the launch traced here: 145 us
  waiting for transfers between devices  54.4 us (37%)
  starting transfers between devices  39.5 us (27%)
  Pallas kernels  29.4 us (20%)
  between operations  15.7 us (11%)
  local copies, waits for them, and re-layouts  3.46 us (2%)
  other arithmetic  2.96 us (2%)
    ppermute x12, waiting for transfers between devices, exchange(): lax.ppermute(array, axis, [(i, i ^ apart) for i in range(lax.axis_size(ax...  31.1 us
    ppermute x12, starting transfers between devices, exchange(): lax.ppermute(array, axis, [(i, i ^ apart) for i in range(lax.axis_size(ax...  21.7 us
    all_to_all x2, waiting for transfers between devices, collect(): lax.all_to_all(sums, ('ly', 'lz', 'dz'), 0, 0, tiled=True)  21 us
    pallas_call x2, Pallas kernels, early(): pl.pallas_call(functools.partial(early_kernel, with_stats), in_specs=[SME...  10.8 us
    all_to_all x2, starting transfers between devices, collect(): lax.all_to_all(sums, ('ly', 'lz', 'dz'), 0, 0, tiled=True)  8.61 us
    pallas_call x2, Pallas kernels, project(): pl.pallas_call(project_kernel, in_specs=[pl.BlockSpec(memory_space=pltpu....  6.67 us
    pallas_call x2, Pallas kernels, late(): pl.pallas_call(functools.partial(late_kernel, with_stats, ways, len(block...  6.22 us
    ppermute x3, starting transfers between devices, turn(): lax.ppermute(array, 'dx', [(i, (i + step) % ways) for i in range(ways)])  4.66 us
  transfers between devices with their start and end apart: 20, of which 7 were waited for; matrix products, arithmetic and copies ran while one was open for 2% of the time, Pallas kernels for 17%

profile of v5, /device:TPU:32, one launch (start us, length us, event | category | flops | bytes accessed | tf_op | source)
XLA Modules:
  0.0 145.3 jit_solution(454450563905877608)
XLA Ops:
  7.2 3.3 %shard_map.94.own.refs_0_ = bf16[144,1152]{1,0:T(8,128)(2,1)} custom-call(bf16[128,1152]{1,0:T(8,128)(2,1)} %bitcast.9, bf16[1152,1152]{1,0:T(8,128)(2,1)} %w.2, s32[1,128]{1,0:T(1,128)} %key.3), custom_call_target="tpu_custom_call" | custom-call | flops 339738624 | bytes 4194304 | tf_op jit(solution)/shard_map/pallas_call | solution.py:85
  11.4 1.7 %collective-permute-start.4 = (bf16[144,1152]{1,0:T(8,128)(2,1)}, bf16[144,1152]{1,0:T(8,128)(2,1)S(1)}, u32[]{:S(2)}, u32[]{:S(2)}) collective-permute-start(bf16[144,1152]{1,0:T(8,128)(2,1)} %shard_map.94.own.refs_0_), channel_id=1, source_target_pairs={{0,64},{64,0},{128,192},{192,128},{1,65},{65,1},{129,193},{193,129... | collective-permute-start | bytes 995336 | tf_op jit(solution)/shard_map/ppermute | solution.py:40
  13.0 2.9 %collective-permute-start.5 = (bf16[144,1152]{1,0:T(8,128)(2,1)}, bf16[144,1152]{1,0:T(8,128)(2,1)S(1)}, u32[]{:S(2)}, u32[]{:S(2)}) collective-permute-start(bf16[144,1152]{1,0:T(8,128)(2,1)} %shard_map.94.own.refs_0_), channel_id=1, source_target_pairs={{0,128},{64,192},{128,0},{192,64},{1,129},{65,193},{129,1},{193,65... | collective-permute-start | bytes 995336 | tf_op jit(solution)/shard_map/ppermute | solution.py:40
  15.9 3.3 %collective-permute-start.8 = (bf16[144,1152]{1,0:T(8,128)(2,1)}, bf16[144,1152]{1,0:T(8,128)(2,1)S(1)}, u32[]{:S(2)}, u32[]{:S(2)}) collective-permute-start(bf16[144,1152]{1,0:T(8,128)(2,1)} %shard_map.94.own.refs_0_), channel_id=1, source_target_pairs={{0,16},{16,0},{32,48},{48,32},{1,17},{17,1},{33,49},{49,33},{2,18}... | collective-permute-start | bytes 995336 | tf_op jit(solution)/shard_map/ppermute | solution.py:40
  19.2 3.4 %shard_map.95.refs_0_.own = bf16[144,1152]{1,0:T(8,128)(2,1)} custom-call(bf16[128,1152]{1,0:T(8,128)(2,1)} %bitcast.7, bf16[1152,1152]{1,0:T(8,128)(2,1)} %w.3, s32[1,128]{1,0:T(1,128)} %key.3), custom_call_target="tpu_custom_call" | custom-call | flops 339738624 | bytes 4194304 | tf_op jit(solution)/shard_map/pallas_call | solution.py:85
  22.7 5.9 %collective-permute-start.9 = (bf16[144,1152]{1,0:T(8,128)(2,1)S(1)}, bf16[144,1152]{1,0:T(8,128)(2,1)S(1)}, u32[]{:S(2)}, u32[]{:S(2)}) collective-permute-start(bf16[144,1152]{1,0:T(8,128)(2,1)S(1)} %copy-done.5), channel_id=1, source_target_pairs={{0,32},{16,48},{32,0},{48,16},{1,33},{17,49},{33,1},{49,17},{2,34}... | collective-permute-start | bytes 995336 | tf_op jit(solution)/shard_map/ppermute | solution.py:40
  28.7 2.7 %collective-permute-done.5.refs_3_ = bf16[144,1152]{1,0:T(8,128)(2,1)S(1)} collective-permute-done((bf16[144,1152]{1,0:T(8,128)(2,1)}, bf16[144,1152]{1,0:T(8,128)(2,1)S(1)}, u32[]{:S(2)}, u32[]{:S(2)}) %collective-permute-start.5) | collective-permute-done | bytes 331808 | tf_op jit(solution)/shard_map/ppermute | solution.py:40
  33.0 21.7 %collective-permute-done.8.refs_4_ = bf16[144,1152]{1,0:T(8,128)(2,1)S(1)} collective-permute-done((bf16[144,1152]{1,0:T(8,128)(2,1)}, bf16[144,1152]{1,0:T(8,128)(2,1)S(1)}, u32[]{:S(2)}, u32[]{:S(2)}) %collective-permute-start.8) | collective-permute-done | bytes 331808 | tf_op jit(solution)/shard_map/ppermute | solution.py:40
  56.7 5.0 %collective-permute-done.1.refs_4_ = bf16[144,1152]{1,0:T(8,128)(2,1)S(1)} collective-permute-done((bf16[144,1152]{1,0:T(8,128)(2,1)}, bf16[144,1152]{1,0:T(8,128)(2,1)S(1)}, u32[]{:S(2)}, u32[]{:S(2)}) %collective-permute-start.1) | collective-permute-done | bytes 331808 | tf_op jit(solution)/shard_map/ppermute | solution.py:40
  61.7 5.9 %collective-permute-start.2 = (bf16[144,1152]{1,0:T(8,128)(2,1)S(1)}, bf16[144,1152]{1,0:T(8,128)(2,1)}, u32[]{:S(2)}, u32[]{:S(2)}) collective-permute-start(bf16[144,1152]{1,0:T(8,128)(2,1)S(1)} %collective-permute-done.1.refs_4_), channel_id=1, source_target_pairs={{0,48},{16,32},{32,16},{48,0},{1,49},{17,33},{33,17},{49,1},{2,50}... | collective-permute-start | bytes 995336 | tf_op jit(solution)/shard_map/ppermute | solution.py:40
  68.2 5.5 %shard_map.97 = (f32[128,1152]{1,0:T(8,128)}, f32[128,1152]{1,0:T(8,128)}, f32[128,128]{1,0:T(8,128)}, f32[128,128]{1,0:T(8,128)}, f32[3,128,128]{2,1,0:T(8,128)}) custom-call(f32[2]{0:T(128)} %pad_maximum_fusion.scal, bf16[128,1152]{1,0:T(8,128)(2,1)} %bitcast.8, bf16[1152,1152]{1,0:T(8,128)(2,1)} %w.3, s32[1,128]{1,0:T(1,128)} %key.3, ...), custom_call_target="tpu_custom_call" | custom-call | flops 377487360 | bytes 8388608 | tf_op jit(solution)/shard_map/pallas_call | solution.py:146
  74.6 3.1 %shard_map.98 = bf16[4,304,128]{2,1,0:T(8,128)(2,1)} custom-call(s32[2]{0:T(128)} %pad_add_fusion.spot, f32[2]{0:T(128)} %pad_maximum_fusion.scal, bf16[144,1152]{1,0:T(8,128)(2,1)} %shard_map.95.refs_0_.own, f32[128,1152]{1,0:T(8,128)} %get-tuple-element.45.total_ref, f32[128,1152]{1,0:T(8,128)} %get-tuple-element.46.unit, ...), custom_call_target="tpu_custom_call" | custom-call | flops 150994944 | bytes 4194304 | tf_op jit(solution)/shard_map/pallas_call | solution.py:207
  77.7 4.4 %all-to-all-start = ((bf16[4,304,128]{2,1,0:T(8,128)(2,1)}), bf16[4,304,128]{2,1,0:T(8,128)(2,1)S(1)}, u32[]{:S(2)}, u32[]{:S(2)}) async-start(bf16[4,304,128]{2,1,0:T(8,128)(2,1)} %shard_map.98), calls=%async_computation | async-start | bytes 622592 | tf_op jit(solution)/shard_map/all_to_all | solution.py:354
  82.2 5.4 %shard_map.96 = (f32[128,1152]{1,0:T(8,128)}, f32[128,1152]{1,0:T(8,128)}, f32[128,128]{1,0:T(8,128)}, f32[128,128]{1,0:T(8,128)}, f32[3,128,128]{2,1,0:T(8,128)}) custom-call(f32[2]{0:T(128)} %pad_maximum_fusion.scal, bf16[128,1152]{1,0:T(8,128)(2,1)} %bitcast.11, bf16[1152,1152]{1,0:T(8,128)(2,1)} %w.2, s32[1,128]{1,0:T(1,128)} %key.3, ...), custom_call_target="tpu_custom_call" | custom-call | flops 377487360 | bytes 8388608 | tf_op jit(solution)/shard_map/pallas_call | solution.py:146
  87.5 1.6 %all-to-all-done.refs_0_ = bf16[4,304,128]{2,1,0:T(8,128)(2,1)S(1)} async-done(((bf16[4,304,128]{2,1,0:T(8,128)(2,1)}), bf16[4,304,128]{2,1,0:T(8,128)(2,1)S(1)}, u32[]{:S(2)}, u32[]{:S(2)}) %all-to-all-start) | async-done | bytes 311328 | tf_op jit(solution)/shard_map/all_to_all | solution.py:354
  89.1 2.0 %shard_map.99 = (f32[32,48,128]{2,1,0:T(8,128)S(1)}, bf16[32,48,128]{2,1,0:T(8,128)(2,1)S(1)}) custom-call(s32[2]{0:T(128)S(1)} %copy-done.3, bf16[512,1152]{1,0:T(8,128)(2,1)S(1)} %copy-done.1, bf16[4,304,128]{2,1,0:T(8,128)(2,1)S(1)} %all-to-all-done.refs_0_), custom_call_target="tpu_custom_call" | custom-call | flops 339738624 | bytes 4194304 | tf_op jit(solution)/shard_map/pallas_call | solution.py:270
  91.2 3.1 %shard_map.101 = (bf16[288,128]{1,0:T(8,128)(2,1)}, bf16[288,128]{1,0:T(8,128)(2,1)}, bf16[288,128]{1,0:T(8,128)(2,1)}, bf16[288,128]{1,0:T(8,128)(2,1)}) custom-call(s32[2]{0:T(128)} %pad_add_fusion.spot, f32[2]{0:T(128)} %pad_maximum_fusion.scal, bf16[144,1152]{1,0:T(8,128)(2,1)} %shard_map.94.own.refs_0_, f32[128,1152]{1,0:T(8,128)} %get-tuple-element.39.total_ref, ...), custom_call_target="tpu_custom_call" | custom-call | flops 150994944 | bytes 4194304 | tf_op jit(solution)/shard_map/pallas_call | solution.py:207
  94.9 2.6 %collective-permute-start.12 = (bf16[288,128]{1,0:T(8,128)(2,1)}, bf16[288,128]{1,0:T(8,128)(2,1)S(1)}, u32[]{:S(2)}, u32[]{:S(2)}) collective-permute-start(bf16[288,128]{1,0:T(8,128)(2,1)} %get-tuple-element.63), channel_id=1, source_target_pairs={{0,2},{1,3},{2,0},{3,1},{4,6},{5,7},{6,4},{7,5},{8,10},{9,11},{10,... | collective-permute-start | bytes 221192 | tf_op jit(solution)/shard_map/ppermute | solution.py:339
  99.9 3.9 %all-to-all-start.1 = ((bf16[32,48,128]{2,1,0:T(8,128)(2,1)}), bf16[32,48,128]{2,1,0:T(8,128)(2,1)S(1)}, u32[]{:S(2)}, u32[]{:S(2)}) async-start(bf16[32,48,128]{2,1,0:T(8,128)(2,1)} %add_convert_fusion.1), calls=%async_computation.1 | async-start | bytes 786432 | tf_op jit(solution)/shard_map/all_to_all | solution.py:347
  106.0 2.0 %shard_map.102 = (f32[32,48,128]{2,1,0:T(8,128)S(1)}, bf16[32,48,128]{2,1,0:T(8,128)(2,1)S(1)}) custom-call(s32[2]{0:T(128)S(1)} %copy-done.4, bf16[512,1152]{1,0:T(8,128)(2,1)S(1)} %copy-done, bf16[288,128]{1,0:T(8,128)(2,1)S(1)} %copy-done.2, bf16[288,128]{1,0:T(8,128)(2,1)S(1)} %collective-permute-done.11.refs_1_, ...), custom_call_target="tpu_custom_call" | custom-call | flops 339738624 | bytes 4194304 | tf_op jit(solution)/shard_map/pallas_call | solution.py:270
  108.1 1.7 %collective-permute-done.14 = bf16[32,48,128]{2,1,0:T(8,128)(2,1)S(1)} collective-permute-done((bf16[32,48,128]{2,1,0:T(8,128)(2,1)S(1)}, bf16[32,48,128]{2,1,0:T(8,128)(2,1)S(1)}, u32[]{:S(2)}, u32[]{:S(2)}) %collective-permute-start.14) | collective-permute-done | bytes 393248 | tf_op jit(solution)/shard_map/ppermute | solution.py:40
  110.6 7.9 %all-to-all-done.1.parts = bf16[32,48,128]{2,1,0:T(8,128)(2,1)S(1)} async-done(((bf16[32,48,128]{2,1,0:T(8,128)(2,1)}), bf16[32,48,128]{2,1,0:T(8,128)(2,1)S(1)}, u32[]{:S(2)}, u32[]{:S(2)}) %all-to-all-start.1) | async-done | bytes 393248 | tf_op jit(solution)/shard_map/all_to_all | solution.py:347
  118.6 4.7 %all-to-all-start.2 = ((bf16[32,48,128]{2,1,0:T(8,128)(2,1)}), bf16[32,48,128]{2,1,0:T(8,128)(2,1)S(1)}, u32[]{:S(2)}, u32[]{:S(2)}) async-start(bf16[32,48,128]{2,1,0:T(8,128)(2,1)} %add_convert_fusion), calls=%async_computation.2 | async-start | bytes 786432 | tf_op jit(solution)/shard_map/all_to_all | solution.py:347
  124.6 13.1 %all-to-all-done.2.parts = bf16[32,48,128]{2,1,0:T(8,128)(2,1)S(1)} async-done(((bf16[32,48,128]{2,1,0:T(8,128)(2,1)}), bf16[32,48,128]{2,1,0:T(8,128)(2,1)S(1)}, u32[]{:S(2)}, u32[]{:S(2)}) %all-to-all-start.2) | async-done | bytes 393248 | tf_op jit(solution)/shard_map/all_to_all | solution.py:347
  (63 shorter events, 13.0 us)
Async XLA Ops:
  7.2 66.6 %all-gather.3.cloned.1.call-start = ((), (), s32[]{:S(2)}) async-start(), calls=%async_computation.3 | async-start | bytes 1474560 | tf_op jit(solution)/shard_map/all_gather | solution.py:325
  10.5 83.8 %all-gather.5.cloned.1.call-start = ((), (), s32[]{:S(2)}) async-start(), calls=%async_computation.4 | async-start | bytes 1474560 | tf_op jit(solution)/shard_map/all_gather | solution.py:326
  11.3 7.9 %collective-permute-start = (bf16[144,1152]{1,0:T(8,128)(2,1)}, bf16[144,1152]{1,0:T(8,128)(2,1)S(1)}, u32[]{:S(2)}, u32[]{:S(2)}) collective-permute-start(bf16[144,1152]{1,0:T(8,128)(2,1)} %shard_map.94.own.refs_0_), channel_id=1, source_target_pairs={{0,8},{8,0},{1,9},{9,1},{2,10},{10,2},{3,11},{11,3},{4,12},{12,4},... | collective-permute-start | bytes 995336 | tf_op jit(solution)/shard_map/ppermute | solution.py:40
  11.4 17.3 %collective-permute-start.4 = (bf16[144,1152]{1,0:T(8,128)(2,1)}, bf16[144,1152]{1,0:T(8,128)(2,1)S(1)}, u32[]{:S(2)}, u32[]{:S(2)}) collective-permute-start(bf16[144,1152]{1,0:T(8,128)(2,1)} %shard_map.94.own.refs_0_), channel_id=1, source_target_pairs={{0,64},{64,0},{128,192},{192,128},{1,65},{65,1},{129,193},{193,129... | collective-permute-start | bytes 995336 | tf_op jit(solution)/shard_map/ppermute | solution.py:40
  13.0 18.3 %collective-permute-start.5 = (bf16[144,1152]{1,0:T(8,128)(2,1)}, bf16[144,1152]{1,0:T(8,128)(2,1)S(1)}, u32[]{:S(2)}, u32[]{:S(2)}) collective-permute-start(bf16[144,1152]{1,0:T(8,128)(2,1)} %shard_map.94.own.refs_0_), channel_id=1, source_target_pairs={{0,128},{64,192},{128,0},{192,64},{1,129},{65,193},{129,1},{193,65... | collective-permute-start | bytes 995336 | tf_op jit(solution)/shard_map/ppermute | solution.py:40
  15.9 38.8 %collective-permute-start.8 = (bf16[144,1152]{1,0:T(8,128)(2,1)}, bf16[144,1152]{1,0:T(8,128)(2,1)S(1)}, u32[]{:S(2)}, u32[]{:S(2)}) collective-permute-start(bf16[144,1152]{1,0:T(8,128)(2,1)} %shard_map.94.own.refs_0_), channel_id=1, source_target_pairs={{0,16},{16,0},{32,48},{48,32},{1,17},{17,1},{33,49},{49,33},{2,18}... | collective-permute-start | bytes 995336 | tf_op jit(solution)/shard_map/ppermute | solution.py:40
  19.2 49.0 %copy-start.10 = (bf16[144,1152]{1,0:T(8,128)(2,1)}, bf16[144,1152]{1,0:T(8,128)(2,1)S(1)}, u32[]{:S(2)}) copy-start(bf16[144,1152]{1,0:T(8,128)(2,1)S(1)} %collective-permute-done.refs_1_) | copy-start | bytes 995332
  22.6 39.1 %collective-permute-start.1 = (bf16[144,1152]{1,0:T(8,128)(2,1)}, bf16[144,1152]{1,0:T(8,128)(2,1)S(1)}, u32[]{:S(2)}, u32[]{:S(2)}) collective-permute-start(bf16[144,1152]{1,0:T(8,128)(2,1)} %shard_map.95.refs_0_.own), channel_id=1, source_target_pairs={{0,16},{16,0},{32,48},{48,32},{1,17},{17,1},{33,49},{49,33},{2,18}... | collective-permute-start | bytes 995336 | tf_op jit(solution)/shard_map/ppermute | solution.py:40
  22.7 51.0 %collective-permute-start.9 = (bf16[144,1152]{1,0:T(8,128)(2,1)S(1)}, bf16[144,1152]{1,0:T(8,128)(2,1)S(1)}, u32[]{:S(2)}, u32[]{:S(2)}) collective-permute-start(bf16[144,1152]{1,0:T(8,128)(2,1)S(1)} %copy-done.5), channel_id=1, source_target_pairs={{0,32},{16,48},{32,0},{48,16},{1,33},{17,49},{33,1},{49,17},{2,34}... | collective-permute-start | bytes 995336 | tf_op jit(solution)/shard_map/ppermute | solution.py:40
  28.7 39.6 %copy-start.11 = (bf16[144,1152]{1,0:T(8,128)(2,1)}, bf16[144,1152]{1,0:T(8,128)(2,1)S(1)}, u32[]{:S(2)}) copy-start(bf16[144,1152]{1,0:T(8,128)(2,1)S(1)} %collective-permute-done.4.refs_2_) | copy-start | bytes 995332
  31.4 36.8 %copy-start.13 = (bf16[144,1152]{1,0:T(8,128)(2,1)}, bf16[144,1152]{1,0:T(8,128)(2,1)S(1)}, u32[]{:S(2)}) copy-start(bf16[144,1152]{1,0:T(8,128)(2,1)S(1)} %collective-permute-done.5.refs_3_) | copy-start | bytes 995332
  31.4 42.4 %collective-permute-start.6 = (bf16[144,1152]{1,0:T(8,128)(2,1)}, bf16[144,1152]{1,0:T(8,128)(2,1)S(1)}, u32[]{:S(2)}, u32[]{:S(2)}) collective-permute-start(bf16[144,1152]{1,0:T(8,128)(2,1)} %shard_map.95.refs_0_.own), channel_id=1, source_target_pairs={{0,64},{64,0},{128,192},{192,128},{1,65},{65,1},{129,193},{193,129... | collective-permute-start | bytes 995336 | tf_op jit(solution)/shard_map/ppermute | solution.py:40
  31.5 42.2 %collective-permute-start.7 = (bf16[144,1152]{1,0:T(8,128)(2,1)}, bf16[144,1152]{1,0:T(8,128)(2,1)S(1)}, u32[]{:S(2)}, u32[]{:S(2)}) collective-permute-start(bf16[144,1152]{1,0:T(8,128)(2,1)} %shard_map.95.refs_0_.own), channel_id=1, source_target_pairs={{0,128},{64,192},{128,0},{192,64},{1,129},{65,193},{129,1},{193,65... | collective-permute-start | bytes 995336 | tf_op jit(solution)/shard_map/ppermute | solution.py:40
  54.7 19.0 %collective-permute-start.3 = (bf16[144,1152]{1,0:T(8,128)(2,1)}, bf16[144,1152]{1,0:T(8,128)(2,1)S(1)}, u32[]{:S(2)}, u32[]{:S(2)}) collective-permute-start(bf16[144,1152]{1,0:T(8,128)(2,1)} %shard_map.95.refs_0_.own), channel_id=1, source_target_pairs={{0,8},{8,0},{1,9},{9,1},{2,10},{10,2},{3,11},{11,3},{4,12},{12,4},... | collective-permute-start | bytes 995336 | tf_op jit(solution)/shard_map/ppermute | solution.py:40
  61.7 25.8 %collective-permute-start.2 = (bf16[144,1152]{1,0:T(8,128)(2,1)S(1)}, bf16[144,1152]{1,0:T(8,128)(2,1)}, u32[]{:S(2)}, u32[]{:S(2)}) collective-permute-start(bf16[144,1152]{1,0:T(8,128)(2,1)S(1)} %collective-permute-done.1.refs_4_), channel_id=1, source_target_pairs={{0,48},{16,32},{32,16},{48,0},{1,49},{17,33},{33,17},{49,1},{2,50}... | collective-permute-start | bytes 995336 | tf_op jit(solution)/shard_map/ppermute | solution.py:40
  77.7 11.4 %all-to-all-start = ((bf16[4,304,128]{2,1,0:T(8,128)(2,1)}), bf16[4,304,128]{2,1,0:T(8,128)(2,1)S(1)}, u32[]{:S(2)}, u32[]{:S(2)}) async-start(bf16[4,304,128]{2,1,0:T(8,128)(2,1)} %shard_map.98), calls=%async_computation | async-start | bytes 622592 | tf_op jit(solution)/shard_map/all_to_all | solution.py:354
  87.5 16.3 %copy-start.4 = (s32[2]{0:T(128)S(1)}, s32[2]{0:T(128)}, u32[]{:S(2)}) copy-start(s32[2]{0:T(128)} %pad_add_fusion.spot) | copy-start | bytes 28
  91.1 7.8 %collective-permute-start.10 = (bf16[32,48,128]{2,1,0:T(8,128)(2,1)S(1)}, bf16[32,48,128]{2,1,0:T(8,128)(2,1)S(1)}, u32[]{:S(2)}, u32[]{:S(2)}) collective-permute-start(bf16[32,48,128]{2,1,0:T(8,128)(2,1)S(1)} %get-tuple-element.52), channel_id=1, source_target_pairs={{0,8},{8,0},{1,9},{9,1},{2,10},{10,2},{3,11},{11,3},{4,12},{12,4},... | collective-permute-start | bytes 1179656 | tf_op jit(solution)/shard_map/ppermute | solution.py:40
  94.3 9.5 %collective-permute-start.11 = (bf16[288,128]{1,0:T(8,128)(2,1)}, bf16[288,128]{1,0:T(8,128)(2,1)S(1)}, u32[]{:S(2)}, u32[]{:S(2)}) collective-permute-start(bf16[288,128]{1,0:T(8,128)(2,1)} %get-tuple-element.62), channel_id=1, source_target_pairs={{0,1},{1,2},{2,3},{3,0},{4,5},{5,6},{6,7},{7,4},{8,9},{9,10},{10,1... | collective-permute-start | bytes 221192 | tf_op jit(solution)/shard_map/ppermute | solution.py:339
  94.9 8.9 %collective-permute-start.12 = (bf16[288,128]{1,0:T(8,128)(2,1)}, bf16[288,128]{1,0:T(8,128)(2,1)S(1)}, u32[]{:S(2)}, u32[]{:S(2)}) collective-permute-start(bf16[288,128]{1,0:T(8,128)(2,1)} %get-tuple-element.63), channel_id=1, source_target_pairs={{0,2},{1,3},{2,0},{3,1},{4,6},{5,7},{6,4},{7,5},{8,10},{9,11},{10,... | collective-permute-start | bytes 221192 | tf_op jit(solution)/shard_map/ppermute | solution.py:339
  97.5 6.3 %collective-permute-start.13 = (bf16[288,128]{1,0:T(8,128)(2,1)}, bf16[288,128]{1,0:T(8,128)(2,1)S(1)}, u32[]{:S(2)}, u32[]{:S(2)}) collective-permute-start(bf16[288,128]{1,0:T(8,128)(2,1)} %get-tuple-element.64), channel_id=1, source_target_pairs={{0,3},{1,0},{2,1},{3,2},{4,7},{5,4},{6,5},{7,6},{8,11},{9,8},{10,9... | collective-permute-start | bytes 221192 | tf_op jit(solution)/shard_map/ppermute | solution.py:339
  99.9 18.7 %all-to-all-start.1 = ((bf16[32,48,128]{2,1,0:T(8,128)(2,1)}), bf16[32,48,128]{2,1,0:T(8,128)(2,1)S(1)}, u32[]{:S(2)}, u32[]{:S(2)}) async-start(bf16[32,48,128]{2,1,0:T(8,128)(2,1)} %add_convert_fusion.1), calls=%async_computation.1 | async-start | bytes 786432 | tf_op jit(solution)/shard_map/all_to_all | solution.py:347
  108.0 1.8 %collective-permute-start.14 = (bf16[32,48,128]{2,1,0:T(8,128)(2,1)S(1)}, bf16[32,48,128]{2,1,0:T(8,128)(2,1)S(1)}, u32[]{:S(2)}, u32[]{:S(2)}) collective-permute-start(bf16[32,48,128]{2,1,0:T(8,128)(2,1)S(1)} %get-tuple-element.66), channel_id=1, source_target_pairs={{0,8},{8,0},{1,9},{9,1},{2,10},{10,2},{3,11},{11,3},{4,12},{12,4},... | collective-permute-start | bytes 1179656 | tf_op jit(solution)/shard_map/ppermute | solution.py:40
  118.6 19.1 %all-to-all-start.2 = ((bf16[32,48,128]{2,1,0:T(8,128)(2,1)}), bf16[32,48,128]{2,1,0:T(8,128)(2,1)S(1)}, u32[]{:S(2)}, u32[]{:S(2)}) async-start(bf16[32,48,128]{2,1,0:T(8,128)(2,1)} %add_convert_fusion), calls=%async_computation.2 | async-start | bytes 786432 | tf_op jit(solution)/shard_map/all_to_all | solution.py:347
  (11 other events, 85.1 us)
Sparse Core Ops, SparseCore 0:
  10.6 29.5 all-gather.2
  42.0 27.5 all-gather.4

commit v6 on v5

--- a/solution.py
+++ b/solution.py
@@ -68,13 +68,8 @@
         copies[2 + k].wait()
         span = slice(k * DEPTH, (k + 1) * DEPTH)
         u += mm(x[:, span], w[span])
-    out_ref[:ROWS, :] = (u / lengths(u)).astype(BF16)
     copies[1].wait()
-    digit = jnp.broadcast_to(key[...], (KEY_ROWS, ROWS))
-    row = lax.broadcasted_iota(jnp.int32, (KEY_ROWS, ROWS), 0)
-    digit = jnp.where(row == 0, digit >> 7, jnp.where(row == 1, digit & 127, 0))
-    out_ref[ROWS:, :] = jnp.zeros((KEY_ROWS, WIDTH), BF16)
-    out_ref[ROWS:, :ROWS] = digit.astype(F32).astype(BF16)
+    write_payload(out_ref, u / lengths(u), key[...])
 
 
 def lengths(u):
@@ -118,17 +113,37 @@
     return total, sums
 
 
-def early_kernel(with_stats, scal, x, w, key, own, *refs):
-    blocks, (total_ref, unit_ref, len_ref, key_ref, sum_ref) = refs[:-5], refs[-5:]
-    u = mm(x[...], w[...])
-    length = lengths(u)
-    unit_ref[...] = u / length
-    len_ref[...] = jnp.broadcast_to(length, len_ref.shape)
+def write_payload(out_ref, unit, key):
+    digit = jnp.broadcast_to(key, (KEY_ROWS, ROWS))
+    row = lax.broadcasted_iota(jnp.int32, (KEY_ROWS, ROWS), 0)
+    digit = jnp.where(row == 0, digit >> 7, jnp.where(row == 1, digit & 127, 0))
+    out_ref[:ROWS, :] = unit.astype(BF16)
+    out_ref[ROWS:, :] = jnp.zeros((KEY_ROWS, WIDTH), BF16)
+    out_ref[ROWS:, :ROWS] = digit.astype(F32).astype(BF16)
+
+
+def early_kernel(first, scal, x, w_hbm, key, *refs):
+    blocks, refs = refs[:-7], refs[-7:]
+    total_ref, unit_ref, len_ref, key_ref, sum_ref, w, sem = refs
+    own, blocks = (blocks[-1], blocks[:-1]) if first else (blocks[0], blocks[1:])
+    copy = pltpu.make_async_copy(w_hbm, w, sem)
+    copy.start()
     key_col = jnp.broadcast_to(key[...].astype(F32), (ROWS, ROWS)).T
     key_ref[...] = key_col
+
+    def norm():
+        copy.wait()
+        u = mm(x[...], w[...])
+        length = lengths(u)
+        unit_ref[...] = u / length
+        len_ref[...] = jnp.broadcast_to(length, len_ref.shape)
+
+    if first:
+        norm()
+        write_payload(own, unit_ref[...], key[...])
     zero = jnp.zeros((ROWS, ROWS), F32)
     total, sums = add_tiles(
-        with_stats,
+        first,
         scal,
         own[:ROWS, :],
         key_col,
@@ -139,18 +154,25 @@
     total_ref[...] = total
     for k in range(3):
         sum_ref[k] = sums[k]
-
-
-def early(with_stats, scal, x, w, keys, own, blocks):
+    if not first:
+        norm()
+
+
+def early(first, scal, x, w, keys, blocks):
     shapes = [(ROWS, WIDTH), (ROWS, WIDTH), (ROWS, LANES), (ROWS, ROWS), (3, ROWS, ROWS)]
-    return pl.pallas_call(
-        functools.partial(early_kernel, with_stats),
-        in_specs=[SMEM] + [VMEM] * (4 + len(blocks)),
-        out_specs=[VMEM] * len(shapes),
-        out_shape=[jax.ShapeDtypeStruct(shape, F32) for shape in shapes],
+    outs = [jax.ShapeDtypeStruct(shape, F32) for shape in shapes]
+    if first:
+        outs = [jax.ShapeDtypeStruct((ROWS + KEY_ROWS, WIDTH), BF16)] + outs
+    hbm = pl.BlockSpec(memory_space=pltpu.HBM)
+    return pl.pallas_call(
+        functools.partial(early_kernel, first),
+        in_specs=[SMEM, VMEM, hbm, VMEM] + [VMEM] * len(blocks),
+        out_specs=[VMEM] * len(outs),
+        out_shape=outs,
+        scratch_shapes=[pltpu.VMEM((WIDTH, WIDTH), BF16), pltpu.SemaphoreType.DMA],
         compiler_params=params(56),
         cost_estimate=cost(4 * 5 * ROWS * ROWS * WIDTH, 8 * 2**20),
-    )(scal, x, w, keys, own, *blocks)
+    )(scal, x, w, keys, *blocks)
 
 
 def late_kernel(with_stats, ways, count, spot, scal, own, total_ref, unit, length, key, acc, *refs):
@@ -318,17 +340,17 @@
     scal = jnp.stack([jnp.exp(heat_log[0]), shift_value[0]])
     txt = project(sentences[0], sentence_weights, keys)
     txt_a = exchange(txt, "lz", 1)
-    txt_b = exchange(txt, "lz", 2)
     txt_y2 = exchange(txt, "ly", 2)
     txt_y1 = exchange(txt, "ly", 1)
     txt_c = exchange(txt, "lc", 1)
     img_feat = lax.all_gather(after(pictures[0], txt), "dx", axis=0, tiled=True)
     txt_feat = lax.all_gather(after(sentences[0], txt), "dx", axis=0, tiled=True)
 
-    img = project(after(pictures[0], txt_c), picture_weights, keys)
-    img_a = exchange(img, "lz", 1)
-    img_c = exchange(img, "lc", 1)
-    img_n = after(img, txt_y1, txt_y2)
+    img, *img_part = early(True, scal, pictures[0], picture_weights, keys, [txt, txt_c])
+    txt_b = exchange(after(txt_a, txt_y1, txt_y2), "lz", 3)
+    img_a = exchange(after(img, txt_a), "lz", 1)
+    img_c = exchange(after(img, txt_a, txt_y1, txt_y2), "lc", 1)
+    img_n = after(img, img_c)
     img_y2 = exchange(img_n, "ly", 2)
     img_y1 = exchange(img_n, "ly", 1)
     img_b = exchange(img_a, "lz", 3)
@@ -346,17 +368,14 @@
     def collect(sums):
         return final(count, lax.all_to_all(sums, ("ly", "lz", "dz"), 0, 0, tiled=True))
 
-    img_part = early(
-        True, scal, pictures[0], picture_weights, keys, img, [txt, txt_c, txt_y1, txt_y2, txt_a]
-    )
     last = after(txt_b, img_feat, img_a, img_c, img_y1, img_y2)
-    img_outs = late(True, ways, spot, scal, img, img_part, [last])[0]
+    img_outs = late(True, ways, spot, scal, img, img_part, [txt_y1, txt_y2, txt_a, last])[0]
     img_cols = lax.all_to_all(img_outs, "dx", 0, 0, tiled=True)
     txt_part = early(
-        False, scal, sentences[0], sentence_weights, keys, txt, [img, img_c, img_y1, img_y2, img_a]
+        False, scal, sentences[0], sentence_weights, keys, [txt, img, img_c, img_y1, img_y2, img_a]
     )
     img_sums = share(True, after(img_feat, img_b, *txt_part), [img_cols])
-    last = after(img_b, img_cols)
+    last = after(img_b, img_sums)
     outs = late(False, ways, spot, scal, txt, txt_part, [last])
     *outs, txt_feat = lax.optimization_barrier((*outs, txt_feat))
     txt_cols = [outs[0]] + [turn(out, step) for step, out in enumerate(outs) if step]

time: 146 us -> 135 us (0.925)
  waiting for transfers between devices: 54.4 us -> 42.7 us
  starting transfers between devices: 39.5 us -> 42.7 us
  Pallas kernels: 29.4 us -> 26.8 us
    ppermute x12, waiting for transfers between devices: 31.1 us -> 19.3 us  [exchange(): lax.ppermute(array, axis, [(i, i ^ apart) for i in range(lax.axis_size(ax...]
    all_to_all x2, starting transfers between devices: 8.61 us -> 13 us  [collect(): lax.all_to_all(sums, ('ly', 'lz', 'dz'), 0, 0, tiled=True)]
    pallas_call x2 -> x1, Pallas kernels: 6.67 us -> 3.29 us  [project(): pl.pallas_call(project_kernel, in_specs=[pl.BlockSpec(memory_space=pltpu....]
  transfers between devices with their start and end apart: 20 -> 20, of which waited for: 7 -> 9; matrix products, arithmetic and copies ran while one was open for 2% -> 3% of each run, Pallas kernels for 17% -> 17%
where the time goes in v6:
time: 135 us; the launch traced here: 134 us
  starting transfers between devices  42.7 us (32%)
  waiting for transfers between devices  42.7 us (32%)
  Pallas kernels  26.8 us (20%)
  between operations  15.6 us (12%)
  local copies, waits for them, and re-layouts  3.59 us (3%)
  other arithmetic  2.86 us (2%)
    all_to_all x2, waiting for transfers between devices, collect(): lax.all_to_all(sums, ('ly', 'lz', 'dz'), 0, 0, tiled=True)  20.7 us
    ppermute x12, starting transfers between devices, exchange(): lax.ppermute(array, axis, [(i, i ^ apart) for i in range(lax.axis_size(ax...  20.6 us
    ppermute x12, waiting for transfers between devices, exchange(): lax.ppermute(array, axis, [(i, i ^ apart) for i in range(lax.axis_size(ax...  19.3 us
    all_to_all x2, starting transfers between devices, collect(): lax.all_to_all(sums, ('ly', 'lz', 'dz'), 0, 0, tiled=True)  13 us
    pallas_call x2, Pallas kernels, early(): pl.pallas_call(functools.partial(early_kernel, first), in_specs=[SMEM, VM...  10.4 us
    pallas_call x2, Pallas kernels, late(): pl.pallas_call(functools.partial(late_kernel, with_stats, ways, len(block...  7.54 us
    ppermute x3, starting transfers between devices, turn(): lax.ppermute(array, 'dx', [(i, (i + step) % ways) for i in range(ways)])  4.64 us
    all_to_all x1, starting transfers between devices, body(): img_cols = lax.all_to_all(img_outs, 'dx', 0, 0, tiled=True)  4.42 us
  transfers between devices with their start and end apart: 20, of which 9 were waited for; matrix products, arithmetic and copies ran while one was open for 3% of the time, Pallas kernels for 17%

profile of v6, /device:TPU:32, one launch (start us, length us, event | category | flops | bytes accessed | tf_op | source)
XLA Modules:
  0.0 134.2 jit_solution(12384514118061665107)
XLA Ops:
  7.2 3.3 %shard_map.94.refs_0_.own = bf16[144,1152]{1,0:T(8,128)(2,1)} custom-call(bf16[128,1152]{1,0:T(8,128)(2,1)} %bitcast.6, bf16[1152,1152]{1,0:T(8,128)(2,1)} %w_hbm.5, s32[1,128]{1,0:T(1,128)} %key.3), custom_call_target="tpu_custom_call" | custom-call | flops 339738624 | bytes 4194304 | tf_op jit(solution)/shard_map/pallas_call | solution.py:80
  10.7 3.4 %collective-permute-start.1 = (bf16[144,1152]{1,0:T(8,128)(2,1)}, bf16[144,1152]{1,0:T(8,128)(2,1)S(1)}, u32[]{:S(2)}, u32[]{:S(2)}) collective-permute-start(bf16[144,1152]{1,0:T(8,128)(2,1)} %shard_map.94.refs_0_.own), channel_id=1, source_target_pairs={{0,16},{16,0},{32,48},{48,32},{1,17},{17,1},{33,49},{49,33},{2,18}... | collective-permute-start | bytes 995336 | tf_op jit(solution)/shard_map/ppermute | solution.py:40
  15.6 2.9 %collective-permute-start.5 = (bf16[144,1152]{1,0:T(8,128)(2,1)}, bf16[144,1152]{1,0:T(8,128)(2,1)S(1)}, u32[]{:S(2)}, u32[]{:S(2)}) collective-permute-start(bf16[144,1152]{1,0:T(8,128)(2,1)} %shard_map.94.refs_0_.own), channel_id=1, source_target_pairs={{0,128},{64,192},{128,0},{192,64},{1,129},{65,193},{129,1},{193,65... | collective-permute-start | bytes 995336 | tf_op jit(solution)/shard_map/ppermute | solution.py:40
  21.2 5.4 %shard_map.95 = (bf16[144,1152]{1,0:T(8,128)(2,1)}, f32[128,1152]{1,0:T(8,128)}, f32[128,1152]{1,0:T(8,128)}, f32[128,128]{1,0:T(8,128)}, f32[128,128]{1,0:T(8,128)}, /*index=5*/f32[3,128,128]{2,1,0:T(8,128)}) custom-call(f32[2]{0:T(128)} %pad_maximum_fusion.scal, bf16[128,1152]{1,0:T(8,128)(2,1)} %bitcast.10, bf16[1152,1152]{1,0:T(8,128)(2,1)} %w_hbm.4, ...), custom_call_target="tpu_custom_call" | custom-call | flops 377487360 | bytes 8388608 | tf_op jit(solution)/shard_map/pallas_call | solution.py:167
  26.6 2.1 %collective-permute-done.1.refs_2_ = bf16[144,1152]{1,0:T(8,128)(2,1)S(1)} collective-permute-done((bf16[144,1152]{1,0:T(8,128)(2,1)}, bf16[144,1152]{1,0:T(8,128)(2,1)S(1)}, u32[]{:S(2)}, u32[]{:S(2)}) %collective-permute-start.1) | collective-permute-done | bytes 331808 | tf_op jit(solution)/shard_map/ppermute | solution.py:40
  28.7 5.0 %collective-permute-done.5.refs_1_ = bf16[144,1152]{1,0:T(8,128)(2,1)S(1)} collective-permute-done((bf16[144,1152]{1,0:T(8,128)(2,1)}, bf16[144,1152]{1,0:T(8,128)(2,1)S(1)}, u32[]{:S(2)}, u32[]{:S(2)}) %collective-permute-start.5) | collective-permute-done | bytes 331808 | tf_op jit(solution)/shard_map/ppermute | solution.py:40
  33.9 4.8 %collective-permute-start.9 = (bf16[144,1152]{1,0:T(8,128)(2,1)S(1)}, bf16[144,1152]{1,0:T(8,128)(2,1)S(1)}, u32[]{:S(2)}, u32[]{:S(2)}) collective-permute-start(bf16[144,1152]{1,0:T(8,128)(2,1)S(1)} %collective-permute-done.1.refs_2_), channel_id=1, source_target_pairs={{0,48},{16,32},{32,16},{48,0},{1,49},{17,33},{33,17},{49,1},{2,50}... | collective-permute-start | bytes 995336 | tf_op jit(solution)/shard_map/ppermute | solution.py:40
  40.4 8.3 %collective-permute-done.2.refs_5_ = bf16[144,1152]{1,0:T(8,128)(2,1)S(1)} collective-permute-done((bf16[144,1152]{1,0:T(8,128)(2,1)}, bf16[144,1152]{1,0:T(8,128)(2,1)S(1)}, u32[]{:S(2)}, u32[]{:S(2)}) %collective-permute-start.2) | collective-permute-done | bytes 331808 | tf_op jit(solution)/shard_map/ppermute | solution.py:40
  48.7 5.5 %collective-permute-start.3 = (bf16[144,1152]{1,0:T(8,128)(2,1)S(1)}, bf16[144,1152]{1,0:T(8,128)(2,1)S(1)}, u32[]{:S(2)}, u32[]{:S(2)}) collective-permute-start(bf16[144,1152]{1,0:T(8,128)(2,1)S(1)} %collective-permute-done.2.refs_5_), channel_id=1, source_target_pairs={{0,48},{16,32},{32,16},{48,0},{1,49},{17,33},{33,17},{49,1},{2,50}... | collective-permute-start | bytes 995336 | tf_op jit(solution)/shard_map/ppermute | solution.py:40
  55.5 4.5 %shard_map.97 = bf16[4,304,128]{2,1,0:T(8,128)(2,1)} custom-call(s32[2]{0:T(128)} %pad_add_fusion.spot, f32[2]{0:T(128)} %pad_maximum_fusion.scal, bf16[144,1152]{1,0:T(8,128)(2,1)} %get-tuple-element.43.refs_1_.own, f32[128,1152]{1,0:T(8,128)} %get-tuple-element.50.total_ref, f32[128,1152]{1,0:T(8,128)} %get-tuple-element.51.unit, ...), custom_call_target="tpu_custom_call" | custom-call | flops 150994944 | bytes 4194304 | tf_op jit(solution)/shard_map/pallas_call | solution.py:229
  60.0 4.4 %all-to-all-start = ((bf16[4,304,128]{2,1,0:T(8,128)(2,1)}), bf16[4,304,128]{2,1,0:T(8,128)(2,1)S(1)}, u32[]{:S(2)}, u32[]{:S(2)}) async-start(bf16[4,304,128]{2,1,0:T(8,128)(2,1)} %shard_map.97), calls=%async_computation | async-start | bytes 622592 | tf_op jit(solution)/shard_map/all_to_all | solution.py:373
  64.5 5.0 %shard_map.96 = (f32[128,1152]{1,0:T(8,128)}, f32[128,1152]{1,0:T(8,128)}, f32[128,128]{1,0:T(8,128)}, f32[128,128]{1,0:T(8,128)}, f32[3,128,128]{2,1,0:T(8,128)}) custom-call(f32[2]{0:T(128)} %pad_maximum_fusion.scal, bf16[128,1152]{1,0:T(8,128)(2,1)} %bitcast.8, bf16[1152,1152]{1,0:T(8,128)(2,1)} %w_hbm.5, s32[1,128]{1,0:T(1,128)} %key.3, ...), custom_call_target="tpu_custom_call" | custom-call | flops 377487360 | bytes 8388608 | tf_op jit(solution)/shard_map/pallas_call | solution.py:167
  69.5 2.7 %all-to-all-done.refs_0_ = bf16[4,304,128]{2,1,0:T(8,128)(2,1)S(1)} async-done(((bf16[4,304,128]{2,1,0:T(8,128)(2,1)}), bf16[4,304,128]{2,1,0:T(8,128)(2,1)S(1)}, u32[]{:S(2)}, u32[]{:S(2)}) %all-to-all-start) | async-done | bytes 311328 | tf_op jit(solution)/shard_map/all_to_all | solution.py:373
  72.2 2.0 %shard_map.98 = (f32[32,48,128]{2,1,0:T(8,128)S(1)}, bf16[32,48,128]{2,1,0:T(8,128)(2,1)S(1)}) custom-call(s32[2]{0:T(128)S(1)} %copy-done.3, bf16[512,1152]{1,0:T(8,128)(2,1)S(1)} %copy-done.1, bf16[4,304,128]{2,1,0:T(8,128)(2,1)S(1)} %all-to-all-done.refs_0_), custom_call_target="tpu_custom_call" | custom-call | flops 339738624 | bytes 4194304 | tf_op jit(solution)/shard_map/pallas_call | solution.py:292
  74.5 1.7 %collective-permute-done.10 = bf16[32,48,128]{2,1,0:T(8,128)(2,1)S(1)} collective-permute-done((bf16[32,48,128]{2,1,0:T(8,128)(2,1)S(1)}, bf16[32,48,128]{2,1,0:T(8,128)(2,1)S(1)}, u32[]{:S(2)}, u32[]{:S(2)}) %collective-permute-start.10) | collective-permute-done | bytes 393248 | tf_op jit(solution)/shard_map/ppermute | solution.py:40
  77.0 3.1 %shard_map.100 = (bf16[288,128]{1,0:T(8,128)(2,1)}, bf16[288,128]{1,0:T(8,128)(2,1)}, bf16[288,128]{1,0:T(8,128)(2,1)}, bf16[288,128]{1,0:T(8,128)(2,1)}) custom-call(s32[2]{0:T(128)} %pad_add_fusion.spot, f32[2]{0:T(128)} %pad_maximum_fusion.scal, bf16[144,1152]{1,0:T(8,128)(2,1)} %shard_map.94.refs_0_.own, f32[128,1152]{1,0:T(8,128)} %get-tuple-element.44.total_ref, ...), custom_call_target="tpu_custom_call" | custom-call | flops 150994944 | bytes 4194304 | tf_op jit(solution)/shard_map/pallas_call | solution.py:229
  80.1 1.7 %collective-permute-start.11 = (bf16[288,128]{1,0:T(8,128)(2,1)}, bf16[288,128]{1,0:T(8,128)(2,1)S(1)}, u32[]{:S(2)}, u32[]{:S(2)}) collective-permute-start(bf16[288,128]{1,0:T(8,128)(2,1)} %get-tuple-element.68), channel_id=1, source_target_pairs={{0,1},{1,2},{2,3},{3,0},{4,5},{5,6},{6,7},{7,4},{8,9},{9,10},{10,1... | collective-permute-start | bytes 221192 | tf_op jit(solution)/shard_map/ppermute | solution.py:361
  81.8 2.0 %collective-permute-start.12 = (bf16[288,128]{1,0:T(8,128)(2,1)}, bf16[288,128]{1,0:T(8,128)(2,1)S(1)}, u32[]{:S(2)}, u32[]{:S(2)}) collective-permute-start(bf16[288,128]{1,0:T(8,128)(2,1)} %get-tuple-element.69), channel_id=1, source_target_pairs={{0,2},{1,3},{2,0},{3,1},{4,6},{5,7},{6,4},{7,5},{8,10},{9,11},{10,... | collective-permute-start | bytes 221192 | tf_op jit(solution)/shard_map/ppermute | solution.py:361
  84.8 8.3 %all-to-all-start.1 = ((bf16[32,48,128]{2,1,0:T(8,128)(2,1)}), bf16[32,48,128]{2,1,0:T(8,128)(2,1)S(1)}, u32[]{:S(2)}, u32[]{:S(2)}) async-start(bf16[32,48,128]{2,1,0:T(8,128)(2,1)} %add_convert_fusion.1), calls=%async_computation.1 | async-start | bytes 786432 | tf_op jit(solution)/shard_map/all_to_all | solution.py:369
  95.3 2.0 %shard_map.101 = (f32[32,48,128]{2,1,0:T(8,128)S(1)}, bf16[32,48,128]{2,1,0:T(8,128)(2,1)S(1)}) custom-call(s32[2]{0:T(128)S(1)} %copy-done.4, bf16[512,1152]{1,0:T(8,128)(2,1)S(1)} %copy-done, bf16[288,128]{1,0:T(8,128)(2,1)S(1)} %copy-done.2, bf16[288,128]{1,0:T(8,128)(2,1)S(1)} %collective-permute-done.11.refs_1_, ...), custom_call_target="tpu_custom_call" | custom-call | flops 339738624 | bytes 4194304 | tf_op jit(solution)/shard_map/pallas_call | solution.py:292
  97.4 1.7 %collective-permute-done.14 = bf16[32,48,128]{2,1,0:T(8,128)(2,1)S(1)} collective-permute-done((bf16[32,48,128]{2,1,0:T(8,128)(2,1)S(1)}, bf16[32,48,128]{2,1,0:T(8,128)(2,1)S(1)}, u32[]{:S(2)}, u32[]{:S(2)}) %collective-permute-start.14) | collective-permute-done | bytes 393248 | tf_op jit(solution)/shard_map/ppermute | solution.py:40
  99.9 7.9 %all-to-all-done.1.parts = bf16[32,48,128]{2,1,0:T(8,128)(2,1)S(1)} async-done(((bf16[32,48,128]{2,1,0:T(8,128)(2,1)}), bf16[32,48,128]{2,1,0:T(8,128)(2,1)S(1)}, u32[]{:S(2)}, u32[]{:S(2)}) %all-to-all-start.1) | async-done | bytes 393248 | tf_op jit(solution)/shard_map/all_to_all | solution.py:369
  107.8 4.7 %all-to-all-start.2 = ((bf16[32,48,128]{2,1,0:T(8,128)(2,1)}), bf16[32,48,128]{2,1,0:T(8,128)(2,1)S(1)}, u32[]{:S(2)}, u32[]{:S(2)}) async-start(bf16[32,48,128]{2,1,0:T(8,128)(2,1)} %add_convert_fusion), calls=%async_computation.2 | async-start | bytes 786432 | tf_op jit(solution)/shard_map/all_to_all | solution.py:369
  113.8 12.8 %all-to-all-done.2.parts = bf16[32,48,128]{2,1,0:T(8,128)(2,1)S(1)} async-done(((bf16[32,48,128]{2,1,0:T(8,128)(2,1)}), bf16[32,48,128]{2,1,0:T(8,128)(2,1)S(1)}, u32[]{:S(2)}, u32[]{:S(2)}) %all-to-all-start.2) | async-done | bytes 393248 | tf_op jit(solution)/shard_map/all_to_all | solution.py:369
  (62 shorter events, 13.6 us)
Async XLA Ops:
  7.2 48.2 %all-gather.3.cloned.1.call-start = ((), (), s32[]{:S(2)}) async-start(), calls=%async_computation.3 | async-start | bytes 1474560 | tf_op jit(solution)/shard_map/all_gather | solution.py:346
  10.5 69.6 %all-gather.5.cloned.1.call-start = ((), (), s32[]{:S(2)}) async-start(), calls=%async_computation.4 | async-start | bytes 1474560 | tf_op jit(solution)/shard_map/all_gather | solution.py:347
  10.6 9.9 %collective-permute-start = (bf16[144,1152]{1,0:T(8,128)(2,1)}, bf16[144,1152]{1,0:T(8,128)(2,1)S(1)}, u32[]{:S(2)}, u32[]{:S(2)}) collective-permute-start(bf16[144,1152]{1,0:T(8,128)(2,1)} %shard_map.94.refs_0_.own), channel_id=1, source_target_pairs={{0,8},{8,0},{1,9},{9,1},{2,10},{10,2},{3,11},{11,3},{4,12},{12,4},... | collective-permute-start | bytes 995336 | tf_op jit(solution)/shard_map/ppermute | solution.py:40
  10.7 18.0 %collective-permute-start.1 = (bf16[144,1152]{1,0:T(8,128)(2,1)}, bf16[144,1152]{1,0:T(8,128)(2,1)S(1)}, u32[]{:S(2)}, u32[]{:S(2)}) collective-permute-start(bf16[144,1152]{1,0:T(8,128)(2,1)} %shard_map.94.refs_0_.own), channel_id=1, source_target_pairs={{0,16},{16,0},{32,48},{48,32},{1,17},{17,1},{33,49},{49,33},{2,18}... | collective-permute-start | bytes 995336 | tf_op jit(solution)/shard_map/ppermute | solution.py:40
  14.0 14.6 %collective-permute-start.4 = (bf16[144,1152]{1,0:T(8,128)(2,1)}, bf16[144,1152]{1,0:T(8,128)(2,1)S(1)}, u32[]{:S(2)}, u32[]{:S(2)}) collective-permute-start(bf16[144,1152]{1,0:T(8,128)(2,1)} %shard_map.94.refs_0_.own), channel_id=1, source_target_pairs={{0,64},{64,0},{128,192},{192,128},{1,65},{65,1},{129,193},{193,129... | collective-permute-start | bytes 995336 | tf_op jit(solution)/shard_map/ppermute | solution.py:40
  15.6 18.0 %collective-permute-start.5 = (bf16[144,1152]{1,0:T(8,128)(2,1)}, bf16[144,1152]{1,0:T(8,128)(2,1)S(1)}, u32[]{:S(2)}, u32[]{:S(2)}) collective-permute-start(bf16[144,1152]{1,0:T(8,128)(2,1)} %shard_map.94.refs_0_.own), channel_id=1, source_target_pairs={{0,128},{64,192},{128,0},{192,64},{1,129},{65,193},{129,1},{193,65... | collective-permute-start | bytes 995336 | tf_op jit(solution)/shard_map/ppermute | solution.py:40
  28.7 26.7 %copy-start.5 = (bf16[144,1152]{1,0:T(8,128)(2,1)}, bf16[144,1152]{1,0:T(8,128)(2,1)S(1)}, u32[]{:S(2)}) copy-start(bf16[144,1152]{1,0:T(8,128)(2,1)S(1)} %collective-permute-done.1.refs_2_) | copy-start | bytes 995332
  28.7 26.7 %copy-start.6 = (bf16[144,1152]{1,0:T(8,128)(2,1)}, bf16[144,1152]{1,0:T(8,128)(2,1)S(1)}, u32[]{:S(2)}) copy-start(bf16[144,1152]{1,0:T(8,128)(2,1)S(1)} %collective-permute-done.4.refs_0_) | copy-start | bytes 995332
  33.7 5.1 %collective-permute-start.6 = (bf16[144,1152]{1,0:T(8,128)(2,1)}, bf16[144,1152]{1,0:T(8,128)(2,1)S(1)}, u32[]{:S(2)}, u32[]{:S(2)}) collective-permute-start(bf16[144,1152]{1,0:T(8,128)(2,1)} %get-tuple-element.43.refs_1_.own), channel_id=1, source_target_pairs={{0,8},{8,0},{1,9},{9,1},{2,10},{10,2},{3,11},{11,3},{4,12},{12,4},... | collective-permute-start | bytes 995336 | tf_op jit(solution)/shard_map/ppermute | solution.py:40
  33.7 15.0 %collective-permute-start.2 = (bf16[144,1152]{1,0:T(8,128)(2,1)}, bf16[144,1152]{1,0:T(8,128)(2,1)S(1)}, u32[]{:S(2)}, u32[]{:S(2)}) collective-permute-start(bf16[144,1152]{1,0:T(8,128)(2,1)} %get-tuple-element.43.refs_1_.own), channel_id=1, source_target_pairs={{0,16},{16,0},{32,48},{48,32},{1,17},{17,1},{33,49},{49,33},{2,18}... | collective-permute-start | bytes 995336 | tf_op jit(solution)/shard_map/ppermute | solution.py:40
  33.9 20.9 %collective-permute-start.9 = (bf16[144,1152]{1,0:T(8,128)(2,1)S(1)}, bf16[144,1152]{1,0:T(8,128)(2,1)S(1)}, u32[]{:S(2)}, u32[]{:S(2)}) collective-permute-start(bf16[144,1152]{1,0:T(8,128)(2,1)S(1)} %collective-permute-done.1.refs_2_), channel_id=1, source_target_pairs={{0,48},{16,32},{32,16},{48,0},{1,49},{17,33},{33,17},{49,1},{2,50}... | collective-permute-start | bytes 995336 | tf_op jit(solution)/shard_map/ppermute | solution.py:40
  38.7 25.7 %copy-start.9 = (bf16[144,1152]{1,0:T(8,128)(2,1)}, bf16[144,1152]{1,0:T(8,128)(2,1)S(1)}, u32[]{:S(2)}) copy-start(bf16[144,1152]{1,0:T(8,128)(2,1)S(1)} %collective-permute-done.6.refs_2_) | copy-start | bytes 995332
  38.7 16.1 %collective-permute-start.7 = (bf16[144,1152]{1,0:T(8,128)(2,1)}, bf16[144,1152]{1,0:T(8,128)(2,1)S(1)}, u32[]{:S(2)}, u32[]{:S(2)}) collective-permute-start(bf16[144,1152]{1,0:T(8,128)(2,1)} %get-tuple-element.43.refs_1_.own), channel_id=1, source_target_pairs={{0,64},{64,0},{128,192},{192,128},{1,65},{65,1},{129,193},{193,129... | collective-permute-start | bytes 995336 | tf_op jit(solution)/shard_map/ppermute | solution.py:40
  38.9 16.5 %collective-permute-start.8 = (bf16[144,1152]{1,0:T(8,128)(2,1)}, bf16[144,1152]{1,0:T(8,128)(2,1)S(1)}, u32[]{:S(2)}, u32[]{:S(2)}) collective-permute-start(bf16[144,1152]{1,0:T(8,128)(2,1)} %get-tuple-element.43.refs_1_.own), channel_id=1, source_target_pairs={{0,128},{64,192},{128,0},{192,64},{1,129},{65,193},{129,1},{193,65... | collective-permute-start | bytes 995336 | tf_op jit(solution)/shard_map/ppermute | solution.py:40
  48.7 20.7 %collective-permute-start.3 = (bf16[144,1152]{1,0:T(8,128)(2,1)S(1)}, bf16[144,1152]{1,0:T(8,128)(2,1)S(1)}, u32[]{:S(2)}, u32[]{:S(2)}) collective-permute-start(bf16[144,1152]{1,0:T(8,128)(2,1)S(1)} %collective-permute-done.2.refs_5_), channel_id=1, source_target_pairs={{0,48},{16,32},{32,16},{48,0},{1,49},{17,33},{33,17},{49,1},{2,50}... | collective-permute-start | bytes 995336 | tf_op jit(solution)/shard_map/ppermute | solution.py:40
  60.0 12.1 %all-to-all-start = ((bf16[4,304,128]{2,1,0:T(8,128)(2,1)}), bf16[4,304,128]{2,1,0:T(8,128)(2,1)S(1)}, u32[]{:S(2)}, u32[]{:S(2)}) async-start(bf16[4,304,128]{2,1,0:T(8,128)(2,1)} %shard_map.97), calls=%async_computation | async-start | bytes 622592 | tf_op jit(solution)/shard_map/all_to_all | solution.py:373
  69.4 23.7 %copy-start.4 = (s32[2]{0:T(128)S(1)}, s32[2]{0:T(128)}, u32[]{:S(2)}) copy-start(s32[2]{0:T(128)} %pad_add_fusion.spot) | copy-start | bytes 28
  74.2 2.0 %collective-permute-start.10 = (bf16[32,48,128]{2,1,0:T(8,128)(2,1)S(1)}, bf16[32,48,128]{2,1,0:T(8,128)(2,1)S(1)}, u32[]{:S(2)}, u32[]{:S(2)}) collective-permute-start(bf16[32,48,128]{2,1,0:T(8,128)(2,1)S(1)} %get-tuple-element.58), channel_id=1, source_target_pairs={{0,8},{8,0},{1,9},{9,1},{2,10},{10,2},{3,11},{11,3},{4,12},{12,4},... | collective-permute-start | bytes 1179656 | tf_op jit(solution)/shard_map/ppermute | solution.py:40
  80.1 13.0 %collective-permute-start.11 = (bf16[288,128]{1,0:T(8,128)(2,1)}, bf16[288,128]{1,0:T(8,128)(2,1)S(1)}, u32[]{:S(2)}, u32[]{:S(2)}) collective-permute-start(bf16[288,128]{1,0:T(8,128)(2,1)} %get-tuple-element.68), channel_id=1, source_target_pairs={{0,1},{1,2},{2,3},{3,0},{4,5},{5,6},{6,7},{7,4},{8,9},{9,10},{10,1... | collective-permute-start | bytes 221192 | tf_op jit(solution)/shard_map/ppermute | solution.py:361
  81.8 11.3 %collective-permute-start.12 = (bf16[288,128]{1,0:T(8,128)(2,1)}, bf16[288,128]{1,0:T(8,128)(2,1)S(1)}, u32[]{:S(2)}, u32[]{:S(2)}) collective-permute-start(bf16[288,128]{1,0:T(8,128)(2,1)} %get-tuple-element.69), channel_id=1, source_target_pairs={{0,2},{1,3},{2,0},{3,1},{4,6},{5,7},{6,4},{7,5},{8,10},{9,11},{10,... | collective-permute-start | bytes 221192 | tf_op jit(solution)/shard_map/ppermute | solution.py:361
  83.8 9.3 %collective-permute-start.13 = (bf16[288,128]{1,0:T(8,128)(2,1)}, bf16[288,128]{1,0:T(8,128)(2,1)S(1)}, u32[]{:S(2)}, u32[]{:S(2)}) collective-permute-start(bf16[288,128]{1,0:T(8,128)(2,1)} %get-tuple-element.70), channel_id=1, source_target_pairs={{0,3},{1,0},{2,1},{3,2},{4,7},{5,4},{6,5},{7,6},{8,11},{9,8},{10,9... | collective-permute-start | bytes 221192 | tf_op jit(solution)/shard_map/ppermute | solution.py:361
  84.8 23.0 %all-to-all-start.1 = ((bf16[32,48,128]{2,1,0:T(8,128)(2,1)}), bf16[32,48,128]{2,1,0:T(8,128)(2,1)S(1)}, u32[]{:S(2)}, u32[]{:S(2)}) async-start(bf16[32,48,128]{2,1,0:T(8,128)(2,1)} %add_convert_fusion.1), calls=%async_computation.1 | async-start | bytes 786432 | tf_op jit(solution)/shard_map/all_to_all | solution.py:369
  97.3 1.8 %collective-permute-start.14 = (bf16[32,48,128]{2,1,0:T(8,128)(2,1)S(1)}, bf16[32,48,128]{2,1,0:T(8,128)(2,1)S(1)}, u32[]{:S(2)}, u32[]{:S(2)}) collective-permute-start(bf16[32,48,128]{2,1,0:T(8,128)(2,1)S(1)} %get-tuple-element.72), channel_id=1, source_target_pairs={{0,8},{8,0},{1,9},{9,1},{2,10},{10,2},{3,11},{11,3},{4,12},{12,4},... | collective-permute-start | bytes 1179656 | tf_op jit(solution)/shard_map/ppermute | solution.py:40
  107.8 18.7 %all-to-all-start.2 = ((bf16[32,48,128]{2,1,0:T(8,128)(2,1)}), bf16[32,48,128]{2,1,0:T(8,128)(2,1)S(1)}, u32[]{:S(2)}, u32[]{:S(2)}) async-start(bf16[32,48,128]{2,1,0:T(8,128)(2,1)} %add_convert_fusion), calls=%async_computation.2 | async-start | bytes 786432 | tf_op jit(solution)/shard_map/all_to_all | solution.py:369
  (11 other events, 91.7 us)
Sparse Core Ops, SparseCore 0:
  10.7 29.5 all-gather.2
  42.0 29.1 all-gather.4

commit v7 on v6

--- a/solution.py
+++ b/solution.py
@@ -19,7 +19,7 @@
 TAIL = COLS - LANES
 QUADS = 16
 STATS = 112
-DEPTH = 384
+DEPTH = 128
 PIECES = WIDTH // DEPTH
 F32 = jnp.float32
 BF16 = jnp.bfloat16
@@ -122,7 +122,7 @@
     out_ref[ROWS:, :ROWS] = digit.astype(F32).astype(BF16)
 
 
-def early_kernel(first, scal, x, w_hbm, key, *refs):
+def early_kernel(first, scal, spot, x, w_hbm, key, *refs):
     blocks, refs = refs[:-7], refs[-7:]
     total_ref, unit_ref, len_ref, key_ref, sum_ref, w, sem = refs
     own, blocks = (blocks[-1], blocks[:-1]) if first else (blocks[0], blocks[1:])
@@ -158,7 +158,7 @@
         norm()
 
 
-def early(first, scal, x, w, keys, blocks):
+def early(first, scal, spot, x, w, keys, blocks):
     shapes = [(ROWS, WIDTH), (ROWS, WIDTH), (ROWS, LANES), (ROWS, ROWS), (3, ROWS, ROWS)]
     outs = [jax.ShapeDtypeStruct(shape, F32) for shape in shapes]
     if first:
@@ -166,13 +166,13 @@
     hbm = pl.BlockSpec(memory_space=pltpu.HBM)
     return pl.pallas_call(
         functools.partial(early_kernel, first),
-        in_specs=[SMEM, VMEM, hbm, VMEM] + [VMEM] * len(blocks),
+        in_specs=[SMEM, SMEM, VMEM, hbm, VMEM] + [VMEM] * len(blocks),
         out_specs=[VMEM] * len(outs),
         out_shape=outs,
         scratch_shapes=[pltpu.VMEM((WIDTH, WIDTH), BF16), pltpu.SemaphoreType.DMA],
         compiler_params=params(56),
         cost_estimate=cost(4 * 5 * ROWS * ROWS * WIDTH, 8 * 2**20),
-    )(scal, x, w, keys, *blocks)
+    )(scal, spot, x, w, keys, *blocks)
 
 
 def late_kernel(with_stats, ways, count, spot, scal, own, total_ref, unit, length, key, acc, *refs):
@@ -209,23 +209,16 @@
         middle = (value - high).astype(BF16).astype(F32)
         low = value - high - middle
         parts = jnp.where(lane < 3, high, jnp.where(lane < 6, middle, low)).astype(BF16)
-        out = outs[0]
-        for w in range(ways):
-            for h in range(2):
-                out[w, h * COLS : (h + 1) * COLS, :] = held[h * ways + w]
-            out[w, 2 * COLS :, :] = parts
-    else:
-        for step, out in enumerate(outs):
-            w = lax.rem(spot[0] + step, ways)
-            for h in range(2):
-                out[h * COLS : (h + 1) * COLS, :] = held[h * ways + w]
+        for out in outs:
+            out[2 * COLS :, :] = parts
+    for step, out in enumerate(outs):
+        w = lax.rem(spot[0] + step, ways)
+        for h in range(2):
+            out[h * COLS : (h + 1) * COLS, :] = held[h * ways + w]
 
 
 def late(with_stats, ways, spot, scal, own, partial, blocks):
-    if with_stats:
-        shapes = [(ways, 2 * COLS + KEY_ROWS, ROWS)]
-    else:
-        shapes = [(2 * COLS, ROWS)] * ways
+    shapes = [(2 * COLS + (KEY_ROWS if with_stats else 0), ROWS)] * ways
     return pl.pallas_call(
         functools.partial(late_kernel, with_stats, ways, len(blocks)),
         in_specs=[SMEM] * 2 + [VMEM] * (6 + len(blocks)),
@@ -239,14 +232,11 @@
 
 def head_kernel(with_stats, spot, feat, *refs):
     spreads, (kept, given, held) = refs[:-3], refs[-3:]
-    if with_stats:
-        spreads = [spreads[0].at[w] for w in range(spreads[0].shape[0])]
     ways = len(spreads)
     total = jnp.zeros((2 * COLS, feat.shape[1]), F32)
     for step, spread in enumerate(spreads):
-        source = step if with_stats else lax.rem(spot[0] + ways - step, ways)
-        start = source * ROWS if with_stats else pl.multiple_of(source * ROWS, ROWS)
-        rows = feat[pl.ds(start, ROWS), :]
+        source = lax.rem(spot[0] + ways - step, ways)
+        rows = feat[pl.ds(pl.multiple_of(source * ROWS, ROWS), ROWS), :]
         total += mm(spread[: 2 * COLS, :], rows)
     spare = None
     if with_stats:
@@ -346,7 +336,7 @@
     img_feat = lax.all_gather(after(pictures[0], txt), "dx", axis=0, tiled=True)
     txt_feat = lax.all_gather(after(sentences[0], txt), "dx", axis=0, tiled=True)
 
-    img, *img_part = early(True, scal, pictures[0], picture_weights, keys, [txt, txt_c])
+    img, *img_part = early(True, scal, spot, pictures[0], picture_weights, keys, [txt, txt_c])
     txt_b = exchange(after(txt_a, txt_y1, txt_y2), "lz", 3)
     img_a = exchange(after(img, txt_a), "lz", 1)
     img_c = exchange(after(img, txt_a, txt_y1, txt_y2), "lc", 1)
@@ -365,23 +355,27 @@
         taken = after(exchange(given, "lc", 1), *others)
         return (kept + taken.astype(F32)).astype(BF16)
 
+    def columns(outs):
+        return [outs[0]] + [turn(out, step) for step, out in enumerate(outs) if step]
+
     def collect(sums):
-        return final(count, lax.all_to_all(sums, ("ly", "lz", "dz"), 0, 0, tiled=True))
+        return lax.all_to_all(sums, ("ly", "lz", "dz"), 0, 0, tiled=True)
 
     last = after(txt_b, img_feat, img_a, img_c, img_y1, img_y2)
-    img_outs = late(True, ways, spot, scal, img, img_part, [txt_y1, txt_y2, txt_a, last])[0]
-    img_cols = lax.all_to_all(img_outs, "dx", 0, 0, tiled=True)
+    img_outs = late(True, ways, spot, scal, img, img_part, [txt_y1, txt_y2, txt_a, last])
+    img_cols = columns(img_outs)
     txt_part = early(
-        False, scal, sentences[0], sentence_weights, keys, [txt, img, img_c, img_y1, img_y2, img_a]
+        False, scal, spot, sentences[0], sentence_weights, keys, [txt, img, img_c, img_y1, img_y2, img_a]
     )
-    img_sums = share(True, after(img_feat, img_b, *txt_part), [img_cols])
+    img_sums = share(True, after(img_feat, img_b, *txt_part), img_cols)
+    img_parts = collect(img_sums)
     last = after(img_b, img_sums)
     outs = late(False, ways, spot, scal, txt, txt_part, [last])
     *outs, txt_feat = lax.optimization_barrier((*outs, txt_feat))
-    txt_cols = [outs[0]] + [turn(out, step) for step, out in enumerate(outs) if step]
-    txt_sums = share(False, txt_feat, txt_cols)
-    grad_img, stats = collect(img_sums)
-    grad_txt, _ = collect(txt_sums)
+    txt_cols = columns(outs)
+    txt_parts = collect(share(False, after(txt_feat, img_parts), txt_cols))
+    grad_img, stats = final(count, img_parts)
+    grad_txt, _ = final(count, txt_parts)
     return grad_img, grad_txt, stats[0, :3]
 
 

time: 135 us -> 135 us (level)
    ppermute x3 -> x6, starting transfers between devices: 4.64 us -> 10.8 us  [turn(): lax.ppermute(array, 'dx', [(i, (i + step) % ways) for i in range(ways)])]
    all_to_all x3 -> x2, starting transfers between devices: 17.4 us -> 12.5 us  [collect(): return lax.all_to_all(sums, ('ly', 'lz', 'dz'), 0, 0, tiled=True)]
    all_to_all x3 -> x2, waiting for transfers between devices: 23.4 us -> 21.2 us  [collect(): return lax.all_to_all(sums, ('ly', 'lz', 'dz'), 0, 0, tiled=True)]
    unnamed x30 -> x32, local copies, waits for them, and re-layouts: 3.08 us -> 2.95 us
  transfers between devices with their start and end apart: 20 -> 22, of which waited for: 9 -> 9; matrix products, arithmetic and copies ran while one was open for 3% -> 2% of each run, Pallas kernels for 17% -> 16%
where the time goes in v7:
time: 135 us; the launch traced here: 134 us
  starting transfers between devices  43.7 us (32%)
  waiting for transfers between devices  41.4 us (31%)
  Pallas kernels  27.1 us (20%)
  between operations  15.6 us (12%)
  local copies, waits for them, and re-layouts  3.46 us (3%)
  other arithmetic  2.85 us (2%)
    all_to_all x2, waiting for transfers between devices, collect(): return lax.all_to_all(sums, ('ly', 'lz', 'dz'), 0, 0, tiled=True)  21.2 us
    ppermute x12, starting transfers between devices, exchange(): lax.ppermute(array, axis, [(i, i ^ apart) for i in range(lax.axis_size(ax...  20.4 us
    ppermute x12, waiting for transfers between devices, exchange(): lax.ppermute(array, axis, [(i, i ^ apart) for i in range(lax.axis_size(ax...  19.2 us
    all_to_all x2, starting transfers between devices, collect(): return lax.all_to_all(sums, ('ly', 'lz', 'dz'), 0, 0, tiled=True)  12.5 us
    ppermute x6, starting transfers between devices, turn(): lax.ppermute(array, 'dx', [(i, (i + step) % ways) for i in range(ways)])  10.8 us
    pallas_call x2, Pallas kernels, early(): pl.pallas_call(functools.partial(early_kernel, first), in_specs=[SMEM, SM...  10.4 us
    pallas_call x2, Pallas kernels, late(): pl.pallas_call(functools.partial(late_kernel, with_stats, ways, len(block...  7.63 us
    pallas_call x2, Pallas kernels, heads(): pl.pallas_call(functools.partial(head_kernel, with_stats), in_specs=[SMEM...  4.03 us
  transfers between devices with their start and end apart: 22, of which 9 were waited for; matrix products, arithmetic and copies ran while one was open for 2% of the time, Pallas kernels for 16%

profile of v7, /device:TPU:32, one launch (start us, length us, event | category | flops | bytes accessed | tf_op | source)
XLA Modules:
  0.0 134.1 jit_solution(5887371110924000397)
XLA Ops:
  7.2 3.4 %shard_map.94.refs_0_.own = bf16[144,1152]{1,0:T(8,128)(2,1)} custom-call(bf16[128,1152]{1,0:T(8,128)(2,1)} %bitcast.6, bf16[1152,1152]{1,0:T(8,128)(2,1)} %w_hbm.5, s32[1,128]{1,0:T(1,128)} %key.3), custom_call_target="tpu_custom_call" | custom-call | flops 339738624 | bytes 4194304 | tf_op jit(solution)/shard_map/pallas_call | solution.py:80
  10.8 3.4 %collective-permute-start.1 = (bf16[144,1152]{1,0:T(8,128)(2,1)}, bf16[144,1152]{1,0:T(8,128)(2,1)S(1)}, u32[]{:S(2)}, u32[]{:S(2)}) collective-permute-start(bf16[144,1152]{1,0:T(8,128)(2,1)} %shard_map.94.refs_0_.own), channel_id=1, source_target_pairs={{0,16},{16,0},{32,48},{48,32},{1,17},{17,1},{33,49},{49,33},{2,18}... | collective-permute-start | bytes 995336 | tf_op jit(solution)/shard_map/ppermute | solution.py:40
  14.1 1.6 %collective-permute-start.4 = (bf16[144,1152]{1,0:T(8,128)(2,1)}, bf16[144,1152]{1,0:T(8,128)(2,1)S(1)}, u32[]{:S(2)}, u32[]{:S(2)}) collective-permute-start(bf16[144,1152]{1,0:T(8,128)(2,1)} %shard_map.94.refs_0_.own), channel_id=1, source_target_pairs={{0,64},{64,0},{128,192},{192,128},{1,65},{65,1},{129,193},{193,129... | collective-permute-start | bytes 995336 | tf_op jit(solution)/shard_map/ppermute | solution.py:40
  15.7 2.9 %collective-permute-start.5 = (bf16[144,1152]{1,0:T(8,128)(2,1)}, bf16[144,1152]{1,0:T(8,128)(2,1)S(1)}, u32[]{:S(2)}, u32[]{:S(2)}) collective-permute-start(bf16[144,1152]{1,0:T(8,128)(2,1)} %shard_map.94.refs_0_.own), channel_id=1, source_target_pairs={{0,128},{64,192},{128,0},{192,64},{1,129},{65,193},{129,1},{193,65... | collective-permute-start | bytes 995336 | tf_op jit(solution)/shard_map/ppermute | solution.py:40
  21.9 5.5 %shard_map.95 = (bf16[144,1152]{1,0:T(8,128)(2,1)}, f32[128,1152]{1,0:T(8,128)}, f32[128,1152]{1,0:T(8,128)}, f32[128,128]{1,0:T(8,128)}, f32[128,128]{1,0:T(8,128)}, /*index=5*/f32[3,128,128]{2,1,0:T(8,128)}) custom-call(f32[2]{0:T(128)} %pad_maximum_fusion.scal, s32[2]{0:T(128)} %pad_add_fusion.spot, bf16[128,1152]{1,0:T(8,128)(2,1)} %bitcast.10, ...), custom_call_target="tpu_custom_call" | custom-call | flops 377487360 | bytes 8388608 | tf_op jit(solution)/shard_map/pallas_call | solution.py:167
  28.8 5.0 %collective-permute-done.5.refs_1_ = bf16[144,1152]{1,0:T(8,128)(2,1)S(1)} collective-permute-done((bf16[144,1152]{1,0:T(8,128)(2,1)}, bf16[144,1152]{1,0:T(8,128)(2,1)S(1)}, u32[]{:S(2)}, u32[]{:S(2)}) %collective-permute-start.5) | collective-permute-done | bytes 331808 | tf_op jit(solution)/shard_map/ppermute | solution.py:40
  34.0 4.8 %collective-permute-start.9 = (bf16[144,1152]{1,0:T(8,128)(2,1)S(1)}, bf16[144,1152]{1,0:T(8,128)(2,1)S(1)}, u32[]{:S(2)}, u32[]{:S(2)}) collective-permute-start(bf16[144,1152]{1,0:T(8,128)(2,1)S(1)} %collective-permute-done.1.refs_2_), channel_id=1, source_target_pairs={{0,48},{16,32},{32,16},{48,0},{1,49},{17,33},{33,17},{49,1},{2,50}... | collective-permute-start | bytes 995336 | tf_op jit(solution)/shard_map/ppermute | solution.py:40
  40.5 8.3 %collective-permute-done.2.refs_5_ = bf16[144,1152]{1,0:T(8,128)(2,1)S(1)} collective-permute-done((bf16[144,1152]{1,0:T(8,128)(2,1)}, bf16[144,1152]{1,0:T(8,128)(2,1)S(1)}, u32[]{:S(2)}, u32[]{:S(2)}) %collective-permute-start.2) | collective-permute-done | bytes 331808 | tf_op jit(solution)/shard_map/ppermute | solution.py:40
  48.8 5.5 %collective-permute-start.3 = (bf16[144,1152]{1,0:T(8,128)(2,1)S(1)}, bf16[144,1152]{1,0:T(8,128)(2,1)S(1)}, u32[]{:S(2)}, u32[]{:S(2)}) collective-permute-start(bf16[144,1152]{1,0:T(8,128)(2,1)S(1)} %collective-permute-done.2.refs_5_), channel_id=1, source_target_pairs={{0,48},{16,32},{32,16},{48,0},{1,49},{17,33},{33,17},{49,1},{2,50}... | collective-permute-start | bytes 995336 | tf_op jit(solution)/shard_map/ppermute | solution.py:40
  55.5 4.6 %shard_map.97 = (bf16[304,128]{1,0:T(8,128)(2,1)}, bf16[304,128]{1,0:T(8,128)(2,1)}, bf16[304,128]{1,0:T(8,128)(2,1)}, bf16[304,128]{1,0:T(8,128)(2,1)}) custom-call(s32[2]{0:T(128)} %pad_add_fusion.spot, f32[2]{0:T(128)} %pad_maximum_fusion.scal, bf16[144,1152]{1,0:T(8,128)(2,1)} %get-tuple-element.48.refs_1_.own, f32[128,1152]{1,0:T(8,128)} %get-tuple-element.55.total_ref, ...), custom_call_target="tpu_custom_call" | custom-call | flops 150994944 | bytes 4194304 | tf_op jit(solution)/shard_map/pallas_call | solution.py:222
  60.1 1.6 %collective-permute-start.10 = (bf16[304,128]{1,0:T(8,128)(2,1)}, bf16[304,128]{1,0:T(8,128)(2,1)S(1)}, u32[]{:S(2)}, u32[]{:S(2)}) collective-permute-start(bf16[304,128]{1,0:T(8,128)(2,1)} %get-tuple-element.63), channel_id=1, source_target_pairs={{0,1},{1,2},{2,3},{3,0},{4,5},{5,6},{6,7},{7,4},{8,9},{9,10},{10,1... | collective-permute-start | bytes 233480 | tf_op jit(solution)/shard_map/ppermute | solution.py:351
  61.6 2.7 %collective-permute-start.11 = (bf16[304,128]{1,0:T(8,128)(2,1)}, bf16[304,128]{1,0:T(8,128)(2,1)S(1)}, u32[]{:S(2)}, u32[]{:S(2)}) collective-permute-start(bf16[304,128]{1,0:T(8,128)(2,1)} %get-tuple-element.64), channel_id=1, source_target_pairs={{0,2},{1,3},{2,0},{3,1},{4,6},{5,7},{6,4},{7,5},{8,10},{9,11},{10,... | collective-permute-start | bytes 233480 | tf_op jit(solution)/shard_map/ppermute | solution.py:351
  65.8 5.0 %shard_map.96 = (f32[128,1152]{1,0:T(8,128)}, f32[128,1152]{1,0:T(8,128)}, f32[128,128]{1,0:T(8,128)}, f32[128,128]{1,0:T(8,128)}, f32[3,128,128]{2,1,0:T(8,128)}) custom-call(f32[2]{0:T(128)} %pad_maximum_fusion.scal, s32[2]{0:T(128)} %pad_add_fusion.spot, bf16[128,1152]{1,0:T(8,128)(2,1)} %bitcast.8, bf16[1152,1152]{1,0:T(8,128)(2,1)} %w_hbm.5, ...), custom_call_target="tpu_custom_call" | custom-call | flops 377487360 | bytes 8388608 | tf_op jit(solution)/shard_map/pallas_call | solution.py:167
  71.8 2.0 %shard_map.98 = (f32[32,48,128]{2,1,0:T(8,128)S(1)}, bf16[32,48,128]{2,1,0:T(8,128)(2,1)S(1)}) custom-call(s32[2]{0:T(128)S(1)} %copy-done.4, bf16[512,1152]{1,0:T(8,128)(2,1)S(1)} %copy-done, bf16[304,128]{1,0:T(8,128)(2,1)S(1)} %copy-done.2, bf16[304,128]{1,0:T(8,128)(2,1)S(1)} %collective-permute-done.10.refs_1_, ...), custom_call_target="tpu_custom_call" | custom-call | flops 339738624 | bytes 4194304 | tf_op jit(solution)/shard_map/pallas_call | solution.py:282
  74.0 1.7 %collective-permute-done.13 = bf16[32,48,128]{2,1,0:T(8,128)(2,1)S(1)} collective-permute-done((bf16[32,48,128]{2,1,0:T(8,128)(2,1)S(1)}, bf16[32,48,128]{2,1,0:T(8,128)(2,1)S(1)}, u32[]{:S(2)}, u32[]{:S(2)}) %collective-permute-start.13) | collective-permute-done | bytes 393248 | tf_op jit(solution)/shard_map/ppermute | solution.py:40
  76.5 7.2 %all-to-all-start = ((bf16[32,48,128]{2,1,0:T(8,128)(2,1)}), bf16[32,48,128]{2,1,0:T(8,128)(2,1)S(1)}, u32[]{:S(2)}, u32[]{:S(2)}) async-start(bf16[32,48,128]{2,1,0:T(8,128)(2,1)} %add_convert_fusion.1), calls=%async_computation | async-start | bytes 786432 | tf_op jit(solution)/shard_map/all_to_all | solution.py:362
  83.7 3.1 %shard_map.100 = (bf16[288,128]{1,0:T(8,128)(2,1)}, bf16[288,128]{1,0:T(8,128)(2,1)}, bf16[288,128]{1,0:T(8,128)(2,1)}, bf16[288,128]{1,0:T(8,128)(2,1)}) custom-call(s32[2]{0:T(128)} %pad_add_fusion.spot, f32[2]{0:T(128)} %pad_maximum_fusion.scal, bf16[144,1152]{1,0:T(8,128)(2,1)} %shard_map.94.refs_0_.own, f32[128,1152]{1,0:T(8,128)} %get-tuple-element.49.total_ref, ...), custom_call_target="tpu_custom_call" | custom-call | flops 150994944 | bytes 4194304 | tf_op jit(solution)/shard_map/pallas_call | solution.py:222
  86.9 3.2 %collective-permute-start.15 = (bf16[288,128]{1,0:T(8,128)(2,1)}, bf16[288,128]{1,0:T(8,128)(2,1)S(1)}, u32[]{:S(2)}, u32[]{:S(2)}) collective-permute-start(bf16[288,128]{1,0:T(8,128)(2,1)} %get-tuple-element.79), channel_id=1, source_target_pairs={{0,2},{1,3},{2,0},{3,1},{4,6},{5,7},{6,4},{7,5},{8,10},{9,11},{10,... | collective-permute-start | bytes 221192 | tf_op jit(solution)/shard_map/ppermute | solution.py:351
  90.0 1.8 %collective-permute-start.16 = (bf16[288,128]{1,0:T(8,128)(2,1)}, bf16[288,128]{1,0:T(8,128)(2,1)S(1)}, u32[]{:S(2)}, u32[]{:S(2)}) collective-permute-start(bf16[288,128]{1,0:T(8,128)(2,1)} %get-tuple-element.80), channel_id=1, source_target_pairs={{0,3},{1,0},{2,1},{3,2},{4,7},{5,4},{6,5},{7,6},{8,11},{9,8},{10,9... | collective-permute-start | bytes 221192 | tf_op jit(solution)/shard_map/ppermute | solution.py:351
  91.9 7.2 %all-to-all-done.parts = bf16[32,48,128]{2,1,0:T(8,128)(2,1)S(1)} async-done(((bf16[32,48,128]{2,1,0:T(8,128)(2,1)}), bf16[32,48,128]{2,1,0:T(8,128)(2,1)S(1)}, u32[]{:S(2)}, u32[]{:S(2)}) %all-to-all-start) | async-done | bytes 393248 | tf_op jit(solution)/shard_map/all_to_all | solution.py:362
  101.2 2.0 %shard_map.101 = (f32[32,48,128]{2,1,0:T(8,128)S(1)}, bf16[32,48,128]{2,1,0:T(8,128)(2,1)S(1)}) custom-call(s32[2]{0:T(128)S(1)} %copy-done.5, bf16[512,1152]{1,0:T(8,128)(2,1)S(1)} %copy-done.1, bf16[288,128]{1,0:T(8,128)(2,1)S(1)} %copy-done.3, bf16[288,128]{1,0:T(8,128)(2,1)S(1)} %collective-permute-done.14.refs_1_, ...), custom_call_target="tpu_custom_call" | custom-call | flops 339738624 | bytes 4194304 | tf_op jit(solution)/shard_map/pallas_call | solution.py:282
  103.3 1.7 %collective-permute-done.17 = bf16[32,48,128]{2,1,0:T(8,128)(2,1)S(1)} collective-permute-done((bf16[32,48,128]{2,1,0:T(8,128)(2,1)S(1)}, bf16[32,48,128]{2,1,0:T(8,128)(2,1)S(1)}, u32[]{:S(2)}, u32[]{:S(2)}) %collective-permute-start.17) | collective-permute-done | bytes 393248 | tf_op jit(solution)/shard_map/ppermute | solution.py:40
  105.9 5.3 %all-to-all-start.1 = ((bf16[32,48,128]{2,1,0:T(8,128)(2,1)}), bf16[32,48,128]{2,1,0:T(8,128)(2,1)S(1)}, u32[]{:S(2)}, u32[]{:S(2)}) async-start(bf16[32,48,128]{2,1,0:T(8,128)(2,1)} %add_convert_fusion), calls=%async_computation.1 | async-start | bytes 786432 | tf_op jit(solution)/shard_map/all_to_all | solution.py:362
  112.5 14.0 %all-to-all-done.1.parts = bf16[32,48,128]{2,1,0:T(8,128)(2,1)S(1)} async-done(((bf16[32,48,128]{2,1,0:T(8,128)(2,1)}), bf16[32,48,128]{2,1,0:T(8,128)(2,1)S(1)}, u32[]{:S(2)}, u32[]{:S(2)}) %all-to-all-start.1) | async-done | bytes 393248 | tf_op jit(solution)/shard_map/all_to_all | solution.py:362
  (68 shorter events, 15.3 us)
Async XLA Ops:
  7.2 48.3 %all-gather.3.cloned.1.call-start = ((), (), s32[]{:S(2)}) async-start(), calls=%async_computation.2 | async-start | bytes 1474560 | tf_op jit(solution)/shard_map/all_gather | solution.py:336
  10.6 76.2 %all-gather.5.cloned.1.call-start = ((), (), s32[]{:S(2)}) async-start(), calls=%async_computation.3 | async-start | bytes 1474560 | tf_op jit(solution)/shard_map/all_gather | solution.py:337
  10.7 10.5 %collective-permute-start = (bf16[144,1152]{1,0:T(8,128)(2,1)}, bf16[144,1152]{1,0:T(8,128)(2,1)S(1)}, u32[]{:S(2)}, u32[]{:S(2)}) collective-permute-start(bf16[144,1152]{1,0:T(8,128)(2,1)} %shard_map.94.refs_0_.own), channel_id=1, source_target_pairs={{0,8},{8,0},{1,9},{9,1},{2,10},{10,2},{3,11},{11,3},{4,12},{12,4},... | collective-permute-start | bytes 995336 | tf_op jit(solution)/shard_map/ppermute | solution.py:40
  10.8 18.0 %collective-permute-start.1 = (bf16[144,1152]{1,0:T(8,128)(2,1)}, bf16[144,1152]{1,0:T(8,128)(2,1)S(1)}, u32[]{:S(2)}, u32[]{:S(2)}) collective-permute-start(bf16[144,1152]{1,0:T(8,128)(2,1)} %shard_map.94.refs_0_.own), channel_id=1, source_target_pairs={{0,16},{16,0},{32,48},{48,32},{1,17},{17,1},{33,49},{49,33},{2,18}... | collective-permute-start | bytes 995336 | tf_op jit(solution)/shard_map/ppermute | solution.py:40
  14.1 14.6 %collective-permute-start.4 = (bf16[144,1152]{1,0:T(8,128)(2,1)}, bf16[144,1152]{1,0:T(8,128)(2,1)S(1)}, u32[]{:S(2)}, u32[]{:S(2)}) collective-permute-start(bf16[144,1152]{1,0:T(8,128)(2,1)} %shard_map.94.refs_0_.own), channel_id=1, source_target_pairs={{0,64},{64,0},{128,192},{192,128},{1,65},{65,1},{129,193},{193,129... | collective-permute-start | bytes 995336 | tf_op jit(solution)/shard_map/ppermute | solution.py:40
  15.7 18.0 %collective-permute-start.5 = (bf16[144,1152]{1,0:T(8,128)(2,1)}, bf16[144,1152]{1,0:T(8,128)(2,1)S(1)}, u32[]{:S(2)}, u32[]{:S(2)}) collective-permute-start(bf16[144,1152]{1,0:T(8,128)(2,1)} %shard_map.94.refs_0_.own), channel_id=1, source_target_pairs={{0,128},{64,192},{128,0},{192,64},{1,129},{65,193},{129,1},{193,65... | collective-permute-start | bytes 995336 | tf_op jit(solution)/shard_map/ppermute | solution.py:40
  33.8 5.1 %collective-permute-start.6 = (bf16[144,1152]{1,0:T(8,128)(2,1)}, bf16[144,1152]{1,0:T(8,128)(2,1)S(1)}, u32[]{:S(2)}, u32[]{:S(2)}) collective-permute-start(bf16[144,1152]{1,0:T(8,128)(2,1)} %get-tuple-element.48.refs_1_.own), channel_id=1, source_target_pairs={{0,8},{8,0},{1,9},{9,1},{2,10},{10,2},{3,11},{11,3},{4,12},{12,4},... | collective-permute-start | bytes 995336 | tf_op jit(solution)/shard_map/ppermute | solution.py:40
  33.8 15.0 %collective-permute-start.2 = (bf16[144,1152]{1,0:T(8,128)(2,1)}, bf16[144,1152]{1,0:T(8,128)(2,1)S(1)}, u32[]{:S(2)}, u32[]{:S(2)}) collective-permute-start(bf16[144,1152]{1,0:T(8,128)(2,1)} %get-tuple-element.48.refs_1_.own), channel_id=1, source_target_pairs={{0,16},{16,0},{32,48},{48,32},{1,17},{17,1},{33,49},{49,33},{2,18}... | collective-permute-start | bytes 995336 | tf_op jit(solution)/shard_map/ppermute | solution.py:40
  34.0 20.3 %collective-permute-start.9 = (bf16[144,1152]{1,0:T(8,128)(2,1)S(1)}, bf16[144,1152]{1,0:T(8,128)(2,1)S(1)}, u32[]{:S(2)}, u32[]{:S(2)}) collective-permute-start(bf16[144,1152]{1,0:T(8,128)(2,1)S(1)} %collective-permute-done.1.refs_2_), channel_id=1, source_target_pairs={{0,48},{16,32},{32,16},{48,0},{1,49},{17,33},{33,17},{49,1},{2,50}... | collective-permute-start | bytes 995336 | tf_op jit(solution)/shard_map/ppermute | solution.py:40
  38.8 27.0 %copy-start.10 = (bf16[144,1152]{1,0:T(8,128)(2,1)}, bf16[144,1152]{1,0:T(8,128)(2,1)S(1)}, u32[]{:S(2)}) copy-start(bf16[144,1152]{1,0:T(8,128)(2,1)S(1)} %collective-permute-done.6.refs_2_) | copy-start | bytes 995332
  38.8 15.5 %collective-permute-start.7 = (bf16[144,1152]{1,0:T(8,128)(2,1)}, bf16[144,1152]{1,0:T(8,128)(2,1)S(1)}, u32[]{:S(2)}, u32[]{:S(2)}) collective-permute-start(bf16[144,1152]{1,0:T(8,128)(2,1)} %get-tuple-element.48.refs_1_.own), channel_id=1, source_target_pairs={{0,64},{64,0},{128,192},{192,128},{1,65},{65,1},{129,193},{193,129... | collective-permute-start | bytes 995336 | tf_op jit(solution)/shard_map/ppermute | solution.py:40
  39.0 16.5 %collective-permute-start.8 = (bf16[144,1152]{1,0:T(8,128)(2,1)}, bf16[144,1152]{1,0:T(8,128)(2,1)S(1)}, u32[]{:S(2)}, u32[]{:S(2)}) collective-permute-start(bf16[144,1152]{1,0:T(8,128)(2,1)} %get-tuple-element.48.refs_1_.own), channel_id=1, source_target_pairs={{0,128},{64,192},{128,0},{192,64},{1,129},{65,193},{129,1},{193,65... | collective-permute-start | bytes 995336 | tf_op jit(solution)/shard_map/ppermute | solution.py:40
  48.8 22.0 %collective-permute-start.3 = (bf16[144,1152]{1,0:T(8,128)(2,1)S(1)}, bf16[144,1152]{1,0:T(8,128)(2,1)S(1)}, u32[]{:S(2)}, u32[]{:S(2)}) collective-permute-start(bf16[144,1152]{1,0:T(8,128)(2,1)S(1)} %collective-permute-done.2.refs_5_), channel_id=1, source_target_pairs={{0,48},{16,32},{32,16},{48,0},{1,49},{17,33},{33,17},{49,1},{2,50}... | collective-permute-start | bytes 995336 | tf_op jit(solution)/shard_map/ppermute | solution.py:40
  60.1 10.8 %collective-permute-start.10 = (bf16[304,128]{1,0:T(8,128)(2,1)}, bf16[304,128]{1,0:T(8,128)(2,1)S(1)}, u32[]{:S(2)}, u32[]{:S(2)}) collective-permute-start(bf16[304,128]{1,0:T(8,128)(2,1)} %get-tuple-element.63), channel_id=1, source_target_pairs={{0,1},{1,2},{2,3},{3,0},{4,5},{5,6},{6,7},{7,4},{8,9},{9,10},{10,1... | collective-permute-start | bytes 233480 | tf_op jit(solution)/shard_map/ppermute | solution.py:351
  61.6 10.2 %collective-permute-start.11 = (bf16[304,128]{1,0:T(8,128)(2,1)}, bf16[304,128]{1,0:T(8,128)(2,1)S(1)}, u32[]{:S(2)}, u32[]{:S(2)}) collective-permute-start(bf16[304,128]{1,0:T(8,128)(2,1)} %get-tuple-element.64), channel_id=1, source_target_pairs={{0,2},{1,3},{2,0},{3,1},{4,6},{5,7},{6,4},{7,5},{8,10},{9,11},{10,... | collective-permute-start | bytes 233480 | tf_op jit(solution)/shard_map/ppermute | solution.py:351
  64.4 7.4 %collective-permute-start.12 = (bf16[304,128]{1,0:T(8,128)(2,1)}, bf16[304,128]{1,0:T(8,128)(2,1)S(1)}, u32[]{:S(2)}, u32[]{:S(2)}) collective-permute-start(bf16[304,128]{1,0:T(8,128)(2,1)} %get-tuple-element.65), channel_id=1, source_target_pairs={{0,3},{1,0},{2,1},{3,2},{4,7},{5,4},{6,5},{7,6},{8,11},{9,8},{10,9... | collective-permute-start | bytes 233480 | tf_op jit(solution)/shard_map/ppermute | solution.py:351
  71.8 27.2 %copy-start.5 = (s32[2]{0:T(128)S(1)}, s32[2]{0:T(128)}, u32[]{:S(2)}) copy-start(s32[2]{0:T(128)} %pad_add_fusion.spot) | copy-start | bytes 28
  73.9 1.8 %collective-permute-start.13 = (bf16[32,48,128]{2,1,0:T(8,128)(2,1)S(1)}, bf16[32,48,128]{2,1,0:T(8,128)(2,1)S(1)}, u32[]{:S(2)}, u32[]{:S(2)}) collective-permute-start(bf16[32,48,128]{2,1,0:T(8,128)(2,1)S(1)} %get-tuple-element.67), channel_id=1, source_target_pairs={{0,8},{8,0},{1,9},{9,1},{2,10},{10,2},{3,11},{11,3},{4,12},{12,4},... | collective-permute-start | bytes 1179656 | tf_op jit(solution)/shard_map/ppermute | solution.py:40
  76.5 22.5 %all-to-all-start = ((bf16[32,48,128]{2,1,0:T(8,128)(2,1)}), bf16[32,48,128]{2,1,0:T(8,128)(2,1)S(1)}, u32[]{:S(2)}, u32[]{:S(2)}) async-start(bf16[32,48,128]{2,1,0:T(8,128)(2,1)} %add_convert_fusion.1), calls=%async_computation | async-start | bytes 786432 | tf_op jit(solution)/shard_map/all_to_all | solution.py:362
  86.8 12.2 %collective-permute-start.14 = (bf16[288,128]{1,0:T(8,128)(2,1)}, bf16[288,128]{1,0:T(8,128)(2,1)S(1)}, u32[]{:S(2)}, u32[]{:S(2)}) collective-permute-start(bf16[288,128]{1,0:T(8,128)(2,1)} %get-tuple-element.78), channel_id=1, source_target_pairs={{0,1},{1,2},{2,3},{3,0},{4,5},{5,6},{6,7},{7,4},{8,9},{9,10},{10,1... | collective-permute-start | bytes 221192 | tf_op jit(solution)/shard_map/ppermute | solution.py:351
  86.9 12.2 %collective-permute-start.15 = (bf16[288,128]{1,0:T(8,128)(2,1)}, bf16[288,128]{1,0:T(8,128)(2,1)S(1)}, u32[]{:S(2)}, u32[]{:S(2)}) collective-permute-start(bf16[288,128]{1,0:T(8,128)(2,1)} %get-tuple-element.79), channel_id=1, source_target_pairs={{0,2},{1,3},{2,0},{3,1},{4,6},{5,7},{6,4},{7,5},{8,10},{9,11},{10,... | collective-permute-start | bytes 221192 | tf_op jit(solution)/shard_map/ppermute | solution.py:351
  90.0 9.0 %collective-permute-start.16 = (bf16[288,128]{1,0:T(8,128)(2,1)}, bf16[288,128]{1,0:T(8,128)(2,1)S(1)}, u32[]{:S(2)}, u32[]{:S(2)}) collective-permute-start(bf16[288,128]{1,0:T(8,128)(2,1)} %get-tuple-element.80), channel_id=1, source_target_pairs={{0,3},{1,0},{2,1},{3,2},{4,7},{5,4},{6,5},{7,6},{8,11},{9,8},{10,9... | collective-permute-start | bytes 221192 | tf_op jit(solution)/shard_map/ppermute | solution.py:351
  103.2 1.8 %collective-permute-start.17 = (bf16[32,48,128]{2,1,0:T(8,128)(2,1)S(1)}, bf16[32,48,128]{2,1,0:T(8,128)(2,1)S(1)}, u32[]{:S(2)}, u32[]{:S(2)}) collective-permute-start(bf16[32,48,128]{2,1,0:T(8,128)(2,1)S(1)} %get-tuple-element.82), channel_id=1, source_target_pairs={{0,8},{8,0},{1,9},{9,1},{2,10},{10,2},{3,11},{11,3},{4,12},{12,4},... | collective-permute-start | bytes 1179656 | tf_op jit(solution)/shard_map/ppermute | solution.py:40
  105.9 20.6 %all-to-all-start.1 = ((bf16[32,48,128]{2,1,0:T(8,128)(2,1)}), bf16[32,48,128]{2,1,0:T(8,128)(2,1)S(1)}, u32[]{:S(2)}, u32[]{:S(2)}) async-start(bf16[32,48,128]{2,1,0:T(8,128)(2,1)} %add_convert_fusion), calls=%async_computation.1 | async-start | bytes 786432 | tf_op jit(solution)/shard_map/all_to_all | solution.py:362
  (14 other events, 166.3 us)
Sparse Core Ops, SparseCore 0:
  10.7 29.5 all-gather.2
  42.1 29.5 all-gather.4

commit v8 on v7

--- a/solution.py
+++ b/solution.py
@@ -21,6 +21,9 @@
 STATS = 112
 DEPTH = 128
 PIECES = WIDTH // DEPTH
+SLAB = SLOT + 8
+LINE = 4
+FAR = 8
 F32 = jnp.float32
 BF16 = jnp.bfloat16
 
@@ -93,12 +96,16 @@
     )(x, w, keys)
 
 
-def add_tiles(with_stats, scal, mine, key_col, blocks, total, sums):
+def caption_row(block):
+    digits = block[ROWS:, :LANES].astype(F32)
+    return digits[0:1] * 128.0 + digits[1:2]
+
+
+def add_tiles(with_stats, scal, mine, key_col, pairs, total, sums):
     heat, shift = scal[0], scal[1]
-    for block in blocks:
+    for block, key_row in pairs:
         vec = block[:ROWS, :]
-        keys = block[ROWS:, :LANES].astype(F32)
-        same = key_col == keys[0:1] * 128.0 + keys[1:2]
+        same = key_col == key_row
         sim = nt(mine, vec)
         logits = heat * sim + shift
         z = jnp.where(same, -logits, logits)
@@ -113,6 +120,15 @@
     return total, sums
 
 
+def pair_up(blocks, rows_ref):
+    pairs = []
+    for k, block in enumerate(blocks):
+        key_row = caption_row(block)
+        rows_ref[k] = jnp.broadcast_to(key_row, (8, LANES))
+        pairs.append((block, key_row))
+    return pairs
+
+
 def write_payload(out_ref, unit, key):
     digit = jnp.broadcast_to(key, (KEY_ROWS, ROWS))
     row = lax.broadcasted_iota(jnp.int32, (KEY_ROWS, ROWS), 0)
@@ -123,9 +139,7 @@
 
 
 def early_kernel(first, scal, spot, x, w_hbm, key, *refs):
-    blocks, refs = refs[:-7], refs[-7:]
-    total_ref, unit_ref, len_ref, key_ref, sum_ref, w, sem = refs
-    own, blocks = (blocks[-1], blocks[:-1]) if first else (blocks[0], blocks[1:])
+    refs, (total_ref, unit_ref, len_ref, key_ref, sum_ref, w, sem) = refs[:-7], refs[-7:]
     copy = pltpu.make_async_copy(w_hbm, w, sem)
     copy.start()
     key_col = jnp.broadcast_to(key[...].astype(F32), (ROWS, ROWS)).T
@@ -139,15 +153,21 @@
         len_ref[...] = jnp.broadcast_to(length, len_ref.shape)
 
     if first:
+        blocks, (own, rows_ref) = refs[:-2], refs[-2:]
         norm()
-        write_payload(own, unit_ref[...], key[...])
+        own[...] = unit_ref[...].astype(BF16)
+        pairs = pair_up(blocks, rows_ref)
+    else:
+        own, near_rows, far_rows, *blocks = refs
+        rows = [near_rows[0], near_rows[1], far_rows[0], far_rows[1], far_rows[2]]
+        pairs = [(block, row[0:1]) for block, row in zip(blocks, rows)]
     zero = jnp.zeros((ROWS, ROWS), F32)
     total, sums = add_tiles(
         first,
         scal,
         own[:ROWS, :],
         key_col,
-        blocks,
+        pairs,
         jnp.zeros((ROWS, WIDTH), F32),
         [zero] * 3,
     )
@@ -162,7 +182,10 @@
     shapes = [(ROWS, WIDTH), (ROWS, WIDTH), (ROWS, LANES), (ROWS, ROWS), (3, ROWS, ROWS)]
     outs = [jax.ShapeDtypeStruct(shape, F32) for shape in shapes]
     if first:
-        outs = [jax.ShapeDtypeStruct((ROWS + KEY_ROWS, WIDTH), BF16)] + outs
+        outs = [
+            jax.ShapeDtypeStruct((ROWS, WIDTH), BF16),
+            jax.ShapeDtypeStruct((len(blocks), 8, LANES), F32),
+        ] + outs
     hbm = pl.BlockSpec(memory_space=pltpu.HBM)
     return pl.pallas_call(
         functools.partial(early_kernel, first),
@@ -178,12 +201,18 @@
 def late_kernel(with_stats, ways, count, spot, scal, own, total_ref, unit, length, key, acc, *refs):
     blocks, outs, held = refs[:count], refs[count:-1], refs[-1]
     heat = scal[0]
+    if with_stats:
+        *outs, rows_ref = outs
+        pairs = pair_up(blocks, rows_ref)
+    else:
+        rows, block = blocks
+        pairs = [(block, rows[3][0:1])]
     total, sums = add_tiles(
         with_stats,
         scal,
         own[:ROWS, :],
         key[...],
-        blocks,
+        pairs,
         total_ref[...],
         [acc[k] for k in range(3)],
     )
@@ -218,12 +247,15 @@
 
 
 def late(with_stats, ways, spot, scal, own, partial, blocks):
-    shapes = [(2 * COLS + (KEY_ROWS if with_stats else 0), ROWS)] * ways
+    rows = 2 * COLS + (KEY_ROWS if with_stats else 0)
+    shapes = [jax.ShapeDtypeStruct((rows, ROWS), BF16)] * ways
+    if with_stats:
+        shapes.append(jax.ShapeDtypeStruct((len(blocks), 8, LANES), F32))
     return pl.pallas_call(
         functools.partial(late_kernel, with_stats, ways, len(blocks)),
         in_specs=[SMEM] * 2 + [VMEM] * (6 + len(blocks)),
         out_specs=[VMEM] * len(shapes),
-        out_shape=[jax.ShapeDtypeStruct(shape, BF16) for shape in shapes],
+        out_shape=shapes,
         scratch_shapes=[pltpu.VMEM((2 * ways, COLS, ROWS), BF16)],
         compiler_params=params(56),
         cost_estimate=cost(4 * 2 * ROWS * ROWS * WIDTH, 4 * 2**20),
@@ -290,43 +322,82 @@
     )(spot, feat, *spreads)
 
 
-def final_kernel(count, parts, out, stats):
-    total = jnp.sum(parts[...].astype(F32), axis=0)
-    out[:, :LANES] = total[:CHUNK]
-    rest = total[SLOT:, :].T
-    out[:, LANES : LANES + 8] = rest[:CHUNK]
-    out[:, LANES + 8 :] = rest[64 : 64 + CHUNK]
-    lane = lax.broadcasted_iota(jnp.int32, (1, LANES), 1)
-    place = lane - STATS
-    row = total[SLOT : SLOT + 1] + total[SLOT + 1 : SLOT + 2]
-    answer = jnp.zeros((1, LANES), F32)
+def mix_kernel(spot, kept_img, taken_img, kept_txt, taken_txt, mine, *outs):
+    def part(place):
+        span = pl.ds(place * FAR, FAR)
+        img = kept_img[span] + taken_img[span].astype(F32)
+        txt = kept_txt[span] + taken_txt[span].astype(F32)
+        return img, txt
+
+    img, txt = part(spot[2])
+    mine[:, :SLAB, :] = img
+    mine[:, SLAB:, :] = txt
+    for step, out in enumerate(outs):
+        img, txt = part(lax.rem(spot[2] + step + 1, LINE))
+        out[:, :SLAB, :] = img.astype(BF16)
+        out[:, SLAB:, :] = txt.astype(BF16)
+
+
+def mix(spot, *arrays):
+    shape = (FAR, 2 * SLAB, LANES)
+    return pl.pallas_call(
+        mix_kernel,
+        in_specs=[SMEM] + [VMEM] * 4,
+        out_specs=[VMEM] * LINE,
+        out_shape=[jax.ShapeDtypeStruct(shape, F32)]
+        + [jax.ShapeDtypeStruct(shape, BF16)] * (LINE - 1),
+        compiler_params=params(16),
+        cost_estimate=cost(4 * FAR * SLAB * LANES, 2**20),
+    )(spot, *arrays)
+
+
+def fold_kernel(mine, *refs):
+    total = mine[...]
+    for part in refs[:-1]:
+        total += part[...].astype(F32)
+    refs[-1][...] = total.astype(BF16)
+
+
+def fold(mine, parts):
+    return pl.pallas_call(
+        fold_kernel,
+        in_specs=[VMEM] * (1 + len(parts)),
+        out_specs=VMEM,
+        out_shape=jax.ShapeDtypeStruct(mine.shape, BF16),
+        compiler_params=params(16),
+        cost_estimate=cost(4 * FAR * SLAB * LANES, 2**20),
+    )(mine, *parts)
+
+
+def final_kernel(count, parts, out_img, out_txt, stats):
+    both = jnp.sum(parts[...].astype(F32), axis=0)
+    for out, total in ((out_img, both[:SLAB]), (out_txt, both[SLAB:])):
+        out[:, :LANES] = total[:CHUNK]
+        rest = total[SLOT:, :].T
+        out[:, LANES : LANES + 8] = rest[:CHUNK]
+        out[:, LANES + 8 :] = rest[64 : 64 + CHUNK]
+    place = lax.broadcasted_iota(jnp.int32, (1, LANES), 1) - STATS
+    row = both[SLOT : SLOT + 1] + both[SLOT + 1 : SLOT + 2]
     for k in range(3):
-        number = jnp.sum(
-            jnp.where((place % 3 == k) & (place >= 0) & (place < 9), row, 0.0),
-            axis=1,
-            keepdims=True,
-        )
-        answer = jnp.where(lane == k, number, answer)
-    stats[...] = answer * (1.0 / count)
+        chosen = jnp.where((place % 3 == k) & (place >= 0) & (place < 9), row, 0.0)
+        stats[k] = jnp.sum(chosen) * (1.0 / count)
 
 
 def final(count, parts):
+    grad = jax.ShapeDtypeStruct((CHUNK, COLS), F32)
     return pl.pallas_call(
         functools.partial(final_kernel, count),
         in_specs=[VMEM],
-        out_specs=[VMEM, VMEM],
-        out_shape=[
-            jax.ShapeDtypeStruct((CHUNK, COLS), F32),
-            jax.ShapeDtypeStruct((1, LANES), F32),
-        ],
+        out_specs=[VMEM, VMEM, SMEM],
+        out_shape=[grad, grad, jax.ShapeDtypeStruct((3,), F32)],
         compiler_params=params(8),
-        cost_estimate=cost(2 * QUADS * 48 * LANES, 2**20),
+        cost_estimate=cost(4 * FAR * SLAB * LANES, 2**20),
     )(parts)
 
 
 def body(pictures, sentences, keys, picture_weights, sentence_weights, heat_log, shift_value):
     ways = lax.axis_size("dx")
-    spot = jnp.stack([lax.axis_index("dx"), lax.axis_index("lc")]).astype(jnp.int32)
+    spot = jnp.stack([lax.axis_index(axis) for axis in ("dx", "lc", "ly")]).astype(jnp.int32)
     scal = jnp.stack([jnp.exp(heat_log[0]), shift_value[0]])
     txt = project(sentences[0], sentence_weights, keys)
     txt_a = exchange(txt, "lz", 1)
@@ -336,7 +407,7 @@
     img_feat = lax.all_gather(after(pictures[0], txt), "dx", axis=0, tiled=True)
     txt_feat = lax.all_gather(after(sentences[0], txt), "dx", axis=0, tiled=True)
 
-    img, *img_part = early(True, scal, spot, pictures[0], picture_weights, keys, [txt, txt_c])
+    img, near_rows, *img_part = early(True, scal, spot, pictures[0], picture_weights, keys, [txt, txt_c])
     txt_b = exchange(after(txt_a, txt_y1, txt_y2), "lz", 3)
     img_a = exchange(after(img, txt_a), "lz", 1)
     img_c = exchange(after(img, txt_a, txt_y1, txt_y2), "lc", 1)
@@ -347,36 +418,39 @@
 
     count = 2 * QUADS * lax.axis_size("dz") * ways
 
-    def turn(array, step):
-        return lax.ppermute(array, "dx", [(i, (i + step) % ways) for i in range(ways)])
-
-    def share(with_stats, feat, spreads, *others):
-        kept, given = heads(with_stats, spot, feat, spreads)
-        taken = after(exchange(given, "lc", 1), *others)
-        return (kept + taken.astype(F32)).astype(BF16)
+    def turn(array, axis, step):
+        size = lax.axis_size(axis)
+        return lax.ppermute(array, axis, [(i, (i + step) % size) for i in range(size)])
 
     def columns(outs):
-        return [outs[0]] + [turn(out, step) for step, out in enumerate(outs) if step]
-
-    def collect(sums):
-        return lax.all_to_all(sums, ("ly", "lz", "dz"), 0, 0, tiled=True)
+        return [outs[0]] + [turn(out, "dx", step) for step, out in enumerate(outs) if step]
 
     last = after(txt_b, img_feat, img_a, img_c, img_y1, img_y2)
-    img_outs = late(True, ways, spot, scal, img, img_part, [txt_y1, txt_y2, txt_a, last])
+    *img_outs, far_rows = late(
+        True, ways, spot, scal, img, img_part, [txt_y1, txt_y2, txt_a, last]
+    )
     img_cols = columns(img_outs)
     txt_part = early(
-        False, scal, spot, sentences[0], sentence_weights, keys, [txt, img, img_c, img_y1, img_y2, img_a]
+        False,
+        scal,
+        spot,
+        sentences[0],
+        sentence_weights,
+        keys,
+        [txt, near_rows, far_rows, img, img_c, img_y1, img_y2, img_a],
     )
-    img_sums = share(True, after(img_feat, img_b, *txt_part), img_cols)
-    img_parts = collect(img_sums)
-    last = after(img_b, img_sums)
-    outs = late(False, ways, spot, scal, txt, txt_part, [last])
-    *outs, txt_feat = lax.optimization_barrier((*outs, txt_feat))
+    last = after(img_b, *img_cols, *txt_part)
+    outs = late(False, ways, spot, scal, txt, txt_part, [far_rows, last])
     txt_cols = columns(outs)
-    txt_parts = collect(share(False, after(txt_feat, img_parts), txt_cols))
-    grad_img, stats = final(count, img_parts)
-    grad_txt, _ = final(count, txt_parts)
-    return grad_img, grad_txt, stats[0, :3]
+    img_kept, img_given = heads(True, spot, after(img_feat, outs[0]), img_cols)
+    img_taken = exchange(img_given, "lc", 1)
+    txt_kept, txt_given = heads(False, spot, txt_feat, txt_cols)
+    txt_taken = exchange(txt_given, "lc", 1)
+    mine, *others = mix(spot, img_kept, img_taken, txt_kept, txt_taken)
+    others = [turn(other, "ly", step + 1) for step, other in enumerate(others)]
+    sums = lax.all_to_all(fold(mine, others), ("lz", "dz"), 0, 0, tiled=True)
+    grad_img, grad_txt, stats = final(count, sums)
+    return grad_img, grad_txt, stats
 
 
 def solution(mesh):

time: 135 us -> 127 us (0.941)
  blocking collectives: 0 us -> 14.7 us
  waiting for transfers between devices: 41.4 us -> 26.8 us
  starting transfers between devices: 43.7 us -> 35.9 us
  other arithmetic: 2.85 us -> 1.15 us
    all_to_all x2 -> x0, waiting for transfers between devices: 21.2 us -> none  [collect(): return lax.all_to_all(sums, ('ly', 'lz', 'dz'), 0, 0, tiled=True)]
    all_to_all x0 -> x1, blocking collectives: none -> 14.7 us  [body(): sums = lax.all_to_all(fold(mine, others), ('lz', 'dz'), 0, 0, tiled=True)]
    all_to_all x2 -> x0, starting transfers between devices: 12.5 us -> none  [collect(): return lax.all_to_all(sums, ('ly', 'lz', 'dz'), 0, 0, tiled=True)]
    ppermute x6 -> x9, waiting for transfers between devices: 0.97 us -> 10.5 us  [turn(): lax.ppermute(array, axis, [(i, (i + step) % size) for i in range(size)])]
    ppermute x12, waiting for transfers between devices: 19.2 us -> 15.6 us  [exchange(): lax.ppermute(array, axis, [(i, i ^ apart) for i in range(lax.axis_size(ax...]
    ppermute x6 -> x9, starting transfers between devices: 10.8 us -> 13.6 us  [turn(): lax.ppermute(array, axis, [(i, (i + step) % size) for i in range(size)])]
    ppermute x12, starting transfers between devices: 20.4 us -> 22.3 us  [exchange(): lax.ppermute(array, axis, [(i, i ^ apart) for i in range(lax.axis_size(ax...]
    convert_element_type x2 -> x0, other arithmetic: 1.68 us -> none  [share(): return (kept + taken.astype(F32)).astype(BF16)]
  transfers between devices with their start and end apart: 22 -> 23, of which waited for: 9 -> 10; matrix products, arithmetic and copies ran while one was open for 2% -> 1% of each run, Pallas kernels for 16% -> 17%
where the time goes in v8:
time: 127 us; the launch traced here: 125 us
  starting transfers between devices  35.9 us (28%)
  Pallas kernels  26.8 us (21%)
  waiting for transfers between devices  26.8 us (21%)
  between operations  15.6 us (12%)
  blocking collectives  14.7 us (12%)
  local copies, waits for them, and re-layouts  4.24 us (3%)
    ppermute x12, starting transfers between devices, exchange(): lax.ppermute(array, axis, [(i, i ^ apart) for i in range(lax.axis_size(ax...  22.3 us
    ppermute x12, waiting for transfers between devices, exchange(): lax.ppermute(array, axis, [(i, i ^ apart) for i in range(lax.axis_size(ax...  15.6 us
    all_to_all x1, blocking collectives, body(): sums = lax.all_to_all(fold(mine, others), ('lz', 'dz'), 0, 0, tiled=True)  14.7 us
    ppermute x9, starting transfers between devices, turn(): lax.ppermute(array, axis, [(i, (i + step) % size) for i in range(size)])  13.6 us
    ppermute x9, waiting for transfers between devices, turn(): lax.ppermute(array, axis, [(i, (i + step) % size) for i in range(size)])  10.5 us
    pallas_call x2, Pallas kernels, early(): pl.pallas_call(functools.partial(early_kernel, first), in_specs=[SMEM, SM...  10.3 us
    pallas_call x2, Pallas kernels, late(): pl.pallas_call(functools.partial(late_kernel, with_stats, ways, len(block...  7.5 us
    unnamed x30, local copies, waits for them, and re-layouts  4.24 us
  transfers between devices with their start and end apart: 23, of which 10 were waited for; matrix products, arithmetic and copies ran while one was open for 1% of the time, Pallas kernels for 17%

profile of v8, /device:TPU:32, one launch (start us, length us, event | category | flops | bytes accessed | tf_op | source)
XLA Modules:
  0.0 125.2 jit_solution(12519385687540512430)
XLA Ops:
  7.2 3.4 %shard_map.94.refs_0_.own = bf16[144,1152]{1,0:T(8,128)(2,1)} custom-call(bf16[128,1152]{1,0:T(8,128)(2,1)} %bitcast.5, bf16[1152,1152]{1,0:T(8,128)(2,1)} %w_hbm.5, s32[1,128]{1,0:T(1,128)} %key.3), custom_call_target="tpu_custom_call" | custom-call | flops 339738624 | bytes 4194304 | tf_op jit(solution)/shard_map/pallas_call | solution.py:83
  11.5 1.7 %collective-permute-start.1 = (bf16[144,1152]{1,0:T(8,128)(2,1)}, bf16[144,1152]{1,0:T(8,128)(2,1)S(1)}, u32[]{:S(2)}, u32[]{:S(2)}) collective-permute-start(bf16[144,1152]{1,0:T(8,128)(2,1)} %shard_map.94.refs_0_.own), channel_id=1, source_target_pairs={{0,64},{64,0},{128,192},{192,128},{1,65},{65,1},{129,193},{193,129... | collective-permute-start | bytes 995336 | tf_op jit(solution)/shard_map/ppermute | solution.py:43
  13.1 2.9 %collective-permute-start.2 = (bf16[144,1152]{1,0:T(8,128)(2,1)}, bf16[144,1152]{1,0:T(8,128)(2,1)S(1)}, u32[]{:S(2)}, u32[]{:S(2)}) collective-permute-start(bf16[144,1152]{1,0:T(8,128)(2,1)} %shard_map.94.refs_0_.own), channel_id=1, source_target_pairs={{0,128},{64,192},{128,0},{192,64},{1,129},{65,193},{129,1},{193,65... | collective-permute-start | bytes 995336 | tf_op jit(solution)/shard_map/ppermute | solution.py:43
  16.0 3.3 %collective-permute-start.3 = (bf16[144,1152]{1,0:T(8,128)(2,1)}, bf16[144,1152]{1,0:T(8,128)(2,1)S(1)}, u32[]{:S(2)}, u32[]{:S(2)}) collective-permute-start(bf16[144,1152]{1,0:T(8,128)(2,1)} %shard_map.94.refs_0_.own), channel_id=1, source_target_pairs={{0,16},{16,0},{32,48},{48,32},{1,17},{17,1},{33,49},{49,33},{2,18}... | collective-permute-start | bytes 995336 | tf_op jit(solution)/shard_map/ppermute | solution.py:43
  22.5 5.2 %shard_map.95 = (bf16[128,1152]{1,0:T(8,128)(2,1)}, f32[2,8,128]{2,1,0:T(8,128)}, f32[128,1152]{1,0:T(8,128)}, f32[128,1152]{1,0:T(8,128)}, f32[128,128]{1,0:T(8...) custom-call(f32[2]{0:T(128)} %pad_maximum_fusion.scal, s32[3]{0:T(128)} %pad_add_fusion.spot, ...), custom_call_target="tpu_custom_call" | custom-call | flops 377487360 | bytes 8388608 | tf_op jit(solution)/shard_map/pallas_call | solution.py:190
  27.8 3.7 %collective-permute-done.2.refs_1_ = bf16[144,1152]{1,0:T(8,128)(2,1)S(1)} collective-permute-done((bf16[144,1152]{1,0:T(8,128)(2,1)}, bf16[144,1152]{1,0:T(8,128)(2,1)S(1)}, u32[]{:S(2)}, u32[]{:S(2)}) %collective-permute-start.2) | collective-permute-done | bytes 331808 | tf_op jit(solution)/shard_map/ppermute | solution.py:43
  31.5 1.9 %collective-permute-done.3.refs_2_ = bf16[144,1152]{1,0:T(8,128)(2,1)S(1)} collective-permute-done((bf16[144,1152]{1,0:T(8,128)(2,1)}, bf16[144,1152]{1,0:T(8,128)(2,1)S(1)}, u32[]{:S(2)}, u32[]{:S(2)}) %collective-permute-start.3) | collective-permute-done | bytes 331808 | tf_op jit(solution)/shard_map/ppermute | solution.py:43
  33.4 3.3 %collective-permute-start.5 = (bf16[128,1152]{1,0:T(8,128)(2,1)}, bf16[128,1152]{1,0:T(8,128)(2,1)S(1)}, u32[]{:S(2)}, u32[]{:S(2)}) collective-permute-start(bf16[128,1152]{1,0:T(8,128)(2,1)} %get-tuple-element.52.own.refs_3_), channel_id=1, source_target_pairs={{0,16},{16,0},{32,48},{48,32},{1,17},{17,1},{33,49},{49,33},{2,18}... | collective-permute-start | bytes 884744 | tf_op jit(solution)/shard_map/ppermute | solution.py:43
  36.7 2.6 %collective-permute-start.4 = (bf16[144,1152]{1,0:T(8,128)(2,1)S(1)}, bf16[144,1152]{1,0:T(8,128)(2,1)S(1)}, u32[]{:S(2)}, u32[]{:S(2)}) collective-permute-start(bf16[144,1152]{1,0:T(8,128)(2,1)S(1)} %collective-permute-done.3.refs_2_), channel_id=1, source_target_pairs={{0,48},{16,32},{32,16},{48,0},{1,49},{17,33},{33,17},{49,1},{2,50}... | collective-permute-start | bytes 995336 | tf_op jit(solution)/shard_map/ppermute | solution.py:43
  39.5 1.5 %collective-permute-start.8 = (bf16[128,1152]{1,0:T(8,128)(2,1)}, bf16[128,1152]{1,0:T(8,128)(2,1)S(1)}, u32[]{:S(2)}, u32[]{:S(2)}) collective-permute-start(bf16[128,1152]{1,0:T(8,128)(2,1)} %get-tuple-element.52.own.refs_3_), channel_id=1, source_target_pairs={{0,128},{64,192},{128,0},{192,64},{1,129},{65,193},{129,1},{193,65... | collective-permute-start | bytes 884744 | tf_op jit(solution)/shard_map/ppermute | solution.py:43
  41.0 7.0 %collective-permute-done.5.refs_7_ = bf16[128,1152]{1,0:T(8,128)(2,1)S(1)} collective-permute-done((bf16[128,1152]{1,0:T(8,128)(2,1)}, bf16[128,1152]{1,0:T(8,128)(2,1)S(1)}, u32[]{:S(2)}, u32[]{:S(2)}) %collective-permute-start.5) | collective-permute-done | bytes 294944 | tf_op jit(solution)/shard_map/ppermute | solution.py:43
  48.0 6.5 %collective-permute-start.9 = (bf16[128,1152]{1,0:T(8,128)(2,1)S(1)}, bf16[128,1152]{1,0:T(8,128)(2,1)S(1)}, u32[]{:S(2)}, u32[]{:S(2)}) collective-permute-start(bf16[128,1152]{1,0:T(8,128)(2,1)S(1)} %collective-permute-done.5.refs_7_), channel_id=1, source_target_pairs={{0,48},{16,32},{32,16},{48,0},{1,49},{17,33},{33,17},{49,1},{2,50}... | collective-permute-start | bytes 884744 | tf_op jit(solution)/shard_map/ppermute | solution.py:43
  56.6 4.4 %shard_map.96 = (bf16[304,128]{1,0:T(8,128)(2,1)}, bf16[304,128]{1,0:T(8,128)(2,1)}, bf16[304,128]{1,0:T(8,128)(2,1)}, bf16[304,128]{1,0:T(8,128)(2,1)}, f32[4,8,128]{2,1,0:T(8,128)}) custom-call(s32[3]{0:T(128)} %pad_add_fusion.spot, f32[2]{0:T(128)} %pad_maximum_fusion.scal, bf16[128,1152]{1,0:T(8,128)(2,1)} %get-tuple-element.52.own.refs_3_, ...), custom_call_target="tpu_custom_call" | custom-call | flops 150994944 | bytes 4194304 | tf_op jit(solution)/shard_map/pallas_call | solution.py:254
  62.5 2.7 %collective-permute-start.11 = (bf16[304,128]{1,0:T(8,128)(2,1)}, bf16[304,128]{1,0:T(8,128)(2,1)S(1)}, u32[]{:S(2)}, u32[]{:S(2)}) collective-permute-start(bf16[304,128]{1,0:T(8,128)(2,1)} %get-tuple-element.62), channel_id=1, source_target_pairs={{0,2},{1,3},{2,0},{3,1},{4,6},{5,7},{6,4},{7,5},{8,10},{9,11},{10,... | collective-permute-start | bytes 233480 | tf_op jit(solution)/shard_map/ppermute | solution.py:423
  66.7 5.0 %shard_map.97 = (f32[128,1152]{1,0:T(8,128)}, f32[128,1152]{1,0:T(8,128)}, f32[128,128]{1,0:T(8,128)}, f32[128,128]{1,0:T(8,128)}, f32[3,128,128]{2,1,0:T(8,128)}) custom-call(f32[2]{0:T(128)} %pad_maximum_fusion.scal, s32[3]{0:T(128)} %pad_add_fusion.spot, bf16[128,1152]{1,0:T(8,128)(2,1)} %bitcast.7, bf16[1152,1152]{1,0:T(8,128)(2,1)} %w_hbm.5, ...), custom_call_target="tpu_custom_call" | custom-call | flops 377487360 | bytes 8388608 | tf_op jit(solution)/shard_map/pallas_call | solution.py:190
  72.5 3.1 %shard_map.98 = (bf16[288,128]{1,0:T(8,128)(2,1)}, bf16[288,128]{1,0:T(8,128)(2,1)}, bf16[288,128]{1,0:T(8,128)(2,1)}, bf16[288,128]{1,0:T(8,128)(2,1)}) custom-call(s32[3]{0:T(128)} %pad_add_fusion.spot, f32[2]{0:T(128)} %pad_maximum_fusion.scal, bf16[144,1152]{1,0:T(8,128)(2,1)} %shard_map.94.refs_0_.own, f32[128,1152]{1,0:T(8,128)} %get-tuple-element.55.total_ref, ...), custom_call_target="tpu_custom_call" | custom-call | flops 150994944 | bytes 4194304 | tf_op jit(solution)/shard_map/pallas_call | solution.py:254
  76.1 2.3 %collective-permute-start.15 = (bf16[288,128]{1,0:T(8,128)(2,1)}, bf16[288,128]{1,0:T(8,128)(2,1)S(1)}, u32[]{:S(2)}, u32[]{:S(2)}) collective-permute-start(bf16[288,128]{1,0:T(8,128)(2,1)} %get-tuple-element.71), channel_id=1, source_target_pairs={{0,2},{1,3},{2,0},{3,1},{4,6},{5,7},{6,4},{7,5},{8,10},{9,11},{10,... | collective-permute-start | bytes 221192 | tf_op jit(solution)/shard_map/ppermute | solution.py:423
  79.3 2.0 %shard_map.99 = (f32[32,48,128]{2,1,0:T(8,128)S(1)}, bf16[32,48,128]{2,1,0:T(8,128)(2,1)S(1)}) custom-call(s32[3]{0:T(128)S(1)} %copy-done.4, bf16[512,1152]{1,0:T(8,128)(2,1)S(1)} %copy-done.1, bf16[304,128]{1,0:T(8,128)(2,1)S(1)} %copy-done.2, bf16[304,128]{1,0:T(8,128)(2,1)S(1)} %collective-permute-done.10.refs_1_, ...), custom_call_target="tpu_custom_call" | custom-call | flops 339738624 | bytes 4194304 | tf_op jit(solution)/shard_map/pallas_call | solution.py:314
  85.2 2.0 %shard_map.100 = (f32[32,48,128]{2,1,0:T(8,128)S(1)}, bf16[32,48,128]{2,1,0:T(8,128)(2,1)S(1)}) custom-call(s32[3]{0:T(128)S(1)} %copy-done.4, bf16[512,1152]{1,0:T(8,128)(2,1)S(1)} %copy-done, bf16[288,128]{1,0:T(8,128)(2,1)S(1)} %copy-done.3, bf16[288,128]{1,0:T(8,128)(2,1)S(1)} %collective-permute-done.14.refs_1_, ...), custom_call_target="tpu_custom_call" | custom-call | flops 339738624 | bytes 4194304 | tf_op jit(solution)/shard_map/pallas_call | solution.py:314
  87.3 1.7 %collective-permute-done.17.taken_txt = bf16[32,48,128]{2,1,0:T(8,128)(2,1)S(1)} collective-permute-done((bf16[32,48,128]{2,1,0:T(8,128)(2,1)S(1)}, bf16[32,48,128]{2,1,0:T(8,128)(2,1)S(1)}, u32[]{:S(2)}, u32[]{:S(2)}) %collective-permute-start.17) | collective-permute-done | bytes 393248 | tf_op jit(solution)/shard_map/ppermute | solution.py:43
  90.5 2.8 %collective-permute-start.19 = (bf16[8,96,128]{2,1,0:T(8,128)(2,1)S(1)}, bf16[8,96,128]{2,1,0:T(8,128)(2,1)S(1)}, u32[]{:S(2)}, u32[]{:S(2)}) collective-permute-start(bf16[8,96,128]{2,1,0:T(8,128)(2,1)S(1)} %get-tuple-element.77), channel_id=1, source_target_pairs={{0,128},{64,192},{128,0},{192,64},{1,129},{65,193},{129,1},{193,65... | collective-permute-start | bytes 589832 | tf_op jit(solution)/shard_map/ppermute | solution.py:423
  93.8 4.5 %collective-permute-done.18.refs_0_ = bf16[8,96,128]{2,1,0:T(8,128)(2,1)S(1)} collective-permute-done((bf16[8,96,128]{2,1,0:T(8,128)(2,1)S(1)}, bf16[8,96,128]{2,1,0:T(8,128)(2,1)S(1)}, u32[]{:S(2)}, u32[]{:S(2)}) %collective-permute-start.18) | collective-permute-done | bytes 196640 | tf_op jit(solution)/shard_map/ppermute | solution.py:423
  98.4 4.0 %collective-permute-done.19.refs_1_ = bf16[8,96,128]{2,1,0:T(8,128)(2,1)S(1)} collective-permute-done((bf16[8,96,128]{2,1,0:T(8,128)(2,1)S(1)}, bf16[8,96,128]{2,1,0:T(8,128)(2,1)S(1)}, u32[]{:S(2)}, u32[]{:S(2)}) %collective-permute-start.19) | collective-permute-done | bytes 196640 | tf_op jit(solution)/shard_map/ppermute | solution.py:423
  102.8 14.7 %all_to_all.5.parts = bf16[8,96,128]{2,1,0:T(8,128)(2,1)S(1)} all-to-all(bf16[8,96,128]{2,1,0:T(8,128)(2,1)S(1)} %shard_map.102), channel_id=1, replica_groups=mesh['ly'=4,'lz'=4,'lc'=2,'dz'=2,'dx'=4] {'lz','dz'}, dimensions={0} | all-to-all | bytes 393216 | tf_op jit(solution)/shard_map/all_to_all | solution.py:451
  (67 shorter events, 17.3 us)
Async XLA Ops:
  7.2 48.7 %all-gather.3.cloned.1.call-start = ((), (), s32[]{:S(2)}) async-start(), calls=%async_computation.1 | async-start | bytes 1474560 | tf_op jit(solution)/shard_map/all_gather | solution.py:407
  10.6 70.8 %all-gather.5.cloned.1.call-start = ((), (), s32[]{:S(2)}) async-start(), calls=%async_computation.2 | async-start | bytes 1474560 | tf_op jit(solution)/shard_map/all_gather | solution.py:408
  11.4 10.4 %collective-permute-start = (bf16[144,1152]{1,0:T(8,128)(2,1)}, bf16[144,1152]{1,0:T(8,128)(2,1)S(1)}, u32[]{:S(2)}, u32[]{:S(2)}) collective-permute-start(bf16[144,1152]{1,0:T(8,128)(2,1)} %shard_map.94.refs_0_.own), channel_id=1, source_target_pairs={{0,8},{8,0},{1,9},{9,1},{2,10},{10,2},{3,11},{11,3},{4,12},{12,4},... | collective-permute-start | bytes 995336 | tf_op jit(solution)/shard_map/ppermute | solution.py:43
  11.5 16.3 %collective-permute-start.1 = (bf16[144,1152]{1,0:T(8,128)(2,1)}, bf16[144,1152]{1,0:T(8,128)(2,1)S(1)}, u32[]{:S(2)}, u32[]{:S(2)}) collective-permute-start(bf16[144,1152]{1,0:T(8,128)(2,1)} %shard_map.94.refs_0_.own), channel_id=1, source_target_pairs={{0,64},{64,0},{128,192},{192,128},{1,65},{65,1},{129,193},{193,129... | collective-permute-start | bytes 995336 | tf_op jit(solution)/shard_map/ppermute | solution.py:43
  13.1 18.3 %collective-permute-start.2 = (bf16[144,1152]{1,0:T(8,128)(2,1)}, bf16[144,1152]{1,0:T(8,128)(2,1)S(1)}, u32[]{:S(2)}, u32[]{:S(2)}) collective-permute-start(bf16[144,1152]{1,0:T(8,128)(2,1)} %shard_map.94.refs_0_.own), channel_id=1, source_target_pairs={{0,128},{64,192},{128,0},{192,64},{1,129},{65,193},{129,1},{193,65... | collective-permute-start | bytes 995336 | tf_op jit(solution)/shard_map/ppermute | solution.py:43
  16.0 17.3 %collective-permute-start.3 = (bf16[144,1152]{1,0:T(8,128)(2,1)}, bf16[144,1152]{1,0:T(8,128)(2,1)S(1)}, u32[]{:S(2)}, u32[]{:S(2)}) collective-permute-start(bf16[144,1152]{1,0:T(8,128)(2,1)} %shard_map.94.refs_0_.own), channel_id=1, source_target_pairs={{0,16},{16,0},{32,48},{48,32},{1,17},{17,1},{33,49},{49,33},{2,18}... | collective-permute-start | bytes 995336 | tf_op jit(solution)/shard_map/ppermute | solution.py:43
  27.8 28.1 %copy-start.5 = (bf16[144,1152]{1,0:T(8,128)(2,1)}, bf16[144,1152]{1,0:T(8,128)(2,1)S(1)}, u32[]{:S(2)}) copy-start(bf16[144,1152]{1,0:T(8,128)(2,1)S(1)} %collective-permute-done.1.refs_0_) | copy-start | bytes 995332
  33.4 6.0 %collective-permute-start.6 = (bf16[128,1152]{1,0:T(8,128)(2,1)}, bf16[128,1152]{1,0:T(8,128)(2,1)S(1)}, u32[]{:S(2)}, u32[]{:S(2)}) collective-permute-start(bf16[128,1152]{1,0:T(8,128)(2,1)} %get-tuple-element.52.own.refs_3_), channel_id=1, source_target_pairs={{0,8},{8,0},{1,9},{9,1},{2,10},{10,2},{3,11},{11,3},{4,12},{12,4},... | collective-permute-start | bytes 884744 | tf_op jit(solution)/shard_map/ppermute | solution.py:43
  33.4 14.6 %collective-permute-start.5 = (bf16[128,1152]{1,0:T(8,128)(2,1)}, bf16[128,1152]{1,0:T(8,128)(2,1)S(1)}, u32[]{:S(2)}, u32[]{:S(2)}) collective-permute-start(bf16[128,1152]{1,0:T(8,128)(2,1)} %get-tuple-element.52.own.refs_3_), channel_id=1, source_target_pairs={{0,16},{16,0},{32,48},{48,32},{1,17},{17,1},{33,49},{49,33},{2,18}... | collective-permute-start | bytes 884744 | tf_op jit(solution)/shard_map/ppermute | solution.py:43
  36.7 19.1 %collective-permute-start.4 = (bf16[144,1152]{1,0:T(8,128)(2,1)S(1)}, bf16[144,1152]{1,0:T(8,128)(2,1)S(1)}, u32[]{:S(2)}, u32[]{:S(2)}) collective-permute-start(bf16[144,1152]{1,0:T(8,128)(2,1)S(1)} %collective-permute-done.3.refs_2_), channel_id=1, source_target_pairs={{0,48},{16,32},{32,16},{48,0},{1,49},{17,33},{33,17},{49,1},{2,50}... | collective-permute-start | bytes 995336 | tf_op jit(solution)/shard_map/ppermute | solution.py:43
  39.3 16.5 %collective-permute-start.7 = (bf16[128,1152]{1,0:T(8,128)(2,1)}, bf16[128,1152]{1,0:T(8,128)(2,1)S(1)}, u32[]{:S(2)}, u32[]{:S(2)}) collective-permute-start(bf16[128,1152]{1,0:T(8,128)(2,1)} %get-tuple-element.52.own.refs_3_), channel_id=1, source_target_pairs={{0,64},{64,0},{128,192},{192,128},{1,65},{65,1},{129,193},{193,129... | collective-permute-start | bytes 884744 | tf_op jit(solution)/shard_map/ppermute | solution.py:43
  39.5 16.3 %collective-permute-start.8 = (bf16[128,1152]{1,0:T(8,128)(2,1)}, bf16[128,1152]{1,0:T(8,128)(2,1)S(1)}, u32[]{:S(2)}, u32[]{:S(2)}) collective-permute-start(bf16[128,1152]{1,0:T(8,128)(2,1)} %get-tuple-element.52.own.refs_3_), channel_id=1, source_target_pairs={{0,128},{64,192},{128,0},{192,64},{1,129},{65,193},{129,1},{193,65... | collective-permute-start | bytes 884744 | tf_op jit(solution)/shard_map/ppermute | solution.py:43
  48.0 23.7 %collective-permute-start.9 = (bf16[128,1152]{1,0:T(8,128)(2,1)S(1)}, bf16[128,1152]{1,0:T(8,128)(2,1)S(1)}, u32[]{:S(2)}, u32[]{:S(2)}) collective-permute-start(bf16[128,1152]{1,0:T(8,128)(2,1)S(1)} %collective-permute-done.5.refs_7_), channel_id=1, source_target_pairs={{0,48},{16,32},{32,16},{48,0},{1,49},{17,33},{33,17},{49,1},{2,50}... | collective-permute-start | bytes 884744 | tf_op jit(solution)/shard_map/ppermute | solution.py:43
  61.0 10.8 %collective-permute-start.10 = (bf16[304,128]{1,0:T(8,128)(2,1)}, bf16[304,128]{1,0:T(8,128)(2,1)S(1)}, u32[]{:S(2)}, u32[]{:S(2)}) collective-permute-start(bf16[304,128]{1,0:T(8,128)(2,1)} %get-tuple-element.61), channel_id=1, source_target_pairs={{0,1},{1,2},{2,3},{3,0},{4,5},{5,6},{6,7},{7,4},{8,9},{9,10},{10,1... | collective-permute-start | bytes 233480 | tf_op jit(solution)/shard_map/ppermute | solution.py:423
  62.5 9.3 %collective-permute-start.11 = (bf16[304,128]{1,0:T(8,128)(2,1)}, bf16[304,128]{1,0:T(8,128)(2,1)S(1)}, u32[]{:S(2)}, u32[]{:S(2)}) collective-permute-start(bf16[304,128]{1,0:T(8,128)(2,1)} %get-tuple-element.62), channel_id=1, source_target_pairs={{0,2},{1,3},{2,0},{3,1},{4,6},{5,7},{6,4},{7,5},{8,10},{9,11},{10,... | collective-permute-start | bytes 233480 | tf_op jit(solution)/shard_map/ppermute | solution.py:423
  65.2 6.6 %collective-permute-start.12 = (bf16[304,128]{1,0:T(8,128)(2,1)}, bf16[304,128]{1,0:T(8,128)(2,1)S(1)}, u32[]{:S(2)}, u32[]{:S(2)}) collective-permute-start(bf16[304,128]{1,0:T(8,128)(2,1)} %get-tuple-element.63), channel_id=1, source_target_pairs={{0,3},{1,0},{2,1},{3,2},{4,7},{5,4},{6,5},{7,6},{8,11},{9,8},{10,9... | collective-permute-start | bytes 233480 | tf_op jit(solution)/shard_map/ppermute | solution.py:423
  75.5 5.9 %collective-permute-start.14 = (bf16[288,128]{1,0:T(8,128)(2,1)}, bf16[288,128]{1,0:T(8,128)(2,1)S(1)}, u32[]{:S(2)}, u32[]{:S(2)}) collective-permute-start(bf16[288,128]{1,0:T(8,128)(2,1)} %get-tuple-element.70), channel_id=1, source_target_pairs={{0,1},{1,2},{2,3},{3,0},{4,5},{5,6},{6,7},{7,4},{8,9},{9,10},{10,1... | collective-permute-start | bytes 221192 | tf_op jit(solution)/shard_map/ppermute | solution.py:423
  76.1 6.1 %collective-permute-start.15 = (bf16[288,128]{1,0:T(8,128)(2,1)}, bf16[288,128]{1,0:T(8,128)(2,1)S(1)}, u32[]{:S(2)}, u32[]{:S(2)}) collective-permute-start(bf16[288,128]{1,0:T(8,128)(2,1)} %get-tuple-element.71), channel_id=1, source_target_pairs={{0,2},{1,3},{2,0},{3,1},{4,6},{5,7},{6,4},{7,5},{8,10},{9,11},{10,... | collective-permute-start | bytes 221192 | tf_op jit(solution)/shard_map/ppermute | solution.py:423
  78.5 4.6 %collective-permute-start.16 = (bf16[288,128]{1,0:T(8,128)(2,1)}, bf16[288,128]{1,0:T(8,128)(2,1)S(1)}, u32[]{:S(2)}, u32[]{:S(2)}) collective-permute-start(bf16[288,128]{1,0:T(8,128)(2,1)} %get-tuple-element.72), channel_id=1, source_target_pairs={{0,3},{1,0},{2,1},{3,2},{4,7},{5,4},{6,5},{7,6},{8,11},{9,8},{10,9... | collective-permute-start | bytes 221192 | tf_op jit(solution)/shard_map/ppermute | solution.py:423
  81.3 6.0 %collective-permute-start.13 = (bf16[32,48,128]{2,1,0:T(8,128)(2,1)S(1)}, bf16[32,48,128]{2,1,0:T(8,128)(2,1)S(1)}, u32[]{:S(2)}, u32[]{:S(2)}) collective-permute-start(bf16[32,48,128]{2,1,0:T(8,128)(2,1)S(1)} %get-tuple-element.68), channel_id=1, source_target_pairs={{0,8},{8,0},{1,9},{9,1},{2,10},{10,2},{3,11},{11,3},{4,12},{12,4},... | collective-permute-start | bytes 1179656 | tf_op jit(solution)/shard_map/ppermute | solution.py:43
  87.2 1.8 %collective-permute-start.17 = (bf16[32,48,128]{2,1,0:T(8,128)(2,1)S(1)}, bf16[32,48,128]{2,1,0:T(8,128)(2,1)S(1)}, u32[]{:S(2)}, u32[]{:S(2)}) collective-permute-start(bf16[32,48,128]{2,1,0:T(8,128)(2,1)S(1)} %get-tuple-element.74), channel_id=1, source_target_pairs={{0,8},{8,0},{1,9},{9,1},{2,10},{10,2},{3,11},{11,3},{4,12},{12,4},... | collective-permute-start | bytes 1179656 | tf_op jit(solution)/shard_map/ppermute | solution.py:43
  89.7 8.7 %collective-permute-start.18 = (bf16[8,96,128]{2,1,0:T(8,128)(2,1)S(1)}, bf16[8,96,128]{2,1,0:T(8,128)(2,1)S(1)}, u32[]{:S(2)}, u32[]{:S(2)}) collective-permute-start(bf16[8,96,128]{2,1,0:T(8,128)(2,1)S(1)} %get-tuple-element.76), channel_id=1, source_target_pairs={{0,64},{64,128},{128,192},{192,0},{1,65},{65,129},{129,193},{193,1... | collective-permute-start | bytes 589832 | tf_op jit(solution)/shard_map/ppermute | solution.py:423
  90.5 11.9 %collective-permute-start.19 = (bf16[8,96,128]{2,1,0:T(8,128)(2,1)S(1)}, bf16[8,96,128]{2,1,0:T(8,128)(2,1)S(1)}, u32[]{:S(2)}, u32[]{:S(2)}) collective-permute-start(bf16[8,96,128]{2,1,0:T(8,128)(2,1)S(1)} %get-tuple-element.77), channel_id=1, source_target_pairs={{0,128},{64,192},{128,0},{192,64},{1,129},{65,193},{129,1},{193,65... | collective-permute-start | bytes 589832 | tf_op jit(solution)/shard_map/ppermute | solution.py:423
  93.3 9.4 %collective-permute-start.20 = (bf16[8,96,128]{2,1,0:T(8,128)(2,1)S(1)}, bf16[8,96,128]{2,1,0:T(8,128)(2,1)S(1)}, u32[]{:S(2)}, u32[]{:S(2)}) collective-permute-start(bf16[8,96,128]{2,1,0:T(8,128)(2,1)S(1)} %get-tuple-element.78), channel_id=1, source_target_pairs={{0,192},{64,0},{128,64},{192,128},{1,193},{65,1},{129,65},{193,129... | collective-permute-start | bytes 589832 | tf_op jit(solution)/shard_map/ppermute | solution.py:423
  (14 other events, 156.7 us)
Sparse Core Ops, SparseCore 0:
  10.7 29.5 all-gather.2
  42.2 29.3 all-gather.4

commit v9 on v8

--- a/solution.py
+++ b/solution.py
@@ -22,8 +22,6 @@
 DEPTH = 128
 PIECES = WIDTH // DEPTH
 SLAB = SLOT + 8
-LINE = 4
-FAR = 8
 F32 = jnp.float32
 BF16 = jnp.bfloat16
 
@@ -96,13 +94,16 @@
     )(x, w, keys)
 
 
+def temperature(heat_log):
+    return jnp.exp(jnp.full((1, 1), heat_log[0], F32))
+
+
 def caption_row(block):
     digits = block[ROWS:, :LANES].astype(F32)
     return digits[0:1] * 128.0 + digits[1:2]
 
 
-def add_tiles(with_stats, scal, mine, key_col, pairs, total, sums):
-    heat, shift = scal[0], scal[1]
+def add_tiles(with_stats, heat, shift, mine, key_col, pairs, total, sums):
     for block, key_row in pairs:
         vec = block[:ROWS, :]
         same = key_col == key_row
@@ -138,7 +139,7 @@
     out_ref[ROWS:, :ROWS] = digit.astype(F32).astype(BF16)
 
 
-def early_kernel(first, scal, spot, x, w_hbm, key, *refs):
+def early_kernel(first, heat_log, shift, x, w_hbm, key, *refs):
     refs, (total_ref, unit_ref, len_ref, key_ref, sum_ref, w, sem) = refs[:-7], refs[-7:]
     copy = pltpu.make_async_copy(w_hbm, w, sem)
     copy.start()
@@ -164,7 +165,8 @@
     zero = jnp.zeros((ROWS, ROWS), F32)
     total, sums = add_tiles(
         first,
-        scal,
+        temperature(heat_log),
+        shift[0],
         own[:ROWS, :],
         key_col,
         pairs,
@@ -178,7 +180,7 @@
         norm()
 
 
-def early(first, scal, spot, x, w, keys, blocks):
+def early(first, scal, x, w, keys, blocks):
     shapes = [(ROWS, WIDTH), (ROWS, WIDTH), (ROWS, LANES), (ROWS, ROWS), (3, ROWS, ROWS)]
     outs = [jax.ShapeDtypeStruct(shape, F32) for shape in shapes]
     if first:
@@ -195,12 +197,13 @@
         scratch_shapes=[pltpu.VMEM((WIDTH, WIDTH), BF16), pltpu.SemaphoreType.DMA],
         compiler_params=params(56),
         cost_estimate=cost(4 * 5 * ROWS * ROWS * WIDTH, 8 * 2**20),
-    )(scal, spot, x, w, keys, *blocks)
-
-
-def late_kernel(with_stats, ways, count, spot, scal, own, total_ref, unit, length, key, acc, *refs):
+    )(*scal, x, w, keys, *blocks)
+
+
+def late_kernel(with_stats, ways, count, spot, heat_log, shift, own, *refs):
+    total_ref, unit, length, key, acc, *refs = refs
     blocks, outs, held = refs[:count], refs[count:-1], refs[-1]
-    heat = scal[0]
+    heat = temperature(heat_log)
     if with_stats:
         *outs, rows_ref = outs
         pairs = pair_up(blocks, rows_ref)
@@ -209,7 +212,8 @@
         pairs = [(block, rows[3][0:1])]
     total, sums = add_tiles(
         with_stats,
-        scal,
+        heat,
+        shift[0],
         own[:ROWS, :],
         key[...],
         pairs,
@@ -253,13 +257,13 @@
         shapes.append(jax.ShapeDtypeStruct((len(blocks), 8, LANES), F32))
     return pl.pallas_call(
         functools.partial(late_kernel, with_stats, ways, len(blocks)),
-        in_specs=[SMEM] * 2 + [VMEM] * (6 + len(blocks)),
+        in_specs=[SMEM] * 3 + [VMEM] * (6 + len(blocks)),
         out_specs=[VMEM] * len(shapes),
         out_shape=shapes,
         scratch_shapes=[pltpu.VMEM((2 * ways, COLS, ROWS), BF16)],
         compiler_params=params(56),
         cost_estimate=cost(4 * 2 * ROWS * ROWS * WIDTH, 4 * 2**20),
-    )(spot, scal, own, *partial, *blocks)
+    )(spot, *scal, own, *partial, *blocks)
 
 
 def head_kernel(with_stats, spot, feat, *refs):
@@ -322,51 +326,20 @@
     )(spot, feat, *spreads)
 
 
-def mix_kernel(spot, kept_img, taken_img, kept_txt, taken_txt, mine, *outs):
-    def part(place):
-        span = pl.ds(place * FAR, FAR)
-        img = kept_img[span] + taken_img[span].astype(F32)
-        txt = kept_txt[span] + taken_txt[span].astype(F32)
-        return img, txt
-
-    img, txt = part(spot[2])
-    mine[:, :SLAB, :] = img
-    mine[:, SLAB:, :] = txt
-    for step, out in enumerate(outs):
-        img, txt = part(lax.rem(spot[2] + step + 1, LINE))
-        out[:, :SLAB, :] = img.astype(BF16)
-        out[:, SLAB:, :] = txt.astype(BF16)
-
-
-def mix(spot, *arrays):
-    shape = (FAR, 2 * SLAB, LANES)
+def mix_kernel(kept_img, taken_img, kept_txt, taken_txt, out):
+    out[:, :SLAB, :] = (kept_img[...] + taken_img[...].astype(F32)).astype(BF16)
+    out[:, SLAB:, :] = (kept_txt[...] + taken_txt[...].astype(F32)).astype(BF16)
+
+
+def mix(*arrays):
     return pl.pallas_call(
         mix_kernel,
-        in_specs=[SMEM] + [VMEM] * 4,
-        out_specs=[VMEM] * LINE,
-        out_shape=[jax.ShapeDtypeStruct(shape, F32)]
-        + [jax.ShapeDtypeStruct(shape, BF16)] * (LINE - 1),
+        in_specs=[VMEM] * 4,
+        out_specs=VMEM,
+        out_shape=jax.ShapeDtypeStruct((2 * QUADS, 2 * SLAB, LANES), BF16),
         compiler_params=params(16),
-        cost_estimate=cost(4 * FAR * SLAB * LANES, 2**20),
-    )(spot, *arrays)
-
-
-def fold_kernel(mine, *refs):
-    total = mine[...]
-    for part in refs[:-1]:
-        total += part[...].astype(F32)
-    refs[-1][...] = total.astype(BF16)
-
-
-def fold(mine, parts):
-    return pl.pallas_call(
-        fold_kernel,
-        in_specs=[VMEM] * (1 + len(parts)),
-        out_specs=VMEM,
-        out_shape=jax.ShapeDtypeStruct(mine.shape, BF16),
-        compiler_params=params(16),
-        cost_estimate=cost(4 * FAR * SLAB * LANES, 2**20),
-    )(mine, *parts)
+        cost_estimate=cost(4 * QUADS * SLAB * LANES, 2**20),
+    )(*arrays)
 
 
 def final_kernel(count, parts, out_img, out_txt, stats):
@@ -391,14 +364,14 @@
         out_specs=[VMEM, VMEM, SMEM],
         out_shape=[grad, grad, jax.ShapeDtypeStruct((3,), F32)],
         compiler_params=params(8),
-        cost_estimate=cost(4 * FAR * SLAB * LANES, 2**20),
+        cost_estimate=cost(4 * QUADS * SLAB * LANES, 2**20),
     )(parts)
 
 
 def body(pictures, sentences, keys, picture_weights, sentence_weights, heat_log, shift_value):
     ways = lax.axis_size("dx")
-    spot = jnp.stack([lax.axis_index(axis) for axis in ("dx", "lc", "ly")]).astype(jnp.int32)
-    scal = jnp.stack([jnp.exp(heat_log[0]), shift_value[0]])
+    spot = jnp.stack([lax.axis_index(axis) for axis in ("dx", "lc")]).astype(jnp.int32)
+    scal = (heat_log, shift_value)
     txt = project(sentences[0], sentence_weights, keys)
     txt_a = exchange(txt, "lz", 1)
     txt_y2 = exchange(txt, "ly", 2)
@@ -407,9 +380,9 @@
     img_feat = lax.all_gather(after(pictures[0], txt), "dx", axis=0, tiled=True)
     txt_feat = lax.all_gather(after(sentences[0], txt), "dx", axis=0, tiled=True)
 
-    img, near_rows, *img_part = early(True, scal, spot, pictures[0], picture_weights, keys, [txt, txt_c])
+    img, near_rows, *img_part = early(True, scal, pictures[0], picture_weights, keys, [txt, txt_c])
     txt_b = exchange(after(txt_a, txt_y1, txt_y2), "lz", 3)
-    img_a = exchange(after(img, txt_a), "lz", 1)
+    img_a = exchange(img, "lz", 1)
     img_c = exchange(after(img, txt_a, txt_y1, txt_y2), "lc", 1)
     img_n = after(img, img_c)
     img_y2 = exchange(img_n, "ly", 2)
@@ -433,7 +406,6 @@
     txt_part = early(
         False,
         scal,
-        spot,
         sentences[0],
         sentence_weights,
         keys,
@@ -442,13 +414,12 @@
     last = after(img_b, *img_cols, *txt_part)
     outs = late(False, ways, spot, scal, txt, txt_part, [far_rows, last])
     txt_cols = columns(outs)
-    img_kept, img_given = heads(True, spot, after(img_feat, outs[0]), img_cols)
+    img_kept, img_given = heads(True, spot, after(img_feat, outs[0], txt_feat), img_cols)
     img_taken = exchange(img_given, "lc", 1)
     txt_kept, txt_given = heads(False, spot, txt_feat, txt_cols)
     txt_taken = exchange(txt_given, "lc", 1)
-    mine, *others = mix(spot, img_kept, img_taken, txt_kept, txt_taken)
-    others = [turn(other, "ly", step + 1) for step, other in enumerate(others)]
-    sums = lax.all_to_all(fold(mine, others), ("lz", "dz"), 0, 0, tiled=True)
+    sums = mix(img_kept, img_taken, txt_kept, txt_taken)
+    sums = lax.all_to_all(sums, ("ly", "lz", "dz"), 0, 0, tiled=True)
     grad_img, grad_txt, stats = final(count, sums)
     return grad_img, grad_txt, stats
 

time: 127 us -> 128 us (level)
  blocking collectives: 14.7 us -> 30.5 us
  waiting for transfers between devices: 26.8 us -> 18.3 us
  starting transfers between devices: 35.9 us -> 32 us
    all_to_all x1, blocking collectives: 14.7 us -> 30.5 us  [body(): sums = lax.all_to_all(sums, ('ly', 'lz', 'dz'), 0, 0, tiled=True)]
    ppermute x9 -> x6, waiting for transfers between devices: 10.5 us -> 1.34 us  [turn(): lax.ppermute(array, axis, [(i, (i + step) % size) for i in range(size)])]
    ppermute x9 -> x6, starting transfers between devices: 13.6 us -> 9.7 us  [turn(): lax.ppermute(array, axis, [(i, (i + step) % size) for i in range(size)])]
  transfers between devices with their start and end apart: 23 -> 20, of which waited for: 10 -> 7; matrix products, arithmetic and copies ran while one was open for 1% -> 1% of each run, Pallas kernels for 17% -> 17%
where the time goes in v9:
time: 128 us; the launch traced here: 127 us
  starting transfers between devices  32 us (25%)
  blocking collectives  30.5 us (24%)
  Pallas kernels  26.1 us (20%)
  waiting for transfers between devices  18.3 us (14%)
  between operations  15.6 us (12%)
  local copies, waits for them, and re-layouts  4.24 us (3%)
    all_to_all x1, blocking collectives, body(): sums = lax.all_to_all(sums, ('ly', 'lz', 'dz'), 0, 0, tiled=True)  30.5 us
    ppermute x12, starting transfers between devices, exchange(): lax.ppermute(array, axis, [(i, i ^ apart) for i in range(lax.axis_size(ax...  22.3 us
    ppermute x12, waiting for transfers between devices, exchange(): lax.ppermute(array, axis, [(i, i ^ apart) for i in range(lax.axis_size(ax...  16.2 us
    pallas_call x2, Pallas kernels, early(): pl.pallas_call(functools.partial(early_kernel, first), in_specs=[SMEM, SM...  10.2 us
    ppermute x6, starting transfers between devices, turn(): lax.ppermute(array, axis, [(i, (i + step) % size) for i in range(size)])  9.7 us
    pallas_call x2, Pallas kernels, late(): pl.pallas_call(functools.partial(late_kernel, with_stats, ways, len(block...  7.5 us
    unnamed x30, local copies, waits for them, and re-layouts  4.24 us
    pallas_call x2, Pallas kernels, heads(): pl.pallas_call(functools.partial(head_kernel, with_stats), in_specs=[SMEM...  4.03 us
  transfers between devices with their start and end apart: 20, of which 7 were waited for; matrix products, arithmetic and copies ran while one was open for 1% of the time, Pallas kernels for 17%

profile of v9, /device:TPU:32, one launch (start us, length us, event | category | flops | bytes accessed | tf_op | source)
XLA Modules:
  0.0 127.4 jit_solution(7818484388439509355)
XLA Ops:
  7.2 3.4 %shard_map.94.refs_0_.own = bf16[144,1152]{1,0:T(8,128)(2,1)} custom-call(bf16[128,1152]{1,0:T(8,128)(2,1)} %bitcast.4, bf16[1152,1152]{1,0:T(8,128)(2,1)} %w_hbm.5, s32[1,128]{1,0:T(1,128)} %key.3), custom_call_target="tpu_custom_call" | custom-call | flops 339738624 | bytes 4194304 | tf_op jit(solution)/shard_map/pallas_call | solution.py:81
  11.5 1.7 %collective-permute-start.1 = (bf16[144,1152]{1,0:T(8,128)(2,1)}, bf16[144,1152]{1,0:T(8,128)(2,1)S(1)}, u32[]{:S(2)}, u32[]{:S(2)}) collective-permute-start(bf16[144,1152]{1,0:T(8,128)(2,1)} %shard_map.94.refs_0_.own), channel_id=1, source_target_pairs={{0,64},{64,0},{128,192},{192,128},{1,65},{65,1},{129,193},{193,129... | collective-permute-start | bytes 995336 | tf_op jit(solution)/shard_map/ppermute | solution.py:41
  13.1 2.9 %collective-permute-start.2 = (bf16[144,1152]{1,0:T(8,128)(2,1)}, bf16[144,1152]{1,0:T(8,128)(2,1)S(1)}, u32[]{:S(2)}, u32[]{:S(2)}) collective-permute-start(bf16[144,1152]{1,0:T(8,128)(2,1)} %shard_map.94.refs_0_.own), channel_id=1, source_target_pairs={{0,128},{64,192},{128,0},{192,64},{1,129},{65,193},{129,1},{193,65... | collective-permute-start | bytes 995336 | tf_op jit(solution)/shard_map/ppermute | solution.py:41
  16.0 3.3 %collective-permute-start.3 = (bf16[144,1152]{1,0:T(8,128)(2,1)}, bf16[144,1152]{1,0:T(8,128)(2,1)S(1)}, u32[]{:S(2)}, u32[]{:S(2)}) collective-permute-start(bf16[144,1152]{1,0:T(8,128)(2,1)} %shard_map.94.refs_0_.own), channel_id=1, source_target_pairs={{0,16},{16,0},{32,48},{48,32},{1,17},{17,1},{33,49},{49,33},{2,18}... | collective-permute-start | bytes 995336 | tf_op jit(solution)/shard_map/ppermute | solution.py:41
  21.4 5.2 %shard_map.95 = (bf16[128,1152]{1,0:T(8,128)(2,1)}, f32[2,8,128]{2,1,0:T(8,128)}, f32[128,1152]{1,0:T(8,128)}, f32[128,1152]{1,0:T(8,128)}, f32[128,128]{1,0:T(8...) custom-call(f32[1]{0:T(128)S(6)} %copy.10.heat_log, f32[1]{0:T(128)S(6)} %copy.11.shift, bf16[128,1152]{1,0:T(8,128)(2,1)} %bitcast.8, ...), custom_call_target="tpu_custom_call" | custom-call | flops 377487360 | bytes 8388608 | tf_op jit(solution)/shard_map/pallas_call | solution.py:192
  26.5 4.9 %collective-permute-done.2.refs_6_ = bf16[144,1152]{1,0:T(8,128)(2,1)S(1)} collective-permute-done((bf16[144,1152]{1,0:T(8,128)(2,1)}, bf16[144,1152]{1,0:T(8,128)(2,1)S(1)}, u32[]{:S(2)}, u32[]{:S(2)}) %collective-permute-start.2) | collective-permute-done | bytes 331808 | tf_op jit(solution)/shard_map/ppermute | solution.py:41
  31.5 1.9 %collective-permute-done.3.refs_7_ = bf16[144,1152]{1,0:T(8,128)(2,1)S(1)} collective-permute-done((bf16[144,1152]{1,0:T(8,128)(2,1)}, bf16[144,1152]{1,0:T(8,128)(2,1)S(1)}, u32[]{:S(2)}, u32[]{:S(2)}) %collective-permute-start.3) | collective-permute-done | bytes 331808 | tf_op jit(solution)/shard_map/ppermute | solution.py:41
  33.4 3.4 %collective-permute-start.5 = (bf16[128,1152]{1,0:T(8,128)(2,1)}, bf16[128,1152]{1,0:T(8,128)(2,1)S(1)}, u32[]{:S(2)}, u32[]{:S(2)}) collective-permute-start(bf16[128,1152]{1,0:T(8,128)(2,1)} %get-tuple-element.46.own.refs_3_), channel_id=1, source_target_pairs={{0,16},{16,0},{32,48},{48,32},{1,17},{17,1},{33,49},{49,33},{2,18}... | collective-permute-start | bytes 884744 | tf_op jit(solution)/shard_map/ppermute | solution.py:41
  36.8 2.5 %collective-permute-start.4 = (bf16[144,1152]{1,0:T(8,128)(2,1)S(1)}, bf16[144,1152]{1,0:T(8,128)(2,1)S(1)}, u32[]{:S(2)}, u32[]{:S(2)}) collective-permute-start(bf16[144,1152]{1,0:T(8,128)(2,1)S(1)} %collective-permute-done.3.refs_7_), channel_id=1, source_target_pairs={{0,48},{16,32},{32,16},{48,0},{1,49},{17,33},{33,17},{49,1},{2,50}... | collective-permute-start | bytes 995336 | tf_op jit(solution)/shard_map/ppermute | solution.py:41
  39.5 1.5 %collective-permute-start.8 = (bf16[128,1152]{1,0:T(8,128)(2,1)}, bf16[128,1152]{1,0:T(8,128)(2,1)S(1)}, u32[]{:S(2)}, u32[]{:S(2)}) collective-permute-start(bf16[128,1152]{1,0:T(8,128)(2,1)} %get-tuple-element.46.own.refs_3_), channel_id=1, source_target_pairs={{0,128},{64,192},{128,0},{192,64},{1,129},{65,193},{129,1},{193,65... | collective-permute-start | bytes 884744 | tf_op jit(solution)/shard_map/ppermute | solution.py:41
  41.0 7.0 %collective-permute-done.5.refs_7_ = bf16[128,1152]{1,0:T(8,128)(2,1)S(1)} collective-permute-done((bf16[128,1152]{1,0:T(8,128)(2,1)}, bf16[128,1152]{1,0:T(8,128)(2,1)S(1)}, u32[]{:S(2)}, u32[]{:S(2)}) %collective-permute-start.5) | collective-permute-done | bytes 294944 | tf_op jit(solution)/shard_map/ppermute | solution.py:41
  48.0 6.5 %collective-permute-start.9 = (bf16[128,1152]{1,0:T(8,128)(2,1)S(1)}, bf16[128,1152]{1,0:T(8,128)(2,1)S(1)}, u32[]{:S(2)}, u32[]{:S(2)}) collective-permute-start(bf16[128,1152]{1,0:T(8,128)(2,1)S(1)} %collective-permute-done.5.refs_7_), channel_id=1, source_target_pairs={{0,48},{16,32},{32,16},{48,0},{1,49},{17,33},{33,17},{49,1},{2,50}... | collective-permute-start | bytes 884744 | tf_op jit(solution)/shard_map/ppermute | solution.py:41
  56.6 4.4 %shard_map.96 = (bf16[304,128]{1,0:T(8,128)(2,1)}, bf16[304,128]{1,0:T(8,128)(2,1)}, bf16[304,128]{1,0:T(8,128)(2,1)}, bf16[304,128]{1,0:T(8,128)(2,1)}, f32[4,8,128]{2,1,0:T(8,128)}) custom-call(s32[2]{0:T(128)} %pad_add_fusion.spot, f32[1]{0:T(128)S(6)} %copy.10.heat_log, f32[1]{0:T(128)S(6)} %copy.11.shift, ...), custom_call_target="tpu_custom_call" | custom-call | flops 150994944 | bytes 4194304 | tf_op jit(solution)/shard_map/pallas_call | solution.py:258
  61.0 1.5 %collective-permute-start.10 = (bf16[304,128]{1,0:T(8,128)(2,1)}, bf16[304,128]{1,0:T(8,128)(2,1)S(1)}, u32[]{:S(2)}, u32[]{:S(2)}) collective-permute-start(bf16[304,128]{1,0:T(8,128)(2,1)} %get-tuple-element.55), channel_id=1, source_target_pairs={{0,1},{1,2},{2,3},{3,0},{4,5},{5,6},{6,7},{7,4},{8,9},{9,10},{10,1... | collective-permute-start | bytes 233480 | tf_op jit(solution)/shard_map/ppermute | solution.py:396
  62.5 2.7 %collective-permute-start.11 = (bf16[304,128]{1,0:T(8,128)(2,1)}, bf16[304,128]{1,0:T(8,128)(2,1)S(1)}, u32[]{:S(2)}, u32[]{:S(2)}) collective-permute-start(bf16[304,128]{1,0:T(8,128)(2,1)} %get-tuple-element.56), channel_id=1, source_target_pairs={{0,2},{1,3},{2,0},{3,1},{4,6},{5,7},{6,4},{7,5},{8,10},{9,11},{10,... | collective-permute-start | bytes 233480 | tf_op jit(solution)/shard_map/ppermute | solution.py:396
  65.2 1.4 %collective-permute-start.12 = (bf16[304,128]{1,0:T(8,128)(2,1)}, bf16[304,128]{1,0:T(8,128)(2,1)S(1)}, u32[]{:S(2)}, u32[]{:S(2)}) collective-permute-start(bf16[304,128]{1,0:T(8,128)(2,1)} %get-tuple-element.57), channel_id=1, source_target_pairs={{0,3},{1,0},{2,1},{3,2},{4,7},{5,4},{6,5},{7,6},{8,11},{9,8},{10,9... | collective-permute-start | bytes 233480 | tf_op jit(solution)/shard_map/ppermute | solution.py:396
  66.7 5.0 %shard_map.97 = (f32[128,1152]{1,0:T(8,128)}, f32[128,1152]{1,0:T(8,128)}, f32[128,128]{1,0:T(8,128)}, f32[128,128]{1,0:T(8,128)}, f32[3,128,128]{2,1,0:T(8,128)}) custom-call(f32[1]{0:T(128)S(6)} %copy.10.heat_log, f32[1]{0:T(128)S(6)} %copy.11.shift, bf16[128,1152]{1,0:T(8,128)(2,1)} %bitcast.6, bf16[1152,1152]{1,0:T(8,128)(2,1)} %w_hbm.5, s32[1,128]{1,0:T(1,128)} %key.3, ...), custom_call_target="tpu_custom_call" | custom-call | flops 377487360 | bytes 8388608 | tf_op jit(solution)/shard_map/pallas_call | solution.py:192
  72.5 3.1 %shard_map.98 = (bf16[288,128]{1,0:T(8,128)(2,1)}, bf16[288,128]{1,0:T(8,128)(2,1)}, bf16[288,128]{1,0:T(8,128)(2,1)}, bf16[288,128]{1,0:T(8,128)(2,1)}) custom-call(s32[2]{0:T(128)} %pad_add_fusion.spot, f32[1]{0:T(128)S(6)} %copy.10.heat_log, f32[1]{0:T(128)S(6)} %copy.11.shift, bf16[144,1152]{1,0:T(8,128)(2,1)} %shard_map.94.refs_0_.own, ...), custom_call_target="tpu_custom_call" | custom-call | flops 150994944 | bytes 4194304 | tf_op jit(solution)/shard_map/pallas_call | solution.py:258
  76.1 2.3 %collective-permute-start.15 = (bf16[288,128]{1,0:T(8,128)(2,1)}, bf16[288,128]{1,0:T(8,128)(2,1)S(1)}, u32[]{:S(2)}, u32[]{:S(2)}) collective-permute-start(bf16[288,128]{1,0:T(8,128)(2,1)} %get-tuple-element.65), channel_id=1, source_target_pairs={{0,2},{1,3},{2,0},{3,1},{4,6},{5,7},{6,4},{7,5},{8,10},{9,11},{10,... | collective-permute-start | bytes 221192 | tf_op jit(solution)/shard_map/ppermute | solution.py:396
  79.6 2.0 %shard_map.99 = (f32[32,48,128]{2,1,0:T(8,128)S(1)}, bf16[32,48,128]{2,1,0:T(8,128)(2,1)S(1)}) custom-call(s32[2]{0:T(128)S(1)} %copy-done.4, bf16[512,1152]{1,0:T(8,128)(2,1)S(1)} %copy-done.1, bf16[304,128]{1,0:T(8,128)(2,1)S(1)} %copy-done.2, bf16[304,128]{1,0:T(8,128)(2,1)S(1)} %collective-permute-done.10.refs_1_, ...), custom_call_target="tpu_custom_call" | custom-call | flops 339738624 | bytes 4194304 | tf_op jit(solution)/shard_map/pallas_call | solution.py:318
  83.0 1.3 copy-done
  85.2 2.0 %shard_map.100 = (f32[32,48,128]{2,1,0:T(8,128)S(1)}, bf16[32,48,128]{2,1,0:T(8,128)(2,1)S(1)}) custom-call(s32[2]{0:T(128)S(1)} %copy-done.4, bf16[512,1152]{1,0:T(8,128)(2,1)S(1)} %copy-done, bf16[288,128]{1,0:T(8,128)(2,1)S(1)} %copy-done.3, bf16[288,128]{1,0:T(8,128)(2,1)S(1)} %collective-permute-done.14.refs_1_, ...), custom_call_target="tpu_custom_call" | custom-call | flops 339738624 | bytes 4194304 | tf_op jit(solution)/shard_map/pallas_call | solution.py:318
  87.3 1.7 %collective-permute-done.17.taken_txt = bf16[32,48,128]{2,1,0:T(8,128)(2,1)S(1)} collective-permute-done((bf16[32,48,128]{2,1,0:T(8,128)(2,1)S(1)}, bf16[32,48,128]{2,1,0:T(8,128)(2,1)S(1)}, u32[]{:S(2)}, u32[]{:S(2)}) %collective-permute-start.17) | collective-permute-done | bytes 393248 | tf_op jit(solution)/shard_map/ppermute | solution.py:41
  89.1 30.5 %all_to_all.5.parts = bf16[32,96,128]{2,1,0:T(8,128)(2,1)S(1)} all-to-all(bf16[32,96,128]{2,1,0:T(8,128)(2,1)S(1)} %shard_map.101), channel_id=1, replica_groups=mesh['ly'=4,'lz'=4,'lc'=2,'dz'=2,'dx'=4] {'ly','lz','dz'}, dimensions={0} | all-to-all | bytes 1572864 | tf_op jit(solution)/shard_map/all_to_all | solution.py:422
  (59 shorter events, 9.6 us)
Async XLA Ops:
  7.2 48.7 %all-gather.3.cloned.1.call-start = ((), (), s32[]{:S(2)}) async-start(), calls=%async_computation.1 | async-start | bytes 1474560 | tf_op jit(solution)/shard_map/all_gather | solution.py:380
  10.6 68.9 %all-gather.5.cloned.1.call-start = ((), (), s32[]{:S(2)}) async-start(), calls=%async_computation.2 | async-start | bytes 1474560 | tf_op jit(solution)/shard_map/all_gather | solution.py:381
  11.4 9.2 %collective-permute-start = (bf16[144,1152]{1,0:T(8,128)(2,1)}, bf16[144,1152]{1,0:T(8,128)(2,1)S(1)}, u32[]{:S(2)}, u32[]{:S(2)}) collective-permute-start(bf16[144,1152]{1,0:T(8,128)(2,1)} %shard_map.94.refs_0_.own), channel_id=1, source_target_pairs={{0,8},{8,0},{1,9},{9,1},{2,10},{10,2},{3,11},{11,3},{4,12},{12,4},... | collective-permute-start | bytes 995336 | tf_op jit(solution)/shard_map/ppermute | solution.py:41
  11.5 15.0 %collective-permute-start.1 = (bf16[144,1152]{1,0:T(8,128)(2,1)}, bf16[144,1152]{1,0:T(8,128)(2,1)S(1)}, u32[]{:S(2)}, u32[]{:S(2)}) collective-permute-start(bf16[144,1152]{1,0:T(8,128)(2,1)} %shard_map.94.refs_0_.own), channel_id=1, source_target_pairs={{0,64},{64,0},{128,192},{192,128},{1,65},{65,1},{129,193},{193,129... | collective-permute-start | bytes 995336 | tf_op jit(solution)/shard_map/ppermute | solution.py:41
  13.1 18.3 %collective-permute-start.2 = (bf16[144,1152]{1,0:T(8,128)(2,1)}, bf16[144,1152]{1,0:T(8,128)(2,1)S(1)}, u32[]{:S(2)}, u32[]{:S(2)}) collective-permute-start(bf16[144,1152]{1,0:T(8,128)(2,1)} %shard_map.94.refs_0_.own), channel_id=1, source_target_pairs={{0,128},{64,192},{128,0},{192,64},{1,129},{65,193},{129,1},{193,65... | collective-permute-start | bytes 995336 | tf_op jit(solution)/shard_map/ppermute | solution.py:41
  16.0 17.3 %collective-permute-start.3 = (bf16[144,1152]{1,0:T(8,128)(2,1)}, bf16[144,1152]{1,0:T(8,128)(2,1)S(1)}, u32[]{:S(2)}, u32[]{:S(2)}) collective-permute-start(bf16[144,1152]{1,0:T(8,128)(2,1)} %shard_map.94.refs_0_.own), channel_id=1, source_target_pairs={{0,16},{16,0},{32,48},{48,32},{1,17},{17,1},{33,49},{49,33},{2,18}... | collective-permute-start | bytes 995336 | tf_op jit(solution)/shard_map/ppermute | solution.py:41
  26.5 29.3 %copy-start.5 = (bf16[144,1152]{1,0:T(8,128)(2,1)}, bf16[144,1152]{1,0:T(8,128)(2,1)S(1)}, u32[]{:S(2)}) copy-start(bf16[144,1152]{1,0:T(8,128)(2,1)S(1)} %collective-permute-done.1.refs_5_) | copy-start | bytes 995332
  31.5 24.4 %copy-start.6 = (bf16[144,1152]{1,0:T(8,128)(2,1)}, bf16[144,1152]{1,0:T(8,128)(2,1)S(1)}, u32[]{:S(2)}) copy-start(bf16[144,1152]{1,0:T(8,128)(2,1)S(1)} %collective-permute-done.2.refs_6_) | copy-start | bytes 995332
  33.4 22.5 %copy-start.7 = (bf16[144,1152]{1,0:T(8,128)(2,1)}, bf16[144,1152]{1,0:T(8,128)(2,1)S(1)}, u32[]{:S(2)}) copy-start(bf16[144,1152]{1,0:T(8,128)(2,1)S(1)} %collective-permute-done.3.refs_7_) | copy-start | bytes 995332
  33.4 6.0 %collective-permute-start.6 = (bf16[128,1152]{1,0:T(8,128)(2,1)}, bf16[128,1152]{1,0:T(8,128)(2,1)S(1)}, u32[]{:S(2)}, u32[]{:S(2)}) collective-permute-start(bf16[128,1152]{1,0:T(8,128)(2,1)} %get-tuple-element.46.own.refs_3_), channel_id=1, source_target_pairs={{0,8},{8,0},{1,9},{9,1},{2,10},{10,2},{3,11},{11,3},{4,12},{12,4},... | collective-permute-start | bytes 884744 | tf_op jit(solution)/shard_map/ppermute | solution.py:41
  33.4 14.6 %collective-permute-start.5 = (bf16[128,1152]{1,0:T(8,128)(2,1)}, bf16[128,1152]{1,0:T(8,128)(2,1)S(1)}, u32[]{:S(2)}, u32[]{:S(2)}) collective-permute-start(bf16[128,1152]{1,0:T(8,128)(2,1)} %get-tuple-element.46.own.refs_3_), channel_id=1, source_target_pairs={{0,16},{16,0},{32,48},{48,32},{1,17},{17,1},{33,49},{49,33},{2,18}... | collective-permute-start | bytes 884744 | tf_op jit(solution)/shard_map/ppermute | solution.py:41
  36.8 19.0 %collective-permute-start.4 = (bf16[144,1152]{1,0:T(8,128)(2,1)S(1)}, bf16[144,1152]{1,0:T(8,128)(2,1)S(1)}, u32[]{:S(2)}, u32[]{:S(2)}) collective-permute-start(bf16[144,1152]{1,0:T(8,128)(2,1)S(1)} %collective-permute-done.3.refs_7_), channel_id=1, source_target_pairs={{0,48},{16,32},{32,16},{48,0},{1,49},{17,33},{33,17},{49,1},{2,50}... | collective-permute-start | bytes 995336 | tf_op jit(solution)/shard_map/ppermute | solution.py:41
  39.3 27.3 %copy-start.11 = (bf16[128,1152]{1,0:T(8,128)(2,1)}, bf16[128,1152]{1,0:T(8,128)(2,1)S(1)}, u32[]{:S(2)}) copy-start(bf16[128,1152]{1,0:T(8,128)(2,1)S(1)} %collective-permute-done.6.refs_4_) | copy-start | bytes 884740
  39.4 16.5 %collective-permute-start.7 = (bf16[128,1152]{1,0:T(8,128)(2,1)}, bf16[128,1152]{1,0:T(8,128)(2,1)S(1)}, u32[]{:S(2)}, u32[]{:S(2)}) collective-permute-start(bf16[128,1152]{1,0:T(8,128)(2,1)} %get-tuple-element.46.own.refs_3_), channel_id=1, source_target_pairs={{0,64},{64,0},{128,192},{192,128},{1,65},{65,1},{129,193},{193,129... | collective-permute-start | bytes 884744 | tf_op jit(solution)/shard_map/ppermute | solution.py:41
  39.5 16.3 %collective-permute-start.8 = (bf16[128,1152]{1,0:T(8,128)(2,1)}, bf16[128,1152]{1,0:T(8,128)(2,1)S(1)}, u32[]{:S(2)}, u32[]{:S(2)}) collective-permute-start(bf16[128,1152]{1,0:T(8,128)(2,1)} %get-tuple-element.46.own.refs_3_), channel_id=1, source_target_pairs={{0,128},{64,192},{128,0},{192,64},{1,129},{65,193},{129,1},{193,65... | collective-permute-start | bytes 884744 | tf_op jit(solution)/shard_map/ppermute | solution.py:41
  48.0 23.7 %collective-permute-start.9 = (bf16[128,1152]{1,0:T(8,128)(2,1)S(1)}, bf16[128,1152]{1,0:T(8,128)(2,1)S(1)}, u32[]{:S(2)}, u32[]{:S(2)}) collective-permute-start(bf16[128,1152]{1,0:T(8,128)(2,1)S(1)} %collective-permute-done.5.refs_7_), channel_id=1, source_target_pairs={{0,48},{16,32},{32,16},{48,0},{1,49},{17,33},{33,17},{49,1},{2,50}... | collective-permute-start | bytes 884744 | tf_op jit(solution)/shard_map/ppermute | solution.py:41
  61.0 10.8 %collective-permute-start.10 = (bf16[304,128]{1,0:T(8,128)(2,1)}, bf16[304,128]{1,0:T(8,128)(2,1)S(1)}, u32[]{:S(2)}, u32[]{:S(2)}) collective-permute-start(bf16[304,128]{1,0:T(8,128)(2,1)} %get-tuple-element.55), channel_id=1, source_target_pairs={{0,1},{1,2},{2,3},{3,0},{4,5},{5,6},{6,7},{7,4},{8,9},{9,10},{10,1... | collective-permute-start | bytes 233480 | tf_op jit(solution)/shard_map/ppermute | solution.py:396
  62.5 9.3 %collective-permute-start.11 = (bf16[304,128]{1,0:T(8,128)(2,1)}, bf16[304,128]{1,0:T(8,128)(2,1)S(1)}, u32[]{:S(2)}, u32[]{:S(2)}) collective-permute-start(bf16[304,128]{1,0:T(8,128)(2,1)} %get-tuple-element.56), channel_id=1, source_target_pairs={{0,2},{1,3},{2,0},{3,1},{4,6},{5,7},{6,4},{7,5},{8,10},{9,11},{10,... | collective-permute-start | bytes 233480 | tf_op jit(solution)/shard_map/ppermute | solution.py:396
  65.2 6.6 %collective-permute-start.12 = (bf16[304,128]{1,0:T(8,128)(2,1)}, bf16[304,128]{1,0:T(8,128)(2,1)S(1)}, u32[]{:S(2)}, u32[]{:S(2)}) collective-permute-start(bf16[304,128]{1,0:T(8,128)(2,1)} %get-tuple-element.57), channel_id=1, source_target_pairs={{0,3},{1,0},{2,1},{3,2},{4,7},{5,4},{6,5},{7,6},{8,11},{9,8},{10,9... | collective-permute-start | bytes 233480 | tf_op jit(solution)/shard_map/ppermute | solution.py:396
  75.5 6.2 %collective-permute-start.14 = (bf16[288,128]{1,0:T(8,128)(2,1)}, bf16[288,128]{1,0:T(8,128)(2,1)S(1)}, u32[]{:S(2)}, u32[]{:S(2)}) collective-permute-start(bf16[288,128]{1,0:T(8,128)(2,1)} %get-tuple-element.64), channel_id=1, source_target_pairs={{0,1},{1,2},{2,3},{3,0},{4,5},{5,6},{6,7},{7,4},{8,9},{9,10},{10,1... | collective-permute-start | bytes 221192 | tf_op jit(solution)/shard_map/ppermute | solution.py:396
  76.1 6.1 %collective-permute-start.15 = (bf16[288,128]{1,0:T(8,128)(2,1)}, bf16[288,128]{1,0:T(8,128)(2,1)S(1)}, u32[]{:S(2)}, u32[]{:S(2)}) collective-permute-start(bf16[288,128]{1,0:T(8,128)(2,1)} %get-tuple-element.65), channel_id=1, source_target_pairs={{0,2},{1,3},{2,0},{3,1},{4,6},{5,7},{6,4},{7,5},{8,10},{9,11},{10,... | collective-permute-start | bytes 221192 | tf_op jit(solution)/shard_map/ppermute | solution.py:396
  78.5 4.6 %collective-permute-start.16 = (bf16[288,128]{1,0:T(8,128)(2,1)}, bf16[288,128]{1,0:T(8,128)(2,1)S(1)}, u32[]{:S(2)}, u32[]{:S(2)}) collective-permute-start(bf16[288,128]{1,0:T(8,128)(2,1)} %get-tuple-element.66), channel_id=1, source_target_pairs={{0,3},{1,0},{2,1},{3,2},{4,7},{5,4},{6,5},{7,6},{8,11},{9,8},{10,9... | collective-permute-start | bytes 221192 | tf_op jit(solution)/shard_map/ppermute | solution.py:396
  81.6 5.7 %collective-permute-start.13 = (bf16[32,48,128]{2,1,0:T(8,128)(2,1)S(1)}, bf16[32,48,128]{2,1,0:T(8,128)(2,1)S(1)}, u32[]{:S(2)}, u32[]{:S(2)}) collective-permute-start(bf16[32,48,128]{2,1,0:T(8,128)(2,1)S(1)} %get-tuple-element.63), channel_id=1, source_target_pairs={{0,8},{8,0},{1,9},{9,1},{2,10},{10,2},{3,11},{11,3},{4,12},{12,4},... | collective-permute-start | bytes 1179656 | tf_op jit(solution)/shard_map/ppermute | solution.py:41
  87.2 1.8 %collective-permute-start.17 = (bf16[32,48,128]{2,1,0:T(8,128)(2,1)S(1)}, bf16[32,48,128]{2,1,0:T(8,128)(2,1)S(1)}, u32[]{:S(2)}, u32[]{:S(2)}) collective-permute-start(bf16[32,48,128]{2,1,0:T(8,128)(2,1)S(1)} %get-tuple-element.68), channel_id=1, source_target_pairs={{0,8},{8,0},{1,9},{9,1},{2,10},{10,2},{3,11},{11,3},{4,12},{12,4},... | collective-permute-start | bytes 1179656 | tf_op jit(solution)/shard_map/ppermute | solution.py:41
  (11 other events, 83.3 us)
Sparse Core Ops, SparseCore 0:
  10.7 29.5 all-gather.2
  42.1 29.2 all-gather.4

commit v10 on v1

v10 whole, which is shorter than its diff:
```python
import functools

import jax
import jax.numpy as jnp
from jax import lax
from jax.experimental import pallas as pl
from jax.experimental.pallas import tpu as pltpu
from jax.sharding import Mesh, PartitionSpec as P

EPSILON = 1e-06
LOSS = ("ly", "lz", "lc")
ROWS = 128
WIDTH = 1152
KEY_ROWS = 16
CHUNK = 36
SLOT = 40
COLS = 144
LANES = 128
TAIL = COLS - LANES
QUADS = 16
STATS = 112
DEPTH = 128
PIECES = WIDTH // DEPTH
SLAB = SLOT + 8
TEXT = ROWS + KEY_ROWS
SPREAD = 2 * COLS + KEY_ROWS
F32 = jnp.float32
BF16 = jnp.bfloat16

VMEM = pl.BlockSpec(memory_space=pltpu.VMEM)
SMEM = pl.BlockSpec(memory_space=pltpu.SMEM)
HBM = pl.BlockSpec(memory_space=pltpu.HBM)


def params(megabytes):
    return pltpu.CompilerParams(vmem_limit_bytes=megabytes * 2**20)


def cost(flops, moved):
    return pl.CostEstimate(flops=flops, bytes_accessed=moved, transcendentals=0)


def exchange(array, axis, apart):
    return lax.ppermute(array, axis, [(i, i ^ apart) for i in range(lax.axis_size(axis))])


def after(array, *others):
    return lax.optimization_barrier((array, *others))[0]


def nt(a, b):
    return lax.dot_general(a, b, (((1,), (1,)), ((), ())), preferred_element_type=F32)


def mm(a, b):
    return jnp.dot(a, b, preferred_element_type=F32)


def project_kernel(xs_hbm, xt_hbm, ws_hbm, wt_hbm, key_hbm, img, txt, both, x, w, key, sems):
    copies = [pltpu.make_async_copy(key_hbm, key, sems.at[0])]
    for t, (x_hbm, w_hbm) in enumerate(((xt_hbm, wt_hbm), (xs_hbm, ws_hbm))):
        base = 1 + t * (1 + PIECES)
        copies.append(pltpu.make_async_copy(x_hbm, x.at[t], sems.at[base]))
        for k in range(PIECES):
            span = pl.ds(k * DEPTH, DEPTH)
            copies.append(
                pltpu.make_async_copy(w_hbm.at[span], w.at[t, span], sems.at[base + 1 + k])
            )
    for copy in copies:
        copy.start()

    def unit(t):
        base = 1 + t * (1 + PIECES)
        copies[base].wait()
        u = jnp.zeros((ROWS, WIDTH), F32)
        for k in range(PIECES):
            copies[base + 1 + k].wait()
            span = slice(k * DEPTH, (k + 1) * DEPTH)
            u += mm(x[t, :, span], w[t, span])
        return (u / lengths(u)).astype(BF16)

    vec = unit(0)
    copies[0].wait()
    digit = jnp.broadcast_to(key[...], (KEY_ROWS, ROWS))
    row = lax.broadcasted_iota(jnp.int32, (KEY_ROWS, ROWS), 0)
    digit = jnp.where(row == 0, digit >> 7, jnp.where(row == 1, digit & 127, 0))
    for out in (txt, both):
        out[:ROWS, :] = vec
        out[ROWS:TEXT, :] = jnp.zeros((KEY_ROWS, WIDTH), BF16)
        out[ROWS:TEXT, :ROWS] = digit.astype(F32).astype(BF16)
    vec = unit(1)
    img[...] = vec
    both[TEXT:, :] = vec


def project(pictures, sentences, picture_weights, sentence_weights, keys):
    return pl.pallas_call(
        project_kernel,
        in_specs=[HBM] * 5,
        out_specs=[VMEM] * 3,
        out_shape=[
            jax.ShapeDtypeStruct((rows, WIDTH), BF16) for rows in (ROWS, TEXT, TEXT + ROWS)
        ],
        scratch_shapes=[
            pltpu.VMEM((2, ROWS, WIDTH), BF16),
            pltpu.VMEM((2, WIDTH, WIDTH), BF16),
            pltpu.VMEM((1, ROWS), jnp.int32),
            pltpu.SemaphoreType.DMA((1 + 2 * (1 + PIECES),)),
        ],
        compiler_params=params(56),
        cost_estimate=cost(4 * ROWS * WIDTH * WIDTH, 8 * 2**20),
    )(pictures, sentences, picture_weights, sentence_weights, keys)


def lengths(u):
    return jnp.sqrt(jnp.sum(u * u, axis=1, keepdims=True) + EPSILON)


def temperature(heat_log):
    return jnp.exp(jnp.full((1, 1), heat_log[0], F32))


def caption_row(block):
    digits = block[ROWS:TEXT, :LANES].astype(F32)
    return digits[0:1] * 128.0 + digits[1:2]


def add_tiles(with_stats, heat, shift, mine, key_col, pairs, total, sums):
    for block, key_row in pairs:
        vec = block[...]
        same = key_col == key_row
        sim = nt(mine, vec)
        logits = heat * sim + shift
        z = jnp.where(same, -logits, logits)
        t = jnp.exp(-jnp.abs(z))
        q = 1.0 / (1.0 + t)
        sig = jnp.where(z >= 0, q, t * q)
        g = jnp.where(same, -sig, sig) * (1.0 / ROWS)
        total += mm(g.astype(BF16), vec)
        if with_stats:
            new = (jnp.maximum(z, 0.0) + jnp.log1p(t), g * sim, g)
            sums = [old + add for old, add in zip(sums, new)]
    return total, sums


def early_kernel(heat_log, shift, xs, xt, ws_hbm, wt_hbm, key, *refs):
    za_txt, za_img, img, txt, core, y1, y2, *refs = refs
    total_img, unit_img, len_img, total_txt, unit_txt, len_txt, key_ref, sum_ref, w, sems = refs
    copies = [
        pltpu.make_async_copy(ws_hbm, w.at[0], sems.at[0]),
        pltpu.make_async_copy(wt_hbm, w.at[1], sems.at[1]),
    ]
    for copy in copies:
        copy.start()
    heat = temperature(heat_log)
    key_col = jnp.broadcast_to(key[...].astype(F32), (ROWS, ROWS)).T
    key_ref[...] = key_col
    rows = [caption_row(block) for block in (txt, core, y1, y2, za_txt)]
    texts = [block.at[:ROWS] for block in (txt, core, y1, y2, za_txt)]
    images = [img] + [block.at[TEXT:] for block in (core, y1, y2)] + [za_img]
    zero = jnp.zeros((ROWS, ROWS), F32)
    none = jnp.zeros((ROWS, WIDTH), F32)
    total, sums = add_tiles(
        True, heat, shift[0], img[...], key_col, zip(texts, rows), none, [zero] * 3
    )
    total_img[...] = total
    for k in range(3):
        sum_ref[k] = sums[k]
    total, _ = add_tiles(
        False, heat, shift[0], txt[:ROWS, :], key_col, zip(images, rows), none, [zero] * 3
    )
    total_txt[...] = total
    for t, (x, unit, length) in enumerate(((xs, unit_img, len_img), (xt, unit_txt, len_txt))):
        copies[t].wait()
        u = mm(x[...], w[t])
        r = lengths(u)
        unit[...] = u / r
        length[...] = jnp.broadcast_to(r, length.shape)


def early(scal, features, weights, keys, *blocks):
    tower = [(ROWS, WIDTH), (ROWS, WIDTH), (ROWS, LANES)]
    shapes = tower + tower + [(ROWS, ROWS), (3, ROWS, ROWS)]
    return pl.pallas_call(
        early_kernel,
        in_specs=[SMEM] * 2 + [VMEM] * 2 + [HBM] * 2 + [VMEM] * (1 + len(blocks)),
        out_specs=[VMEM] * len(shapes),
        out_shape=[jax.ShapeDtypeStruct(shape, F32) for shape in shapes],
        scratch_shapes=[pltpu.VMEM((2, WIDTH, WIDTH), BF16), pltpu.SemaphoreType.DMA((2,))],
        compiler_params=params(56),
        cost_estimate=cost(4 * 10 * ROWS * ROWS * WIDTH, 8 * 2**20),
    )(*scal, *features, *weights, keys, *blocks)


def directions(total, unit, length):
    u = unit[...]
    inner = jnp.sum(u * total, axis=1, keepdims=True)
    return ((total - u * inner) / length[:, :1]).T.astype(BF16)


def late_image_kernel(heat_log, shift, own, total_ref, unit, length, key, acc, block, *outs):
    held, parts_ref, row_ref = outs
    heat = temperature(heat_log)
    key_row = caption_row(block)
    row_ref[...] = jnp.broadcast_to(key_row, (8, LANES))
    total, sums = add_tiles(
        True,
        heat,
        shift[0],
        own[...],
        key[...],
        [(block.at[:ROWS], key_row)],
        total_ref[...],
        [acc[k] for k in range(3)],
    )
    held[...] = directions(total * heat, unit, length).reshape(held.shape)

    def full(x):
        return jnp.sum(jnp.sum(x, axis=1, keepdims=True), axis=0, keepdims=True)

    lane = lax.broadcasted_iota(jnp.int32, (KEY_ROWS, LANES), 1)
    row = lax.broadcasted_iota(jnp.int32, (KEY_ROWS, LANES), 0)
    kind = lane % 3
    value = jnp.where(
        kind == 0,
        full(sums[0]) * (1.0 / ROWS),
        jnp.where(kind == 1, full(sums[1]) * heat, full(sums[2])),
    )
    value = jnp.where((row == 0) & (lane < 9), value, 0.0)
    high = value.astype(BF16).astype(F32)
    middle = (value - high).astype(BF16).astype(F32)
    low = value - high - middle
    parts_ref[...] = jnp.where(lane < 3, high, jnp.where(lane < 6, middle, low)).astype(BF16)


def late_image(ways, scal, *arrays):
    return pl.pallas_call(
        late_image_kernel,
        in_specs=[SMEM] * 2 + [VMEM] * len(arrays),
        out_specs=[VMEM] * 3,
        out_shape=[
            jax.ShapeDtypeStruct((2 * ways, COLS, ROWS), BF16),
            jax.ShapeDtypeStruct((KEY_ROWS, LANES), BF16),
            jax.ShapeDtypeStruct((8, LANES), F32),
        ],
        compiler_params=params(56),
        cost_estimate=cost(4 * ROWS * ROWS * WIDTH, 4 * 2**20),
    )(*scal, *arrays)


def late_text_kernel(ways, spot, heat_log, shift, own, total_ref, unit, length, key, *refs):
    block, row, held_img, parts, *outs, held = refs
    heat = temperature(heat_log)
    pairs = [(block, row[0:1])]
    zero = jnp.zeros((ROWS, ROWS), F32)
    total, _ = add_tiles(
        False, heat, shift[0], own[:ROWS, :], key[...], pairs, total_ref[...], [zero] * 3
    )
    held[...] = directions(total * heat, unit, length).reshape(held.shape)
    for step, out in enumerate(outs):
        w = lax.rem(spot[0] + step, ways)
        for h in range(2):
            out[h * COLS : (h + 1) * COLS, :] = held_img[h * ways + w]
            out[SPREAD + h * COLS : SPREAD + (h + 1) * COLS, :] = held[h * ways + w]
        out[2 * COLS : SPREAD, :] = parts[...]


def late_text(ways, spot, scal, *arrays):
    return pl.pallas_call(
        functools.partial(late_text_kernel, ways),
        in_specs=[SMEM] * 3 + [VMEM] * len(arrays),
        out_specs=[VMEM] * ways,
        out_shape=[jax.ShapeDtypeStruct((SPREAD + 2 * COLS, ROWS), BF16)] * ways,
        scratch_shapes=[pltpu.VMEM((2 * ways, COLS, ROWS), BF16)],
        compiler_params=params(56),
        cost_estimate=cost(4 * ROWS * ROWS * WIDTH, 4 * 2**20),
    )(spot, *scal, *arrays)


def head_kernel(spot, feat_img, feat_txt, *refs):
    spreads, (kept, given, held) = refs[:-3], refs[-3:]
    ways = len(spreads)
    parts = jnp.zeros((KEY_ROWS, LANES), F32)
    for spread in spreads:
        parts += spread[2 * COLS : SPREAD, :].astype(F32)
    lane = lax.broadcasted_iota(jnp.int32, (8, LANES), 1)
    row = lax.broadcasted_iota(jnp.int32, (8, LANES), 0)
    place = lane - STATS
    summed = jnp.zeros((8, LANES), F32)
    for k in range(3):
        number = jnp.sum(
            jnp.where((lane[:1] % 3 == k) & (lane[:1] < 9), parts[0:1], 0.0),
            axis=1,
            keepdims=True,
        )
        summed = jnp.where(place % 3 == k, number, summed)
    value = jnp.where((row == spot[1]) & (place >= 0) & (place < 9), summed, 0.0)
    high = value.astype(BF16).astype(F32)
    middle = (value - high).astype(BF16).astype(F32)
    low = value - high - middle
    spare = jnp.where(place < 3, high, jnp.where(place < 6, middle, low))
    for t, feat in enumerate((feat_img, feat_txt)):
        total = jnp.zeros((2 * COLS, WIDTH), F32)
        for step, spread in enumerate(spreads):
            source = lax.rem(spot[0] + ways - step, ways)
            rows = feat[pl.ds(pl.multiple_of(source * ROWS, ROWS), ROWS), :]
            total += mm(spread[t * SPREAD : t * SPREAD + 2 * COLS, :], rows)
        top = t * SLAB
        for h in range(2):
            main = total[h * COLS : h * COLS + LANES, :].T
            rest = total[h * COLS + LANES : (h + 1) * COLS, :]
            for m in range(QUADS):
                for side in range(2):
                    start = (2 * m + side) * CHUNK
                    target = held.at[side, 2 * m + h]
                    target[top : top + CHUNK, :] = main[start : start + CHUNK]
                    target[top + CHUNK : top + SLOT, :] = jnp.zeros((SLOT - CHUNK, LANES), F32)
                    target[top + SLOT : top + SLAB, :] = spare * (1 - t)
                    for k in range(2):
                        target[top + SLOT : top + SLAB, 64 * k : 64 * k + CHUNK] = rest[
                            8 * k : 8 * k + 8, start : start + CHUNK
                        ]
    kept[...] = held[spot[1]]
    given[...] = held[1 - spot[1]].astype(BF16)


def heads(spot, feat_img, feat_txt, spreads):
    shape = (2 * QUADS, 2 * SLAB, LANES)
    return pl.pallas_call(
        head_kernel,
        in_specs=[SMEM] + [VMEM] * (2 + len(spreads)),
        out_specs=[VMEM, VMEM],
        out_shape=[jax.ShapeDtypeStruct(shape, F32), jax.ShapeDtypeStruct(shape, BF16)],
        scratch_shapes=[pltpu.VMEM((2, *shape), F32)],
        compiler_params=params(24),
        cost_estimate=cost(16 * ROWS * 2 * COLS * WIDTH, 4 * 2**20),
    )(spot, feat_img, feat_txt, *spreads)


def final_kernel(count, parts, out_img, out_txt, stats):
    both = jnp.sum(parts[...].astype(F32), axis=0)
    for out, total in ((out_img, both[:SLAB]), (out_txt, both[SLAB:])):
        out[:, :LANES] = total[:CHUNK]
        rest = total[SLOT:, :].T
        out[:, LANES : LANES + 8] = rest[:CHUNK]
        out[:, LANES + 8 :] = rest[64 : 64 + CHUNK]
    place = lax.broadcasted_iota(jnp.int32, (1, LANES), 1) - STATS
    row = both[SLOT : SLOT + 1] + both[SLOT + 1 : SLOT + 2]
    for k in range(3):
        chosen = jnp.where((place % 3 == k) & (place >= 0) & (place < 9), row, 0.0)
        stats[k] = jnp.sum(chosen) * (1.0 / count)


def final(count, parts):
    grad = jax.ShapeDtypeStruct((CHUNK, COLS), F32)
    return pl.pallas_call(
        functools.partial(final_kernel, count),
        in_specs=[VMEM],
        out_specs=[VMEM, VMEM, SMEM],
        out_shape=[grad, grad, jax.ShapeDtypeStruct((3,), F32)],
        compiler_params=params(8),
        cost_estimate=cost(4 * QUADS * SLAB * LANES, 2**20),
    )(parts)


def body(pictures, sentences, keys, picture_weights, sentence_weights, heat_log, shift_value):
    ways = lax.axis_size("dx")
    spot = jnp.stack([lax.axis_index(axis) for axis in ("dx", "lc")]).astype(jnp.int32)
    scal = (heat_log, shift_value)
    features = (pictures[0], sentences[0])
    weights = (picture_weights, sentence_weights)
    img, txt, both = project(*features, *weights, keys)
    za_txt = exchange(txt, "lz", 1)
    za_img = exchange(img, "lz", 1)
    y1 = exchange(both, "ly", 1)
    y2 = exchange(both, "ly", 2)
    core = exchange(both, "lc", 1)
    zb_txt = exchange(za_txt, "lz", 3)
    zb_img = exchange(za_img, "lz", 3)
    img_feat = lax.all_gather(after(pictures[0], img), "dx", axis=0, tiled=True)
    txt_feat = lax.all_gather(after(sentences[0], img), "dx", axis=0, tiled=True)

    def turn(array, step):
        return lax.ppermute(array, "dx", [(i, (i + step) % ways) for i in range(ways)])

    first = early(scal, features, weights, keys, za_txt, za_img, img, txt, core, y1, y2)
    key_col, acc = first[6:]
    held, parts, row = late_image(ways, scal, img, *first[:3], key_col, acc, zb_txt)
    outs = late_text(
        ways, spot, scal, txt, *first[3:6], key_col, after(zb_img, held), row, held, parts
    )
    cols = [outs[0]] + [turn(out, step) for step, out in enumerate(outs) if step]
    kept, given = heads(spot, after(img_feat, txt_feat), txt_feat, cols)
    taken = exchange(given, "lc", 1)
    sums = (kept + taken.astype(F32)).astype(BF16)
    sums = lax.all_to_all(sums, ("ly", "lz", "dz"), 0, 0, tiled=True)
    grad_img, grad_txt, stats = final(2 * QUADS * lax.axis_size("dz") * ways, sums)
    return grad_img, grad_txt, stats


def solution(mesh):
    split = Mesh(mesh.devices.reshape(4, 4, 2, 2, 4), ("ly", "lz", "lc", "dz", "dx"))
    dp = ("dz", "dx")
    return jax.shard_map(
        body,
        mesh=split,
        in_specs=(P(dp, LOSS, None), P(dp, LOSS, None), P(dp, LOSS), P(), P(), P(), P()),
        out_specs=(P(LOSS, dp), P(LOSS, dp), P()),
        check_vma=False,
    )
```

time: 193 us -> 134 us (0.69)
  matrix products: 28 us -> 0 us
  waiting for transfers between devices: 60.1 us -> 33.3 us
  Pallas kernels: 0 us -> 23.6 us
  other arithmetic: 14.4 us -> 0.86 us
  local copies, waits for them, and re-layouts: 12.9 us -> 6.78 us
  starting transfers between devices: 32 us -> 26 us
    dot_general x17 -> x0, matrix products: 28 us -> none  [the longest x12 17 us: project_rows(): projected = jnp.dot(features, weight, preferred_element_type=jnp.float32)]
    ppermute x11 -> x8, waiting for transfers between devices: 52.3 us -> 28.1 us  [exchange(): lax.ppermute(array, axis, [(i, i ^ apart) for i in range(lax.axis_size(ax...]
    pallas_call x0 -> x6, Pallas kernels: none -> 23.6 us  [the longest x1 7.75 us: early(): pl.pallas_call(early_kernel, in_specs=[SMEM] * 2 + [VMEM] * 2 + [HBM] * 2...]
    all_to_all x1 -> x0, waiting for transfers between devices: 7.76 us -> none  [body(): spread = lax.all_to_all(spread, 'dp', 0, 0, tiled=True)]
    ppermute x11 -> x8, starting transfers between devices: 26.5 us -> 20.2 us  [exchange(): lax.ppermute(array, axis, [(i, i ^ apart) for i in range(lax.axis_size(ax...]
    ppermute x0 -> x3, starting transfers between devices: none -> 5.67 us  [turn(): lax.ppermute(array, 'dx', [(i, (i + step) % ways) for i in range(ways)])]
    all_to_all x1 -> x0, starting transfers between devices: 5.47 us -> none  [body(): spread = lax.all_to_all(spread, 'dp', 0, 0, tiled=True)]
    concatenate x7 -> x0, other arithmetic: 4.59 us -> none  [the longest x1 2.13 us: body(): own = jnp.concatenate([pictures[0], sentences[0]], axis=0)]
  transfers between devices with their start and end apart: 13 -> 13, of which waited for: 7 -> 6; matrix products, arithmetic and copies ran while one was open for 18% -> 0% of each run, Pallas kernels for 0% -> 10%
where the time goes in v10:
time: 134 us
  waiting for transfers between devices  33.3 us (25%)
  blocking collectives  27.7 us (21%)
  starting transfers between devices  26 us (19%)
  Pallas kernels  23.6 us (18%)
  between operations  15.5 us (12%)
  local copies, waits for them, and re-layouts  6.78 us (5%)
    ppermute x8, waiting for transfers between devices, exchange(): lax.ppermute(array, axis, [(i, i ^ apart) for i in range(lax.axis_size(ax...  28.1 us
    all_to_all x1, blocking collectives, body(): sums = lax.all_to_all(sums, ('ly', 'lz', 'dz'), 0, 0, tiled=True)  27.7 us
    ppermute x8, starting transfers between devices, exchange(): lax.ppermute(array, axis, [(i, i ^ apart) for i in range(lax.axis_size(ax...  20.2 us
    pallas_call x1, Pallas kernels, early(): pl.pallas_call(early_kernel, in_specs=[SMEM] * 2 + [VMEM] * 2 + [HBM] * 2...  7.75 us
    unnamed x22, local copies, waits for them, and re-layouts  6.78 us
    pallas_call x1, Pallas kernels, project(): pl.pallas_call(project_kernel, in_specs=[HBM] * 5, out_specs=[VMEM] * 3,...  5.81 us
    ppermute x3, starting transfers between devices, turn(): lax.ppermute(array, 'dx', [(i, (i + step) % ways) for i in range(ways)])  5.67 us
    ppermute x3, waiting for transfers between devices, turn(): lax.ppermute(array, 'dx', [(i, (i + step) % ways) for i in range(ways)])  4.46 us
  transfers between devices with their start and end apart: 13, of which 6 were waited for; matrix products, arithmetic and copies ran while one was open for 0% of the time, Pallas kernels for 10%

profile of v10, /device:TPU:32, one launch (start us, length us, event | category | flops | bytes accessed | tf_op | source)
XLA Modules:
  0.0 133.6 jit_solution(5442158817745368985)
XLA Ops:
  7.2 5.8 %shard_map.94 = (bf16[128,1152]{1,0:T(8,128)(2,1)}, bf16[144,1152]{1,0:T(8,128)(2,1)}, bf16[272,1152]{1,0:T(8,128)(2,1)}) custom-call(bf16[128,1152]{1,0:T(8,128)(2,1)} %bitcast.7, bf16[128,1152]{1,0:T(8,128)(2,1)} %bitcast.4, bf16[1152,1152]{1,0:T(8,128)(2,1)} %ws_hbm.3, bf16[1152,1152]{1,0:T(8,128)(2,1)} %wt_hbm.3, s32[1,128]{1,0:T(1,128)} %key.1), custom_call_target="tpu_custom_call" | custom-call | flops 679477248 | bytes 8388608 | tf_op jit(solution)/shard_map/pallas_call | solution.py:97
  13.9 1.7 %collective-permute-start.3 = (bf16[272,1152]{1,0:T(8,128)(2,1)}, bf16[272,1152]{1,0:T(8,128)(2,1)S(1)}, u32[]{:S(2)}, u32[]{:S(2)}) collective-permute-start(bf16[272,1152]{1,0:T(8,128)(2,1)} %get-tuple-element.32), channel_id=1, source_target_pairs={{0,64},{64,0},{128,192},{192,128},{1,65},{65,1},{129,193},{193,129... | collective-permute-start | bytes 1880072 | tf_op jit(solution)/shard_map/ppermute | solution.py:44
  15.6 2.9 %collective-permute-start.4 = (bf16[272,1152]{1,0:T(8,128)(2,1)}, bf16[272,1152]{1,0:T(8,128)(2,1)S(1)}, u32[]{:S(2)}, u32[]{:S(2)}) collective-permute-start(bf16[272,1152]{1,0:T(8,128)(2,1)} %get-tuple-element.32), channel_id=1, source_target_pairs={{0,128},{64,192},{128,0},{192,64},{1,129},{65,193},{129,1},{193,65... | collective-permute-start | bytes 1880072 | tf_op jit(solution)/shard_map/ppermute | solution.py:44
  18.5 3.3 %collective-permute-start = (bf16[144,1152]{1,0:T(8,128)(2,1)}, bf16[144,1152]{1,0:T(8,128)(2,1)S(1)}, u32[]{:S(2)}, u32[]{:S(2)}) collective-permute-start(bf16[144,1152]{1,0:T(8,128)(2,1)} %get-tuple-element.31.refs_3_.own), channel_id=1, source_target_pairs={{0,16},{16,0},{32,48},{48,32},{1,17},{17,1},{33,49},{49,33},{2,18}... | collective-permute-start | bytes 995336 | tf_op jit(solution)/shard_map/ppermute | solution.py:44
  21.8 20.4 %collective-permute-done.refs_0_ = bf16[144,1152]{1,0:T(8,128)(2,1)S(1)} collective-permute-done((bf16[144,1152]{1,0:T(8,128)(2,1)}, bf16[144,1152]{1,0:T(8,128)(2,1)S(1)}, u32[]{:S(2)}, u32[]{:S(2)}) %collective-permute-start) | collective-permute-done | bytes 331808 | tf_op jit(solution)/shard_map/ppermute | solution.py:44
  42.2 6.4 %collective-permute-start.6 = (bf16[144,1152]{1,0:T(8,128)(2,1)S(1)}, bf16[144,1152]{1,0:T(8,128)(2,1)S(1)}, u32[]{:S(2)}, u32[]{:S(2)}) collective-permute-start(bf16[144,1152]{1,0:T(8,128)(2,1)S(1)} %collective-permute-done.refs_0_), channel_id=1, source_target_pairs={{0,48},{16,32},{32,16},{48,0},{1,49},{17,33},{33,17},{49,1},{2,50}... | collective-permute-start | bytes 995336 | tf_op jit(solution)/shard_map/ppermute | solution.py:44
  48.6 5.8 %collective-permute-start.5 = (bf16[128,1152]{1,0:T(8,128)(2,1)S(1)}, bf16[128,1152]{1,0:T(8,128)(2,1)S(1)}, u32[]{:S(2)}, u32[]{:S(2)}) collective-permute-start(bf16[128,1152]{1,0:T(8,128)(2,1)S(1)} %collective-permute-done.1.refs_1_), channel_id=1, source_target_pairs={{0,48},{16,32},{32,16},{48,0},{1,49},{17,33},{33,17},{49,1},{2,50}... | collective-permute-start | bytes 884744 | tf_op jit(solution)/shard_map/ppermute | solution.py:44
  58.3 7.8 %shard_map.95 = (f32[128,1152]{1,0:T(8,128)}, f32[128,1152]{1,0:T(8,128)}, f32[128,128]{1,0:T(8,128)}, f32[128,1152]{1,0:T(8,128)}, f32[128,1152]{1,0:T(8,128)},...) custom-call(f32[1]{0:T(128)S(6)} %copy.10.heat_log, f32[1]{0:T(128)S(6)} %copy.11.shift, ...), custom_call_target="tpu_custom_call" | custom-call | flops 754974720 | bytes 8388608 | tf_op jit(solution)/shard_map/pallas_call | solution.py:184
  66.0 4.3 %collective-permute-done.6.block = bf16[144,1152]{1,0:T(8,128)(2,1)S(1)} collective-permute-done((bf16[144,1152]{1,0:T(8,128)(2,1)S(1)}, bf16[144,1152]{1,0:T(8,128)(2,1)S(1)}, u32[]{:S(2)}, u32[]{:S(2)}) %collective-permute-start.6) | collective-permute-done | bytes 331808 | tf_op jit(solution)/shard_map/ppermute | solution.py:44
  71.1 3.0 %shard_map.96 = (bf16[8,144,128]{2,1,0:T(8,128)(2,1)}, bf16[16,128]{1,0:T(8,128)(2,1)}, f32[8,128]{1,0:T(8,128)}) custom-call(f32[1]{0:T(128)S(6)} %copy.10.heat_log, f32[1]{0:T(128)S(6)} %copy.11.shift, bf16[128,1152]{1,0:T(8,128)(2,1)} %get-tuple-element.27.refs_2_.own, f32[128,1152]{1,0:T(8,128)} %get-tuple-element.37.total_ref, ...), custom_call_target="tpu_custom_call" | custom-call | flops 75497472 | bytes 4194304 | tf_op jit(solution)/shard_map/pallas_call | solution.py:237
  74.1 1.1 collective-permute-done.5.refs_0_
  75.9 3.2 %shard_map.97 = (bf16[592,128]{1,0:T(8,128)(2,1)}, bf16[592,128]{1,0:T(8,128)(2,1)}, bf16[592,128]{1,0:T(8,128)(2,1)}, bf16[592,128]{1,0:T(8,128)(2,1)}) custom-call(s32[2]{0:T(128)} %pad_add_fusion.spot, f32[1]{0:T(128)S(6)} %copy.10.heat_log, f32[1]{0:T(128)S(6)} %copy.11.shift, bf16[144,1152]{1,0:T(8,128)(2,1)} %get-tuple-element.31.refs_3_.own, ...), custom_call_target="tpu_custom_call" | custom-call | flops 75497472 | bytes 4194304 | tf_op jit(solution)/shard_map/pallas_call | solution.py:269
  79.1 1.5 %collective-permute-start.7 = (bf16[592,128]{1,0:T(8,128)(2,1)}, bf16[592,128]{1,0:T(8,128)(2,1)S(1)}, u32[]{:S(2)}, u32[]{:S(2)}) collective-permute-start(bf16[592,128]{1,0:T(8,128)(2,1)} %get-tuple-element.46), channel_id=1, source_target_pairs={{0,1},{1,2},{2,3},{3,0},{4,5},{5,6},{6,7},{7,4},{8,9},{9,10},{10,1... | collective-permute-start | bytes 454664 | tf_op jit(solution)/shard_map/ppermute | solution.py:384
  80.6 2.7 %collective-permute-start.8 = (bf16[592,128]{1,0:T(8,128)(2,1)}, bf16[592,128]{1,0:T(8,128)(2,1)S(1)}, u32[]{:S(2)}, u32[]{:S(2)}) collective-permute-start(bf16[592,128]{1,0:T(8,128)(2,1)} %get-tuple-element.47), channel_id=1, source_target_pairs={{0,2},{1,3},{2,0},{3,1},{4,6},{5,7},{6,4},{7,5},{8,10},{9,11},{10,... | collective-permute-start | bytes 454664 | tf_op jit(solution)/shard_map/ppermute | solution.py:384
  83.3 1.4 %collective-permute-start.9 = (bf16[592,128]{1,0:T(8,128)(2,1)}, bf16[592,128]{1,0:T(8,128)(2,1)S(1)}, u32[]{:S(2)}, u32[]{:S(2)}) collective-permute-start(bf16[592,128]{1,0:T(8,128)(2,1)} %get-tuple-element.48), channel_id=1, source_target_pairs={{0,3},{1,0},{2,1},{3,2},{4,7},{5,4},{6,5},{7,6},{8,11},{9,8},{10,9... | collective-permute-start | bytes 454664 | tf_op jit(solution)/shard_map/ppermute | solution.py:384
  84.8 2.6 %collective-permute-done.7.refs_1_ = bf16[592,128]{1,0:T(8,128)(2,1)S(1)} collective-permute-done((bf16[592,128]{1,0:T(8,128)(2,1)}, bf16[592,128]{1,0:T(8,128)(2,1)S(1)}, u32[]{:S(2)}, u32[]{:S(2)}) %collective-permute-start.7) | collective-permute-done | bytes 151584 | tf_op jit(solution)/shard_map/ppermute | solution.py:384
  87.3 1.9 %collective-permute-done.8.refs_2_ = bf16[592,128]{1,0:T(8,128)(2,1)S(1)} collective-permute-done((bf16[592,128]{1,0:T(8,128)(2,1)}, bf16[592,128]{1,0:T(8,128)(2,1)S(1)}, u32[]{:S(2)}, u32[]{:S(2)}) %collective-permute-start.8) | collective-permute-done | bytes 151584 | tf_op jit(solution)/shard_map/ppermute | solution.py:384
  89.2 1.3 copy-done
  90.5 1.3 copy-done.1
  91.8 0.9 copy-done.2
  92.7 2.9 %shard_map.98 = (f32[32,96,128]{2,1,0:T(8,128)S(1)}, bf16[32,96,128]{2,1,0:T(8,128)(2,1)S(1)}) custom-call(s32[2]{0:T(128)S(1)} %copy-done.3, bf16[512,1152]{1,0:T(8,128)(2,1)S(1)} %copy-done.1, bf16[512,1152]{1,0:T(8,128)(2,1)S(1)} %copy-done, bf16[592,128]{1,0:T(8,128)(2,1)S(1)} %copy-done.2, bf16[592,128]{1,0:T(8,128)(2,1)S(1)} %collective-permute-done.7.refs_1_, ...), custom_call_target="tpu_custom_call" | custom-call | flops 679477248 | bytes 4194304 | tf_op jit(solution)/shard_map/pallas_call | solution.py:329
  95.7 2.3 %collective-permute-done.10 = bf16[32,96,128]{2,1,0:T(8,128)(2,1)S(1)} collective-permute-done((bf16[32,96,128]{2,1,0:T(8,128)(2,1)S(1)}, bf16[32,96,128]{2,1,0:T(8,128)(2,1)S(1)}, u32[]{:S(2)}, u32[]{:S(2)}) %collective-permute-start.10) | collective-permute-done | bytes 786464 | tf_op jit(solution)/shard_map/ppermute | solution.py:44
  98.2 27.7 %all_to_all.5.parts = bf16[32,96,128]{2,1,0:T(8,128)(2,1)S(1)} all-to-all(bf16[32,96,128]{2,1,0:T(8,128)(2,1)S(1)} %add_convert_fusion), channel_id=1, replica_groups=mesh['ly'=4,'lz'=4,'lc'=2,'dz'=2,'dx'=4] {'ly','lz','dz'}, dimensions={0} | all-to-all | bytes 1572864 | tf_op jit(solution)/shard_map/all_to_all | solution.py:396
  125.9 0.9 shard_map.99
  (35 shorter events, 5.2 us)
Async XLA Ops:
  7.2 77.6 %all-gather.5.cloned.1.call-start = ((), (), s32[]{:S(2)}) async-start(), calls=%async_computation.2 | async-start | bytes 1474560 | tf_op jit(solution)/shard_map/all_gather | solution.py:381
  13.1 71.7 %all-gather.3.cloned.1.call-start = ((), (), s32[]{:S(2)}) async-start(), calls=%async_computation.1 | async-start | bytes 1474560 | tf_op jit(solution)/shard_map/all_gather | solution.py:380
  13.8 42.6 %collective-permute-start.2 = (bf16[272,1152]{1,0:T(8,128)(2,1)}, bf16[272,1152]{1,0:T(8,128)(2,1)S(1)}, u32[]{:S(2)}, u32[]{:S(2)}) collective-permute-start(bf16[272,1152]{1,0:T(8,128)(2,1)} %get-tuple-element.32), channel_id=1, source_target_pairs={{0,8},{8,0},{1,9},{9,1},{2,10},{10,2},{3,11},{11,3},{4,12},{12,4},... | collective-permute-start | bytes 1880072 | tf_op jit(solution)/shard_map/ppermute | solution.py:44
  13.9 42.5 %collective-permute-start.3 = (bf16[272,1152]{1,0:T(8,128)(2,1)}, bf16[272,1152]{1,0:T(8,128)(2,1)S(1)}, u32[]{:S(2)}, u32[]{:S(2)}) collective-permute-start(bf16[272,1152]{1,0:T(8,128)(2,1)} %get-tuple-element.32), channel_id=1, source_target_pairs={{0,64},{64,0},{128,192},{192,128},{1,65},{65,1},{129,193},{193,129... | collective-permute-start | bytes 1880072 | tf_op jit(solution)/shard_map/ppermute | solution.py:44
  15.6 40.8 %collective-permute-start.4 = (bf16[272,1152]{1,0:T(8,128)(2,1)}, bf16[272,1152]{1,0:T(8,128)(2,1)S(1)}, u32[]{:S(2)}, u32[]{:S(2)}) collective-permute-start(bf16[272,1152]{1,0:T(8,128)(2,1)} %get-tuple-element.32), channel_id=1, source_target_pairs={{0,128},{64,192},{128,0},{192,64},{1,129},{65,193},{129,1},{193,65... | collective-permute-start | bytes 1880072 | tf_op jit(solution)/shard_map/ppermute | solution.py:44
  18.5 23.7 %collective-permute-start = (bf16[144,1152]{1,0:T(8,128)(2,1)}, bf16[144,1152]{1,0:T(8,128)(2,1)S(1)}, u32[]{:S(2)}, u32[]{:S(2)}) collective-permute-start(bf16[144,1152]{1,0:T(8,128)(2,1)} %get-tuple-element.31.refs_3_.own), channel_id=1, source_target_pairs={{0,16},{16,0},{32,48},{48,32},{1,17},{17,1},{33,49},{49,33},{2,18}... | collective-permute-start | bytes 995336 | tf_op jit(solution)/shard_map/ppermute | solution.py:44
  21.7 26.9 %collective-permute-start.1 = (bf16[128,1152]{1,0:T(8,128)(2,1)}, bf16[128,1152]{1,0:T(8,128)(2,1)S(1)}, u32[]{:S(2)}, u32[]{:S(2)}) collective-permute-start(bf16[128,1152]{1,0:T(8,128)(2,1)} %get-tuple-element.27.refs_2_.own), channel_id=1, source_target_pairs={{0,16},{16,0},{32,48},{48,32},{1,17},{17,1},{33,49},{49,33},{2,18}... | collective-permute-start | bytes 884744 | tf_op jit(solution)/shard_map/ppermute | solution.py:44
  42.2 14.2 %copy-start.7 = (bf16[144,1152]{1,0:T(8,128)(2,1)}, bf16[144,1152]{1,0:T(8,128)(2,1)S(1)}, u32[]{:S(2)}) copy-start(bf16[144,1152]{1,0:T(8,128)(2,1)S(1)} %collective-permute-done.refs_0_) | copy-start | bytes 995332
  42.2 28.1 %collective-permute-start.6 = (bf16[144,1152]{1,0:T(8,128)(2,1)S(1)}, bf16[144,1152]{1,0:T(8,128)(2,1)S(1)}, u32[]{:S(2)}, u32[]{:S(2)}) collective-permute-start(bf16[144,1152]{1,0:T(8,128)(2,1)S(1)} %collective-permute-done.refs_0_), channel_id=1, source_target_pairs={{0,48},{16,32},{32,16},{48,0},{1,49},{17,33},{33,17},{49,1},{2,50}... | collective-permute-start | bytes 995336 | tf_op jit(solution)/shard_map/ppermute | solution.py:44
  48.6 7.8 %copy-start.9 = (bf16[128,1152]{1,0:T(8,128)(2,1)}, bf16[128,1152]{1,0:T(8,128)(2,1)S(1)}, u32[]{:S(2)}) copy-start(bf16[128,1152]{1,0:T(8,128)(2,1)S(1)} %collective-permute-done.1.refs_1_) | copy-start | bytes 884740
  48.6 26.5 %collective-permute-start.5 = (bf16[128,1152]{1,0:T(8,128)(2,1)S(1)}, bf16[128,1152]{1,0:T(8,128)(2,1)S(1)}, u32[]{:S(2)}, u32[]{:S(2)}) collective-permute-start(bf16[128,1152]{1,0:T(8,128)(2,1)S(1)} %collective-permute-done.1.refs_1_), channel_id=1, source_target_pairs={{0,48},{16,32},{32,16},{48,0},{1,49},{17,33},{33,17},{49,1},{2,50}... | collective-permute-start | bytes 884744 | tf_op jit(solution)/shard_map/ppermute | solution.py:44
  56.4 0.8 copy-start.4
  56.4 1.0 copy-start.5
  57.4 0.8 copy-start.6
  70.3 0.7 copy-start.8
  74.1 15.1 %copy-start.3 = (s32[2]{0:T(128)S(1)}, s32[2]{0:T(128)}, u32[]{:S(2)}) copy-start(s32[2]{0:T(128)} %pad_add_fusion.spot) | copy-start | bytes 28
  75.2 0.7 copy-start.10
  79.1 8.2 %collective-permute-start.7 = (bf16[592,128]{1,0:T(8,128)(2,1)}, bf16[592,128]{1,0:T(8,128)(2,1)S(1)}, u32[]{:S(2)}, u32[]{:S(2)}) collective-permute-start(bf16[592,128]{1,0:T(8,128)(2,1)} %get-tuple-element.46), channel_id=1, source_target_pairs={{0,1},{1,2},{2,3},{3,0},{4,5},{5,6},{6,7},{7,4},{8,9},{9,10},{10,1... | collective-permute-start | bytes 454664 | tf_op jit(solution)/shard_map/ppermute | solution.py:384
  80.6 8.6 %collective-permute-start.8 = (bf16[592,128]{1,0:T(8,128)(2,1)}, bf16[592,128]{1,0:T(8,128)(2,1)S(1)}, u32[]{:S(2)}, u32[]{:S(2)}) collective-permute-start(bf16[592,128]{1,0:T(8,128)(2,1)} %get-tuple-element.47), channel_id=1, source_target_pairs={{0,2},{1,3},{2,0},{3,1},{4,6},{5,7},{6,4},{7,5},{8,10},{9,11},{10,... | collective-permute-start | bytes 454664 | tf_op jit(solution)/shard_map/ppermute | solution.py:384
  83.3 5.9 %collective-permute-start.9 = (bf16[592,128]{1,0:T(8,128)(2,1)}, bf16[592,128]{1,0:T(8,128)(2,1)S(1)}, u32[]{:S(2)}, u32[]{:S(2)}) collective-permute-start(bf16[592,128]{1,0:T(8,128)(2,1)} %get-tuple-element.48), channel_id=1, source_target_pairs={{0,3},{1,0},{2,1},{3,2},{4,7},{5,4},{6,5},{7,6},{8,11},{9,8},{10,9... | collective-permute-start | bytes 454664 | tf_op jit(solution)/shard_map/ppermute | solution.py:384
  89.2 1.3 copy-start
  90.5 1.3 copy-start.1
  91.8 0.9 copy-start.2
  95.6 2.4 %collective-permute-start.10 = (bf16[32,96,128]{2,1,0:T(8,128)(2,1)S(1)}, bf16[32,96,128]{2,1,0:T(8,128)(2,1)S(1)}, u32[]{:S(2)}, u32[]{:S(2)}) collective-permute-start(bf16[32,96,128]{2,1,0:T(8,128)(2,1)S(1)} %get-tuple-element.50), channel_id=1, source_target_pairs={{0,8},{8,0},{1,9},{9,1},{2,10},{10,2},{3,11},{11,3},{4,12},{12,4},... | collective-permute-start | bytes 2359304 | tf_op jit(solution)/shard_map/ppermute | solution.py:44
Sparse Core Ops, SparseCore 0:
  13.2 29.5 all-gather.4
  44.5 27.7 all-gather.2

commit v11 on v9

--- a/solution.py
+++ b/solution.py
@@ -9,6 +9,7 @@
 
 EPSILON = 1e-06
 LOSS = ("ly", "lz", "lc")
+QUAD = ("ly", "lz", "dz")
 ROWS = 128
 WIDTH = 1152
 KEY_ROWS = 16
@@ -342,8 +343,9 @@
     )(*arrays)
 
 
-def final_kernel(count, parts, out_img, out_txt, stats):
-    both = jnp.sum(parts[...].astype(F32), axis=0)
+def final_kernel(count, slot, parts, own_img, own_txt, out_img, out_txt, stats):
+    both = jnp.sum(parts[...].astype(F32), axis=0) - parts[slot[0]].astype(F32)
+    both = both + jnp.concatenate([own_img[...], own_txt[...]], axis=0)
     for out, total in ((out_img, both[:SLAB]), (out_txt, both[SLAB:])):
         out[:, :LANES] = total[:CHUNK]
         rest = total[SLOT:, :].T
@@ -356,16 +358,16 @@
         stats[k] = jnp.sum(chosen) * (1.0 / count)
 
 
-def final(count, parts):
+def final(count, slot, *arrays):
     grad = jax.ShapeDtypeStruct((CHUNK, COLS), F32)
     return pl.pallas_call(
         functools.partial(final_kernel, count),
-        in_specs=[VMEM],
+        in_specs=[SMEM] + [VMEM] * len(arrays),
         out_specs=[VMEM, VMEM, SMEM],
         out_shape=[grad, grad, jax.ShapeDtypeStruct((3,), F32)],
         compiler_params=params(8),
         cost_estimate=cost(4 * QUADS * SLAB * LANES, 2**20),
-    )(parts)
+    )(slot, *arrays)
 
 
 def body(pictures, sentences, keys, picture_weights, sentence_weights, heat_log, shift_value):
@@ -400,7 +402,7 @@
 
     last = after(txt_b, img_feat, img_a, img_c, img_y1, img_y2)
     *img_outs, far_rows = late(
-        True, ways, spot, scal, img, img_part, [txt_y1, txt_y2, txt_a, last]
+        True, ways, spot, scal, img, img_part, [txt_a, txt_y1, txt_y2, last]
     )
     img_cols = columns(img_outs)
     txt_part = early(
@@ -409,7 +411,7 @@
         sentences[0],
         sentence_weights,
         keys,
-        [txt, near_rows, far_rows, img, img_c, img_y1, img_y2, img_a],
+        [txt, near_rows, far_rows, img, img_c, img_a, img_y1, img_y2],
     )
     last = after(img_b, *img_cols, *txt_part)
     outs = late(False, ways, spot, scal, txt, txt_part, [far_rows, last])
@@ -419,8 +421,14 @@
     txt_kept, txt_given = heads(False, spot, txt_feat, txt_cols)
     txt_taken = exchange(txt_given, "lc", 1)
     sums = mix(img_kept, img_taken, txt_kept, txt_taken)
-    sums = lax.all_to_all(sums, ("ly", "lz", "dz"), 0, 0, tiled=True)
-    grad_img, grad_txt, stats = final(count, sums)
+    sums = lax.all_to_all(sums, QUAD, 0, 0, tiled=True)
+    slot = lax.axis_index(QUAD)
+
+    def own_part(kept, taken):
+        return kept[slot] + taken[slot].astype(F32)
+
+    mine = (own_part(img_kept, img_taken), own_part(txt_kept, txt_taken))
+    grad_img, grad_txt, stats = final(count, slot.astype(jnp.int32)[None], sums, *mine)
     return grad_img, grad_txt, stats
 
 

time: 128 us -> 133 us (1.039)
  blocking collectives: 30.5 us -> 0 us
  waiting for transfers between devices: 18.3 us -> 43.8 us
  starting transfers between devices: 32 us -> 42.2 us
    all_to_all x1 -> x0, blocking collectives: 30.5 us -> none  [body(): sums = lax.all_to_all(sums, ('ly', 'lz', 'dz'), 0, 0, tiled=True)]
    all_to_all x0 -> x1, waiting for transfers between devices: none -> 23.2 us  [body(): sums = lax.all_to_all(sums, QUAD, 0, 0, tiled=True)]
    all_to_all x0 -> x1, starting transfers between devices: none -> 12.1 us  [body(): sums = lax.all_to_all(sums, QUAD, 0, 0, tiled=True)]
    ppermute x12, starting transfers between devices: 22.3 us -> 20.3 us  [exchange(): lax.ppermute(array, axis, [(i, i ^ apart) for i in range(lax.axis_size(ax...]
  transfers between devices with their start and end apart: 20 -> 21, of which waited for: 7 -> 9; matrix products, arithmetic and copies ran while one was open for 1% -> 1% of each run, Pallas kernels for 17% -> 16%
where the time goes in v11:
time: 133 us
  waiting for transfers between devices  43.8 us (33%)
  starting transfers between devices  42.2 us (32%)
  Pallas kernels  27.1 us (20%)
  between operations  15.6 us (12%)
  local copies, waits for them, and re-layouts  3.58 us (3%)
    all_to_all x1, waiting for transfers between devices, body(): sums = lax.all_to_all(sums, QUAD, 0, 0, tiled=True)  23.2 us
    ppermute x12, starting transfers between devices, exchange(): lax.ppermute(array, axis, [(i, i ^ apart) for i in range(lax.axis_size(ax...  20.3 us
    ppermute x12, waiting for transfers between devices, exchange(): lax.ppermute(array, axis, [(i, i ^ apart) for i in range(lax.axis_size(ax...  17.4 us
    all_to_all x1, starting transfers between devices, body(): sums = lax.all_to_all(sums, QUAD, 0, 0, tiled=True)  12.1 us
    pallas_call x2, Pallas kernels, early(): pl.pallas_call(functools.partial(early_kernel, first), in_specs=[SMEM, SM...  10.2 us
    ppermute x6, starting transfers between devices, turn(): lax.ppermute(array, axis, [(i, (i + step) % size) for i in range(size)])  9.73 us
    pallas_call x2, Pallas kernels, late(): pl.pallas_call(functools.partial(late_kernel, with_stats, ways, len(block...  7.51 us
    pallas_call x2, Pallas kernels, heads(): pl.pallas_call(functools.partial(head_kernel, with_stats), in_specs=[SMEM...  4.03 us
  transfers between devices with their start and end apart: 21, of which 9 were waited for; matrix products, arithmetic and copies ran while one was open for 1% of the time, Pallas kernels for 16%

profile of v11, /device:TPU:32, one launch (start us, length us, event | category | flops | bytes accessed | tf_op | source)
XLA Modules:
  0.0 133.0 jit_solution(18286524726161784348)
XLA Ops:
  7.2 3.4 %shard_map.94.refs_0_.own = bf16[144,1152]{1,0:T(8,128)(2,1)} custom-call(bf16[128,1152]{1,0:T(8,128)(2,1)} %bitcast.9, bf16[1152,1152]{1,0:T(8,128)(2,1)} %w_hbm.5, s32[1,128]{1,0:T(1,128)} %key.3), custom_call_target="tpu_custom_call" | custom-call | flops 339738624 | bytes 4194304 | tf_op jit(solution)/shard_map/pallas_call | solution.py:82
  11.5 3.4 %collective-permute-start.1 = (bf16[144,1152]{1,0:T(8,128)(2,1)}, bf16[144,1152]{1,0:T(8,128)(2,1)S(1)}, u32[]{:S(2)}, u32[]{:S(2)}) collective-permute-start(bf16[144,1152]{1,0:T(8,128)(2,1)} %shard_map.94.refs_0_.own), channel_id=1, source_target_pairs={{0,16},{16,0},{32,48},{48,32},{1,17},{17,1},{33,49},{49,33},{2,18}... | collective-permute-start | bytes 995336 | tf_op jit(solution)/shard_map/ppermute | solution.py:42
  14.8 1.6 %collective-permute-start.2 = (bf16[144,1152]{1,0:T(8,128)(2,1)}, bf16[144,1152]{1,0:T(8,128)(2,1)S(1)}, u32[]{:S(2)}, u32[]{:S(2)}) collective-permute-start(bf16[144,1152]{1,0:T(8,128)(2,1)} %shard_map.94.refs_0_.own), channel_id=1, source_target_pairs={{0,64},{64,0},{128,192},{192,128},{1,65},{65,1},{129,193},{193,129... | collective-permute-start | bytes 995336 | tf_op jit(solution)/shard_map/ppermute | solution.py:42
  16.4 2.9 %collective-permute-start.3 = (bf16[144,1152]{1,0:T(8,128)(2,1)}, bf16[144,1152]{1,0:T(8,128)(2,1)S(1)}, u32[]{:S(2)}, u32[]{:S(2)}) collective-permute-start(bf16[144,1152]{1,0:T(8,128)(2,1)} %shard_map.94.refs_0_.own), channel_id=1, source_target_pairs={{0,128},{64,192},{128,0},{192,64},{1,129},{65,193},{129,1},{193,65... | collective-permute-start | bytes 995336 | tf_op jit(solution)/shard_map/ppermute | solution.py:42
  21.4 5.1 %shard_map.95 = (bf16[128,1152]{1,0:T(8,128)(2,1)}, f32[2,8,128]{2,1,0:T(8,128)}, f32[128,1152]{1,0:T(8,128)}, f32[128,1152]{1,0:T(8,128)}, f32[128,128]{1,0:T(8...) custom-call(f32[1]{0:T(128)S(6)} %copy.10.heat_log, f32[1]{0:T(128)S(6)} %copy.11.shift, bf16[128,1152]{1,0:T(8,128)(2,1)} %bitcast.13, ...), custom_call_target="tpu_custom_call" | custom-call | flops 377487360 | bytes 8388608 | tf_op jit(solution)/shard_map/pallas_call | solution.py:193
  26.5 3.0 %collective-permute-done.1.refs_5_ = bf16[144,1152]{1,0:T(8,128)(2,1)S(1)} collective-permute-done((bf16[144,1152]{1,0:T(8,128)(2,1)}, bf16[144,1152]{1,0:T(8,128)(2,1)S(1)}, u32[]{:S(2)}, u32[]{:S(2)}) %collective-permute-start.1) | collective-permute-done | bytes 331808 | tf_op jit(solution)/shard_map/ppermute | solution.py:42
  29.5 5.0 %collective-permute-done.3.refs_7_ = bf16[144,1152]{1,0:T(8,128)(2,1)S(1)} collective-permute-done((bf16[144,1152]{1,0:T(8,128)(2,1)}, bf16[144,1152]{1,0:T(8,128)(2,1)S(1)}, u32[]{:S(2)}, u32[]{:S(2)}) %collective-permute-start.3) | collective-permute-done | bytes 331808 | tf_op jit(solution)/shard_map/ppermute | solution.py:42
  34.7 4.8 %collective-permute-start.4 = (bf16[144,1152]{1,0:T(8,128)(2,1)S(1)}, bf16[144,1152]{1,0:T(8,128)(2,1)S(1)}, u32[]{:S(2)}, u32[]{:S(2)}) collective-permute-start(bf16[144,1152]{1,0:T(8,128)(2,1)S(1)} %collective-permute-done.1.refs_5_), channel_id=1, source_target_pairs={{0,48},{16,32},{32,16},{48,0},{1,49},{17,33},{33,17},{49,1},{2,50}... | collective-permute-start | bytes 995336 | tf_op jit(solution)/shard_map/ppermute | solution.py:42
  39.7 1.5 %collective-permute-start.8 = (bf16[128,1152]{1,0:T(8,128)(2,1)}, bf16[128,1152]{1,0:T(8,128)(2,1)S(1)}, u32[]{:S(2)}, u32[]{:S(2)}) collective-permute-start(bf16[128,1152]{1,0:T(8,128)(2,1)} %get-tuple-element.46.own.refs_3_), channel_id=1, source_target_pairs={{0,128},{64,192},{128,0},{192,64},{1,129},{65,193},{129,1},{193,65... | collective-permute-start | bytes 884744 | tf_op jit(solution)/shard_map/ppermute | solution.py:42
  41.2 6.8 %collective-permute-done.5.refs_5_ = bf16[128,1152]{1,0:T(8,128)(2,1)S(1)} collective-permute-done((bf16[128,1152]{1,0:T(8,128)(2,1)}, bf16[128,1152]{1,0:T(8,128)(2,1)S(1)}, u32[]{:S(2)}, u32[]{:S(2)}) %collective-permute-start.5) | collective-permute-done | bytes 294944 | tf_op jit(solution)/shard_map/ppermute | solution.py:42
  48.0 5.4 %collective-permute-start.9 = (bf16[128,1152]{1,0:T(8,128)(2,1)S(1)}, bf16[128,1152]{1,0:T(8,128)(2,1)S(1)}, u32[]{:S(2)}, u32[]{:S(2)}) collective-permute-start(bf16[128,1152]{1,0:T(8,128)(2,1)S(1)} %collective-permute-done.5.refs_5_), channel_id=1, source_target_pairs={{0,48},{16,32},{32,16},{48,0},{1,49},{17,33},{33,17},{49,1},{2,50}... | collective-permute-start | bytes 884744 | tf_op jit(solution)/shard_map/ppermute | solution.py:42
  55.8 4.4 %shard_map.96 = (bf16[304,128]{1,0:T(8,128)(2,1)}, bf16[304,128]{1,0:T(8,128)(2,1)}, bf16[304,128]{1,0:T(8,128)(2,1)}, bf16[304,128]{1,0:T(8,128)(2,1)}, f32[4,8,128]{2,1,0:T(8,128)}) custom-call(s32[2]{0:T(128)} %pad_add_fusion.spot, f32[1]{0:T(128)S(6)} %copy.10.heat_log, f32[1]{0:T(128)S(6)} %copy.11.shift, ...), custom_call_target="tpu_custom_call" | custom-call | flops 150994944 | bytes 4194304 | tf_op jit(solution)/shard_map/pallas_call | solution.py:259
  60.2 1.5 %collective-permute-start.10 = (bf16[304,128]{1,0:T(8,128)(2,1)}, bf16[304,128]{1,0:T(8,128)(2,1)S(1)}, u32[]{:S(2)}, u32[]{:S(2)}) collective-permute-start(bf16[304,128]{1,0:T(8,128)(2,1)} %get-tuple-element.55), channel_id=1, source_target_pairs={{0,1},{1,2},{2,3},{3,0},{4,5},{5,6},{6,7},{7,4},{8,9},{9,10},{10,1... | collective-permute-start | bytes 233480 | tf_op jit(solution)/shard_map/ppermute | solution.py:398
  61.7 2.7 %collective-permute-start.11 = (bf16[304,128]{1,0:T(8,128)(2,1)}, bf16[304,128]{1,0:T(8,128)(2,1)S(1)}, u32[]{:S(2)}, u32[]{:S(2)}) collective-permute-start(bf16[304,128]{1,0:T(8,128)(2,1)} %get-tuple-element.56), channel_id=1, source_target_pairs={{0,2},{1,3},{2,0},{3,1},{4,6},{5,7},{6,4},{7,5},{8,10},{9,11},{10,... | collective-permute-start | bytes 233480 | tf_op jit(solution)/shard_map/ppermute | solution.py:398
  64.4 1.4 %collective-permute-start.12 = (bf16[304,128]{1,0:T(8,128)(2,1)}, bf16[304,128]{1,0:T(8,128)(2,1)S(1)}, u32[]{:S(2)}, u32[]{:S(2)}) collective-permute-start(bf16[304,128]{1,0:T(8,128)(2,1)} %get-tuple-element.57), channel_id=1, source_target_pairs={{0,3},{1,0},{2,1},{3,2},{4,7},{5,4},{6,5},{7,6},{8,11},{9,8},{10,9... | collective-permute-start | bytes 233480 | tf_op jit(solution)/shard_map/ppermute | solution.py:398
  65.9 5.0 %shard_map.97 = (f32[128,1152]{1,0:T(8,128)}, f32[128,1152]{1,0:T(8,128)}, f32[128,128]{1,0:T(8,128)}, f32[128,128]{1,0:T(8,128)}, f32[3,128,128]{2,1,0:T(8,128)}) custom-call(f32[1]{0:T(128)S(6)} %copy.10.heat_log, f32[1]{0:T(128)S(6)} %copy.11.shift, bf16[128,1152]{1,0:T(8,128)(2,1)} %bitcast.11, bf16[1152,1152]{1,0:T(8,128)(2,1)} %w_hbm.5, s32[1,128]{1,0:T(1,128)} %key.3, ...), custom_call_target="tpu_custom_call" | custom-call | flops 377487360 | bytes 8388608 | tf_op jit(solution)/shard_map/pallas_call | solution.py:193
  71.7 3.1 %shard_map.98 = (bf16[288,128]{1,0:T(8,128)(2,1)}, bf16[288,128]{1,0:T(8,128)(2,1)}, bf16[288,128]{1,0:T(8,128)(2,1)}, bf16[288,128]{1,0:T(8,128)(2,1)}) custom-call(s32[2]{0:T(128)} %pad_add_fusion.spot, f32[1]{0:T(128)S(6)} %copy.10.heat_log, f32[1]{0:T(128)S(6)} %copy.11.shift, bf16[144,1152]{1,0:T(8,128)(2,1)} %shard_map.94.refs_0_.own, ...), custom_call_target="tpu_custom_call" | custom-call | flops 150994944 | bytes 4194304 | tf_op jit(solution)/shard_map/pallas_call | solution.py:259
  75.3 2.9 %collective-permute-start.15 = (bf16[288,128]{1,0:T(8,128)(2,1)}, bf16[288,128]{1,0:T(8,128)(2,1)S(1)}, u32[]{:S(2)}, u32[]{:S(2)}) collective-permute-start(bf16[288,128]{1,0:T(8,128)(2,1)} %get-tuple-element.65), channel_id=1, source_target_pairs={{0,2},{1,3},{2,0},{3,1},{4,6},{5,7},{6,4},{7,5},{8,10},{9,11},{10,... | collective-permute-start | bytes 221192 | tf_op jit(solution)/shard_map/ppermute | solution.py:398
  78.9 2.0 %shard_map.99 = (f32[32,48,128]{2,1,0:T(8,128)S(1)}, bf16[32,48,128]{2,1,0:T(8,128)(2,1)S(1)}) custom-call(s32[2]{0:T(128)S(1)} %copy-done.4, bf16[512,1152]{1,0:T(8,128)(2,1)S(1)} %copy-done.1, bf16[304,128]{1,0:T(8,128)(2,1)S(1)} %copy-done.2, bf16[304,128]{1,0:T(8,128)(2,1)S(1)} %collective-permute-done.10.refs_1_, ...), custom_call_target="tpu_custom_call" | custom-call | flops 339738624 | bytes 4194304 | tf_op jit(solution)/shard_map/pallas_call | solution.py:319
  82.7 1.3 copy-done
  84.9 2.0 %shard_map.100 = (f32[32,48,128]{2,1,0:T(8,128)S(1)}, bf16[32,48,128]{2,1,0:T(8,128)(2,1)S(1)}) custom-call(s32[2]{0:T(128)S(1)} %copy-done.4, bf16[512,1152]{1,0:T(8,128)(2,1)S(1)} %copy-done, bf16[288,128]{1,0:T(8,128)(2,1)S(1)} %copy-done.3, bf16[288,128]{1,0:T(8,128)(2,1)S(1)} %collective-permute-done.14.refs_1_, ...), custom_call_target="tpu_custom_call" | custom-call | flops 339738624 | bytes 4194304 | tf_op jit(solution)/shard_map/pallas_call | solution.py:319
  87.0 1.7 %collective-permute-done.17.taken_txt = bf16[32,48,128]{2,1,0:T(8,128)(2,1)S(1)} collective-permute-done((bf16[32,48,128]{2,1,0:T(8,128)(2,1)S(1)}, bf16[32,48,128]{2,1,0:T(8,128)(2,1)S(1)}, u32[]{:S(2)}, u32[]{:S(2)}) %collective-permute-start.17) | collective-permute-done | bytes 393248 | tf_op jit(solution)/shard_map/ppermute | solution.py:42
  89.7 12.1 %all-to-all-start = ((bf16[32,96,128]{2,1,0:T(8,128)(2,1)}), bf16[32,96,128]{2,1,0:T(8,128)(2,1)S(1)}, u32[]{:S(2)}, u32[]{:S(2)}) async-start(bf16[32,96,128]{2,1,0:T(8,128)(2,1)} %shard_map.101), calls=%async_computation | async-start | bytes 1572864 | tf_op jit(solution)/shard_map/all_to_all | solution.py:424
  101.9 23.2 %all-to-all-done.parts = bf16[32,96,128]{2,1,0:T(8,128)(2,1)S(1)} async-done(((bf16[32,96,128]{2,1,0:T(8,128)(2,1)}), bf16[32,96,128]{2,1,0:T(8,128)(2,1)S(1)}, u32[]{:S(2)}, u32[]{:S(2)}) %all-to-all-start) | async-done | bytes 786464 | tf_op jit(solution)/shard_map/all_to_all | solution.py:424
  (62 shorter events, 11.1 us)
Async XLA Ops:
  7.2 47.9 %all-gather.3.cloned.1.call-start = ((), (), s32[]{:S(2)}) async-start(), calls=%async_computation.1 | async-start | bytes 1474560 | tf_op jit(solution)/shard_map/all_gather | solution.py:382
  10.6 68.3 %all-gather.5.cloned.1.call-start = ((), (), s32[]{:S(2)}) async-start(), calls=%async_computation.2 | async-start | bytes 1474560 | tf_op jit(solution)/shard_map/all_gather | solution.py:383
  11.4 9.2 %collective-permute-start = (bf16[144,1152]{1,0:T(8,128)(2,1)}, bf16[144,1152]{1,0:T(8,128)(2,1)S(1)}, u32[]{:S(2)}, u32[]{:S(2)}) collective-permute-start(bf16[144,1152]{1,0:T(8,128)(2,1)} %shard_map.94.refs_0_.own), channel_id=1, source_target_pairs={{0,8},{8,0},{1,9},{9,1},{2,10},{10,2},{3,11},{11,3},{4,12},{12,4},... | collective-permute-start | bytes 995336 | tf_op jit(solution)/shard_map/ppermute | solution.py:42
  11.5 18.0 %collective-permute-start.1 = (bf16[144,1152]{1,0:T(8,128)(2,1)}, bf16[144,1152]{1,0:T(8,128)(2,1)S(1)}, u32[]{:S(2)}, u32[]{:S(2)}) collective-permute-start(bf16[144,1152]{1,0:T(8,128)(2,1)} %shard_map.94.refs_0_.own), channel_id=1, source_target_pairs={{0,16},{16,0},{32,48},{48,32},{1,17},{17,1},{33,49},{49,33},{2,18}... | collective-permute-start | bytes 995336 | tf_op jit(solution)/shard_map/ppermute | solution.py:42
  14.8 14.6 %collective-permute-start.2 = (bf16[144,1152]{1,0:T(8,128)(2,1)}, bf16[144,1152]{1,0:T(8,128)(2,1)S(1)}, u32[]{:S(2)}, u32[]{:S(2)}) collective-permute-start(bf16[144,1152]{1,0:T(8,128)(2,1)} %shard_map.94.refs_0_.own), channel_id=1, source_target_pairs={{0,64},{64,0},{128,192},{192,128},{1,65},{65,1},{129,193},{193,129... | collective-permute-start | bytes 995336 | tf_op jit(solution)/shard_map/ppermute | solution.py:42
  16.4 18.0 %collective-permute-start.3 = (bf16[144,1152]{1,0:T(8,128)(2,1)}, bf16[144,1152]{1,0:T(8,128)(2,1)S(1)}, u32[]{:S(2)}, u32[]{:S(2)}) collective-permute-start(bf16[144,1152]{1,0:T(8,128)(2,1)} %shard_map.94.refs_0_.own), channel_id=1, source_target_pairs={{0,128},{64,192},{128,0},{192,64},{1,129},{65,193},{129,1},{193,65... | collective-permute-start | bytes 995336 | tf_op jit(solution)/shard_map/ppermute | solution.py:42
  29.5 25.6 %copy-start.5 = (bf16[144,1152]{1,0:T(8,128)(2,1)}, bf16[144,1152]{1,0:T(8,128)(2,1)S(1)}, u32[]{:S(2)}) copy-start(bf16[144,1152]{1,0:T(8,128)(2,1)S(1)} %collective-permute-done.1.refs_5_) | copy-start | bytes 995332
  29.5 25.6 %copy-start.6 = (bf16[144,1152]{1,0:T(8,128)(2,1)}, bf16[144,1152]{1,0:T(8,128)(2,1)S(1)}, u32[]{:S(2)}) copy-start(bf16[144,1152]{1,0:T(8,128)(2,1)S(1)} %collective-permute-done.2.refs_6_) | copy-start | bytes 995332
  34.5 5.1 %collective-permute-start.6 = (bf16[128,1152]{1,0:T(8,128)(2,1)}, bf16[128,1152]{1,0:T(8,128)(2,1)S(1)}, u32[]{:S(2)}, u32[]{:S(2)}) collective-permute-start(bf16[128,1152]{1,0:T(8,128)(2,1)} %get-tuple-element.46.own.refs_3_), channel_id=1, source_target_pairs={{0,8},{8,0},{1,9},{9,1},{2,10},{10,2},{3,11},{11,3},{4,12},{12,4},... | collective-permute-start | bytes 884744 | tf_op jit(solution)/shard_map/ppermute | solution.py:42
  34.5 13.5 %collective-permute-start.5 = (bf16[128,1152]{1,0:T(8,128)(2,1)}, bf16[128,1152]{1,0:T(8,128)(2,1)S(1)}, u32[]{:S(2)}, u32[]{:S(2)}) collective-permute-start(bf16[128,1152]{1,0:T(8,128)(2,1)} %get-tuple-element.46.own.refs_3_), channel_id=1, source_target_pairs={{0,16},{16,0},{32,48},{48,32},{1,17},{17,1},{33,49},{49,33},{2,18}... | collective-permute-start | bytes 884744 | tf_op jit(solution)/shard_map/ppermute | solution.py:42
  34.7 20.3 %collective-permute-start.4 = (bf16[144,1152]{1,0:T(8,128)(2,1)S(1)}, bf16[144,1152]{1,0:T(8,128)(2,1)S(1)}, u32[]{:S(2)}, u32[]{:S(2)}) collective-permute-start(bf16[144,1152]{1,0:T(8,128)(2,1)S(1)} %collective-permute-done.1.refs_5_), channel_id=1, source_target_pairs={{0,48},{16,32},{32,16},{48,0},{1,49},{17,33},{33,17},{49,1},{2,50}... | collective-permute-start | bytes 995336 | tf_op jit(solution)/shard_map/ppermute | solution.py:42
  39.5 26.3 %copy-start.11 = (bf16[128,1152]{1,0:T(8,128)(2,1)}, bf16[128,1152]{1,0:T(8,128)(2,1)S(1)}, u32[]{:S(2)}) copy-start(bf16[128,1152]{1,0:T(8,128)(2,1)S(1)} %collective-permute-done.6.refs_4_) | copy-start | bytes 884740
  39.5 15.5 %collective-permute-start.7 = (bf16[128,1152]{1,0:T(8,128)(2,1)}, bf16[128,1152]{1,0:T(8,128)(2,1)S(1)}, u32[]{:S(2)}, u32[]{:S(2)}) collective-permute-start(bf16[128,1152]{1,0:T(8,128)(2,1)} %get-tuple-element.46.own.refs_3_), channel_id=1, source_target_pairs={{0,64},{64,0},{128,192},{192,128},{1,65},{65,1},{129,193},{193,129... | collective-permute-start | bytes 884744 | tf_op jit(solution)/shard_map/ppermute | solution.py:42
  39.7 15.3 %collective-permute-start.8 = (bf16[128,1152]{1,0:T(8,128)(2,1)}, bf16[128,1152]{1,0:T(8,128)(2,1)S(1)}, u32[]{:S(2)}, u32[]{:S(2)}) collective-permute-start(bf16[128,1152]{1,0:T(8,128)(2,1)} %get-tuple-element.46.own.refs_3_), channel_id=1, source_target_pairs={{0,128},{64,192},{128,0},{192,64},{1,129},{65,193},{129,1},{193,65... | collective-permute-start | bytes 884744 | tf_op jit(solution)/shard_map/ppermute | solution.py:42
  48.0 22.9 %collective-permute-start.9 = (bf16[128,1152]{1,0:T(8,128)(2,1)S(1)}, bf16[128,1152]{1,0:T(8,128)(2,1)S(1)}, u32[]{:S(2)}, u32[]{:S(2)}) collective-permute-start(bf16[128,1152]{1,0:T(8,128)(2,1)S(1)} %collective-permute-done.5.refs_5_), channel_id=1, source_target_pairs={{0,48},{16,32},{32,16},{48,0},{1,49},{17,33},{33,17},{49,1},{2,50}... | collective-permute-start | bytes 884744 | tf_op jit(solution)/shard_map/ppermute | solution.py:42
  60.2 10.8 %collective-permute-start.10 = (bf16[304,128]{1,0:T(8,128)(2,1)}, bf16[304,128]{1,0:T(8,128)(2,1)S(1)}, u32[]{:S(2)}, u32[]{:S(2)}) collective-permute-start(bf16[304,128]{1,0:T(8,128)(2,1)} %get-tuple-element.55), channel_id=1, source_target_pairs={{0,1},{1,2},{2,3},{3,0},{4,5},{5,6},{6,7},{7,4},{8,9},{9,10},{10,1... | collective-permute-start | bytes 233480 | tf_op jit(solution)/shard_map/ppermute | solution.py:398
  61.7 10.0 %collective-permute-start.11 = (bf16[304,128]{1,0:T(8,128)(2,1)}, bf16[304,128]{1,0:T(8,128)(2,1)S(1)}, u32[]{:S(2)}, u32[]{:S(2)}) collective-permute-start(bf16[304,128]{1,0:T(8,128)(2,1)} %get-tuple-element.56), channel_id=1, source_target_pairs={{0,2},{1,3},{2,0},{3,1},{4,6},{5,7},{6,4},{7,5},{8,10},{9,11},{10,... | collective-permute-start | bytes 233480 | tf_op jit(solution)/shard_map/ppermute | solution.py:398
  64.4 7.3 %collective-permute-start.12 = (bf16[304,128]{1,0:T(8,128)(2,1)}, bf16[304,128]{1,0:T(8,128)(2,1)S(1)}, u32[]{:S(2)}, u32[]{:S(2)}) collective-permute-start(bf16[304,128]{1,0:T(8,128)(2,1)} %get-tuple-element.57), channel_id=1, source_target_pairs={{0,3},{1,0},{2,1},{3,2},{4,7},{5,4},{6,5},{7,6},{8,11},{9,8},{10,9... | collective-permute-start | bytes 233480 | tf_op jit(solution)/shard_map/ppermute | solution.py:398
  74.8 6.3 %collective-permute-start.14 = (bf16[288,128]{1,0:T(8,128)(2,1)}, bf16[288,128]{1,0:T(8,128)(2,1)S(1)}, u32[]{:S(2)}, u32[]{:S(2)}) collective-permute-start(bf16[288,128]{1,0:T(8,128)(2,1)} %get-tuple-element.64), channel_id=1, source_target_pairs={{0,1},{1,2},{2,3},{3,0},{4,5},{5,6},{6,7},{7,4},{8,9},{9,10},{10,1... | collective-permute-start | bytes 221192 | tf_op jit(solution)/shard_map/ppermute | solution.py:398
  75.3 6.2 %collective-permute-start.15 = (bf16[288,128]{1,0:T(8,128)(2,1)}, bf16[288,128]{1,0:T(8,128)(2,1)S(1)}, u32[]{:S(2)}, u32[]{:S(2)}) collective-permute-start(bf16[288,128]{1,0:T(8,128)(2,1)} %get-tuple-element.65), channel_id=1, source_target_pairs={{0,2},{1,3},{2,0},{3,1},{4,6},{5,7},{6,4},{7,5},{8,10},{9,11},{10,... | collective-permute-start | bytes 221192 | tf_op jit(solution)/shard_map/ppermute | solution.py:398
  78.2 4.6 %collective-permute-start.16 = (bf16[288,128]{1,0:T(8,128)(2,1)}, bf16[288,128]{1,0:T(8,128)(2,1)S(1)}, u32[]{:S(2)}, u32[]{:S(2)}) collective-permute-start(bf16[288,128]{1,0:T(8,128)(2,1)} %get-tuple-element.66), channel_id=1, source_target_pairs={{0,3},{1,0},{2,1},{3,2},{4,7},{5,4},{6,5},{7,6},{8,11},{9,8},{10,9... | collective-permute-start | bytes 221192 | tf_op jit(solution)/shard_map/ppermute | solution.py:398
  80.9 6.1 %collective-permute-start.13 = (bf16[32,48,128]{2,1,0:T(8,128)(2,1)S(1)}, bf16[32,48,128]{2,1,0:T(8,128)(2,1)S(1)}, u32[]{:S(2)}, u32[]{:S(2)}) collective-permute-start(bf16[32,48,128]{2,1,0:T(8,128)(2,1)S(1)} %get-tuple-element.63), channel_id=1, source_target_pairs={{0,8},{8,0},{1,9},{9,1},{2,10},{10,2},{3,11},{11,3},{4,12},{12,4},... | collective-permute-start | bytes 1179656 | tf_op jit(solution)/shard_map/ppermute | solution.py:42
  86.9 1.8 %collective-permute-start.17 = (bf16[32,48,128]{2,1,0:T(8,128)(2,1)S(1)}, bf16[32,48,128]{2,1,0:T(8,128)(2,1)S(1)}, u32[]{:S(2)}, u32[]{:S(2)}) collective-permute-start(bf16[32,48,128]{2,1,0:T(8,128)(2,1)S(1)} %get-tuple-element.68), channel_id=1, source_target_pairs={{0,8},{8,0},{1,9},{9,1},{2,10},{10,2},{3,11},{11,3},{4,12},{12,4},... | collective-permute-start | bytes 1179656 | tf_op jit(solution)/shard_map/ppermute | solution.py:42
  89.7 35.4 %all-to-all-start = ((bf16[32,96,128]{2,1,0:T(8,128)(2,1)}), bf16[32,96,128]{2,1,0:T(8,128)(2,1)S(1)}, u32[]{:S(2)}, u32[]{:S(2)}) async-start(bf16[32,96,128]{2,1,0:T(8,128)(2,1)} %shard_map.101), calls=%async_computation | async-start | bytes 1572864 | tf_op jit(solution)/shard_map/all_to_all | solution.py:424
  (12 other events, 103.6 us)
Sparse Core Ops, SparseCore 0:
  10.7 29.5 all-gather.2
  42.1 29.5 all-gather.4

commit v12 on v9

--- a/solution.py
+++ b/solution.py
@@ -139,65 +139,91 @@
     out_ref[ROWS:, :ROWS] = digit.astype(F32).astype(BF16)
 
 
-def early_kernel(first, heat_log, shift, x, w_hbm, key, *refs):
-    refs, (total_ref, unit_ref, len_ref, key_ref, sum_ref, w, sem) = refs[:-7], refs[-7:]
-    copy = pltpu.make_async_copy(w_hbm, w, sem)
-    copy.start()
+def early_kernel(spot, heat_log, shift, xs, xt, ws_hbm, wt_hbm, key, *refs):
+    *blocks, own, rows_ref, total_ref, unit_img, len_img, unit_txt, len_txt = refs[:-4]
+    key_ref, sum_ref, w, sems = refs[-4:]
+    copies = [
+        pltpu.make_async_copy(ws_hbm, w.at[0], sems.at[0]),
+        pltpu.make_async_copy(wt_hbm, w.at[1], sems.at[1]),
+    ]
+    for copy in copies:
+        copy.start()
     key_col = jnp.broadcast_to(key[...].astype(F32), (ROWS, ROWS)).T
     key_ref[...] = key_col
-
-    def norm():
-        copy.wait()
-        u = mm(x[...], w[...])
+    towers = ((xs, unit_img, len_img), (xt, unit_txt, len_txt))
+
+    def norm(t):
+        x, unit_ref, len_ref = towers[t]
+        copies[t].wait()
+        u = mm(x[...], w[t])
         length = lengths(u)
         unit_ref[...] = u / length
         len_ref[...] = jnp.broadcast_to(length, len_ref.shape)
 
-    if first:
-        blocks, (own, rows_ref) = refs[:-2], refs[-2:]
-        norm()
-        own[...] = unit_ref[...].astype(BF16)
-        pairs = pair_up(blocks, rows_ref)
-    else:
-        own, near_rows, far_rows, *blocks = refs
-        rows = [near_rows[0], near_rows[1], far_rows[0], far_rows[1], far_rows[2]]
-        pairs = [(block, row[0:1]) for block, row in zip(blocks, rows)]
+    norm(0)
+    own[...] = unit_img[...].astype(BF16)
     zero = jnp.zeros((ROWS, ROWS), F32)
     total, sums = add_tiles(
-        first,
+        True,
+        temperature(heat_log),
+        shift[0],
+        own[...],
+        key_col,
+        pair_up(blocks, rows_ref),
+        jnp.zeros((ROWS, WIDTH), F32),
+        [zero] * 3,
+    )
+    total_ref[...] = total
+    for k in range(3):
+        sum_ref[k] = sums[k]
+    norm(1)
+
+
+def early(spot, scal, features, weights, keys, blocks):
+    shapes = [(ROWS, WIDTH), (ROWS, LANES)]
+    shapes = [(ROWS, WIDTH), *shapes, *shapes, (ROWS, ROWS), (3, ROWS, ROWS)]
+    outs = [
+        jax.ShapeDtypeStruct((ROWS, WIDTH), BF16),
+        jax.ShapeDtypeStruct((len(blocks), 8, LANES), F32),
+    ] + [jax.ShapeDtypeStruct(shape, F32) for shape in shapes]
+    hbm = pl.BlockSpec(memory_space=pltpu.HBM)
+    return pl.pallas_call(
+        early_kernel,
+        in_specs=[SMEM] * 3 + [VMEM] * 2 + [hbm] * 2 + [VMEM] * (1 + len(blocks)),
+        out_specs=[VMEM] * len(outs),
+        out_shape=outs,
+        scratch_shapes=[pltpu.VMEM((2, WIDTH, WIDTH), BF16), pltpu.SemaphoreType.DMA((2,))],
+        compiler_params=params(56),
+        cost_estimate=cost(4 * 5 * ROWS * ROWS * WIDTH, 8 * 2**20),
+    )(spot, *scal, *features, *weights, keys, *blocks)
+
+
+def middle_kernel(heat_log, shift, own, key, near_rows, far_rows, *refs):
+    *blocks, total_ref = refs
+    rows = [near_rows[0], near_rows[1], far_rows[0], far_rows[1], far_rows[2]]
+    zero = jnp.zeros((ROWS, ROWS), F32)
+    total, _ = add_tiles(
+        False,
         temperature(heat_log),
         shift[0],
         own[:ROWS, :],
-        key_col,
-        pairs,
+        key[...],
+        [(block, row[0:1]) for block, row in zip(blocks, rows)],
         jnp.zeros((ROWS, WIDTH), F32),
         [zero] * 3,
     )
     total_ref[...] = total
-    for k in range(3):
-        sum_ref[k] = sums[k]
-    if not first:
-        norm()
-
-
-def early(first, scal, x, w, keys, blocks):
-    shapes = [(ROWS, WIDTH), (ROWS, WIDTH), (ROWS, LANES), (ROWS, ROWS), (3, ROWS, ROWS)]
-    outs = [jax.ShapeDtypeStruct(shape, F32) for shape in shapes]
-    if first:
-        outs = [
-            jax.ShapeDtypeStruct((ROWS, WIDTH), BF16),
-            jax.ShapeDtypeStruct((len(blocks), 8, LANES), F32),
-        ] + outs
-    hbm = pl.BlockSpec(memory_space=pltpu.HBM)
-    return pl.pallas_call(
-        functools.partial(early_kernel, first),
-        in_specs=[SMEM, SMEM, VMEM, hbm, VMEM] + [VMEM] * len(blocks),
-        out_specs=[VMEM] * len(outs),
-        out_shape=outs,
-        scratch_shapes=[pltpu.VMEM((WIDTH, WIDTH), BF16), pltpu.SemaphoreType.DMA],
+
+
+def middle(scal, *arrays):
+    return pl.pallas_call(
+        middle_kernel,
+        in_specs=[SMEM] * 2 + [VMEM] * len(arrays),
+        out_specs=VMEM,
+        out_shape=jax.ShapeDtypeStruct((ROWS, WIDTH), F32),
         compiler_params=params(56),
-        cost_estimate=cost(4 * 5 * ROWS * ROWS * WIDTH, 8 * 2**20),
-    )(*scal, x, w, keys, *blocks)
+        cost_estimate=cost(4 * 5 * ROWS * ROWS * WIDTH, 4 * 2**20),
+    )(*scal, *arrays)
 
 
 def late_kernel(with_stats, ways, count, spot, heat_log, shift, own, *refs):
@@ -218,7 +244,7 @@
         key[...],
         pairs,
         total_ref[...],
-        [acc[k] for k in range(3)],
+        [acc[k] for k in range(3)] if with_stats else [acc[...]] * 3,
     )
     total = total * heat
     u = unit[...]
@@ -380,7 +406,10 @@
     img_feat = lax.all_gather(after(pictures[0], txt), "dx", axis=0, tiled=True)
     txt_feat = lax.all_gather(after(sentences[0], txt), "dx", axis=0, tiled=True)
 
-    img, near_rows, *img_part = early(True, scal, pictures[0], picture_weights, keys, [txt, txt_c])
+    features = (pictures[0], sentences[0])
+    weights = (picture_weights, sentence_weights)
+    img, near_rows, *first = early(spot, scal, features, weights, keys, [txt, txt_c])
+    img_part = (*first[:3], *first[5:])
     txt_b = exchange(after(txt_a, txt_y1, txt_y2), "lz", 3)
     img_a = exchange(img, "lz", 1)
     img_c = exchange(after(img, txt_a, txt_y1, txt_y2), "lc", 1)
@@ -403,18 +432,14 @@
         True, ways, spot, scal, img, img_part, [txt_y1, txt_y2, txt_a, last]
     )
     img_cols = columns(img_outs)
-    txt_part = early(
-        False,
-        scal,
-        sentences[0],
-        sentence_weights,
-        keys,
-        [txt, near_rows, far_rows, img, img_c, img_y1, img_y2, img_a],
-    )
-    last = after(img_b, *img_cols, *txt_part)
+    txt_total = middle(
+        scal, txt, first[5], near_rows, far_rows, img, img_c, img_y1, img_y2, img_a
+    )
+    txt_part = (txt_total, *first[3:5], first[5], first[5])
+    last = after(img_b, txt_feat, *img_cols, txt_total)
     outs = late(False, ways, spot, scal, txt, txt_part, [far_rows, last])
     txt_cols = columns(outs)
-    img_kept, img_given = heads(True, spot, after(img_feat, outs[0], txt_feat), img_cols)
+    img_kept, img_given = heads(True, spot, after(img_feat, outs[0]), img_cols)
     img_taken = exchange(img_given, "lc", 1)
     txt_kept, txt_given = heads(False, spot, txt_feat, txt_cols)
     txt_taken = exchange(txt_given, "lc", 1)

time: 128 us -> 130 us (1.016)
  blocking collectives: 30.5 us -> 33.4 us
  local copies, waits for them, and re-layouts: 4.24 us -> 2.34 us
    all_to_all x1, blocking collectives: 30.5 us -> 33.4 us  [body(): sums = lax.all_to_all(sums, ('ly', 'lz', 'dz'), 0, 0, tiled=True)]
    unnamed x30, local copies, waits for them, and re-layouts: 4.24 us -> 2.34 us
  transfers between devices with their start and end apart: 20 -> 20, of which waited for: 7 -> 9; matrix products, arithmetic and copies ran while one was open for 1% -> 0% of each run, Pallas kernels for 17% -> 14%
where the time goes in v12:
time: 130 us; the launch traced here: 129 us
  blocking collectives  33.4 us (26%)
  starting transfers between devices  32.6 us (25%)
  Pallas kernels  26 us (20%)
  waiting for transfers between devices  18.9 us (15%)
  between operations  15.5 us (12%)
  local copies, waits for them, and re-layouts  2.34 us (2%)
    all_to_all x1, blocking collectives, body(): sums = lax.all_to_all(sums, ('ly', 'lz', 'dz'), 0, 0, tiled=True)  33.4 us
    ppermute x12, starting transfers between devices, exchange(): lax.ppermute(array, axis, [(i, i ^ apart) for i in range(lax.axis_size(ax...  22.3 us
    ppermute x12, waiting for transfers between devices, exchange(): lax.ppermute(array, axis, [(i, i ^ apart) for i in range(lax.axis_size(ax...  15.4 us
    ppermute x6, starting transfers between devices, turn(): lax.ppermute(array, axis, [(i, (i + step) % size) for i in range(size)])  10.3 us
    pallas_call x2, Pallas kernels, late(): pl.pallas_call(functools.partial(late_kernel, with_stats, ways, len(block...  7.56 us
    pallas_call x1, Pallas kernels, early(): pl.pallas_call(early_kernel, in_specs=[SMEM] * 3 + [VMEM] * 2 + [hbm] * 2...  6.03 us
    pallas_call x2, Pallas kernels, heads(): pl.pallas_call(functools.partial(head_kernel, with_stats), in_specs=[SMEM...  4.02 us
    pallas_call x1, Pallas kernels, middle(): pl.pallas_call(middle_kernel, in_specs=[SMEM] * 2 + [VMEM] * len(arrays),...  3.98 us
  transfers between devices with their start and end apart: 20, of which 9 were waited for; matrix products, arithmetic and copies ran while one was open for 0% of the time, Pallas kernels for 14%

profile of v12, /device:TPU:32, one launch (start us, length us, event | category | flops | bytes accessed | tf_op | source)
XLA Modules:
  0.0 129.4 jit_solution(7133133273380718388)
XLA Ops:
  7.2 3.4 %shard_map.94.refs_0_.own = bf16[144,1152]{1,0:T(8,128)(2,1)} custom-call(bf16[128,1152]{1,0:T(8,128)(2,1)} %bitcast.4, bf16[1152,1152]{1,0:T(8,128)(2,1)} %wt_hbm.1, s32[1,128]{1,0:T(1,128)} %key.1), custom_call_target="tpu_custom_call" | custom-call | flops 339738624 | bytes 4194304 | tf_op jit(solution)/shard_map/pallas_call | solution.py:81
  11.5 1.7 %collective-permute-start.1 = (bf16[144,1152]{1,0:T(8,128)(2,1)}, bf16[144,1152]{1,0:T(8,128)(2,1)S(1)}, u32[]{:S(2)}, u32[]{:S(2)}) collective-permute-start(bf16[144,1152]{1,0:T(8,128)(2,1)} %shard_map.94.refs_0_.own), channel_id=1, source_target_pairs={{0,64},{64,0},{128,192},{192,128},{1,65},{65,1},{129,193},{193,129... | collective-permute-start | bytes 995336 | tf_op jit(solution)/shard_map/ppermute | solution.py:41
  13.2 2.9 %collective-permute-start.2 = (bf16[144,1152]{1,0:T(8,128)(2,1)}, bf16[144,1152]{1,0:T(8,128)(2,1)S(1)}, u32[]{:S(2)}, u32[]{:S(2)}) collective-permute-start(bf16[144,1152]{1,0:T(8,128)(2,1)} %shard_map.94.refs_0_.own), channel_id=1, source_target_pairs={{0,128},{64,192},{128,0},{192,64},{1,129},{65,193},{129,1},{193,65... | collective-permute-start | bytes 995336 | tf_op jit(solution)/shard_map/ppermute | solution.py:41
  16.1 3.3 %collective-permute-start.3 = (bf16[144,1152]{1,0:T(8,128)(2,1)}, bf16[144,1152]{1,0:T(8,128)(2,1)S(1)}, u32[]{:S(2)}, u32[]{:S(2)}) collective-permute-start(bf16[144,1152]{1,0:T(8,128)(2,1)} %shard_map.94.refs_0_.own), channel_id=1, source_target_pairs={{0,16},{16,0},{32,48},{48,32},{1,17},{17,1},{33,49},{49,33},{2,18}... | collective-permute-start | bytes 995336 | tf_op jit(solution)/shard_map/ppermute | solution.py:41
  22.0 6.0 %shard_map.95 = (bf16[128,1152]{1,0:T(8,128)(2,1)}, f32[2,8,128]{2,1,0:T(8,128)}, f32[128,1152]{1,0:T(8,128)}, f32[128,1152]{1,0:T(8,128)}, f32[128,128]{1,0:T(8...) custom-call(s32[2]{0:T(128)} %pad_add_fusion.spot, ...), custom_call_target="tpu_custom_call" | custom-call | flops 377487360 | bytes 8388608 | tf_op jit(solution)/shard_map/pallas_call | solution.py:190
  28.0 3.5 %collective-permute-done.2.refs_6_ = bf16[144,1152]{1,0:T(8,128)(2,1)S(1)} collective-permute-done((bf16[144,1152]{1,0:T(8,128)(2,1)}, bf16[144,1152]{1,0:T(8,128)(2,1)S(1)}, u32[]{:S(2)}, u32[]{:S(2)}) %collective-permute-start.2) | collective-permute-done | bytes 331808 | tf_op jit(solution)/shard_map/ppermute | solution.py:41
  31.5 1.9 %collective-permute-done.3.refs_7_ = bf16[144,1152]{1,0:T(8,128)(2,1)S(1)} collective-permute-done((bf16[144,1152]{1,0:T(8,128)(2,1)}, bf16[144,1152]{1,0:T(8,128)(2,1)S(1)}, u32[]{:S(2)}, u32[]{:S(2)}) %collective-permute-start.3) | collective-permute-done | bytes 331808 | tf_op jit(solution)/shard_map/ppermute | solution.py:41
  33.4 3.4 %collective-permute-start.5 = (bf16[128,1152]{1,0:T(8,128)(2,1)}, bf16[128,1152]{1,0:T(8,128)(2,1)S(1)}, u32[]{:S(2)}, u32[]{:S(2)}) collective-permute-start(bf16[128,1152]{1,0:T(8,128)(2,1)} %get-tuple-element.43.own.refs_0_), channel_id=1, source_target_pairs={{0,16},{16,0},{32,48},{48,32},{1,17},{17,1},{33,49},{49,33},{2,18}... | collective-permute-start | bytes 884744 | tf_op jit(solution)/shard_map/ppermute | solution.py:41
  36.8 2.5 %collective-permute-start.4 = (bf16[144,1152]{1,0:T(8,128)(2,1)S(1)}, bf16[144,1152]{1,0:T(8,128)(2,1)S(1)}, u32[]{:S(2)}, u32[]{:S(2)}) collective-permute-start(bf16[144,1152]{1,0:T(8,128)(2,1)S(1)} %collective-permute-done.3.refs_7_), channel_id=1, source_target_pairs={{0,48},{16,32},{32,16},{48,0},{1,49},{17,33},{33,17},{49,1},{2,50}... | collective-permute-start | bytes 995336 | tf_op jit(solution)/shard_map/ppermute | solution.py:41
  39.5 1.5 %collective-permute-start.8 = (bf16[128,1152]{1,0:T(8,128)(2,1)}, bf16[128,1152]{1,0:T(8,128)(2,1)S(1)}, u32[]{:S(2)}, u32[]{:S(2)}) collective-permute-start(bf16[128,1152]{1,0:T(8,128)(2,1)} %get-tuple-element.43.own.refs_0_), channel_id=1, source_target_pairs={{0,128},{64,192},{128,0},{192,64},{1,129},{65,193},{129,1},{193,65... | collective-permute-start | bytes 884744 | tf_op jit(solution)/shard_map/ppermute | solution.py:41
  41.0 7.0 %collective-permute-done.5.refs_4_ = bf16[128,1152]{1,0:T(8,128)(2,1)S(1)} collective-permute-done((bf16[128,1152]{1,0:T(8,128)(2,1)}, bf16[128,1152]{1,0:T(8,128)(2,1)S(1)}, u32[]{:S(2)}, u32[]{:S(2)}) %collective-permute-start.5) | collective-permute-done | bytes 294944 | tf_op jit(solution)/shard_map/ppermute | solution.py:41
  48.0 6.5 %collective-permute-start.9 = (bf16[128,1152]{1,0:T(8,128)(2,1)S(1)}, bf16[128,1152]{1,0:T(8,128)(2,1)S(1)}, u32[]{:S(2)}, u32[]{:S(2)}) collective-permute-start(bf16[128,1152]{1,0:T(8,128)(2,1)S(1)} %collective-permute-done.5.refs_4_), channel_id=1, source_target_pairs={{0,48},{16,32},{32,16},{48,0},{1,49},{17,33},{33,17},{49,1},{2,50}... | collective-permute-start | bytes 884744 | tf_op jit(solution)/shard_map/ppermute | solution.py:41
  56.6 4.5 %shard_map.96 = (bf16[304,128]{1,0:T(8,128)(2,1)}, bf16[304,128]{1,0:T(8,128)(2,1)}, bf16[304,128]{1,0:T(8,128)(2,1)}, bf16[304,128]{1,0:T(8,128)(2,1)}, f32[4,8,128]{2,1,0:T(8,128)}) custom-call(s32[2]{0:T(128)} %pad_add_fusion.spot, f32[1]{0:T(128)S(6)} %copy.10.heat_log, f32[1]{0:T(128)S(6)} %copy.11.shift, ...), custom_call_target="tpu_custom_call" | custom-call | flops 150994944 | bytes 4194304 | tf_op jit(solution)/shard_map/pallas_call | solution.py:284
  61.1 1.6 %collective-permute-start.10 = (bf16[304,128]{1,0:T(8,128)(2,1)}, bf16[304,128]{1,0:T(8,128)(2,1)S(1)}, u32[]{:S(2)}, u32[]{:S(2)}) collective-permute-start(bf16[304,128]{1,0:T(8,128)(2,1)} %get-tuple-element.50), channel_id=1, source_target_pairs={{0,1},{1,2},{2,3},{3,0},{4,5},{5,6},{6,7},{7,4},{8,9},{9,10},{10,1... | collective-permute-start | bytes 233480 | tf_op jit(solution)/shard_map/ppermute | solution.py:425
  62.6 2.7 %collective-permute-start.11 = (bf16[304,128]{1,0:T(8,128)(2,1)}, bf16[304,128]{1,0:T(8,128)(2,1)S(1)}, u32[]{:S(2)}, u32[]{:S(2)}) collective-permute-start(bf16[304,128]{1,0:T(8,128)(2,1)} %get-tuple-element.51), channel_id=1, source_target_pairs={{0,2},{1,3},{2,0},{3,1},{4,6},{5,7},{6,4},{7,5},{8,10},{9,11},{10,... | collective-permute-start | bytes 233480 | tf_op jit(solution)/shard_map/ppermute | solution.py:425
  65.4 1.4 %collective-permute-start.12 = (bf16[304,128]{1,0:T(8,128)(2,1)}, bf16[304,128]{1,0:T(8,128)(2,1)S(1)}, u32[]{:S(2)}, u32[]{:S(2)}) collective-permute-start(bf16[304,128]{1,0:T(8,128)(2,1)} %get-tuple-element.52), channel_id=1, source_target_pairs={{0,3},{1,0},{2,1},{3,2},{4,7},{5,4},{6,5},{7,6},{8,11},{9,8},{10,9... | collective-permute-start | bytes 233480 | tf_op jit(solution)/shard_map/ppermute | solution.py:425
  66.8 4.0 %shard_map.97.refs_0_ = f32[128,1152]{1,0:T(8,128)} custom-call(f32[1]{0:T(128)S(6)} %copy.10.heat_log, f32[1]{0:T(128)S(6)} %copy.11.shift, bf16[144,1152]{1,0:T(8,128)(2,1)} %shard_map.94.refs_0_.own, f32[128,128]{1,0:T(8,128)} %get-tuple-element.34.refs_3_.key.refs_4_, f32[2,8,128]{2,1,0:T(8,128)} %get-tuple-element.35.near_rows, ...), custom_call_target="tpu_custom_call" | custom-call | flops 377487360 | bytes 4194304 | tf_op jit(solution)/shard_map/pallas_call | solution.py:219
  71.8 3.1 %shard_map.98 = (bf16[288,128]{1,0:T(8,128)(2,1)}, bf16[288,128]{1,0:T(8,128)(2,1)}, bf16[288,128]{1,0:T(8,128)(2,1)}, bf16[288,128]{1,0:T(8,128)(2,1)}) custom-call(s32[2]{0:T(128)} %pad_add_fusion.spot, f32[1]{0:T(128)S(6)} %copy.10.heat_log, f32[1]{0:T(128)S(6)} %copy.11.shift, bf16[144,1152]{1,0:T(8,128)(2,1)} %shard_map.94.refs_0_.own, ...), custom_call_target="tpu_custom_call" | custom-call | flops 150994944 | bytes 4194304 | tf_op jit(solution)/shard_map/pallas_call | solution.py:284
  74.9 1.4 %collective-permute-start.14 = (bf16[288,128]{1,0:T(8,128)(2,1)}, bf16[288,128]{1,0:T(8,128)(2,1)S(1)}, u32[]{:S(2)}, u32[]{:S(2)}) collective-permute-start(bf16[288,128]{1,0:T(8,128)(2,1)} %get-tuple-element.58), channel_id=1, source_target_pairs={{0,1},{1,2},{2,3},{3,0},{4,5},{5,6},{6,7},{7,4},{8,9},{9,10},{10,1... | collective-permute-start | bytes 221192 | tf_op jit(solution)/shard_map/ppermute | solution.py:425
  76.3 2.5 %collective-permute-start.15 = (bf16[288,128]{1,0:T(8,128)(2,1)}, bf16[288,128]{1,0:T(8,128)(2,1)S(1)}, u32[]{:S(2)}, u32[]{:S(2)}) collective-permute-start(bf16[288,128]{1,0:T(8,128)(2,1)} %get-tuple-element.59), channel_id=1, source_target_pairs={{0,2},{1,3},{2,0},{3,1},{4,6},{5,7},{6,4},{7,5},{8,10},{9,11},{10,... | collective-permute-start | bytes 221192 | tf_op jit(solution)/shard_map/ppermute | solution.py:425
  79.4 2.0 %shard_map.99 = (f32[32,48,128]{2,1,0:T(8,128)S(1)}, bf16[32,48,128]{2,1,0:T(8,128)(2,1)S(1)}) custom-call(s32[2]{0:T(128)S(1)} %copy-done.4, bf16[512,1152]{1,0:T(8,128)(2,1)S(1)} %copy-done.1, bf16[304,128]{1,0:T(8,128)(2,1)S(1)} %copy-done.2, bf16[304,128]{1,0:T(8,128)(2,1)S(1)} %collective-permute-done.10.refs_1_, ...), custom_call_target="tpu_custom_call" | custom-call | flops 339738624 | bytes 4194304 | tf_op jit(solution)/shard_map/pallas_call | solution.py:344
  84.3 2.0 %shard_map.100 = (f32[32,48,128]{2,1,0:T(8,128)S(1)}, bf16[32,48,128]{2,1,0:T(8,128)(2,1)S(1)}) custom-call(s32[2]{0:T(128)S(1)} %copy-done.4, bf16[512,1152]{1,0:T(8,128)(2,1)S(1)} %copy-done, bf16[288,128]{1,0:T(8,128)(2,1)S(1)} %copy-done.3, bf16[288,128]{1,0:T(8,128)(2,1)S(1)} %collective-permute-done.14.refs_1_, ...), custom_call_target="tpu_custom_call" | custom-call | flops 339738624 | bytes 4194304 | tf_op jit(solution)/shard_map/pallas_call | solution.py:344
  86.4 1.7 %collective-permute-done.17.taken_txt = bf16[32,48,128]{2,1,0:T(8,128)(2,1)S(1)} collective-permute-done((bf16[32,48,128]{2,1,0:T(8,128)(2,1)S(1)}, bf16[32,48,128]{2,1,0:T(8,128)(2,1)S(1)}, u32[]{:S(2)}, u32[]{:S(2)}) %collective-permute-start.17) | collective-permute-done | bytes 393248 | tf_op jit(solution)/shard_map/ppermute | solution.py:41
  88.2 33.4 %all_to_all.5.parts = bf16[32,96,128]{2,1,0:T(8,128)(2,1)S(1)} all-to-all(bf16[32,96,128]{2,1,0:T(8,128)(2,1)S(1)} %shard_map.101), channel_id=1, replica_groups=mesh['ly'=4,'lz'=4,'lc'=2,'dz'=2,'dx'=4] {'ly','lz','dz'}, dimensions={0} | all-to-all | bytes 1572864 | tf_op jit(solution)/shard_map/all_to_all | solution.py:447
  (59 shorter events, 9.9 us)
Async XLA Ops:
  7.2 48.7 %all-gather.3.cloned.1.call-start = ((), (), s32[]{:S(2)}) async-start(), calls=%async_computation.1 | async-start | bytes 1474560 | tf_op jit(solution)/shard_map/all_gather | solution.py:406
  10.6 60.9 %all-gather.5.cloned.1.call-start = ((), (), s32[]{:S(2)}) async-start(), calls=%async_computation.2 | async-start | bytes 1474560 | tf_op jit(solution)/shard_map/all_gather | solution.py:407
  11.4 9.8 %collective-permute-start = (bf16[144,1152]{1,0:T(8,128)(2,1)}, bf16[144,1152]{1,0:T(8,128)(2,1)S(1)}, u32[]{:S(2)}, u32[]{:S(2)}) collective-permute-start(bf16[144,1152]{1,0:T(8,128)(2,1)} %shard_map.94.refs_0_.own), channel_id=1, source_target_pairs={{0,8},{8,0},{1,9},{9,1},{2,10},{10,2},{3,11},{11,3},{4,12},{12,4},... | collective-permute-start | bytes 995336 | tf_op jit(solution)/shard_map/ppermute | solution.py:41
  11.5 16.5 %collective-permute-start.1 = (bf16[144,1152]{1,0:T(8,128)(2,1)}, bf16[144,1152]{1,0:T(8,128)(2,1)S(1)}, u32[]{:S(2)}, u32[]{:S(2)}) collective-permute-start(bf16[144,1152]{1,0:T(8,128)(2,1)} %shard_map.94.refs_0_.own), channel_id=1, source_target_pairs={{0,64},{64,0},{128,192},{192,128},{1,65},{65,1},{129,193},{193,129... | collective-permute-start | bytes 995336 | tf_op jit(solution)/shard_map/ppermute | solution.py:41
  13.2 18.3 %collective-permute-start.2 = (bf16[144,1152]{1,0:T(8,128)(2,1)}, bf16[144,1152]{1,0:T(8,128)(2,1)S(1)}, u32[]{:S(2)}, u32[]{:S(2)}) collective-permute-start(bf16[144,1152]{1,0:T(8,128)(2,1)} %shard_map.94.refs_0_.own), channel_id=1, source_target_pairs={{0,128},{64,192},{128,0},{192,64},{1,129},{65,193},{129,1},{193,65... | collective-permute-start | bytes 995336 | tf_op jit(solution)/shard_map/ppermute | solution.py:41
  16.1 17.3 %collective-permute-start.3 = (bf16[144,1152]{1,0:T(8,128)(2,1)}, bf16[144,1152]{1,0:T(8,128)(2,1)S(1)}, u32[]{:S(2)}, u32[]{:S(2)}) collective-permute-start(bf16[144,1152]{1,0:T(8,128)(2,1)} %shard_map.94.refs_0_.own), channel_id=1, source_target_pairs={{0,16},{16,0},{32,48},{48,32},{1,17},{17,1},{33,49},{49,33},{2,18}... | collective-permute-start | bytes 995336 | tf_op jit(solution)/shard_map/ppermute | solution.py:41
  28.0 27.9 %copy-start.5 = (bf16[144,1152]{1,0:T(8,128)(2,1)}, bf16[144,1152]{1,0:T(8,128)(2,1)S(1)}, u32[]{:S(2)}) copy-start(bf16[144,1152]{1,0:T(8,128)(2,1)S(1)} %collective-permute-done.1.refs_5_) | copy-start | bytes 995332
  31.5 24.4 %copy-start.6 = (bf16[144,1152]{1,0:T(8,128)(2,1)}, bf16[144,1152]{1,0:T(8,128)(2,1)S(1)}, u32[]{:S(2)}) copy-start(bf16[144,1152]{1,0:T(8,128)(2,1)S(1)} %collective-permute-done.2.refs_6_) | copy-start | bytes 995332
  33.4 22.5 %copy-start.7 = (bf16[144,1152]{1,0:T(8,128)(2,1)}, bf16[144,1152]{1,0:T(8,128)(2,1)S(1)}, u32[]{:S(2)}) copy-start(bf16[144,1152]{1,0:T(8,128)(2,1)S(1)} %collective-permute-done.3.refs_7_) | copy-start | bytes 995332
  33.4 6.0 %collective-permute-start.6 = (bf16[128,1152]{1,0:T(8,128)(2,1)}, bf16[128,1152]{1,0:T(8,128)(2,1)S(1)}, u32[]{:S(2)}, u32[]{:S(2)}) collective-permute-start(bf16[128,1152]{1,0:T(8,128)(2,1)} %get-tuple-element.43.own.refs_0_), channel_id=1, source_target_pairs={{0,8},{8,0},{1,9},{9,1},{2,10},{10,2},{3,11},{11,3},{4,12},{12,4},... | collective-permute-start | bytes 884744 | tf_op jit(solution)/shard_map/ppermute | solution.py:41
  33.4 14.6 %collective-permute-start.5 = (bf16[128,1152]{1,0:T(8,128)(2,1)}, bf16[128,1152]{1,0:T(8,128)(2,1)S(1)}, u32[]{:S(2)}, u32[]{:S(2)}) collective-permute-start(bf16[128,1152]{1,0:T(8,128)(2,1)} %get-tuple-element.43.own.refs_0_), channel_id=1, source_target_pairs={{0,16},{16,0},{32,48},{48,32},{1,17},{17,1},{33,49},{49,33},{2,18}... | collective-permute-start | bytes 884744 | tf_op jit(solution)/shard_map/ppermute | solution.py:41
  36.8 19.0 %collective-permute-start.4 = (bf16[144,1152]{1,0:T(8,128)(2,1)S(1)}, bf16[144,1152]{1,0:T(8,128)(2,1)S(1)}, u32[]{:S(2)}, u32[]{:S(2)}) collective-permute-start(bf16[144,1152]{1,0:T(8,128)(2,1)S(1)} %collective-permute-done.3.refs_7_), channel_id=1, source_target_pairs={{0,48},{16,32},{32,16},{48,0},{1,49},{17,33},{33,17},{49,1},{2,50}... | collective-permute-start | bytes 995336 | tf_op jit(solution)/shard_map/ppermute | solution.py:41
  39.4 27.5 %copy-start.10 = (bf16[128,1152]{1,0:T(8,128)(2,1)}, bf16[128,1152]{1,0:T(8,128)(2,1)S(1)}, u32[]{:S(2)}) copy-start(bf16[128,1152]{1,0:T(8,128)(2,1)S(1)} %collective-permute-done.6.refs_1_) | copy-start | bytes 884740
  39.4 16.5 %collective-permute-start.7 = (bf16[128,1152]{1,0:T(8,128)(2,1)}, bf16[128,1152]{1,0:T(8,128)(2,1)S(1)}, u32[]{:S(2)}, u32[]{:S(2)}) collective-permute-start(bf16[128,1152]{1,0:T(8,128)(2,1)} %get-tuple-element.43.own.refs_0_), channel_id=1, source_target_pairs={{0,64},{64,0},{128,192},{192,128},{1,65},{65,1},{129,193},{193,129... | collective-permute-start | bytes 884744 | tf_op jit(solution)/shard_map/ppermute | solution.py:41
  39.5 16.3 %collective-permute-start.8 = (bf16[128,1152]{1,0:T(8,128)(2,1)}, bf16[128,1152]{1,0:T(8,128)(2,1)S(1)}, u32[]{:S(2)}, u32[]{:S(2)}) collective-permute-start(bf16[128,1152]{1,0:T(8,128)(2,1)} %get-tuple-element.43.own.refs_0_), channel_id=1, source_target_pairs={{0,128},{64,192},{128,0},{192,64},{1,129},{65,193},{129,1},{193,65... | collective-permute-start | bytes 884744 | tf_op jit(solution)/shard_map/ppermute | solution.py:41
  48.0 22.8 %collective-permute-start.9 = (bf16[128,1152]{1,0:T(8,128)(2,1)S(1)}, bf16[128,1152]{1,0:T(8,128)(2,1)S(1)}, u32[]{:S(2)}, u32[]{:S(2)}) collective-permute-start(bf16[128,1152]{1,0:T(8,128)(2,1)S(1)} %collective-permute-done.5.refs_4_), channel_id=1, source_target_pairs={{0,48},{16,32},{32,16},{48,0},{1,49},{17,33},{33,17},{49,1},{2,50}... | collective-permute-start | bytes 884744 | tf_op jit(solution)/shard_map/ppermute | solution.py:41
  61.1 10.5 %collective-permute-start.10 = (bf16[304,128]{1,0:T(8,128)(2,1)}, bf16[304,128]{1,0:T(8,128)(2,1)S(1)}, u32[]{:S(2)}, u32[]{:S(2)}) collective-permute-start(bf16[304,128]{1,0:T(8,128)(2,1)} %get-tuple-element.50), channel_id=1, source_target_pairs={{0,1},{1,2},{2,3},{3,0},{4,5},{5,6},{6,7},{7,4},{8,9},{9,10},{10,1... | collective-permute-start | bytes 233480 | tf_op jit(solution)/shard_map/ppermute | solution.py:425
  62.6 9.2 %collective-permute-start.11 = (bf16[304,128]{1,0:T(8,128)(2,1)}, bf16[304,128]{1,0:T(8,128)(2,1)S(1)}, u32[]{:S(2)}, u32[]{:S(2)}) collective-permute-start(bf16[304,128]{1,0:T(8,128)(2,1)} %get-tuple-element.51), channel_id=1, source_target_pairs={{0,2},{1,3},{2,0},{3,1},{4,6},{5,7},{6,4},{7,5},{8,10},{9,11},{10,... | collective-permute-start | bytes 233480 | tf_op jit(solution)/shard_map/ppermute | solution.py:425
  65.4 6.5 %collective-permute-start.12 = (bf16[304,128]{1,0:T(8,128)(2,1)}, bf16[304,128]{1,0:T(8,128)(2,1)S(1)}, u32[]{:S(2)}, u32[]{:S(2)}) collective-permute-start(bf16[304,128]{1,0:T(8,128)(2,1)} %get-tuple-element.52), channel_id=1, source_target_pairs={{0,3},{1,0},{2,1},{3,2},{4,7},{5,4},{6,5},{7,6},{8,11},{9,8},{10,9... | collective-permute-start | bytes 233480 | tf_op jit(solution)/shard_map/ppermute | solution.py:425
  74.9 6.7 %collective-permute-start.14 = (bf16[288,128]{1,0:T(8,128)(2,1)}, bf16[288,128]{1,0:T(8,128)(2,1)S(1)}, u32[]{:S(2)}, u32[]{:S(2)}) collective-permute-start(bf16[288,128]{1,0:T(8,128)(2,1)} %get-tuple-element.58), channel_id=1, source_target_pairs={{0,1},{1,2},{2,3},{3,0},{4,5},{5,6},{6,7},{7,4},{8,9},{9,10},{10,1... | collective-permute-start | bytes 221192 | tf_op jit(solution)/shard_map/ppermute | solution.py:425
  76.3 6.1 %collective-permute-start.15 = (bf16[288,128]{1,0:T(8,128)(2,1)}, bf16[288,128]{1,0:T(8,128)(2,1)S(1)}, u32[]{:S(2)}, u32[]{:S(2)}) collective-permute-start(bf16[288,128]{1,0:T(8,128)(2,1)} %get-tuple-element.59), channel_id=1, source_target_pairs={{0,2},{1,3},{2,0},{3,1},{4,6},{5,7},{6,4},{7,5},{8,10},{9,11},{10,... | collective-permute-start | bytes 221192 | tf_op jit(solution)/shard_map/ppermute | solution.py:425
  78.8 4.6 %collective-permute-start.16 = (bf16[288,128]{1,0:T(8,128)(2,1)}, bf16[288,128]{1,0:T(8,128)(2,1)S(1)}, u32[]{:S(2)}, u32[]{:S(2)}) collective-permute-start(bf16[288,128]{1,0:T(8,128)(2,1)} %get-tuple-element.60), channel_id=1, source_target_pairs={{0,3},{1,0},{2,1},{3,2},{4,7},{5,4},{6,5},{7,6},{8,11},{9,8},{10,9... | collective-permute-start | bytes 221192 | tf_op jit(solution)/shard_map/ppermute | solution.py:425
  81.5 4.9 %collective-permute-start.13 = (bf16[32,48,128]{2,1,0:T(8,128)(2,1)S(1)}, bf16[32,48,128]{2,1,0:T(8,128)(2,1)S(1)}, u32[]{:S(2)}, u32[]{:S(2)}) collective-permute-start(bf16[32,48,128]{2,1,0:T(8,128)(2,1)S(1)} %get-tuple-element.57), channel_id=1, source_target_pairs={{0,8},{8,0},{1,9},{9,1},{2,10},{10,2},{3,11},{11,3},{4,12},{12,4},... | collective-permute-start | bytes 1179656 | tf_op jit(solution)/shard_map/ppermute | solution.py:41
  86.3 1.8 %collective-permute-start.17 = (bf16[32,48,128]{2,1,0:T(8,128)(2,1)S(1)}, bf16[32,48,128]{2,1,0:T(8,128)(2,1)S(1)}, u32[]{:S(2)}, u32[]{:S(2)}) collective-permute-start(bf16[32,48,128]{2,1,0:T(8,128)(2,1)S(1)} %get-tuple-element.62), channel_id=1, source_target_pairs={{0,8},{8,0},{1,9},{9,1},{2,10},{10,2},{3,11},{11,3},{4,12},{12,4},... | collective-permute-start | bytes 1179656 | tf_op jit(solution)/shard_map/ppermute | solution.py:41
  (11 other events, 111.2 us)
Sparse Core Ops, SparseCore 0:
  10.8 29.5 all-gather.2
  42.1 29.3 all-gather.4

commit v13 on v12

--- a/solution.py
+++ b/solution.py
@@ -436,10 +436,10 @@
         scal, txt, first[5], near_rows, far_rows, img, img_c, img_y1, img_y2, img_a
     )
     txt_part = (txt_total, *first[3:5], first[5], first[5])
-    last = after(img_b, txt_feat, *img_cols, txt_total)
+    last = after(img_b, *img_cols, txt_total)
     outs = late(False, ways, spot, scal, txt, txt_part, [far_rows, last])
     txt_cols = columns(outs)
-    img_kept, img_given = heads(True, spot, after(img_feat, outs[0]), img_cols)
+    img_kept, img_given = heads(True, spot, after(img_feat, outs[0], txt_feat), img_cols)
     img_taken = exchange(img_given, "lc", 1)
     txt_kept, txt_given = heads(False, spot, txt_feat, txt_cols)
     txt_taken = exchange(txt_given, "lc", 1)

time: 130 us -> 128 us (0.985)
  blocking collectives: 33.4 us -> 30.6 us
    all_to_all x1, blocking collectives: 33.4 us -> 30.6 us  [body(): sums = lax.all_to_all(sums, ('ly', 'lz', 'dz'), 0, 0, tiled=True)]
  transfers between devices with their start and end apart: 20 -> 20, of which waited for: 9 -> 8; matrix products, arithmetic and copies ran while one was open for 0% -> 0% of each run, Pallas kernels for 14% -> 17%
where the time goes in v13:
time: 128 us
  starting transfers between devices  32.6 us (25%)
  blocking collectives  30.6 us (24%)
  Pallas kernels  26 us (20%)
  waiting for transfers between devices  18.5 us (14%)
  between operations  15.5 us (12%)
  local copies, waits for them, and re-layouts  3.6 us (3%)
    all_to_all x1, blocking collectives, body(): sums = lax.all_to_all(sums, ('ly', 'lz', 'dz'), 0, 0, tiled=True)  30.6 us
    ppermute x12, starting transfers between devices, exchange(): lax.ppermute(array, axis, [(i, i ^ apart) for i in range(lax.axis_size(ax...  22.3 us
    ppermute x12, waiting for transfers between devices, exchange(): lax.ppermute(array, axis, [(i, i ^ apart) for i in range(lax.axis_size(ax...  15.4 us
    ppermute x6, starting transfers between devices, turn(): lax.ppermute(array, axis, [(i, (i + step) % size) for i in range(size)])  10.3 us
    pallas_call x2, Pallas kernels, late(): pl.pallas_call(functools.partial(late_kernel, with_stats, ways, len(block...  7.52 us
    pallas_call x1, Pallas kernels, early(): pl.pallas_call(early_kernel, in_specs=[SMEM] * 3 + [VMEM] * 2 + [hbm] * 2...  6.03 us
    pallas_call x2, Pallas kernels, heads(): pl.pallas_call(functools.partial(head_kernel, with_stats), in_specs=[SMEM...  4.03 us
    pallas_call x1, Pallas kernels, middle(): pl.pallas_call(middle_kernel, in_specs=[SMEM] * 2 + [VMEM] * len(arrays),...  3.98 us
  transfers between devices with their start and end apart: 20, of which 8 were waited for; matrix products, arithmetic and copies ran while one was open for 0% of the time, Pallas kernels for 17%

profile of v13, /device:TPU:32, one launch (start us, length us, event | category | flops | bytes accessed | tf_op | source)
XLA Modules:
  0.0 127.5 jit_solution(4797400028567683559)
XLA Ops:
  7.2 3.4 %shard_map.94.refs_0_.own = bf16[144,1152]{1,0:T(8,128)(2,1)} custom-call(bf16[128,1152]{1,0:T(8,128)(2,1)} %bitcast.4, bf16[1152,1152]{1,0:T(8,128)(2,1)} %wt_hbm.1, s32[1,128]{1,0:T(1,128)} %key.1), custom_call_target="tpu_custom_call" | custom-call | flops 339738624 | bytes 4194304 | tf_op jit(solution)/shard_map/pallas_call | solution.py:81
  11.5 1.7 %collective-permute-start.1 = (bf16[144,1152]{1,0:T(8,128)(2,1)}, bf16[144,1152]{1,0:T(8,128)(2,1)S(1)}, u32[]{:S(2)}, u32[]{:S(2)}) collective-permute-start(bf16[144,1152]{1,0:T(8,128)(2,1)} %shard_map.94.refs_0_.own), channel_id=1, source_target_pairs={{0,64},{64,0},{128,192},{192,128},{1,65},{65,1},{129,193},{193,129... | collective-permute-start | bytes 995336 | tf_op jit(solution)/shard_map/ppermute | solution.py:41
  13.2 2.9 %collective-permute-start.2 = (bf16[144,1152]{1,0:T(8,128)(2,1)}, bf16[144,1152]{1,0:T(8,128)(2,1)S(1)}, u32[]{:S(2)}, u32[]{:S(2)}) collective-permute-start(bf16[144,1152]{1,0:T(8,128)(2,1)} %shard_map.94.refs_0_.own), channel_id=1, source_target_pairs={{0,128},{64,192},{128,0},{192,64},{1,129},{65,193},{129,1},{193,65... | collective-permute-start | bytes 995336 | tf_op jit(solution)/shard_map/ppermute | solution.py:41
  16.1 3.3 %collective-permute-start.3 = (bf16[144,1152]{1,0:T(8,128)(2,1)}, bf16[144,1152]{1,0:T(8,128)(2,1)S(1)}, u32[]{:S(2)}, u32[]{:S(2)}) collective-permute-start(bf16[144,1152]{1,0:T(8,128)(2,1)} %shard_map.94.refs_0_.own), channel_id=1, source_target_pairs={{0,16},{16,0},{32,48},{48,32},{1,17},{17,1},{33,49},{49,33},{2,18}... | collective-permute-start | bytes 995336 | tf_op jit(solution)/shard_map/ppermute | solution.py:41
  22.0 6.0 %shard_map.95 = (bf16[128,1152]{1,0:T(8,128)(2,1)}, f32[2,8,128]{2,1,0:T(8,128)}, f32[128,1152]{1,0:T(8,128)}, f32[128,1152]{1,0:T(8,128)}, f32[128,128]{1,0:T(8...) custom-call(s32[2]{0:T(128)} %pad_add_fusion.spot, ...), custom_call_target="tpu_custom_call" | custom-call | flops 377487360 | bytes 8388608 | tf_op jit(solution)/shard_map/pallas_call | solution.py:190
  28.0 3.5 %collective-permute-done.2.refs_6_ = bf16[144,1152]{1,0:T(8,128)(2,1)S(1)} collective-permute-done((bf16[144,1152]{1,0:T(8,128)(2,1)}, bf16[144,1152]{1,0:T(8,128)(2,1)S(1)}, u32[]{:S(2)}, u32[]{:S(2)}) %collective-permute-start.2) | collective-permute-done | bytes 331808 | tf_op jit(solution)/shard_map/ppermute | solution.py:41
  31.5 1.9 %collective-permute-done.3.refs_7_ = bf16[144,1152]{1,0:T(8,128)(2,1)S(1)} collective-permute-done((bf16[144,1152]{1,0:T(8,128)(2,1)}, bf16[144,1152]{1,0:T(8,128)(2,1)S(1)}, u32[]{:S(2)}, u32[]{:S(2)}) %collective-permute-start.3) | collective-permute-done | bytes 331808 | tf_op jit(solution)/shard_map/ppermute | solution.py:41
  33.4 3.4 %collective-permute-start.5 = (bf16[128,1152]{1,0:T(8,128)(2,1)}, bf16[128,1152]{1,0:T(8,128)(2,1)S(1)}, u32[]{:S(2)}, u32[]{:S(2)}) collective-permute-start(bf16[128,1152]{1,0:T(8,128)(2,1)} %get-tuple-element.43.own.refs_0_), channel_id=1, source_target_pairs={{0,16},{16,0},{32,48},{48,32},{1,17},{17,1},{33,49},{49,33},{2,18}... | collective-permute-start | bytes 884744 | tf_op jit(solution)/shard_map/ppermute | solution.py:41
  36.8 2.5 %collective-permute-start.4 = (bf16[144,1152]{1,0:T(8,128)(2,1)S(1)}, bf16[144,1152]{1,0:T(8,128)(2,1)S(1)}, u32[]{:S(2)}, u32[]{:S(2)}) collective-permute-start(bf16[144,1152]{1,0:T(8,128)(2,1)S(1)} %collective-permute-done.3.refs_7_), channel_id=1, source_target_pairs={{0,48},{16,32},{32,16},{48,0},{1,49},{17,33},{33,17},{49,1},{2,50}... | collective-permute-start | bytes 995336 | tf_op jit(solution)/shard_map/ppermute | solution.py:41
  39.5 1.5 %collective-permute-start.8 = (bf16[128,1152]{1,0:T(8,128)(2,1)}, bf16[128,1152]{1,0:T(8,128)(2,1)S(1)}, u32[]{:S(2)}, u32[]{:S(2)}) collective-permute-start(bf16[128,1152]{1,0:T(8,128)(2,1)} %get-tuple-element.43.own.refs_0_), channel_id=1, source_target_pairs={{0,128},{64,192},{128,0},{192,64},{1,129},{65,193},{129,1},{193,65... | collective-permute-start | bytes 884744 | tf_op jit(solution)/shard_map/ppermute | solution.py:41
  41.0 7.0 %collective-permute-done.5.refs_4_ = bf16[128,1152]{1,0:T(8,128)(2,1)S(1)} collective-permute-done((bf16[128,1152]{1,0:T(8,128)(2,1)}, bf16[128,1152]{1,0:T(8,128)(2,1)S(1)}, u32[]{:S(2)}, u32[]{:S(2)}) %collective-permute-start.5) | collective-permute-done | bytes 294944 | tf_op jit(solution)/shard_map/ppermute | solution.py:41
  48.0 6.5 %collective-permute-start.9 = (bf16[128,1152]{1,0:T(8,128)(2,1)S(1)}, bf16[128,1152]{1,0:T(8,128)(2,1)S(1)}, u32[]{:S(2)}, u32[]{:S(2)}) collective-permute-start(bf16[128,1152]{1,0:T(8,128)(2,1)S(1)} %collective-permute-done.5.refs_4_), channel_id=1, source_target_pairs={{0,48},{16,32},{32,16},{48,0},{1,49},{17,33},{33,17},{49,1},{2,50}... | collective-permute-start | bytes 884744 | tf_op jit(solution)/shard_map/ppermute | solution.py:41
  54.5 1.3 %collective-permute-done.4.refs_8_ = bf16[144,1152]{1,0:T(8,128)(2,1)S(1)} collective-permute-done((bf16[144,1152]{1,0:T(8,128)(2,1)S(1)}, bf16[144,1152]{1,0:T(8,128)(2,1)S(1)}, u32[]{:S(2)}, u32[]{:S(2)}) %collective-permute-start.4) | collective-permute-done | bytes 331808 | tf_op jit(solution)/shard_map/ppermute | solution.py:41
  56.6 4.5 %shard_map.96 = (bf16[304,128]{1,0:T(8,128)(2,1)}, bf16[304,128]{1,0:T(8,128)(2,1)}, bf16[304,128]{1,0:T(8,128)(2,1)}, bf16[304,128]{1,0:T(8,128)(2,1)}, f32[4,8,128]{2,1,0:T(8,128)}) custom-call(s32[2]{0:T(128)} %pad_add_fusion.spot, f32[1]{0:T(128)S(6)} %copy.10.heat_log, f32[1]{0:T(128)S(6)} %copy.11.shift, ...), custom_call_target="tpu_custom_call" | custom-call | flops 150994944 | bytes 4194304 | tf_op jit(solution)/shard_map/pallas_call | solution.py:284
  61.1 1.6 %collective-permute-start.10 = (bf16[304,128]{1,0:T(8,128)(2,1)}, bf16[304,128]{1,0:T(8,128)(2,1)S(1)}, u32[]{:S(2)}, u32[]{:S(2)}) collective-permute-start(bf16[304,128]{1,0:T(8,128)(2,1)} %get-tuple-element.49), channel_id=1, source_target_pairs={{0,1},{1,2},{2,3},{3,0},{4,5},{5,6},{6,7},{7,4},{8,9},{9,10},{10,1... | collective-permute-start | bytes 233480 | tf_op jit(solution)/shard_map/ppermute | solution.py:425
  62.6 2.7 %collective-permute-start.11 = (bf16[304,128]{1,0:T(8,128)(2,1)}, bf16[304,128]{1,0:T(8,128)(2,1)S(1)}, u32[]{:S(2)}, u32[]{:S(2)}) collective-permute-start(bf16[304,128]{1,0:T(8,128)(2,1)} %get-tuple-element.50), channel_id=1, source_target_pairs={{0,2},{1,3},{2,0},{3,1},{4,6},{5,7},{6,4},{7,5},{8,10},{9,11},{10,... | collective-permute-start | bytes 233480 | tf_op jit(solution)/shard_map/ppermute | solution.py:425
  65.4 1.4 %collective-permute-start.12 = (bf16[304,128]{1,0:T(8,128)(2,1)}, bf16[304,128]{1,0:T(8,128)(2,1)S(1)}, u32[]{:S(2)}, u32[]{:S(2)}) collective-permute-start(bf16[304,128]{1,0:T(8,128)(2,1)} %get-tuple-element.51), channel_id=1, source_target_pairs={{0,3},{1,0},{2,1},{3,2},{4,7},{5,4},{6,5},{7,6},{8,11},{9,8},{10,9... | collective-permute-start | bytes 233480 | tf_op jit(solution)/shard_map/ppermute | solution.py:425
  66.8 4.0 %shard_map.97.refs_0_ = f32[128,1152]{1,0:T(8,128)} custom-call(f32[1]{0:T(128)S(6)} %copy.10.heat_log, f32[1]{0:T(128)S(6)} %copy.11.shift, bf16[144,1152]{1,0:T(8,128)(2,1)} %shard_map.94.refs_0_.own, f32[128,128]{1,0:T(8,128)} %get-tuple-element.34.refs_3_.key.refs_4_, f32[2,8,128]{2,1,0:T(8,128)} %get-tuple-element.35.near_rows, ...), custom_call_target="tpu_custom_call" | custom-call | flops 377487360 | bytes 4194304 | tf_op jit(solution)/shard_map/pallas_call | solution.py:219
  71.8 3.0 %shard_map.98 = (bf16[288,128]{1,0:T(8,128)(2,1)}, bf16[288,128]{1,0:T(8,128)(2,1)}, bf16[288,128]{1,0:T(8,128)(2,1)}, bf16[288,128]{1,0:T(8,128)(2,1)}) custom-call(s32[2]{0:T(128)} %pad_add_fusion.spot, f32[1]{0:T(128)S(6)} %copy.10.heat_log, f32[1]{0:T(128)S(6)} %copy.11.shift, bf16[144,1152]{1,0:T(8,128)(2,1)} %shard_map.94.refs_0_.own, ...), custom_call_target="tpu_custom_call" | custom-call | flops 150994944 | bytes 4194304 | tf_op jit(solution)/shard_map/pallas_call | solution.py:284
  75.2 3.3 %collective-permute-start.15 = (bf16[288,128]{1,0:T(8,128)(2,1)}, bf16[288,128]{1,0:T(8,128)(2,1)S(1)}, u32[]{:S(2)}, u32[]{:S(2)}) collective-permute-start(bf16[288,128]{1,0:T(8,128)(2,1)} %get-tuple-element.59), channel_id=1, source_target_pairs={{0,2},{1,3},{2,0},{3,1},{4,6},{5,7},{6,4},{7,5},{8,10},{9,11},{10,... | collective-permute-start | bytes 221192 | tf_op jit(solution)/shard_map/ppermute | solution.py:425
  79.4 2.0 %shard_map.99 = (f32[32,48,128]{2,1,0:T(8,128)S(1)}, bf16[32,48,128]{2,1,0:T(8,128)(2,1)S(1)}) custom-call(s32[2]{0:T(128)S(1)} %copy-done.4, bf16[512,1152]{1,0:T(8,128)(2,1)S(1)} %copy-done.1, bf16[304,128]{1,0:T(8,128)(2,1)S(1)} %copy-done.2, bf16[304,128]{1,0:T(8,128)(2,1)S(1)} %collective-permute-done.10.refs_1_, ...), custom_call_target="tpu_custom_call" | custom-call | flops 339738624 | bytes 4194304 | tf_op jit(solution)/shard_map/pallas_call | solution.py:344
  85.2 2.0 %shard_map.100 = (f32[32,48,128]{2,1,0:T(8,128)S(1)}, bf16[32,48,128]{2,1,0:T(8,128)(2,1)S(1)}) custom-call(s32[2]{0:T(128)S(1)} %copy-done.4, bf16[512,1152]{1,0:T(8,128)(2,1)S(1)} %copy-done, bf16[288,128]{1,0:T(8,128)(2,1)S(1)} %copy-done.3, bf16[288,128]{1,0:T(8,128)(2,1)S(1)} %collective-permute-done.14.refs_1_, ...), custom_call_target="tpu_custom_call" | custom-call | flops 339738624 | bytes 4194304 | tf_op jit(solution)/shard_map/pallas_call | solution.py:344
  87.3 1.7 %collective-permute-done.17.taken_txt = bf16[32,48,128]{2,1,0:T(8,128)(2,1)S(1)} collective-permute-done((bf16[32,48,128]{2,1,0:T(8,128)(2,1)S(1)}, bf16[32,48,128]{2,1,0:T(8,128)(2,1)S(1)}, u32[]{:S(2)}, u32[]{:S(2)}) %collective-permute-start.17) | collective-permute-done | bytes 393248 | tf_op jit(solution)/shard_map/ppermute | solution.py:41
  89.1 30.6 %all_to_all.5.parts = bf16[32,96,128]{2,1,0:T(8,128)(2,1)S(1)} all-to-all(bf16[32,96,128]{2,1,0:T(8,128)(2,1)S(1)} %shard_map.101), channel_id=1, replica_groups=mesh['ly'=4,'lz'=4,'lc'=2,'dz'=2,'dx'=4] {'ly','lz','dz'}, dimensions={0} | all-to-all | bytes 1572864 | tf_op jit(solution)/shard_map/all_to_all | solution.py:447
  (59 shorter events, 10.2 us)
Async XLA Ops:
  7.2 48.7 %all-gather.3.cloned.1.call-start = ((), (), s32[]{:S(2)}) async-start(), calls=%async_computation.1 | async-start | bytes 1474560 | tf_op jit(solution)/shard_map/all_gather | solution.py:406
  10.6 68.8 %all-gather.5.cloned.1.call-start = ((), (), s32[]{:S(2)}) async-start(), calls=%async_computation.2 | async-start | bytes 1474560 | tf_op jit(solution)/shard_map/all_gather | solution.py:407
  11.4 9.8 %collective-permute-start = (bf16[144,1152]{1,0:T(8,128)(2,1)}, bf16[144,1152]{1,0:T(8,128)(2,1)S(1)}, u32[]{:S(2)}, u32[]{:S(2)}) collective-permute-start(bf16[144,1152]{1,0:T(8,128)(2,1)} %shard_map.94.refs_0_.own), channel_id=1, source_target_pairs={{0,8},{8,0},{1,9},{9,1},{2,10},{10,2},{3,11},{11,3},{4,12},{12,4},... | collective-permute-start | bytes 995336 | tf_op jit(solution)/shard_map/ppermute | solution.py:41
  11.5 16.5 %collective-permute-start.1 = (bf16[144,1152]{1,0:T(8,128)(2,1)}, bf16[144,1152]{1,0:T(8,128)(2,1)S(1)}, u32[]{:S(2)}, u32[]{:S(2)}) collective-permute-start(bf16[144,1152]{1,0:T(8,128)(2,1)} %shard_map.94.refs_0_.own), channel_id=1, source_target_pairs={{0,64},{64,0},{128,192},{192,128},{1,65},{65,1},{129,193},{193,129... | collective-permute-start | bytes 995336 | tf_op jit(solution)/shard_map/ppermute | solution.py:41
  13.2 18.3 %collective-permute-start.2 = (bf16[144,1152]{1,0:T(8,128)(2,1)}, bf16[144,1152]{1,0:T(8,128)(2,1)S(1)}, u32[]{:S(2)}, u32[]{:S(2)}) collective-permute-start(bf16[144,1152]{1,0:T(8,128)(2,1)} %shard_map.94.refs_0_.own), channel_id=1, source_target_pairs={{0,128},{64,192},{128,0},{192,64},{1,129},{65,193},{129,1},{193,65... | collective-permute-start | bytes 995336 | tf_op jit(solution)/shard_map/ppermute | solution.py:41
  16.1 17.3 %collective-permute-start.3 = (bf16[144,1152]{1,0:T(8,128)(2,1)}, bf16[144,1152]{1,0:T(8,128)(2,1)S(1)}, u32[]{:S(2)}, u32[]{:S(2)}) collective-permute-start(bf16[144,1152]{1,0:T(8,128)(2,1)} %shard_map.94.refs_0_.own), channel_id=1, source_target_pairs={{0,16},{16,0},{32,48},{48,32},{1,17},{17,1},{33,49},{49,33},{2,18}... | collective-permute-start | bytes 995336 | tf_op jit(solution)/shard_map/ppermute | solution.py:41
  28.0 27.9 %copy-start.5 = (bf16[144,1152]{1,0:T(8,128)(2,1)}, bf16[144,1152]{1,0:T(8,128)(2,1)S(1)}, u32[]{:S(2)}) copy-start(bf16[144,1152]{1,0:T(8,128)(2,1)S(1)} %collective-permute-done.1.refs_5_) | copy-start | bytes 995332
  31.5 24.4 %copy-start.6 = (bf16[144,1152]{1,0:T(8,128)(2,1)}, bf16[144,1152]{1,0:T(8,128)(2,1)S(1)}, u32[]{:S(2)}) copy-start(bf16[144,1152]{1,0:T(8,128)(2,1)S(1)} %collective-permute-done.2.refs_6_) | copy-start | bytes 995332
  33.4 22.5 %copy-start.7 = (bf16[144,1152]{1,0:T(8,128)(2,1)}, bf16[144,1152]{1,0:T(8,128)(2,1)S(1)}, u32[]{:S(2)}) copy-start(bf16[144,1152]{1,0:T(8,128)(2,1)S(1)} %collective-permute-done.3.refs_7_) | copy-start | bytes 995332
  33.4 6.0 %collective-permute-start.6 = (bf16[128,1152]{1,0:T(8,128)(2,1)}, bf16[128,1152]{1,0:T(8,128)(2,1)S(1)}, u32[]{:S(2)}, u32[]{:S(2)}) collective-permute-start(bf16[128,1152]{1,0:T(8,128)(2,1)} %get-tuple-element.43.own.refs_0_), channel_id=1, source_target_pairs={{0,8},{8,0},{1,9},{9,1},{2,10},{10,2},{3,11},{11,3},{4,12},{12,4},... | collective-permute-start | bytes 884744 | tf_op jit(solution)/shard_map/ppermute | solution.py:41
  33.4 14.6 %collective-permute-start.5 = (bf16[128,1152]{1,0:T(8,128)(2,1)}, bf16[128,1152]{1,0:T(8,128)(2,1)S(1)}, u32[]{:S(2)}, u32[]{:S(2)}) collective-permute-start(bf16[128,1152]{1,0:T(8,128)(2,1)} %get-tuple-element.43.own.refs_0_), channel_id=1, source_target_pairs={{0,16},{16,0},{32,48},{48,32},{1,17},{17,1},{33,49},{49,33},{2,18}... | collective-permute-start | bytes 884744 | tf_op jit(solution)/shard_map/ppermute | solution.py:41
  36.8 19.0 %collective-permute-start.4 = (bf16[144,1152]{1,0:T(8,128)(2,1)S(1)}, bf16[144,1152]{1,0:T(8,128)(2,1)S(1)}, u32[]{:S(2)}, u32[]{:S(2)}) collective-permute-start(bf16[144,1152]{1,0:T(8,128)(2,1)S(1)} %collective-permute-done.3.refs_7_), channel_id=1, source_target_pairs={{0,48},{16,32},{32,16},{48,0},{1,49},{17,33},{33,17},{49,1},{2,50}... | collective-permute-start | bytes 995336 | tf_op jit(solution)/shard_map/ppermute | solution.py:41
  39.4 27.5 %copy-start.10 = (bf16[128,1152]{1,0:T(8,128)(2,1)}, bf16[128,1152]{1,0:T(8,128)(2,1)S(1)}, u32[]{:S(2)}) copy-start(bf16[128,1152]{1,0:T(8,128)(2,1)S(1)} %collective-permute-done.6.refs_1_) | copy-start | bytes 884740
  39.4 16.5 %collective-permute-start.7 = (bf16[128,1152]{1,0:T(8,128)(2,1)}, bf16[128,1152]{1,0:T(8,128)(2,1)S(1)}, u32[]{:S(2)}, u32[]{:S(2)}) collective-permute-start(bf16[128,1152]{1,0:T(8,128)(2,1)} %get-tuple-element.43.own.refs_0_), channel_id=1, source_target_pairs={{0,64},{64,0},{128,192},{192,128},{1,65},{65,1},{129,193},{193,129... | collective-permute-start | bytes 884744 | tf_op jit(solution)/shard_map/ppermute | solution.py:41
  39.5 16.3 %collective-permute-start.8 = (bf16[128,1152]{1,0:T(8,128)(2,1)}, bf16[128,1152]{1,0:T(8,128)(2,1)S(1)}, u32[]{:S(2)}, u32[]{:S(2)}) collective-permute-start(bf16[128,1152]{1,0:T(8,128)(2,1)} %get-tuple-element.43.own.refs_0_), channel_id=1, source_target_pairs={{0,128},{64,192},{128,0},{192,64},{1,129},{65,193},{129,1},{193,65... | collective-permute-start | bytes 884744 | tf_op jit(solution)/shard_map/ppermute | solution.py:41
  48.0 22.8 %collective-permute-start.9 = (bf16[128,1152]{1,0:T(8,128)(2,1)S(1)}, bf16[128,1152]{1,0:T(8,128)(2,1)S(1)}, u32[]{:S(2)}, u32[]{:S(2)}) collective-permute-start(bf16[128,1152]{1,0:T(8,128)(2,1)S(1)} %collective-permute-done.5.refs_4_), channel_id=1, source_target_pairs={{0,48},{16,32},{32,16},{48,0},{1,49},{17,33},{33,17},{49,1},{2,50}... | collective-permute-start | bytes 884744 | tf_op jit(solution)/shard_map/ppermute | solution.py:41
  61.1 9.8 %collective-permute-start.10 = (bf16[304,128]{1,0:T(8,128)(2,1)}, bf16[304,128]{1,0:T(8,128)(2,1)S(1)}, u32[]{:S(2)}, u32[]{:S(2)}) collective-permute-start(bf16[304,128]{1,0:T(8,128)(2,1)} %get-tuple-element.49), channel_id=1, source_target_pairs={{0,1},{1,2},{2,3},{3,0},{4,5},{5,6},{6,7},{7,4},{8,9},{9,10},{10,1... | collective-permute-start | bytes 233480 | tf_op jit(solution)/shard_map/ppermute | solution.py:425
  62.6 9.2 %collective-permute-start.11 = (bf16[304,128]{1,0:T(8,128)(2,1)}, bf16[304,128]{1,0:T(8,128)(2,1)S(1)}, u32[]{:S(2)}, u32[]{:S(2)}) collective-permute-start(bf16[304,128]{1,0:T(8,128)(2,1)} %get-tuple-element.50), channel_id=1, source_target_pairs={{0,2},{1,3},{2,0},{3,1},{4,6},{5,7},{6,4},{7,5},{8,10},{9,11},{10,... | collective-permute-start | bytes 233480 | tf_op jit(solution)/shard_map/ppermute | solution.py:425
  65.4 6.5 %collective-permute-start.12 = (bf16[304,128]{1,0:T(8,128)(2,1)}, bf16[304,128]{1,0:T(8,128)(2,1)S(1)}, u32[]{:S(2)}, u32[]{:S(2)}) collective-permute-start(bf16[304,128]{1,0:T(8,128)(2,1)} %get-tuple-element.51), channel_id=1, source_target_pairs={{0,3},{1,0},{2,1},{3,2},{4,7},{5,4},{6,5},{7,6},{8,11},{9,8},{10,9... | collective-permute-start | bytes 233480 | tf_op jit(solution)/shard_map/ppermute | solution.py:425
  74.9 6.7 %collective-permute-start.14 = (bf16[288,128]{1,0:T(8,128)(2,1)}, bf16[288,128]{1,0:T(8,128)(2,1)S(1)}, u32[]{:S(2)}, u32[]{:S(2)}) collective-permute-start(bf16[288,128]{1,0:T(8,128)(2,1)} %get-tuple-element.58), channel_id=1, source_target_pairs={{0,1},{1,2},{2,3},{3,0},{4,5},{5,6},{6,7},{7,4},{8,9},{9,10},{10,1... | collective-permute-start | bytes 221192 | tf_op jit(solution)/shard_map/ppermute | solution.py:425
  75.2 6.6 %collective-permute-start.15 = (bf16[288,128]{1,0:T(8,128)(2,1)}, bf16[288,128]{1,0:T(8,128)(2,1)S(1)}, u32[]{:S(2)}, u32[]{:S(2)}) collective-permute-start(bf16[288,128]{1,0:T(8,128)(2,1)} %get-tuple-element.59), channel_id=1, source_target_pairs={{0,2},{1,3},{2,0},{3,1},{4,6},{5,7},{6,4},{7,5},{8,10},{9,11},{10,... | collective-permute-start | bytes 221192 | tf_op jit(solution)/shard_map/ppermute | solution.py:425
  78.5 4.6 %collective-permute-start.16 = (bf16[288,128]{1,0:T(8,128)(2,1)}, bf16[288,128]{1,0:T(8,128)(2,1)S(1)}, u32[]{:S(2)}, u32[]{:S(2)}) collective-permute-start(bf16[288,128]{1,0:T(8,128)(2,1)} %get-tuple-element.60), channel_id=1, source_target_pairs={{0,3},{1,0},{2,1},{3,2},{4,7},{5,4},{6,5},{7,6},{8,11},{9,8},{10,9... | collective-permute-start | bytes 221192 | tf_op jit(solution)/shard_map/ppermute | solution.py:425
  81.5 5.8 %collective-permute-start.13 = (bf16[32,48,128]{2,1,0:T(8,128)(2,1)S(1)}, bf16[32,48,128]{2,1,0:T(8,128)(2,1)S(1)}, u32[]{:S(2)}, u32[]{:S(2)}) collective-permute-start(bf16[32,48,128]{2,1,0:T(8,128)(2,1)S(1)} %get-tuple-element.57), channel_id=1, source_target_pairs={{0,8},{8,0},{1,9},{9,1},{2,10},{10,2},{3,11},{11,3},{4,12},{12,4},... | collective-permute-start | bytes 1179656 | tf_op jit(solution)/shard_map/ppermute | solution.py:41
  87.2 1.8 %collective-permute-start.17 = (bf16[32,48,128]{2,1,0:T(8,128)(2,1)S(1)}, bf16[32,48,128]{2,1,0:T(8,128)(2,1)S(1)}, u32[]{:S(2)}, u32[]{:S(2)}) collective-permute-start(bf16[32,48,128]{2,1,0:T(8,128)(2,1)S(1)} %get-tuple-element.62), channel_id=1, source_target_pairs={{0,8},{8,0},{1,9},{9,1},{2,10},{10,2},{3,11},{11,3},{4,12},{12,4},... | collective-permute-start | bytes 1179656 | tf_op jit(solution)/shard_map/ppermute | solution.py:41
  (11 other events, 100.5 us)
Sparse Core Ops, SparseCore 0:
  10.8 29.5 all-gather.2
  42.1 29.3 all-gather.4

commit v14 on v13

--- a/solution.py
+++ b/solution.py
@@ -198,6 +198,35 @@
     )(spot, *scal, *features, *weights, keys, *blocks)
 
 
+def image_kernel(heat_log, shift, own, total_ref, key, acc, *refs):
+    *blocks, out_ref, sum_ref, rows_ref = refs
+    total, sums = add_tiles(
+        True,
+        temperature(heat_log),
+        shift[0],
+        own[...],
+        key[...],
+        pair_up(blocks, rows_ref),
+        total_ref[...],
+        [acc[k] for k in range(3)],
+    )
+    out_ref[...] = total
+    for k in range(3):
+        sum_ref[k] = sums[k]
+
+
+def image_tiles(scal, own, total, key, acc, blocks):
+    shapes = [(ROWS, WIDTH), (3, ROWS, ROWS), (len(blocks), 8, LANES)]
+    return pl.pallas_call(
+        image_kernel,
+        in_specs=[SMEM] * 2 + [VMEM] * (4 + len(blocks)),
+        out_specs=[VMEM] * 3,
+        out_shape=[jax.ShapeDtypeStruct(shape, F32) for shape in shapes],
+        compiler_params=params(56),
+        cost_estimate=cost(4 * 3 * ROWS * ROWS * WIDTH, 4 * 2**20),
+    )(*scal, own, total, key, acc, *blocks)
+
+
 def middle_kernel(heat_log, shift, own, key, near_rows, far_rows, *refs):
     *blocks, total_ref = refs
     rows = [near_rows[0], near_rows[1], far_rows[0], far_rows[1], far_rows[2]]
@@ -235,7 +264,7 @@
         pairs = pair_up(blocks, rows_ref)
     else:
         rows, block = blocks
-        pairs = [(block, rows[3][0:1])]
+        pairs = [(block, rows[0][0:1])]
     total, sums = add_tiles(
         with_stats,
         heat,
@@ -409,11 +438,14 @@
     features = (pictures[0], sentences[0])
     weights = (picture_weights, sentence_weights)
     img, near_rows, *first = early(spot, scal, features, weights, keys, [txt, txt_c])
-    img_part = (*first[:3], *first[5:])
     txt_b = exchange(after(txt_a, txt_y1, txt_y2), "lz", 3)
     img_a = exchange(img, "lz", 1)
     img_c = exchange(after(img, txt_a, txt_y1, txt_y2), "lc", 1)
-    img_n = after(img, img_c)
+    total, acc, mid_rows = image_tiles(
+        scal, img, first[0], first[5], first[6], [after(txt_y1, img_c), txt_y2, txt_a]
+    )
+    img_part = (total, *first[1:3], first[5], acc)
+    img_n = after(img, img_c, acc)
     img_y2 = exchange(img_n, "ly", 2)
     img_y1 = exchange(img_n, "ly", 1)
     img_b = exchange(img_a, "lz", 3)
@@ -429,11 +461,11 @@
 
     last = after(txt_b, img_feat, img_a, img_c, img_y1, img_y2)
     *img_outs, far_rows = late(
-        True, ways, spot, scal, img, img_part, [txt_y1, txt_y2, txt_a, last]
+        True, ways, spot, scal, img, img_part, [last]
     )
     img_cols = columns(img_outs)
     txt_total = middle(
-        scal, txt, first[5], near_rows, far_rows, img, img_c, img_y1, img_y2, img_a
+        scal, txt, first[5], near_rows, mid_rows, img, img_c, img_y1, img_y2, img_a
     )
     txt_part = (txt_total, *first[3:5], first[5], first[5])
     last = after(img_b, *img_cols, txt_total)

time: 128 us -> 128 us (level)
  blocking collectives: 30.6 us -> 27.9 us
  Pallas kernels: 26 us -> 28.4 us
    pallas_call x0 -> x1, Pallas kernels: none -> 3.8 us  [image_tiles(): pl.pallas_call(image_kernel, in_specs=[SMEM] * 2 + [VMEM] * (4 + len(bloc...]
    all_to_all x1, blocking collectives: 30.6 us -> 27.9 us  [body(): sums = lax.all_to_all(sums, ('ly', 'lz', 'dz'), 0, 0, tiled=True)]
    pallas_call x2, Pallas kernels: 7.52 us -> 6.13 us  [late(): pl.pallas_call(functools.partial(late_kernel, with_stats, ways, len(block...]
  transfers between devices with their start and end apart: 20 -> 20, of which waited for: 8 -> 8; matrix products, arithmetic and copies ran while one was open for 0% -> 1% of each run, Pallas kernels for 17% -> 19%
where the time goes in v14:
time: 128 us; the launch traced here: 127 us
  starting transfers between devices  31.9 us (25%)
  Pallas kernels  28.4 us (22%)
  blocking collectives  27.9 us (22%)
  waiting for transfers between devices  18.3 us (14%)
  between operations  15.5 us (12%)
  local copies, waits for them, and re-layouts  4.32 us (3%)
    all_to_all x1, blocking collectives, body(): sums = lax.all_to_all(sums, ('ly', 'lz', 'dz'), 0, 0, tiled=True)  27.9 us
    ppermute x12, starting transfers between devices, exchange(): lax.ppermute(array, axis, [(i, i ^ apart) for i in range(lax.axis_size(ax...  22.7 us
    ppermute x12, waiting for transfers between devices, exchange(): lax.ppermute(array, axis, [(i, i ^ apart) for i in range(lax.axis_size(ax...  15.6 us
    ppermute x6, starting transfers between devices, turn(): lax.ppermute(array, axis, [(i, (i + step) % size) for i in range(size)])  9.1 us
    pallas_call x2, Pallas kernels, late(): pl.pallas_call(functools.partial(late_kernel, with_stats, ways, len(block...  6.13 us
    pallas_call x1, Pallas kernels, early(): pl.pallas_call(early_kernel, in_specs=[SMEM] * 3 + [VMEM] * 2 + [hbm] * 2...  6.06 us
    unnamed x30, local copies, waits for them, and re-layouts  4.32 us
    pallas_call x2, Pallas kernels, heads(): pl.pallas_call(functools.partial(head_kernel, with_stats), in_specs=[SMEM...  4.03 us
  transfers between devices with their start and end apart: 20, of which 8 were waited for; matrix products, arithmetic and copies ran while one was open for 1% of the time, Pallas kernels for 19%

profile of v14, /device:TPU:32, one launch (start us, length us, event | category | flops | bytes accessed | tf_op | source)
XLA Modules:
  0.0 127.0 jit_solution(15882235323757855443)
XLA Ops:
  7.2 3.4 %shard_map.94.refs_0_.own = bf16[144,1152]{1,0:T(8,128)(2,1)} custom-call(bf16[128,1152]{1,0:T(8,128)(2,1)} %bitcast.4, bf16[1152,1152]{1,0:T(8,128)(2,1)} %wt_hbm.1, s32[1,128]{1,0:T(1,128)} %key.1), custom_call_target="tpu_custom_call" | custom-call | flops 339738624 | bytes 4194304 | tf_op jit(solution)/shard_map/pallas_call | solution.py:81
  11.5 1.7 %collective-permute-start.1 = (bf16[144,1152]{1,0:T(8,128)(2,1)}, bf16[144,1152]{1,0:T(8,128)(2,1)S(1)}, u32[]{:S(2)}, u32[]{:S(2)}) collective-permute-start(bf16[144,1152]{1,0:T(8,128)(2,1)} %shard_map.94.refs_0_.own), channel_id=1, source_target_pairs={{0,64},{64,0},{128,192},{192,128},{1,65},{65,1},{129,193},{193,129... | collective-permute-start | bytes 995336 | tf_op jit(solution)/shard_map/ppermute | solution.py:41
  13.2 3.3 %collective-permute-start.2 = (bf16[144,1152]{1,0:T(8,128)(2,1)}, bf16[144,1152]{1,0:T(8,128)(2,1)S(1)}, u32[]{:S(2)}, u32[]{:S(2)}) collective-permute-start(bf16[144,1152]{1,0:T(8,128)(2,1)} %shard_map.94.refs_0_.own), channel_id=1, source_target_pairs={{0,16},{16,0},{32,48},{48,32},{1,17},{17,1},{33,49},{49,33},{2,18}... | collective-permute-start | bytes 995336 | tf_op jit(solution)/shard_map/ppermute | solution.py:41
  16.4 2.9 %collective-permute-start.3 = (bf16[144,1152]{1,0:T(8,128)(2,1)}, bf16[144,1152]{1,0:T(8,128)(2,1)S(1)}, u32[]{:S(2)}, u32[]{:S(2)}) collective-permute-start(bf16[144,1152]{1,0:T(8,128)(2,1)} %shard_map.94.refs_0_.own), channel_id=1, source_target_pairs={{0,128},{64,192},{128,0},{192,64},{1,129},{65,193},{129,1},{193,65... | collective-permute-start | bytes 995336 | tf_op jit(solution)/shard_map/ppermute | solution.py:41
  22.0 6.1 %shard_map.95 = (bf16[128,1152]{1,0:T(8,128)(2,1)}, f32[2,8,128]{2,1,0:T(8,128)}, f32[128,1152]{1,0:T(8,128)}, f32[128,1152]{1,0:T(8,128)}, f32[128,128]{1,0:T(8...) custom-call(s32[2]{0:T(128)} %pad_add_fusion.spot, ...), custom_call_target="tpu_custom_call" | custom-call | flops 377487360 | bytes 8388608 | tf_op jit(solution)/shard_map/pallas_call | solution.py:190
  28.1 2.6 %collective-permute-done.2.refs_2_ = bf16[144,1152]{1,0:T(8,128)(2,1)S(1)} collective-permute-done((bf16[144,1152]{1,0:T(8,128)(2,1)}, bf16[144,1152]{1,0:T(8,128)(2,1)S(1)}, u32[]{:S(2)}, u32[]{:S(2)}) %collective-permute-start.2) | collective-permute-done | bytes 331808 | tf_op jit(solution)/shard_map/ppermute | solution.py:41
  31.5 3.3 %collective-permute-start.7 = (bf16[128,1152]{1,0:T(8,128)(2,1)}, bf16[128,1152]{1,0:T(8,128)(2,1)S(1)}, u32[]{:S(2)}, u32[]{:S(2)}) collective-permute-start(bf16[128,1152]{1,0:T(8,128)(2,1)} %get-tuple-element.47.own.refs_0_), channel_id=1, source_target_pairs={{0,16},{16,0},{32,48},{48,32},{1,17},{17,1},{33,49},{49,33},{2,18}... | collective-permute-start | bytes 884744 | tf_op jit(solution)/shard_map/ppermute | solution.py:41
  34.8 3.6 %collective-permute-start.8 = (bf16[144,1152]{1,0:T(8,128)(2,1)S(1)}, bf16[144,1152]{1,0:T(8,128)(2,1)S(1)}, u32[]{:S(2)}, u32[]{:S(2)}) collective-permute-start(bf16[144,1152]{1,0:T(8,128)(2,1)S(1)} %collective-permute-done.2.refs_2_), channel_id=1, source_target_pairs={{0,48},{16,32},{32,16},{48,0},{1,49},{17,33},{33,17},{49,1},{2,50}... | collective-permute-start | bytes 995336 | tf_op jit(solution)/shard_map/ppermute | solution.py:41
  38.4 3.8 %shard_map.96 = (f32[128,1152]{1,0:T(8,128)}, f32[3,128,128]{2,1,0:T(8,128)}, f32[3,8,128]{2,1,0:T(8,128)}) custom-call(f32[1]{0:T(128)S(6)} %copy.10.heat_log, f32[1]{0:T(128)S(6)} %copy.11.shift, bf16[128,1152]{1,0:T(8,128)(2,1)} %get-tuple-element.47.own.refs_0_, f32[128,1152]{1,0:T(8,128)} %get-tuple-element.41.total_ref, ...), custom_call_target="tpu_custom_call" | custom-call | flops 226492416 | bytes 4194304 | tf_op jit(solution)/shard_map/pallas_call | solution.py:220
  42.3 2.1 %collective-permute-start.6 = (bf16[128,1152]{1,0:T(8,128)(2,1)}, bf16[128,1152]{1,0:T(8,128)(2,1)S(1)}, u32[]{:S(2)}, u32[]{:S(2)}) collective-permute-start(bf16[128,1152]{1,0:T(8,128)(2,1)} %get-tuple-element.47.own.refs_0_), channel_id=1, source_target_pairs={{0,128},{64,192},{128,0},{192,64},{1,129},{65,193},{129,1},{193,65... | collective-permute-start | bytes 884744 | tf_op jit(solution)/shard_map/ppermute | solution.py:41
  44.4 3.5 %collective-permute-done.7.refs_4_ = bf16[128,1152]{1,0:T(8,128)(2,1)S(1)} collective-permute-done((bf16[128,1152]{1,0:T(8,128)(2,1)}, bf16[128,1152]{1,0:T(8,128)(2,1)S(1)}, u32[]{:S(2)}, u32[]{:S(2)}) %collective-permute-start.7) | collective-permute-done | bytes 294944 | tf_op jit(solution)/shard_map/ppermute | solution.py:41
  47.9 5.5 %collective-permute-start.9 = (bf16[128,1152]{1,0:T(8,128)(2,1)S(1)}, bf16[128,1152]{1,0:T(8,128)(2,1)S(1)}, u32[]{:S(2)}, u32[]{:S(2)}) collective-permute-start(bf16[128,1152]{1,0:T(8,128)(2,1)S(1)} %collective-permute-done.7.refs_4_), channel_id=1, source_target_pairs={{0,48},{16,32},{32,16},{48,0},{1,49},{17,33},{33,17},{49,1},{2,50}... | collective-permute-start | bytes 884744 | tf_op jit(solution)/shard_map/ppermute | solution.py:41
  53.4 7.1 %collective-permute-done.8.refs_5_ = bf16[144,1152]{1,0:T(8,128)(2,1)S(1)} collective-permute-done((bf16[144,1152]{1,0:T(8,128)(2,1)S(1)}, bf16[144,1152]{1,0:T(8,128)(2,1)S(1)}, u32[]{:S(2)}, u32[]{:S(2)}) %collective-permute-start.8) | collective-permute-done | bytes 331808 | tf_op jit(solution)/shard_map/ppermute | solution.py:41
  61.3 3.1 %shard_map.98 = (bf16[304,128]{1,0:T(8,128)(2,1)}, bf16[304,128]{1,0:T(8,128)(2,1)}, bf16[304,128]{1,0:T(8,128)(2,1)}, bf16[304,128]{1,0:T(8,128)(2,1)}, f32[1,8,128]{2,1,0:T(8,128)}) custom-call(s32[2]{0:T(128)} %pad_add_fusion.spot, f32[1]{0:T(128)S(6)} %copy.10.heat_log, f32[1]{0:T(128)S(6)} %copy.11.shift, ...), custom_call_target="tpu_custom_call" | custom-call | flops 150994944 | bytes 4194304 | tf_op jit(solution)/shard_map/pallas_call | solution.py:313
  64.4 1.6 %collective-permute-start.10 = (bf16[304,128]{1,0:T(8,128)(2,1)}, bf16[304,128]{1,0:T(8,128)(2,1)S(1)}, u32[]{:S(2)}, u32[]{:S(2)}) collective-permute-start(bf16[304,128]{1,0:T(8,128)(2,1)} %get-tuple-element.57), channel_id=1, source_target_pairs={{0,1},{1,2},{2,3},{3,0},{4,5},{5,6},{6,7},{7,4},{8,9},{9,10},{10,1... | collective-permute-start | bytes 233480 | tf_op jit(solution)/shard_map/ppermute | solution.py:457
  65.9 2.8 %collective-permute-start.11 = (bf16[304,128]{1,0:T(8,128)(2,1)}, bf16[304,128]{1,0:T(8,128)(2,1)S(1)}, u32[]{:S(2)}, u32[]{:S(2)}) collective-permute-start(bf16[304,128]{1,0:T(8,128)(2,1)} %get-tuple-element.58), channel_id=1, source_target_pairs={{0,2},{1,3},{2,0},{3,1},{4,6},{5,7},{6,4},{7,5},{8,10},{9,11},{10,... | collective-permute-start | bytes 233480 | tf_op jit(solution)/shard_map/ppermute | solution.py:457
  68.7 1.4 %collective-permute-start.12 = (bf16[304,128]{1,0:T(8,128)(2,1)}, bf16[304,128]{1,0:T(8,128)(2,1)S(1)}, u32[]{:S(2)}, u32[]{:S(2)}) collective-permute-start(bf16[304,128]{1,0:T(8,128)(2,1)} %get-tuple-element.59), channel_id=1, source_target_pairs={{0,3},{1,0},{2,1},{3,2},{4,7},{5,4},{6,5},{7,6},{8,11},{9,8},{10,9... | collective-permute-start | bytes 233480 | tf_op jit(solution)/shard_map/ppermute | solution.py:457
  70.1 4.0 %shard_map.97.refs_0_ = f32[128,1152]{1,0:T(8,128)} custom-call(f32[1]{0:T(128)S(6)} %copy.10.heat_log, f32[1]{0:T(128)S(6)} %copy.11.shift, bf16[144,1152]{1,0:T(8,128)(2,1)} %shard_map.94.refs_0_.own, f32[128,128]{1,0:T(8,128)} %get-tuple-element.38.key.refs_3_.refs_4_, f32[2,8,128]{2,1,0:T(8,128)} %get-tuple-element.39.near_rows, ...), custom_call_target="tpu_custom_call" | custom-call | flops 377487360 | bytes 4194304 | tf_op jit(solution)/shard_map/pallas_call | solution.py:248
  74.8 3.0 %shard_map.99 = (bf16[288,128]{1,0:T(8,128)(2,1)}, bf16[288,128]{1,0:T(8,128)(2,1)}, bf16[288,128]{1,0:T(8,128)(2,1)}, bf16[288,128]{1,0:T(8,128)(2,1)}) custom-call(s32[2]{0:T(128)} %pad_add_fusion.spot, f32[1]{0:T(128)S(6)} %copy.10.heat_log, f32[1]{0:T(128)S(6)} %copy.11.shift, bf16[144,1152]{1,0:T(8,128)(2,1)} %shard_map.94.refs_0_.own, ...), custom_call_target="tpu_custom_call" | custom-call | flops 150994944 | bytes 4194304 | tf_op jit(solution)/shard_map/pallas_call | solution.py:313
  78.4 2.0 %collective-permute-start.15 = (bf16[288,128]{1,0:T(8,128)(2,1)}, bf16[288,128]{1,0:T(8,128)(2,1)S(1)}, u32[]{:S(2)}, u32[]{:S(2)}) collective-permute-start(bf16[288,128]{1,0:T(8,128)(2,1)} %get-tuple-element.67), channel_id=1, source_target_pairs={{0,2},{1,3},{2,0},{3,1},{4,6},{5,7},{6,4},{7,5},{8,10},{9,11},{10,... | collective-permute-start | bytes 221192 | tf_op jit(solution)/shard_map/ppermute | solution.py:457
  81.2 2.0 %shard_map.100 = (f32[32,48,128]{2,1,0:T(8,128)S(1)}, bf16[32,48,128]{2,1,0:T(8,128)(2,1)S(1)}) custom-call(s32[2]{0:T(128)S(1)} %copy-done.4, bf16[512,1152]{1,0:T(8,128)(2,1)S(1)} %copy-done.1, bf16[304,128]{1,0:T(8,128)(2,1)S(1)} %copy-done.2, bf16[304,128]{1,0:T(8,128)(2,1)S(1)} %collective-permute-done.10.refs_1_, ...), custom_call_target="tpu_custom_call" | custom-call | flops 339738624 | bytes 4194304 | tf_op jit(solution)/shard_map/pallas_call | solution.py:373
  87.4 2.0 %shard_map.101 = (f32[32,48,128]{2,1,0:T(8,128)S(1)}, bf16[32,48,128]{2,1,0:T(8,128)(2,1)S(1)}) custom-call(s32[2]{0:T(128)S(1)} %copy-done.4, bf16[512,1152]{1,0:T(8,128)(2,1)S(1)} %copy-done, bf16[288,128]{1,0:T(8,128)(2,1)S(1)} %copy-done.3, bf16[288,128]{1,0:T(8,128)(2,1)S(1)} %collective-permute-done.14.refs_1_, ...), custom_call_target="tpu_custom_call" | custom-call | flops 339738624 | bytes 4194304 | tf_op jit(solution)/shard_map/pallas_call | solution.py:373
  89.5 1.7 %collective-permute-done.17.taken_txt = bf16[32,48,128]{2,1,0:T(8,128)(2,1)S(1)} collective-permute-done((bf16[32,48,128]{2,1,0:T(8,128)(2,1)S(1)}, bf16[32,48,128]{2,1,0:T(8,128)(2,1)S(1)}, u32[]{:S(2)}, u32[]{:S(2)}) %collective-permute-start.17) | collective-permute-done | bytes 393248 | tf_op jit(solution)/shard_map/ppermute | solution.py:41
  91.4 27.9 %all_to_all.5.parts = bf16[32,96,128]{2,1,0:T(8,128)(2,1)S(1)} all-to-all(bf16[32,96,128]{2,1,0:T(8,128)(2,1)S(1)} %shard_map.102), channel_id=1, replica_groups=mesh['ly'=4,'lz'=4,'lc'=2,'dz'=2,'dx'=4] {'ly','lz','dz'}, dimensions={0} | all-to-all | bytes 1572864 | tf_op jit(solution)/shard_map/all_to_all | solution.py:479
  (60 shorter events, 11.2 us)
Async XLA Ops:
  7.2 53.4 %all-gather.3.cloned.1.call-start = ((), (), s32[]{:S(2)}) async-start(), calls=%async_computation.1 | async-start | bytes 1474560 | tf_op jit(solution)/shard_map/all_gather | solution.py:435
  10.6 70.6 %all-gather.5.cloned.1.call-start = ((), (), s32[]{:S(2)}) async-start(), calls=%async_computation.2 | async-start | bytes 1474560 | tf_op jit(solution)/shard_map/all_gather | solution.py:436
  11.4 9.9 %collective-permute-start = (bf16[144,1152]{1,0:T(8,128)(2,1)}, bf16[144,1152]{1,0:T(8,128)(2,1)S(1)}, u32[]{:S(2)}, u32[]{:S(2)}) collective-permute-start(bf16[144,1152]{1,0:T(8,128)(2,1)} %shard_map.94.refs_0_.own), channel_id=1, source_target_pairs={{0,8},{8,0},{1,9},{9,1},{2,10},{10,2},{3,11},{11,3},{4,12},{12,4},... | collective-permute-start | bytes 995336 | tf_op jit(solution)/shard_map/ppermute | solution.py:41
  11.5 16.6 %collective-permute-start.1 = (bf16[144,1152]{1,0:T(8,128)(2,1)}, bf16[144,1152]{1,0:T(8,128)(2,1)S(1)}, u32[]{:S(2)}, u32[]{:S(2)}) collective-permute-start(bf16[144,1152]{1,0:T(8,128)(2,1)} %shard_map.94.refs_0_.own), channel_id=1, source_target_pairs={{0,64},{64,0},{128,192},{192,128},{1,65},{65,1},{129,193},{193,129... | collective-permute-start | bytes 995336 | tf_op jit(solution)/shard_map/ppermute | solution.py:41
  13.2 17.6 %collective-permute-start.2 = (bf16[144,1152]{1,0:T(8,128)(2,1)}, bf16[144,1152]{1,0:T(8,128)(2,1)S(1)}, u32[]{:S(2)}, u32[]{:S(2)}) collective-permute-start(bf16[144,1152]{1,0:T(8,128)(2,1)} %shard_map.94.refs_0_.own), channel_id=1, source_target_pairs={{0,16},{16,0},{32,48},{48,32},{1,17},{17,1},{33,49},{49,33},{2,18}... | collective-permute-start | bytes 995336 | tf_op jit(solution)/shard_map/ppermute | solution.py:41
  16.4 15.1 %collective-permute-start.3 = (bf16[144,1152]{1,0:T(8,128)(2,1)}, bf16[144,1152]{1,0:T(8,128)(2,1)S(1)}, u32[]{:S(2)}, u32[]{:S(2)}) collective-permute-start(bf16[144,1152]{1,0:T(8,128)(2,1)} %shard_map.94.refs_0_.own), channel_id=1, source_target_pairs={{0,128},{64,192},{128,0},{192,64},{1,129},{65,193},{129,1},{193,65... | collective-permute-start | bytes 995336 | tf_op jit(solution)/shard_map/ppermute | solution.py:41
  31.5 6.9 %collective-permute-start.4 = (bf16[128,1152]{1,0:T(8,128)(2,1)}, bf16[128,1152]{1,0:T(8,128)(2,1)S(1)}, u32[]{:S(2)}, u32[]{:S(2)}) collective-permute-start(bf16[128,1152]{1,0:T(8,128)(2,1)} %get-tuple-element.47.own.refs_0_), channel_id=1, source_target_pairs={{0,8},{8,0},{1,9},{9,1},{2,10},{10,2},{3,11},{11,3},{4,12},{12,4},... | collective-permute-start | bytes 884744 | tf_op jit(solution)/shard_map/ppermute | solution.py:41
  31.5 16.4 %collective-permute-start.7 = (bf16[128,1152]{1,0:T(8,128)(2,1)}, bf16[128,1152]{1,0:T(8,128)(2,1)S(1)}, u32[]{:S(2)}, u32[]{:S(2)}) collective-permute-start(bf16[128,1152]{1,0:T(8,128)(2,1)} %get-tuple-element.47.own.refs_0_), channel_id=1, source_target_pairs={{0,16},{16,0},{32,48},{48,32},{1,17},{17,1},{33,49},{49,33},{2,18}... | collective-permute-start | bytes 884744 | tf_op jit(solution)/shard_map/ppermute | solution.py:41
  34.8 25.7 %collective-permute-start.8 = (bf16[144,1152]{1,0:T(8,128)(2,1)S(1)}, bf16[144,1152]{1,0:T(8,128)(2,1)S(1)}, u32[]{:S(2)}, u32[]{:S(2)}) collective-permute-start(bf16[144,1152]{1,0:T(8,128)(2,1)S(1)} %collective-permute-done.2.refs_2_), channel_id=1, source_target_pairs={{0,48},{16,32},{32,16},{48,0},{1,49},{17,33},{33,17},{49,1},{2,50}... | collective-permute-start | bytes 995336 | tf_op jit(solution)/shard_map/ppermute | solution.py:41
  38.3 31.8 %copy-start.10 = (bf16[128,1152]{1,0:T(8,128)(2,1)}, bf16[128,1152]{1,0:T(8,128)(2,1)S(1)}, u32[]{:S(2)}) copy-start(bf16[128,1152]{1,0:T(8,128)(2,1)S(1)} %collective-permute-done.4.refs_1_) | copy-start | bytes 884740
  42.2 18.3 %collective-permute-start.5 = (bf16[128,1152]{1,0:T(8,128)(2,1)}, bf16[128,1152]{1,0:T(8,128)(2,1)S(1)}, u32[]{:S(2)}, u32[]{:S(2)}) collective-permute-start(bf16[128,1152]{1,0:T(8,128)(2,1)} %get-tuple-element.47.own.refs_0_), channel_id=1, source_target_pairs={{0,64},{64,0},{128,192},{192,128},{1,65},{65,1},{129,193},{193,129... | collective-permute-start | bytes 884744 | tf_op jit(solution)/shard_map/ppermute | solution.py:41
  42.3 18.2 %collective-permute-start.6 = (bf16[128,1152]{1,0:T(8,128)(2,1)}, bf16[128,1152]{1,0:T(8,128)(2,1)S(1)}, u32[]{:S(2)}, u32[]{:S(2)}) collective-permute-start(bf16[128,1152]{1,0:T(8,128)(2,1)} %get-tuple-element.47.own.refs_0_), channel_id=1, source_target_pairs={{0,128},{64,192},{128,0},{192,64},{1,129},{65,193},{129,1},{193,65... | collective-permute-start | bytes 884744 | tf_op jit(solution)/shard_map/ppermute | solution.py:41
  47.9 22.2 %copy-start.11 = (bf16[128,1152]{1,0:T(8,128)(2,1)}, bf16[128,1152]{1,0:T(8,128)(2,1)S(1)}, u32[]{:S(2)}) copy-start(bf16[128,1152]{1,0:T(8,128)(2,1)S(1)} %collective-permute-done.7.refs_4_) | copy-start | bytes 884740
  47.9 26.2 %collective-permute-start.9 = (bf16[128,1152]{1,0:T(8,128)(2,1)S(1)}, bf16[128,1152]{1,0:T(8,128)(2,1)S(1)}, u32[]{:S(2)}, u32[]{:S(2)}) collective-permute-start(bf16[128,1152]{1,0:T(8,128)(2,1)S(1)} %collective-permute-done.7.refs_4_), channel_id=1, source_target_pairs={{0,48},{16,32},{32,16},{48,0},{1,49},{17,33},{33,17},{49,1},{2,50}... | collective-permute-start | bytes 884744 | tf_op jit(solution)/shard_map/ppermute | solution.py:41
  64.4 16.8 %copy-start.1 = (bf16[512,1152]{1,0:T(8,128)(2,1)S(1)}, bf16[512,1152]{1,0:T(8,128)(2,1)}, u32[]{:S(2)}) copy-start(bf16[512,1152]{1,0:T(8,128)(2,1)} %all-gather.3.cloned.1.call-done.feat) | copy-start | bytes 3538948
  64.4 16.8 %copy-start.2 = (bf16[304,128]{1,0:T(8,128)(2,1)S(1)}, bf16[304,128]{1,0:T(8,128)(2,1)}, u32[]{:S(2)}) copy-start(bf16[304,128]{1,0:T(8,128)(2,1)} %get-tuple-element.56.refs_0_) | copy-start | bytes 233476
  64.4 9.7 %collective-permute-start.10 = (bf16[304,128]{1,0:T(8,128)(2,1)}, bf16[304,128]{1,0:T(8,128)(2,1)S(1)}, u32[]{:S(2)}, u32[]{:S(2)}) collective-permute-start(bf16[304,128]{1,0:T(8,128)(2,1)} %get-tuple-element.57), channel_id=1, source_target_pairs={{0,1},{1,2},{2,3},{3,0},{4,5},{5,6},{6,7},{7,4},{8,9},{9,10},{10,1... | collective-permute-start | bytes 233480 | tf_op jit(solution)/shard_map/ppermute | solution.py:457
  65.9 8.2 %collective-permute-start.11 = (bf16[304,128]{1,0:T(8,128)(2,1)}, bf16[304,128]{1,0:T(8,128)(2,1)S(1)}, u32[]{:S(2)}, u32[]{:S(2)}) collective-permute-start(bf16[304,128]{1,0:T(8,128)(2,1)} %get-tuple-element.58), channel_id=1, source_target_pairs={{0,2},{1,3},{2,0},{3,1},{4,6},{5,7},{6,4},{7,5},{8,10},{9,11},{10,... | collective-permute-start | bytes 233480 | tf_op jit(solution)/shard_map/ppermute | solution.py:457
  68.7 5.4 %collective-permute-start.12 = (bf16[304,128]{1,0:T(8,128)(2,1)}, bf16[304,128]{1,0:T(8,128)(2,1)S(1)}, u32[]{:S(2)}, u32[]{:S(2)}) collective-permute-start(bf16[304,128]{1,0:T(8,128)(2,1)} %get-tuple-element.59), channel_id=1, source_target_pairs={{0,3},{1,0},{2,1},{3,2},{4,7},{5,4},{6,5},{7,6},{8,11},{9,8},{10,9... | collective-permute-start | bytes 233480 | tf_op jit(solution)/shard_map/ppermute | solution.py:457
  77.8 5.8 %collective-permute-start.14 = (bf16[288,128]{1,0:T(8,128)(2,1)}, bf16[288,128]{1,0:T(8,128)(2,1)S(1)}, u32[]{:S(2)}, u32[]{:S(2)}) collective-permute-start(bf16[288,128]{1,0:T(8,128)(2,1)} %get-tuple-element.66), channel_id=1, source_target_pairs={{0,1},{1,2},{2,3},{3,0},{4,5},{5,6},{6,7},{7,4},{8,9},{9,10},{10,1... | collective-permute-start | bytes 221192 | tf_op jit(solution)/shard_map/ppermute | solution.py:457
  78.4 6.1 %collective-permute-start.15 = (bf16[288,128]{1,0:T(8,128)(2,1)}, bf16[288,128]{1,0:T(8,128)(2,1)S(1)}, u32[]{:S(2)}, u32[]{:S(2)}) collective-permute-start(bf16[288,128]{1,0:T(8,128)(2,1)} %get-tuple-element.67), channel_id=1, source_target_pairs={{0,2},{1,3},{2,0},{3,1},{4,6},{5,7},{6,4},{7,5},{8,10},{9,11},{10,... | collective-permute-start | bytes 221192 | tf_op jit(solution)/shard_map/ppermute | solution.py:457
  80.5 4.8 %collective-permute-start.16 = (bf16[288,128]{1,0:T(8,128)(2,1)}, bf16[288,128]{1,0:T(8,128)(2,1)S(1)}, u32[]{:S(2)}, u32[]{:S(2)}) collective-permute-start(bf16[288,128]{1,0:T(8,128)(2,1)} %get-tuple-element.68), channel_id=1, source_target_pairs={{0,3},{1,0},{2,1},{3,2},{4,7},{5,4},{6,5},{7,6},{8,11},{9,8},{10,9... | collective-permute-start | bytes 221192 | tf_op jit(solution)/shard_map/ppermute | solution.py:457
  83.3 6.3 %collective-permute-start.13 = (bf16[32,48,128]{2,1,0:T(8,128)(2,1)S(1)}, bf16[32,48,128]{2,1,0:T(8,128)(2,1)S(1)}, u32[]{:S(2)}, u32[]{:S(2)}) collective-permute-start(bf16[32,48,128]{2,1,0:T(8,128)(2,1)S(1)} %get-tuple-element.65), channel_id=1, source_target_pairs={{0,8},{8,0},{1,9},{9,1},{2,10},{10,2},{3,11},{11,3},{4,12},{12,4},... | collective-permute-start | bytes 1179656 | tf_op jit(solution)/shard_map/ppermute | solution.py:41
  89.4 1.8 %collective-permute-start.17 = (bf16[32,48,128]{2,1,0:T(8,128)(2,1)S(1)}, bf16[32,48,128]{2,1,0:T(8,128)(2,1)S(1)}, u32[]{:S(2)}, u32[]{:S(2)}) collective-permute-start(bf16[32,48,128]{2,1,0:T(8,128)(2,1)S(1)} %get-tuple-element.70), channel_id=1, source_target_pairs={{0,8},{8,0},{1,9},{9,1},{2,10},{10,2},{3,11},{11,3},{4,12},{12,4},... | collective-permute-start | bytes 1179656 | tf_op jit(solution)/shard_map/ppermute | solution.py:41
  (11 other events, 65.2 us)
Sparse Core Ops, SparseCore 0:
  10.8 29.5 all-gather.2
  42.1 28.9 all-gather.4

commit v15 on v14

--- a/solution.py
+++ b/solution.py
@@ -459,10 +459,11 @@
     def columns(outs):
         return [outs[0]] + [turn(out, "dx", step) for step, out in enumerate(outs) if step]
 
-    last = after(txt_b, img_feat, img_a, img_c, img_y1, img_y2)
+    last = after(txt_b, img_feat, img_a, img_c)
     *img_outs, far_rows = late(
         True, ways, spot, scal, img, img_part, [last]
     )
+    img_outs = list(lax.optimization_barrier((*img_outs, img_y1, img_y2))[:-2])
     img_cols = columns(img_outs)
     txt_total = middle(
         scal, txt, first[5], near_rows, mid_rows, img, img_c, img_y1, img_y2, img_a

time: 128 us -> 126 us (0.984)
  blocking collectives: 27.9 us -> 26.5 us
    all_to_all x1, blocking collectives: 27.9 us -> 26.5 us  [body(): sums = lax.all_to_all(sums, ('ly', 'lz', 'dz'), 0, 0, tiled=True)]
where the time goes in v15:
time: 126 us
  starting transfers between devices  31.9 us (25%)
  Pallas kernels  28.4 us (23%)
  blocking collectives  26.5 us (21%)
  waiting for transfers between devices  18.3 us (15%)
  between operations  15.5 us (12%)
  local copies, waits for them, and re-layouts  4.37 us (3%)
    all_to_all x1, blocking collectives, body(): sums = lax.all_to_all(sums, ('ly', 'lz', 'dz'), 0, 0, tiled=True)  26.5 us
    ppermute x12, starting transfers between devices, exchange(): lax.ppermute(array, axis, [(i, i ^ apart) for i in range(lax.axis_size(ax...  22.7 us
    ppermute x12, waiting for transfers between devices, exchange(): lax.ppermute(array, axis, [(i, i ^ apart) for i in range(lax.axis_size(ax...  15.6 us
    ppermute x6, starting transfers between devices, turn(): lax.ppermute(array, axis, [(i, (i + step) % size) for i in range(size)])  9.11 us
    pallas_call x2, Pallas kernels, late(): pl.pallas_call(functools.partial(late_kernel, with_stats, ways, len(block...  6.13 us
    pallas_call x1, Pallas kernels, early(): pl.pallas_call(early_kernel, in_specs=[SMEM] * 3 + [VMEM] * 2 + [hbm] * 2...  6.06 us
    unnamed x30, local copies, waits for them, and re-layouts  4.37 us
    pallas_call x2, Pallas kernels, heads(): pl.pallas_call(functools.partial(head_kernel, with_stats), in_specs=[SMEM...  4.03 us
  transfers between devices with their start and end apart: 20, of which 8 were waited for; matrix products, arithmetic and copies ran while one was open for 1% of the time, Pallas kernels for 19%

profile of v15, /device:TPU:32, one launch (start us, length us, event | category | flops | bytes accessed | tf_op | source)
XLA Modules:
  0.0 125.7 jit_solution(1313208886778047817)
XLA Ops:
  7.2 3.4 %shard_map.94.refs_0_.own = bf16[144,1152]{1,0:T(8,128)(2,1)} custom-call(bf16[128,1152]{1,0:T(8,128)(2,1)} %bitcast.4, bf16[1152,1152]{1,0:T(8,128)(2,1)} %wt_hbm.1, s32[1,128]{1,0:T(1,128)} %key.1), custom_call_target="tpu_custom_call" | custom-call | flops 339738624 | bytes 4194304 | tf_op jit(solution)/shard_map/pallas_call | solution.py:81
  11.5 1.7 %collective-permute-start.1 = (bf16[144,1152]{1,0:T(8,128)(2,1)}, bf16[144,1152]{1,0:T(8,128)(2,1)S(1)}, u32[]{:S(2)}, u32[]{:S(2)}) collective-permute-start(bf16[144,1152]{1,0:T(8,128)(2,1)} %shard_map.94.refs_0_.own), channel_id=1, source_target_pairs={{0,64},{64,0},{128,192},{192,128},{1,65},{65,1},{129,193},{193,129... | collective-permute-start | bytes 995336 | tf_op jit(solution)/shard_map/ppermute | solution.py:41
  13.2 3.3 %collective-permute-start.2 = (bf16[144,1152]{1,0:T(8,128)(2,1)}, bf16[144,1152]{1,0:T(8,128)(2,1)S(1)}, u32[]{:S(2)}, u32[]{:S(2)}) collective-permute-start(bf16[144,1152]{1,0:T(8,128)(2,1)} %shard_map.94.refs_0_.own), channel_id=1, source_target_pairs={{0,16},{16,0},{32,48},{48,32},{1,17},{17,1},{33,49},{49,33},{2,18}... | collective-permute-start | bytes 995336 | tf_op jit(solution)/shard_map/ppermute | solution.py:41
  16.4 2.9 %collective-permute-start.3 = (bf16[144,1152]{1,0:T(8,128)(2,1)}, bf16[144,1152]{1,0:T(8,128)(2,1)S(1)}, u32[]{:S(2)}, u32[]{:S(2)}) collective-permute-start(bf16[144,1152]{1,0:T(8,128)(2,1)} %shard_map.94.refs_0_.own), channel_id=1, source_target_pairs={{0,128},{64,192},{128,0},{192,64},{1,129},{65,193},{129,1},{193,65... | collective-permute-start | bytes 995336 | tf_op jit(solution)/shard_map/ppermute | solution.py:41
  22.0 6.1 %shard_map.95 = (bf16[128,1152]{1,0:T(8,128)(2,1)}, f32[2,8,128]{2,1,0:T(8,128)}, f32[128,1152]{1,0:T(8,128)}, f32[128,1152]{1,0:T(8,128)}, f32[128,128]{1,0:T(8...) custom-call(s32[2]{0:T(128)} %pad_add_fusion.spot, ...), custom_call_target="tpu_custom_call" | custom-call | flops 377487360 | bytes 8388608 | tf_op jit(solution)/shard_map/pallas_call | solution.py:190
  28.1 2.6 %collective-permute-done.2.refs_2_ = bf16[144,1152]{1,0:T(8,128)(2,1)S(1)} collective-permute-done((bf16[144,1152]{1,0:T(8,128)(2,1)}, bf16[144,1152]{1,0:T(8,128)(2,1)S(1)}, u32[]{:S(2)}, u32[]{:S(2)}) %collective-permute-start.2) | collective-permute-done | bytes 331808 | tf_op jit(solution)/shard_map/ppermute | solution.py:41
  31.5 3.3 %collective-permute-start.7 = (bf16[128,1152]{1,0:T(8,128)(2,1)}, bf16[128,1152]{1,0:T(8,128)(2,1)S(1)}, u32[]{:S(2)}, u32[]{:S(2)}) collective-permute-start(bf16[128,1152]{1,0:T(8,128)(2,1)} %get-tuple-element.51.own.refs_0_), channel_id=1, source_target_pairs={{0,16},{16,0},{32,48},{48,32},{1,17},{17,1},{33,49},{49,33},{2,18}... | collective-permute-start | bytes 884744 | tf_op jit(solution)/shard_map/ppermute | solution.py:41
  34.8 3.6 %collective-permute-start.8 = (bf16[144,1152]{1,0:T(8,128)(2,1)S(1)}, bf16[144,1152]{1,0:T(8,128)(2,1)S(1)}, u32[]{:S(2)}, u32[]{:S(2)}) collective-permute-start(bf16[144,1152]{1,0:T(8,128)(2,1)S(1)} %collective-permute-done.2.refs_2_), channel_id=1, source_target_pairs={{0,48},{16,32},{32,16},{48,0},{1,49},{17,33},{33,17},{49,1},{2,50}... | collective-permute-start | bytes 995336 | tf_op jit(solution)/shard_map/ppermute | solution.py:41
  38.4 3.8 %shard_map.96 = (f32[128,1152]{1,0:T(8,128)}, f32[3,128,128]{2,1,0:T(8,128)}, f32[3,8,128]{2,1,0:T(8,128)}) custom-call(f32[1]{0:T(128)S(6)} %copy.10.heat_log, f32[1]{0:T(128)S(6)} %copy.11.shift, bf16[128,1152]{1,0:T(8,128)(2,1)} %get-tuple-element.51.own.refs_0_, f32[128,1152]{1,0:T(8,128)} %get-tuple-element.45.total_ref, ...), custom_call_target="tpu_custom_call" | custom-call | flops 226492416 | bytes 4194304 | tf_op jit(solution)/shard_map/pallas_call | solution.py:220
  42.3 2.1 %collective-permute-start.6 = (bf16[128,1152]{1,0:T(8,128)(2,1)}, bf16[128,1152]{1,0:T(8,128)(2,1)S(1)}, u32[]{:S(2)}, u32[]{:S(2)}) collective-permute-start(bf16[128,1152]{1,0:T(8,128)(2,1)} %get-tuple-element.51.own.refs_0_), channel_id=1, source_target_pairs={{0,128},{64,192},{128,0},{192,64},{1,129},{65,193},{129,1},{193,65... | collective-permute-start | bytes 884744 | tf_op jit(solution)/shard_map/ppermute | solution.py:41
  44.4 3.5 %collective-permute-done.7.refs_4_ = bf16[128,1152]{1,0:T(8,128)(2,1)S(1)} collective-permute-done((bf16[128,1152]{1,0:T(8,128)(2,1)}, bf16[128,1152]{1,0:T(8,128)(2,1)S(1)}, u32[]{:S(2)}, u32[]{:S(2)}) %collective-permute-start.7) | collective-permute-done | bytes 294944 | tf_op jit(solution)/shard_map/ppermute | solution.py:41
  47.9 5.5 %collective-permute-start.9 = (bf16[128,1152]{1,0:T(8,128)(2,1)S(1)}, bf16[128,1152]{1,0:T(8,128)(2,1)S(1)}, u32[]{:S(2)}, u32[]{:S(2)}) collective-permute-start(bf16[128,1152]{1,0:T(8,128)(2,1)S(1)} %collective-permute-done.7.refs_4_), channel_id=1, source_target_pairs={{0,48},{16,32},{32,16},{48,0},{1,49},{17,33},{33,17},{49,1},{2,50}... | collective-permute-start | bytes 884744 | tf_op jit(solution)/shard_map/ppermute | solution.py:41
  53.4 7.1 %collective-permute-done.8.refs_5_ = bf16[144,1152]{1,0:T(8,128)(2,1)S(1)} collective-permute-done((bf16[144,1152]{1,0:T(8,128)(2,1)S(1)}, bf16[144,1152]{1,0:T(8,128)(2,1)S(1)}, u32[]{:S(2)}, u32[]{:S(2)}) %collective-permute-start.8) | collective-permute-done | bytes 331808 | tf_op jit(solution)/shard_map/ppermute | solution.py:41
  61.3 3.1 %shard_map.98 = (bf16[304,128]{1,0:T(8,128)(2,1)}, bf16[304,128]{1,0:T(8,128)(2,1)}, bf16[304,128]{1,0:T(8,128)(2,1)}, bf16[304,128]{1,0:T(8,128)(2,1)}, f32[1,8,128]{2,1,0:T(8,128)}) custom-call(s32[2]{0:T(128)} %pad_add_fusion.spot, f32[1]{0:T(128)S(6)} %copy.10.heat_log, f32[1]{0:T(128)S(6)} %copy.11.shift, ...), custom_call_target="tpu_custom_call" | custom-call | flops 150994944 | bytes 4194304 | tf_op jit(solution)/shard_map/pallas_call | solution.py:313
  64.4 1.6 %collective-permute-start.10 = (bf16[304,128]{1,0:T(8,128)(2,1)}, bf16[304,128]{1,0:T(8,128)(2,1)S(1)}, u32[]{:S(2)}, u32[]{:S(2)}) collective-permute-start(bf16[304,128]{1,0:T(8,128)(2,1)} %get-tuple-element.65), channel_id=1, source_target_pairs={{0,1},{1,2},{2,3},{3,0},{4,5},{5,6},{6,7},{7,4},{8,9},{9,10},{10,1... | collective-permute-start | bytes 233480 | tf_op jit(solution)/shard_map/ppermute | solution.py:457
  66.0 2.8 %collective-permute-start.11 = (bf16[304,128]{1,0:T(8,128)(2,1)}, bf16[304,128]{1,0:T(8,128)(2,1)S(1)}, u32[]{:S(2)}, u32[]{:S(2)}) collective-permute-start(bf16[304,128]{1,0:T(8,128)(2,1)} %get-tuple-element.66), channel_id=1, source_target_pairs={{0,2},{1,3},{2,0},{3,1},{4,6},{5,7},{6,4},{7,5},{8,10},{9,11},{10,... | collective-permute-start | bytes 233480 | tf_op jit(solution)/shard_map/ppermute | solution.py:457
  68.7 1.4 %collective-permute-start.12 = (bf16[304,128]{1,0:T(8,128)(2,1)}, bf16[304,128]{1,0:T(8,128)(2,1)S(1)}, u32[]{:S(2)}, u32[]{:S(2)}) collective-permute-start(bf16[304,128]{1,0:T(8,128)(2,1)} %get-tuple-element.67), channel_id=1, source_target_pairs={{0,3},{1,0},{2,1},{3,2},{4,7},{5,4},{6,5},{7,6},{8,11},{9,8},{10,9... | collective-permute-start | bytes 233480 | tf_op jit(solution)/shard_map/ppermute | solution.py:457
  70.2 4.0 %shard_map.97.refs_0_ = f32[128,1152]{1,0:T(8,128)} custom-call(f32[1]{0:T(128)S(6)} %copy.10.heat_log, f32[1]{0:T(128)S(6)} %copy.11.shift, bf16[144,1152]{1,0:T(8,128)(2,1)} %shard_map.94.refs_0_.own, f32[128,128]{1,0:T(8,128)} %get-tuple-element.42.key.refs_3_.refs_4_, f32[2,8,128]{2,1,0:T(8,128)} %get-tuple-element.43.near_rows, ...), custom_call_target="tpu_custom_call" | custom-call | flops 377487360 | bytes 4194304 | tf_op jit(solution)/shard_map/pallas_call | solution.py:248
  74.9 3.0 %shard_map.99 = (bf16[288,128]{1,0:T(8,128)(2,1)}, bf16[288,128]{1,0:T(8,128)(2,1)}, bf16[288,128]{1,0:T(8,128)(2,1)}, bf16[288,128]{1,0:T(8,128)(2,1)}) custom-call(s32[2]{0:T(128)} %pad_add_fusion.spot, f32[1]{0:T(128)S(6)} %copy.10.heat_log, f32[1]{0:T(128)S(6)} %copy.11.shift, bf16[144,1152]{1,0:T(8,128)(2,1)} %shard_map.94.refs_0_.own, ...), custom_call_target="tpu_custom_call" | custom-call | flops 150994944 | bytes 4194304 | tf_op jit(solution)/shard_map/pallas_call | solution.py:313
  78.5 2.0 %collective-permute-start.15 = (bf16[288,128]{1,0:T(8,128)(2,1)}, bf16[288,128]{1,0:T(8,128)(2,1)S(1)}, u32[]{:S(2)}, u32[]{:S(2)}) collective-permute-start(bf16[288,128]{1,0:T(8,128)(2,1)} %get-tuple-element.75), channel_id=1, source_target_pairs={{0,2},{1,3},{2,0},{3,1},{4,6},{5,7},{6,4},{7,5},{8,10},{9,11},{10,... | collective-permute-start | bytes 221192 | tf_op jit(solution)/shard_map/ppermute | solution.py:457
  81.3 2.0 %shard_map.100 = (f32[32,48,128]{2,1,0:T(8,128)S(1)}, bf16[32,48,128]{2,1,0:T(8,128)(2,1)S(1)}) custom-call(s32[2]{0:T(128)S(1)} %copy-done.4, bf16[512,1152]{1,0:T(8,128)(2,1)S(1)} %copy-done.1, bf16[304,128]{1,0:T(8,128)(2,1)S(1)} %copy-done.2, bf16[304,128]{1,0:T(8,128)(2,1)S(1)} %collective-permute-done.10.refs_1_, ...), custom_call_target="tpu_custom_call" | custom-call | flops 339738624 | bytes 4194304 | tf_op jit(solution)/shard_map/pallas_call | solution.py:373
  87.5 2.0 %shard_map.101 = (f32[32,48,128]{2,1,0:T(8,128)S(1)}, bf16[32,48,128]{2,1,0:T(8,128)(2,1)S(1)}) custom-call(s32[2]{0:T(128)S(1)} %copy-done.4, bf16[512,1152]{1,0:T(8,128)(2,1)S(1)} %copy-done, bf16[288,128]{1,0:T(8,128)(2,1)S(1)} %copy-done.3, bf16[288,128]{1,0:T(8,128)(2,1)S(1)} %collective-permute-done.14.refs_1_, ...), custom_call_target="tpu_custom_call" | custom-call | flops 339738624 | bytes 4194304 | tf_op jit(solution)/shard_map/pallas_call | solution.py:373
  89.6 1.7 %collective-permute-done.17.taken_txt = bf16[32,48,128]{2,1,0:T(8,128)(2,1)S(1)} collective-permute-done((bf16[32,48,128]{2,1,0:T(8,128)(2,1)S(1)}, bf16[32,48,128]{2,1,0:T(8,128)(2,1)S(1)}, u32[]{:S(2)}, u32[]{:S(2)}) %collective-permute-start.17) | collective-permute-done | bytes 393248 | tf_op jit(solution)/shard_map/ppermute | solution.py:41
  91.4 26.5 %all_to_all.5.parts = bf16[32,96,128]{2,1,0:T(8,128)(2,1)S(1)} all-to-all(bf16[32,96,128]{2,1,0:T(8,128)(2,1)S(1)} %shard_map.102), channel_id=1, replica_groups=mesh['ly'=4,'lz'=4,'lc'=2,'dz'=2,'dx'=4] {'ly','lz','dz'}, dimensions={0} | all-to-all | bytes 1572864 | tf_op jit(solution)/shard_map/all_to_all | solution.py:480
  (60 shorter events, 11.3 us)
Async XLA Ops:
  7.2 53.3 %all-gather.3.cloned.1.call-start = ((), (), s32[]{:S(2)}) async-start(), calls=%async_computation.1 | async-start | bytes 1474560 | tf_op jit(solution)/shard_map/all_gather | solution.py:435
  10.6 70.6 %all-gather.5.cloned.1.call-start = ((), (), s32[]{:S(2)}) async-start(), calls=%async_computation.2 | async-start | bytes 1474560 | tf_op jit(solution)/shard_map/all_gather | solution.py:436
  11.4 9.9 %collective-permute-start = (bf16[144,1152]{1,0:T(8,128)(2,1)}, bf16[144,1152]{1,0:T(8,128)(2,1)S(1)}, u32[]{:S(2)}, u32[]{:S(2)}) collective-permute-start(bf16[144,1152]{1,0:T(8,128)(2,1)} %shard_map.94.refs_0_.own), channel_id=1, source_target_pairs={{0,8},{8,0},{1,9},{9,1},{2,10},{10,2},{3,11},{11,3},{4,12},{12,4},... | collective-permute-start | bytes 995336 | tf_op jit(solution)/shard_map/ppermute | solution.py:41
  11.5 16.6 %collective-permute-start.1 = (bf16[144,1152]{1,0:T(8,128)(2,1)}, bf16[144,1152]{1,0:T(8,128)(2,1)S(1)}, u32[]{:S(2)}, u32[]{:S(2)}) collective-permute-start(bf16[144,1152]{1,0:T(8,128)(2,1)} %shard_map.94.refs_0_.own), channel_id=1, source_target_pairs={{0,64},{64,0},{128,192},{192,128},{1,65},{65,1},{129,193},{193,129... | collective-permute-start | bytes 995336 | tf_op jit(solution)/shard_map/ppermute | solution.py:41
  13.2 17.6 %collective-permute-start.2 = (bf16[144,1152]{1,0:T(8,128)(2,1)}, bf16[144,1152]{1,0:T(8,128)(2,1)S(1)}, u32[]{:S(2)}, u32[]{:S(2)}) collective-permute-start(bf16[144,1152]{1,0:T(8,128)(2,1)} %shard_map.94.refs_0_.own), channel_id=1, source_target_pairs={{0,16},{16,0},{32,48},{48,32},{1,17},{17,1},{33,49},{49,33},{2,18}... | collective-permute-start | bytes 995336 | tf_op jit(solution)/shard_map/ppermute | solution.py:41
  16.4 15.1 %collective-permute-start.3 = (bf16[144,1152]{1,0:T(8,128)(2,1)}, bf16[144,1152]{1,0:T(8,128)(2,1)S(1)}, u32[]{:S(2)}, u32[]{:S(2)}) collective-permute-start(bf16[144,1152]{1,0:T(8,128)(2,1)} %shard_map.94.refs_0_.own), channel_id=1, source_target_pairs={{0,128},{64,192},{128,0},{192,64},{1,129},{65,193},{129,1},{193,65... | collective-permute-start | bytes 995336 | tf_op jit(solution)/shard_map/ppermute | solution.py:41
  31.5 6.9 %collective-permute-start.4 = (bf16[128,1152]{1,0:T(8,128)(2,1)}, bf16[128,1152]{1,0:T(8,128)(2,1)S(1)}, u32[]{:S(2)}, u32[]{:S(2)}) collective-permute-start(bf16[128,1152]{1,0:T(8,128)(2,1)} %get-tuple-element.51.own.refs_0_), channel_id=1, source_target_pairs={{0,8},{8,0},{1,9},{9,1},{2,10},{10,2},{3,11},{11,3},{4,12},{12,4},... | collective-permute-start | bytes 884744 | tf_op jit(solution)/shard_map/ppermute | solution.py:41
  31.5 16.4 %collective-permute-start.7 = (bf16[128,1152]{1,0:T(8,128)(2,1)}, bf16[128,1152]{1,0:T(8,128)(2,1)S(1)}, u32[]{:S(2)}, u32[]{:S(2)}) collective-permute-start(bf16[128,1152]{1,0:T(8,128)(2,1)} %get-tuple-element.51.own.refs_0_), channel_id=1, source_target_pairs={{0,16},{16,0},{32,48},{48,32},{1,17},{17,1},{33,49},{49,33},{2,18}... | collective-permute-start | bytes 884744 | tf_op jit(solution)/shard_map/ppermute | solution.py:41
  34.8 25.7 %collective-permute-start.8 = (bf16[144,1152]{1,0:T(8,128)(2,1)S(1)}, bf16[144,1152]{1,0:T(8,128)(2,1)S(1)}, u32[]{:S(2)}, u32[]{:S(2)}) collective-permute-start(bf16[144,1152]{1,0:T(8,128)(2,1)S(1)} %collective-permute-done.2.refs_2_), channel_id=1, source_target_pairs={{0,48},{16,32},{32,16},{48,0},{1,49},{17,33},{33,17},{49,1},{2,50}... | collective-permute-start | bytes 995336 | tf_op jit(solution)/shard_map/ppermute | solution.py:41
  38.3 31.8 %copy-start.10 = (bf16[128,1152]{1,0:T(8,128)(2,1)}, bf16[128,1152]{1,0:T(8,128)(2,1)S(1)}, u32[]{:S(2)}) copy-start(bf16[128,1152]{1,0:T(8,128)(2,1)S(1)} %collective-permute-done.4.refs_1_) | copy-start | bytes 884740
  42.2 22.2 %collective-permute-start.5 = (bf16[128,1152]{1,0:T(8,128)(2,1)}, bf16[128,1152]{1,0:T(8,128)(2,1)S(1)}, u32[]{:S(2)}, u32[]{:S(2)}) collective-permute-start(bf16[128,1152]{1,0:T(8,128)(2,1)} %get-tuple-element.51.own.refs_0_), channel_id=1, source_target_pairs={{0,64},{64,0},{128,192},{192,128},{1,65},{65,1},{129,193},{193,129... | collective-permute-start | bytes 884744 | tf_op jit(solution)/shard_map/ppermute | solution.py:41
  42.3 22.1 %collective-permute-start.6 = (bf16[128,1152]{1,0:T(8,128)(2,1)}, bf16[128,1152]{1,0:T(8,128)(2,1)S(1)}, u32[]{:S(2)}, u32[]{:S(2)}) collective-permute-start(bf16[128,1152]{1,0:T(8,128)(2,1)} %get-tuple-element.51.own.refs_0_), channel_id=1, source_target_pairs={{0,128},{64,192},{128,0},{192,64},{1,129},{65,193},{129,1},{193,65... | collective-permute-start | bytes 884744 | tf_op jit(solution)/shard_map/ppermute | solution.py:41
  47.9 22.2 %copy-start.11 = (bf16[128,1152]{1,0:T(8,128)(2,1)}, bf16[128,1152]{1,0:T(8,128)(2,1)S(1)}, u32[]{:S(2)}) copy-start(bf16[128,1152]{1,0:T(8,128)(2,1)S(1)} %collective-permute-done.7.refs_4_) | copy-start | bytes 884740
  47.9 26.2 %collective-permute-start.9 = (bf16[128,1152]{1,0:T(8,128)(2,1)S(1)}, bf16[128,1152]{1,0:T(8,128)(2,1)S(1)}, u32[]{:S(2)}, u32[]{:S(2)}) collective-permute-start(bf16[128,1152]{1,0:T(8,128)(2,1)S(1)} %collective-permute-done.7.refs_4_), channel_id=1, source_target_pairs={{0,48},{16,32},{32,16},{48,0},{1,49},{17,33},{33,17},{49,1},{2,50}... | collective-permute-start | bytes 884744 | tf_op jit(solution)/shard_map/ppermute | solution.py:41
  64.4 16.9 %copy-start.1 = (bf16[512,1152]{1,0:T(8,128)(2,1)S(1)}, bf16[512,1152]{1,0:T(8,128)(2,1)}, u32[]{:S(2)}) copy-start(bf16[512,1152]{1,0:T(8,128)(2,1)} %all-gather.3.cloned.1.call-done.feat) | copy-start | bytes 3538948
  64.4 16.9 %copy-start.2 = (bf16[304,128]{1,0:T(8,128)(2,1)S(1)}, bf16[304,128]{1,0:T(8,128)(2,1)}, u32[]{:S(2)}) copy-start(bf16[304,128]{1,0:T(8,128)(2,1)} %get-tuple-element.64.refs_0_) | copy-start | bytes 233476
  64.4 9.7 %collective-permute-start.10 = (bf16[304,128]{1,0:T(8,128)(2,1)}, bf16[304,128]{1,0:T(8,128)(2,1)S(1)}, u32[]{:S(2)}, u32[]{:S(2)}) collective-permute-start(bf16[304,128]{1,0:T(8,128)(2,1)} %get-tuple-element.65), channel_id=1, source_target_pairs={{0,1},{1,2},{2,3},{3,0},{4,5},{5,6},{6,7},{7,4},{8,9},{9,10},{10,1... | collective-permute-start | bytes 233480 | tf_op jit(solution)/shard_map/ppermute | solution.py:457
  66.0 8.2 %collective-permute-start.11 = (bf16[304,128]{1,0:T(8,128)(2,1)}, bf16[304,128]{1,0:T(8,128)(2,1)S(1)}, u32[]{:S(2)}, u32[]{:S(2)}) collective-permute-start(bf16[304,128]{1,0:T(8,128)(2,1)} %get-tuple-element.66), channel_id=1, source_target_pairs={{0,2},{1,3},{2,0},{3,1},{4,6},{5,7},{6,4},{7,5},{8,10},{9,11},{10,... | collective-permute-start | bytes 233480 | tf_op jit(solution)/shard_map/ppermute | solution.py:457
  68.7 5.4 %collective-permute-start.12 = (bf16[304,128]{1,0:T(8,128)(2,1)}, bf16[304,128]{1,0:T(8,128)(2,1)S(1)}, u32[]{:S(2)}, u32[]{:S(2)}) collective-permute-start(bf16[304,128]{1,0:T(8,128)(2,1)} %get-tuple-element.67), channel_id=1, source_target_pairs={{0,3},{1,0},{2,1},{3,2},{4,7},{5,4},{6,5},{7,6},{8,11},{9,8},{10,9... | collective-permute-start | bytes 233480 | tf_op jit(solution)/shard_map/ppermute | solution.py:457
  77.9 5.8 %collective-permute-start.14 = (bf16[288,128]{1,0:T(8,128)(2,1)}, bf16[288,128]{1,0:T(8,128)(2,1)S(1)}, u32[]{:S(2)}, u32[]{:S(2)}) collective-permute-start(bf16[288,128]{1,0:T(8,128)(2,1)} %get-tuple-element.74), channel_id=1, source_target_pairs={{0,1},{1,2},{2,3},{3,0},{4,5},{5,6},{6,7},{7,4},{8,9},{9,10},{10,1... | collective-permute-start | bytes 221192 | tf_op jit(solution)/shard_map/ppermute | solution.py:457
  78.5 6.1 %collective-permute-start.15 = (bf16[288,128]{1,0:T(8,128)(2,1)}, bf16[288,128]{1,0:T(8,128)(2,1)S(1)}, u32[]{:S(2)}, u32[]{:S(2)}) collective-permute-start(bf16[288,128]{1,0:T(8,128)(2,1)} %get-tuple-element.75), channel_id=1, source_target_pairs={{0,2},{1,3},{2,0},{3,1},{4,6},{5,7},{6,4},{7,5},{8,10},{9,11},{10,... | collective-permute-start | bytes 221192 | tf_op jit(solution)/shard_map/ppermute | solution.py:457
  80.5 4.8 %collective-permute-start.16 = (bf16[288,128]{1,0:T(8,128)(2,1)}, bf16[288,128]{1,0:T(8,128)(2,1)S(1)}, u32[]{:S(2)}, u32[]{:S(2)}) collective-permute-start(bf16[288,128]{1,0:T(8,128)(2,1)} %get-tuple-element.76), channel_id=1, source_target_pairs={{0,3},{1,0},{2,1},{3,2},{4,7},{5,4},{6,5},{7,6},{8,11},{9,8},{10,9... | collective-permute-start | bytes 221192 | tf_op jit(solution)/shard_map/ppermute | solution.py:457
  83.3 6.3 %collective-permute-start.13 = (bf16[32,48,128]{2,1,0:T(8,128)(2,1)S(1)}, bf16[32,48,128]{2,1,0:T(8,128)(2,1)S(1)}, u32[]{:S(2)}, u32[]{:S(2)}) collective-permute-start(bf16[32,48,128]{2,1,0:T(8,128)(2,1)S(1)} %get-tuple-element.73), channel_id=1, source_target_pairs={{0,8},{8,0},{1,9},{9,1},{2,10},{10,2},{3,11},{11,3},{4,12},{12,4},... | collective-permute-start | bytes 1179656 | tf_op jit(solution)/shard_map/ppermute | solution.py:41
  89.5 1.8 %collective-permute-start.17 = (bf16[32,48,128]{2,1,0:T(8,128)(2,1)S(1)}, bf16[32,48,128]{2,1,0:T(8,128)(2,1)S(1)}, u32[]{:S(2)}, u32[]{:S(2)}) collective-permute-start(bf16[32,48,128]{2,1,0:T(8,128)(2,1)S(1)} %get-tuple-element.78), channel_id=1, source_target_pairs={{0,8},{8,0},{1,9},{9,1},{2,10},{10,2},{3,11},{11,3},{4,12},{12,4},... | collective-permute-start | bytes 1179656 | tf_op jit(solution)/shard_map/ppermute | solution.py:41
  (11 other events, 57.5 us)
Sparse Core Ops, SparseCore 0:
  10.8 29.5 all-gather.2
  42.1 28.1 all-gather.4

commit v16 on v15

--- a/solution.py
+++ b/solution.py
@@ -469,7 +469,7 @@
         scal, txt, first[5], near_rows, mid_rows, img, img_c, img_y1, img_y2, img_a
     )
     txt_part = (txt_total, *first[3:5], first[5], first[5])
-    last = after(img_b, *img_cols, txt_total)
+    last = after(img_b, img_cols[1], img_cols[3], txt_total)
     outs = late(False, ways, spot, scal, txt, txt_part, [far_rows, last])
     txt_cols = columns(outs)
     img_kept, img_given = heads(True, spot, after(img_feat, outs[0], txt_feat), img_cols)

time: 126 us -> 125 us (level)
  transfers between devices with their start and end apart: 20 -> 20, of which waited for: 8 -> 7; matrix products, arithmetic and copies ran while one was open for 1% -> 1% of each run, Pallas kernels for 19% -> 19%
where the time goes in v16:
time: 125 us
  starting transfers between devices  32.3 us (26%)
  Pallas kernels  28.4 us (23%)
  blocking collectives  26.5 us (21%)
  waiting for transfers between devices  17.2 us (14%)
  between operations  15.5 us (12%)
  local copies, waits for them, and re-layouts  4.38 us (4%)
    all_to_all x1, blocking collectives, body(): sums = lax.all_to_all(sums, ('ly', 'lz', 'dz'), 0, 0, tiled=True)  26.5 us
    ppermute x12, starting transfers between devices, exchange(): lax.ppermute(array, axis, [(i, i ^ apart) for i in range(lax.axis_size(ax...  22.7 us
    ppermute x12, waiting for transfers between devices, exchange(): lax.ppermute(array, axis, [(i, i ^ apart) for i in range(lax.axis_size(ax...  15.6 us
    ppermute x6, starting transfers between devices, turn(): lax.ppermute(array, axis, [(i, (i + step) % size) for i in range(size)])  9.5 us
    pallas_call x2, Pallas kernels, late(): pl.pallas_call(functools.partial(late_kernel, with_stats, ways, len(block...  6.11 us
    pallas_call x1, Pallas kernels, early(): pl.pallas_call(early_kernel, in_specs=[SMEM] * 3 + [VMEM] * 2 + [hbm] * 2...  6.06 us
    unnamed x30, local copies, waits for them, and re-layouts  4.38 us
    pallas_call x2, Pallas kernels, heads(): pl.pallas_call(functools.partial(head_kernel, with_stats), in_specs=[SMEM...  4.03 us
  transfers between devices with their start and end apart: 20, of which 7 were waited for; matrix products, arithmetic and copies ran while one was open for 1% of the time, Pallas kernels for 19%

profile of v16, /device:TPU:32, one launch (start us, length us, event | category | flops | bytes accessed | tf_op | source)
XLA Modules:
  0.0 125.1 jit_solution(15647120960407610884)
XLA Ops:
  7.2 3.4 %shard_map.94.refs_0_.own = bf16[144,1152]{1,0:T(8,128)(2,1)} custom-call(bf16[128,1152]{1,0:T(8,128)(2,1)} %bitcast.4, bf16[1152,1152]{1,0:T(8,128)(2,1)} %wt_hbm.1, s32[1,128]{1,0:T(1,128)} %key.1), custom_call_target="tpu_custom_call" | custom-call | flops 339738624 | bytes 4194304 | tf_op jit(solution)/shard_map/pallas_call | solution.py:81
  11.5 1.7 %collective-permute-start.1 = (bf16[144,1152]{1,0:T(8,128)(2,1)}, bf16[144,1152]{1,0:T(8,128)(2,1)S(1)}, u32[]{:S(2)}, u32[]{:S(2)}) collective-permute-start(bf16[144,1152]{1,0:T(8,128)(2,1)} %shard_map.94.refs_0_.own), channel_id=1, source_target_pairs={{0,64},{64,0},{128,192},{192,128},{1,65},{65,1},{129,193},{193,129... | collective-permute-start | bytes 995336 | tf_op jit(solution)/shard_map/ppermute | solution.py:41
  13.2 3.3 %collective-permute-start.2 = (bf16[144,1152]{1,0:T(8,128)(2,1)}, bf16[144,1152]{1,0:T(8,128)(2,1)S(1)}, u32[]{:S(2)}, u32[]{:S(2)}) collective-permute-start(bf16[144,1152]{1,0:T(8,128)(2,1)} %shard_map.94.refs_0_.own), channel_id=1, source_target_pairs={{0,16},{16,0},{32,48},{48,32},{1,17},{17,1},{33,49},{49,33},{2,18}... | collective-permute-start | bytes 995336 | tf_op jit(solution)/shard_map/ppermute | solution.py:41
  16.4 2.9 %collective-permute-start.3 = (bf16[144,1152]{1,0:T(8,128)(2,1)}, bf16[144,1152]{1,0:T(8,128)(2,1)S(1)}, u32[]{:S(2)}, u32[]{:S(2)}) collective-permute-start(bf16[144,1152]{1,0:T(8,128)(2,1)} %shard_map.94.refs_0_.own), channel_id=1, source_target_pairs={{0,128},{64,192},{128,0},{192,64},{1,129},{65,193},{129,1},{193,65... | collective-permute-start | bytes 995336 | tf_op jit(solution)/shard_map/ppermute | solution.py:41
  22.0 6.1 %shard_map.95 = (bf16[128,1152]{1,0:T(8,128)(2,1)}, f32[2,8,128]{2,1,0:T(8,128)}, f32[128,1152]{1,0:T(8,128)}, f32[128,1152]{1,0:T(8,128)}, f32[128,128]{1,0:T(8...) custom-call(s32[2]{0:T(128)} %pad_add_fusion.spot, ...), custom_call_target="tpu_custom_call" | custom-call | flops 377487360 | bytes 8388608 | tf_op jit(solution)/shard_map/pallas_call | solution.py:190
  28.1 2.6 %collective-permute-done.2.refs_2_ = bf16[144,1152]{1,0:T(8,128)(2,1)S(1)} collective-permute-done((bf16[144,1152]{1,0:T(8,128)(2,1)}, bf16[144,1152]{1,0:T(8,128)(2,1)S(1)}, u32[]{:S(2)}, u32[]{:S(2)}) %collective-permute-start.2) | collective-permute-done | bytes 331808 | tf_op jit(solution)/shard_map/ppermute | solution.py:41
  31.5 3.3 %collective-permute-start.7 = (bf16[128,1152]{1,0:T(8,128)(2,1)}, bf16[128,1152]{1,0:T(8,128)(2,1)S(1)}, u32[]{:S(2)}, u32[]{:S(2)}) collective-permute-start(bf16[128,1152]{1,0:T(8,128)(2,1)} %get-tuple-element.51.own.refs_0_), channel_id=1, source_target_pairs={{0,16},{16,0},{32,48},{48,32},{1,17},{17,1},{33,49},{49,33},{2,18}... | collective-permute-start | bytes 884744 | tf_op jit(solution)/shard_map/ppermute | solution.py:41
  34.8 3.6 %collective-permute-start.8 = (bf16[144,1152]{1,0:T(8,128)(2,1)S(1)}, bf16[144,1152]{1,0:T(8,128)(2,1)S(1)}, u32[]{:S(2)}, u32[]{:S(2)}) collective-permute-start(bf16[144,1152]{1,0:T(8,128)(2,1)S(1)} %collective-permute-done.2.refs_2_), channel_id=1, source_target_pairs={{0,48},{16,32},{32,16},{48,0},{1,49},{17,33},{33,17},{49,1},{2,50}... | collective-permute-start | bytes 995336 | tf_op jit(solution)/shard_map/ppermute | solution.py:41
  38.4 3.8 %shard_map.96 = (f32[128,1152]{1,0:T(8,128)}, f32[3,128,128]{2,1,0:T(8,128)}, f32[3,8,128]{2,1,0:T(8,128)}) custom-call(f32[1]{0:T(128)S(6)} %copy.10.heat_log, f32[1]{0:T(128)S(6)} %copy.11.shift, bf16[128,1152]{1,0:T(8,128)(2,1)} %get-tuple-element.51.own.refs_0_, f32[128,1152]{1,0:T(8,128)} %get-tuple-element.45.total_ref, ...), custom_call_target="tpu_custom_call" | custom-call | flops 226492416 | bytes 4194304 | tf_op jit(solution)/shard_map/pallas_call | solution.py:220
  42.3 2.1 %collective-permute-start.6 = (bf16[128,1152]{1,0:T(8,128)(2,1)}, bf16[128,1152]{1,0:T(8,128)(2,1)S(1)}, u32[]{:S(2)}, u32[]{:S(2)}) collective-permute-start(bf16[128,1152]{1,0:T(8,128)(2,1)} %get-tuple-element.51.own.refs_0_), channel_id=1, source_target_pairs={{0,128},{64,192},{128,0},{192,64},{1,129},{65,193},{129,1},{193,65... | collective-permute-start | bytes 884744 | tf_op jit(solution)/shard_map/ppermute | solution.py:41
  44.4 3.5 %collective-permute-done.7.refs_4_ = bf16[128,1152]{1,0:T(8,128)(2,1)S(1)} collective-permute-done((bf16[128,1152]{1,0:T(8,128)(2,1)}, bf16[128,1152]{1,0:T(8,128)(2,1)S(1)}, u32[]{:S(2)}, u32[]{:S(2)}) %collective-permute-start.7) | collective-permute-done | bytes 294944 | tf_op jit(solution)/shard_map/ppermute | solution.py:41
  47.9 5.5 %collective-permute-start.9 = (bf16[128,1152]{1,0:T(8,128)(2,1)S(1)}, bf16[128,1152]{1,0:T(8,128)(2,1)S(1)}, u32[]{:S(2)}, u32[]{:S(2)}) collective-permute-start(bf16[128,1152]{1,0:T(8,128)(2,1)S(1)} %collective-permute-done.7.refs_4_), channel_id=1, source_target_pairs={{0,48},{16,32},{32,16},{48,0},{1,49},{17,33},{33,17},{49,1},{2,50}... | collective-permute-start | bytes 884744 | tf_op jit(solution)/shard_map/ppermute | solution.py:41
  53.4 7.1 %collective-permute-done.8.refs_5_ = bf16[144,1152]{1,0:T(8,128)(2,1)S(1)} collective-permute-done((bf16[144,1152]{1,0:T(8,128)(2,1)S(1)}, bf16[144,1152]{1,0:T(8,128)(2,1)S(1)}, u32[]{:S(2)}, u32[]{:S(2)}) %collective-permute-start.8) | collective-permute-done | bytes 331808 | tf_op jit(solution)/shard_map/ppermute | solution.py:41
  61.3 3.1 %shard_map.98 = (bf16[304,128]{1,0:T(8,128)(2,1)}, bf16[304,128]{1,0:T(8,128)(2,1)}, bf16[304,128]{1,0:T(8,128)(2,1)}, bf16[304,128]{1,0:T(8,128)(2,1)}, f32[1,8,128]{2,1,0:T(8,128)}) custom-call(s32[2]{0:T(128)} %pad_add_fusion.spot, f32[1]{0:T(128)S(6)} %copy.10.heat_log, f32[1]{0:T(128)S(6)} %copy.11.shift, ...), custom_call_target="tpu_custom_call" | custom-call | flops 150994944 | bytes 4194304 | tf_op jit(solution)/shard_map/pallas_call | solution.py:313
  66.0 1.7 %collective-permute-start.11 = (bf16[304,128]{1,0:T(8,128)(2,1)}, bf16[304,128]{1,0:T(8,128)(2,1)S(1)}, u32[]{:S(2)}, u32[]{:S(2)}) collective-permute-start(bf16[304,128]{1,0:T(8,128)(2,1)} %get-tuple-element.65), channel_id=1, source_target_pairs={{0,3},{1,0},{2,1},{3,2},{4,7},{5,4},{6,5},{7,6},{8,11},{9,8},{10,9... | collective-permute-start | bytes 233480 | tf_op jit(solution)/shard_map/ppermute | solution.py:457
  67.7 1.8 %collective-permute-start.12 = (bf16[304,128]{1,0:T(8,128)(2,1)}, bf16[304,128]{1,0:T(8,128)(2,1)S(1)}, u32[]{:S(2)}, u32[]{:S(2)}) collective-permute-start(bf16[304,128]{1,0:T(8,128)(2,1)} %get-tuple-element.71), channel_id=1, source_target_pairs={{0,2},{1,3},{2,0},{3,1},{4,6},{5,7},{6,4},{7,5},{8,10},{9,11},{10,... | collective-permute-start | bytes 233480 | tf_op jit(solution)/shard_map/ppermute | solution.py:457
  69.6 4.0 %shard_map.97.refs_0_ = f32[128,1152]{1,0:T(8,128)} custom-call(f32[1]{0:T(128)S(6)} %copy.10.heat_log, f32[1]{0:T(128)S(6)} %copy.11.shift, bf16[144,1152]{1,0:T(8,128)(2,1)} %shard_map.94.refs_0_.own, f32[128,128]{1,0:T(8,128)} %get-tuple-element.42.key.refs_3_.refs_4_, f32[2,8,128]{2,1,0:T(8,128)} %get-tuple-element.43.near_rows, ...), custom_call_target="tpu_custom_call" | custom-call | flops 377487360 | bytes 4194304 | tf_op jit(solution)/shard_map/pallas_call | solution.py:248
  74.2 3.0 %shard_map.99 = (bf16[288,128]{1,0:T(8,128)(2,1)}, bf16[288,128]{1,0:T(8,128)(2,1)}, bf16[288,128]{1,0:T(8,128)(2,1)}, bf16[288,128]{1,0:T(8,128)(2,1)}) custom-call(s32[2]{0:T(128)} %pad_add_fusion.spot, f32[1]{0:T(128)S(6)} %copy.10.heat_log, f32[1]{0:T(128)S(6)} %copy.11.shift, bf16[144,1152]{1,0:T(8,128)(2,1)} %shard_map.94.refs_0_.own, ...), custom_call_target="tpu_custom_call" | custom-call | flops 150994944 | bytes 4194304 | tf_op jit(solution)/shard_map/pallas_call | solution.py:313
  77.9 2.0 %collective-permute-start.15 = (bf16[288,128]{1,0:T(8,128)(2,1)}, bf16[288,128]{1,0:T(8,128)(2,1)S(1)}, u32[]{:S(2)}, u32[]{:S(2)}) collective-permute-start(bf16[288,128]{1,0:T(8,128)(2,1)} %get-tuple-element.75), channel_id=1, source_target_pairs={{0,2},{1,3},{2,0},{3,1},{4,6},{5,7},{6,4},{7,5},{8,10},{9,11},{10,... | collective-permute-start | bytes 221192 | tf_op jit(solution)/shard_map/ppermute | solution.py:457
  79.9 1.7 %collective-permute-start.16 = (bf16[288,128]{1,0:T(8,128)(2,1)}, bf16[288,128]{1,0:T(8,128)(2,1)S(1)}, u32[]{:S(2)}, u32[]{:S(2)}) collective-permute-start(bf16[288,128]{1,0:T(8,128)(2,1)} %get-tuple-element.76), channel_id=1, source_target_pairs={{0,3},{1,0},{2,1},{3,2},{4,7},{5,4},{6,5},{7,6},{8,11},{9,8},{10,9... | collective-permute-start | bytes 221192 | tf_op jit(solution)/shard_map/ppermute | solution.py:457
  81.6 2.0 %shard_map.100 = (f32[32,48,128]{2,1,0:T(8,128)S(1)}, bf16[32,48,128]{2,1,0:T(8,128)(2,1)S(1)}) custom-call(s32[2]{0:T(128)S(1)} %copy-done.4, bf16[512,1152]{1,0:T(8,128)(2,1)S(1)} %copy-done.1, bf16[304,128]{1,0:T(8,128)(2,1)S(1)} %copy-done.2, bf16[304,128]{1,0:T(8,128)(2,1)S(1)} %collective-permute-done.10.refs_1_, ...), custom_call_target="tpu_custom_call" | custom-call | flops 339738624 | bytes 4194304 | tf_op jit(solution)/shard_map/pallas_call | solution.py:373
  86.8 2.0 %shard_map.101 = (f32[32,48,128]{2,1,0:T(8,128)S(1)}, bf16[32,48,128]{2,1,0:T(8,128)(2,1)S(1)}) custom-call(s32[2]{0:T(128)S(1)} %copy-done.4, bf16[512,1152]{1,0:T(8,128)(2,1)S(1)} %copy-done, bf16[288,128]{1,0:T(8,128)(2,1)S(1)} %copy-done.3, bf16[288,128]{1,0:T(8,128)(2,1)S(1)} %collective-permute-done.14.refs_1_, ...), custom_call_target="tpu_custom_call" | custom-call | flops 339738624 | bytes 4194304 | tf_op jit(solution)/shard_map/pallas_call | solution.py:373
  88.9 1.7 %collective-permute-done.17.taken_txt = bf16[32,48,128]{2,1,0:T(8,128)(2,1)S(1)} collective-permute-done((bf16[32,48,128]{2,1,0:T(8,128)(2,1)S(1)}, bf16[32,48,128]{2,1,0:T(8,128)(2,1)S(1)}, u32[]{:S(2)}, u32[]{:S(2)}) %collective-permute-start.17) | collective-permute-done | bytes 393248 | tf_op jit(solution)/shard_map/ppermute | solution.py:41
  90.8 26.5 %all_to_all.5.parts = bf16[32,96,128]{2,1,0:T(8,128)(2,1)S(1)} all-to-all(bf16[32,96,128]{2,1,0:T(8,128)(2,1)S(1)} %shard_map.102), channel_id=1, replica_groups=mesh['ly'=4,'lz'=4,'lc'=2,'dz'=2,'dx'=4] {'ly','lz','dz'}, dimensions={0} | all-to-all | bytes 1572864 | tf_op jit(solution)/shard_map/all_to_all | solution.py:480
  (60 shorter events, 11.1 us)
Async XLA Ops:
  7.2 53.3 %all-gather.3.cloned.1.call-start = ((), (), s32[]{:S(2)}) async-start(), calls=%async_computation.1 | async-start | bytes 1474560 | tf_op jit(solution)/shard_map/all_gather | solution.py:435
  10.6 71.0 %all-gather.5.cloned.1.call-start = ((), (), s32[]{:S(2)}) async-start(), calls=%async_computation.2 | async-start | bytes 1474560 | tf_op jit(solution)/shard_map/all_gather | solution.py:436
  11.4 9.9 %collective-permute-start = (bf16[144,1152]{1,0:T(8,128)(2,1)}, bf16[144,1152]{1,0:T(8,128)(2,1)S(1)}, u32[]{:S(2)}, u32[]{:S(2)}) collective-permute-start(bf16[144,1152]{1,0:T(8,128)(2,1)} %shard_map.94.refs_0_.own), channel_id=1, source_target_pairs={{0,8},{8,0},{1,9},{9,1},{2,10},{10,2},{3,11},{11,3},{4,12},{12,4},... | collective-permute-start | bytes 995336 | tf_op jit(solution)/shard_map/ppermute | solution.py:41
  11.5 16.6 %collective-permute-start.1 = (bf16[144,1152]{1,0:T(8,128)(2,1)}, bf16[144,1152]{1,0:T(8,128)(2,1)S(1)}, u32[]{:S(2)}, u32[]{:S(2)}) collective-permute-start(bf16[144,1152]{1,0:T(8,128)(2,1)} %shard_map.94.refs_0_.own), channel_id=1, source_target_pairs={{0,64},{64,0},{128,192},{192,128},{1,65},{65,1},{129,193},{193,129... | collective-permute-start | bytes 995336 | tf_op jit(solution)/shard_map/ppermute | solution.py:41
  13.2 17.6 %collective-permute-start.2 = (bf16[144,1152]{1,0:T(8,128)(2,1)}, bf16[144,1152]{1,0:T(8,128)(2,1)S(1)}, u32[]{:S(2)}, u32[]{:S(2)}) collective-permute-start(bf16[144,1152]{1,0:T(8,128)(2,1)} %shard_map.94.refs_0_.own), channel_id=1, source_target_pairs={{0,16},{16,0},{32,48},{48,32},{1,17},{17,1},{33,49},{49,33},{2,18}... | collective-permute-start | bytes 995336 | tf_op jit(solution)/shard_map/ppermute | solution.py:41
  16.4 15.1 %collective-permute-start.3 = (bf16[144,1152]{1,0:T(8,128)(2,1)}, bf16[144,1152]{1,0:T(8,128)(2,1)S(1)}, u32[]{:S(2)}, u32[]{:S(2)}) collective-permute-start(bf16[144,1152]{1,0:T(8,128)(2,1)} %shard_map.94.refs_0_.own), channel_id=1, source_target_pairs={{0,128},{64,192},{128,0},{192,64},{1,129},{65,193},{129,1},{193,65... | collective-permute-start | bytes 995336 | tf_op jit(solution)/shard_map/ppermute | solution.py:41
  31.5 6.9 %collective-permute-start.4 = (bf16[128,1152]{1,0:T(8,128)(2,1)}, bf16[128,1152]{1,0:T(8,128)(2,1)S(1)}, u32[]{:S(2)}, u32[]{:S(2)}) collective-permute-start(bf16[128,1152]{1,0:T(8,128)(2,1)} %get-tuple-element.51.own.refs_0_), channel_id=1, source_target_pairs={{0,8},{8,0},{1,9},{9,1},{2,10},{10,2},{3,11},{11,3},{4,12},{12,4},... | collective-permute-start | bytes 884744 | tf_op jit(solution)/shard_map/ppermute | solution.py:41
  31.5 16.4 %collective-permute-start.7 = (bf16[128,1152]{1,0:T(8,128)(2,1)}, bf16[128,1152]{1,0:T(8,128)(2,1)S(1)}, u32[]{:S(2)}, u32[]{:S(2)}) collective-permute-start(bf16[128,1152]{1,0:T(8,128)(2,1)} %get-tuple-element.51.own.refs_0_), channel_id=1, source_target_pairs={{0,16},{16,0},{32,48},{48,32},{1,17},{17,1},{33,49},{49,33},{2,18}... | collective-permute-start | bytes 884744 | tf_op jit(solution)/shard_map/ppermute | solution.py:41
  34.8 25.7 %collective-permute-start.8 = (bf16[144,1152]{1,0:T(8,128)(2,1)S(1)}, bf16[144,1152]{1,0:T(8,128)(2,1)S(1)}, u32[]{:S(2)}, u32[]{:S(2)}) collective-permute-start(bf16[144,1152]{1,0:T(8,128)(2,1)S(1)} %collective-permute-done.2.refs_2_), channel_id=1, source_target_pairs={{0,48},{16,32},{32,16},{48,0},{1,49},{17,33},{33,17},{49,1},{2,50}... | collective-permute-start | bytes 995336 | tf_op jit(solution)/shard_map/ppermute | solution.py:41
  38.3 31.2 %copy-start.10 = (bf16[128,1152]{1,0:T(8,128)(2,1)}, bf16[128,1152]{1,0:T(8,128)(2,1)S(1)}, u32[]{:S(2)}) copy-start(bf16[128,1152]{1,0:T(8,128)(2,1)S(1)} %collective-permute-done.4.refs_1_) | copy-start | bytes 884740
  42.2 22.2 %collective-permute-start.5 = (bf16[128,1152]{1,0:T(8,128)(2,1)}, bf16[128,1152]{1,0:T(8,128)(2,1)S(1)}, u32[]{:S(2)}, u32[]{:S(2)}) collective-permute-start(bf16[128,1152]{1,0:T(8,128)(2,1)} %get-tuple-element.51.own.refs_0_), channel_id=1, source_target_pairs={{0,64},{64,0},{128,192},{192,128},{1,65},{65,1},{129,193},{193,129... | collective-permute-start | bytes 884744 | tf_op jit(solution)/shard_map/ppermute | solution.py:41
  42.3 22.1 %collective-permute-start.6 = (bf16[128,1152]{1,0:T(8,128)(2,1)}, bf16[128,1152]{1,0:T(8,128)(2,1)S(1)}, u32[]{:S(2)}, u32[]{:S(2)}) collective-permute-start(bf16[128,1152]{1,0:T(8,128)(2,1)} %get-tuple-element.51.own.refs_0_), channel_id=1, source_target_pairs={{0,128},{64,192},{128,0},{192,64},{1,129},{65,193},{129,1},{193,65... | collective-permute-start | bytes 884744 | tf_op jit(solution)/shard_map/ppermute | solution.py:41
  47.9 21.6 %copy-start.11 = (bf16[128,1152]{1,0:T(8,128)(2,1)}, bf16[128,1152]{1,0:T(8,128)(2,1)S(1)}, u32[]{:S(2)}) copy-start(bf16[128,1152]{1,0:T(8,128)(2,1)S(1)} %collective-permute-done.7.refs_4_) | copy-start | bytes 884740
  47.9 25.6 %collective-permute-start.9 = (bf16[128,1152]{1,0:T(8,128)(2,1)S(1)}, bf16[128,1152]{1,0:T(8,128)(2,1)S(1)}, u32[]{:S(2)}, u32[]{:S(2)}) collective-permute-start(bf16[128,1152]{1,0:T(8,128)(2,1)S(1)} %collective-permute-done.7.refs_4_), channel_id=1, source_target_pairs={{0,48},{16,32},{32,16},{48,0},{1,49},{17,33},{33,17},{49,1},{2,50}... | collective-permute-start | bytes 884744 | tf_op jit(solution)/shard_map/ppermute | solution.py:41
  64.4 17.3 %copy-start.2 = (bf16[304,128]{1,0:T(8,128)(2,1)S(1)}, bf16[304,128]{1,0:T(8,128)(2,1)}, u32[]{:S(2)}) copy-start(bf16[304,128]{1,0:T(8,128)(2,1)} %get-tuple-element.70.refs_0_) | copy-start | bytes 233476
  64.4 17.3 %copy-start.4 = (s32[2]{0:T(128)S(1)}, s32[2]{0:T(128)}, u32[]{:S(2)}) copy-start(s32[2]{0:T(128)} %pad_add_fusion.spot) | copy-start | bytes 28
  64.4 9.1 %collective-permute-start.10 = (bf16[304,128]{1,0:T(8,128)(2,1)}, bf16[304,128]{1,0:T(8,128)(2,1)S(1)}, u32[]{:S(2)}, u32[]{:S(2)}) collective-permute-start(bf16[304,128]{1,0:T(8,128)(2,1)} %get-tuple-element.64), channel_id=1, source_target_pairs={{0,1},{1,2},{2,3},{3,0},{4,5},{5,6},{6,7},{7,4},{8,9},{9,10},{10,1... | collective-permute-start | bytes 233480 | tf_op jit(solution)/shard_map/ppermute | solution.py:457
  66.0 7.5 %collective-permute-start.11 = (bf16[304,128]{1,0:T(8,128)(2,1)}, bf16[304,128]{1,0:T(8,128)(2,1)S(1)}, u32[]{:S(2)}, u32[]{:S(2)}) collective-permute-start(bf16[304,128]{1,0:T(8,128)(2,1)} %get-tuple-element.65), channel_id=1, source_target_pairs={{0,3},{1,0},{2,1},{3,2},{4,7},{5,4},{6,5},{7,6},{8,11},{9,8},{10,9... | collective-permute-start | bytes 233480 | tf_op jit(solution)/shard_map/ppermute | solution.py:457
  67.7 13.9 %collective-permute-start.12 = (bf16[304,128]{1,0:T(8,128)(2,1)}, bf16[304,128]{1,0:T(8,128)(2,1)S(1)}, u32[]{:S(2)}, u32[]{:S(2)}) collective-permute-start(bf16[304,128]{1,0:T(8,128)(2,1)} %get-tuple-element.71), channel_id=1, source_target_pairs={{0,2},{1,3},{2,0},{3,1},{4,6},{5,7},{6,4},{7,5},{8,10},{9,11},{10,... | collective-permute-start | bytes 233480 | tf_op jit(solution)/shard_map/ppermute | solution.py:457
  77.2 6.5 %collective-permute-start.14 = (bf16[288,128]{1,0:T(8,128)(2,1)}, bf16[288,128]{1,0:T(8,128)(2,1)S(1)}, u32[]{:S(2)}, u32[]{:S(2)}) collective-permute-start(bf16[288,128]{1,0:T(8,128)(2,1)} %get-tuple-element.74), channel_id=1, source_target_pairs={{0,1},{1,2},{2,3},{3,0},{4,5},{5,6},{6,7},{7,4},{8,9},{9,10},{10,1... | collective-permute-start | bytes 221192 | tf_op jit(solution)/shard_map/ppermute | solution.py:457
  77.9 6.1 %collective-permute-start.15 = (bf16[288,128]{1,0:T(8,128)(2,1)}, bf16[288,128]{1,0:T(8,128)(2,1)S(1)}, u32[]{:S(2)}, u32[]{:S(2)}) collective-permute-start(bf16[288,128]{1,0:T(8,128)(2,1)} %get-tuple-element.75), channel_id=1, source_target_pairs={{0,2},{1,3},{2,0},{3,1},{4,6},{5,7},{6,4},{7,5},{8,10},{9,11},{10,... | collective-permute-start | bytes 221192 | tf_op jit(solution)/shard_map/ppermute | solution.py:457
  79.9 4.8 %collective-permute-start.16 = (bf16[288,128]{1,0:T(8,128)(2,1)}, bf16[288,128]{1,0:T(8,128)(2,1)S(1)}, u32[]{:S(2)}, u32[]{:S(2)}) collective-permute-start(bf16[288,128]{1,0:T(8,128)(2,1)} %get-tuple-element.76), channel_id=1, source_target_pairs={{0,3},{1,0},{2,1},{3,2},{4,7},{5,4},{6,5},{7,6},{8,11},{9,8},{10,9... | collective-permute-start | bytes 221192 | tf_op jit(solution)/shard_map/ppermute | solution.py:457
  83.7 5.3 %collective-permute-start.13 = (bf16[32,48,128]{2,1,0:T(8,128)(2,1)S(1)}, bf16[32,48,128]{2,1,0:T(8,128)(2,1)S(1)}, u32[]{:S(2)}, u32[]{:S(2)}) collective-permute-start(bf16[32,48,128]{2,1,0:T(8,128)(2,1)S(1)} %get-tuple-element.73), channel_id=1, source_target_pairs={{0,8},{8,0},{1,9},{9,1},{2,10},{10,2},{3,11},{11,3},{4,12},{12,4},... | collective-permute-start | bytes 1179656 | tf_op jit(solution)/shard_map/ppermute | solution.py:41
  88.8 1.8 %collective-permute-start.17 = (bf16[32,48,128]{2,1,0:T(8,128)(2,1)S(1)}, bf16[32,48,128]{2,1,0:T(8,128)(2,1)S(1)}, u32[]{:S(2)}, u32[]{:S(2)}) collective-permute-start(bf16[32,48,128]{2,1,0:T(8,128)(2,1)S(1)} %get-tuple-element.78), channel_id=1, source_target_pairs={{0,8},{8,0},{1,9},{9,1},{2,10},{10,2},{3,11},{11,3},{4,12},{12,4},... | collective-permute-start | bytes 1179656 | tf_op jit(solution)/shard_map/ppermute | solution.py:41
  (11 other events, 56.7 us)
Sparse Core Ops, SparseCore 0:
  10.8 29.5 all-gather.2
  42.1 28.0 all-gather.4

commit v17 on v16

--- a/solution.py
+++ b/solution.py
@@ -459,15 +459,15 @@
     def columns(outs):
         return [outs[0]] + [turn(out, "dx", step) for step, out in enumerate(outs) if step]
 
-    last = after(txt_b, img_feat, img_a, img_c)
+    txt_total = middle(
+        scal, txt, first[5], near_rows, mid_rows, img, img_c, img_y1, img_y2, img_a
+    )
+    last = after(txt_b, img_feat, img_a, img_c, txt_total)
     *img_outs, far_rows = late(
         True, ways, spot, scal, img, img_part, [last]
     )
     img_outs = list(lax.optimization_barrier((*img_outs, img_y1, img_y2))[:-2])
     img_cols = columns(img_outs)
-    txt_total = middle(
-        scal, txt, first[5], near_rows, mid_rows, img, img_c, img_y1, img_y2, img_a
-    )
     txt_part = (txt_total, *first[3:5], first[5], first[5])
     last = after(img_b, img_cols[1], img_cols[3], txt_total)
     outs = late(False, ways, spot, scal, txt, txt_part, [far_rows, last])

time: 125 us -> 129 us (1.032)
  blocking collectives: 26.5 us -> 30 us
    all_to_all x1, blocking collectives: 26.5 us -> 30 us  [body(): sums = lax.all_to_all(sums, ('ly', 'lz', 'dz'), 0, 0, tiled=True)]
    ppermute x12, waiting for transfers between devices: 15.6 us -> 13 us  [exchange(): lax.ppermute(array, axis, [(i, i ^ apart) for i in range(lax.axis_size(ax...]
    ppermute x6, waiting for transfers between devices: 0.89 us -> 2.69 us  [turn(): lax.ppermute(array, axis, [(i, (i + step) % size) for i in range(size)])]
  transfers between devices with their start and end apart: 20 -> 20, of which waited for: 7 -> 8; matrix products, arithmetic and copies ran while one was open for 1% -> 1% of each run, Pallas kernels for 19% -> 19%
where the time goes in v17:
time: 129 us
  starting transfers between devices  32.7 us (25%)
  blocking collectives  30 us (23%)
  Pallas kernels  28.4 us (22%)
  waiting for transfers between devices  16.4 us (13%)
  between operations  15.5 us (12%)
  local copies, waits for them, and re-layouts  5.2 us (4%)
    all_to_all x1, blocking collectives, body(): sums = lax.all_to_all(sums, ('ly', 'lz', 'dz'), 0, 0, tiled=True)  30 us
    ppermute x12, starting transfers between devices, exchange(): lax.ppermute(array, axis, [(i, i ^ apart) for i in range(lax.axis_size(ax...  22.7 us
    ppermute x12, waiting for transfers between devices, exchange(): lax.ppermute(array, axis, [(i, i ^ apart) for i in range(lax.axis_size(ax...  13 us
    ppermute x6, starting transfers between devices, turn(): lax.ppermute(array, axis, [(i, (i + step) % size) for i in range(size)])  9.83 us
    pallas_call x2, Pallas kernels, late(): pl.pallas_call(functools.partial(late_kernel, with_stats, ways, len(block...  6.17 us
    pallas_call x1, Pallas kernels, early(): pl.pallas_call(early_kernel, in_specs=[SMEM] * 3 + [VMEM] * 2 + [hbm] * 2...  6.06 us
    unnamed x30, local copies, waits for them, and re-layouts  5.2 us
    pallas_call x2, Pallas kernels, heads(): pl.pallas_call(functools.partial(head_kernel, with_stats), in_specs=[SMEM...  4.02 us
  transfers between devices with their start and end apart: 20, of which 8 were waited for; matrix products, arithmetic and copies ran while one was open for 1% of the time, Pallas kernels for 19%

profile of v17, /device:TPU:32, one launch (start us, length us, event | category | flops | bytes accessed | tf_op | source)
XLA Modules:
  0.0 128.9 jit_solution(11943008367557453473)
XLA Ops:
  7.2 3.4 %shard_map.94.refs_0_.own = bf16[144,1152]{1,0:T(8,128)(2,1)} custom-call(bf16[128,1152]{1,0:T(8,128)(2,1)} %bitcast.4, bf16[1152,1152]{1,0:T(8,128)(2,1)} %wt_hbm.1, s32[1,128]{1,0:T(1,128)} %key.1), custom_call_target="tpu_custom_call" | custom-call | flops 339738624 | bytes 4194304 | tf_op jit(solution)/shard_map/pallas_call | solution.py:81
  11.5 1.7 %collective-permute-start.1 = (bf16[144,1152]{1,0:T(8,128)(2,1)}, bf16[144,1152]{1,0:T(8,128)(2,1)S(1)}, u32[]{:S(2)}, u32[]{:S(2)}) collective-permute-start(bf16[144,1152]{1,0:T(8,128)(2,1)} %shard_map.94.refs_0_.own), channel_id=1, source_target_pairs={{0,64},{64,0},{128,192},{192,128},{1,65},{65,1},{129,193},{193,129... | collective-permute-start | bytes 995336 | tf_op jit(solution)/shard_map/ppermute | solution.py:41
  13.2 3.3 %collective-permute-start.2 = (bf16[144,1152]{1,0:T(8,128)(2,1)}, bf16[144,1152]{1,0:T(8,128)(2,1)S(1)}, u32[]{:S(2)}, u32[]{:S(2)}) collective-permute-start(bf16[144,1152]{1,0:T(8,128)(2,1)} %shard_map.94.refs_0_.own), channel_id=1, source_target_pairs={{0,16},{16,0},{32,48},{48,32},{1,17},{17,1},{33,49},{49,33},{2,18}... | collective-permute-start | bytes 995336 | tf_op jit(solution)/shard_map/ppermute | solution.py:41
  16.4 2.9 %collective-permute-start.3 = (bf16[144,1152]{1,0:T(8,128)(2,1)}, bf16[144,1152]{1,0:T(8,128)(2,1)S(1)}, u32[]{:S(2)}, u32[]{:S(2)}) collective-permute-start(bf16[144,1152]{1,0:T(8,128)(2,1)} %shard_map.94.refs_0_.own), channel_id=1, source_target_pairs={{0,128},{64,192},{128,0},{192,64},{1,129},{65,193},{129,1},{193,65... | collective-permute-start | bytes 995336 | tf_op jit(solution)/shard_map/ppermute | solution.py:41
  22.1 6.1 %shard_map.95 = (bf16[128,1152]{1,0:T(8,128)(2,1)}, f32[2,8,128]{2,1,0:T(8,128)}, f32[128,1152]{1,0:T(8,128)}, f32[128,1152]{1,0:T(8,128)}, f32[128,128]{1,0:T(8...) custom-call(s32[2]{0:T(128)} %pad_add_fusion.spot, ...), custom_call_target="tpu_custom_call" | custom-call | flops 377487360 | bytes 8388608 | tf_op jit(solution)/shard_map/pallas_call | solution.py:190
  28.1 2.6 %collective-permute-done.2.refs_2_ = bf16[144,1152]{1,0:T(8,128)(2,1)S(1)} collective-permute-done((bf16[144,1152]{1,0:T(8,128)(2,1)}, bf16[144,1152]{1,0:T(8,128)(2,1)S(1)}, u32[]{:S(2)}, u32[]{:S(2)}) %collective-permute-start.2) | collective-permute-done | bytes 331808 | tf_op jit(solution)/shard_map/ppermute | solution.py:41
  31.5 3.3 %collective-permute-start.7 = (bf16[128,1152]{1,0:T(8,128)(2,1)}, bf16[128,1152]{1,0:T(8,128)(2,1)S(1)}, u32[]{:S(2)}, u32[]{:S(2)}) collective-permute-start(bf16[128,1152]{1,0:T(8,128)(2,1)} %get-tuple-element.51.own.refs_0_), channel_id=1, source_target_pairs={{0,16},{16,0},{32,48},{48,32},{1,17},{17,1},{33,49},{49,33},{2,18}... | collective-permute-start | bytes 884744 | tf_op jit(solution)/shard_map/ppermute | solution.py:41
  34.8 3.6 %collective-permute-start.8 = (bf16[144,1152]{1,0:T(8,128)(2,1)S(1)}, bf16[144,1152]{1,0:T(8,128)(2,1)S(1)}, u32[]{:S(2)}, u32[]{:S(2)}) collective-permute-start(bf16[144,1152]{1,0:T(8,128)(2,1)S(1)} %collective-permute-done.2.refs_2_), channel_id=1, source_target_pairs={{0,48},{16,32},{32,16},{48,0},{1,49},{17,33},{33,17},{49,1},{2,50}... | collective-permute-start | bytes 995336 | tf_op jit(solution)/shard_map/ppermute | solution.py:41
  38.4 3.8 %shard_map.96 = (f32[128,1152]{1,0:T(8,128)}, f32[3,128,128]{2,1,0:T(8,128)}, f32[3,8,128]{2,1,0:T(8,128)}) custom-call(f32[1]{0:T(128)S(6)} %copy.10.heat_log, f32[1]{0:T(128)S(6)} %copy.11.shift, bf16[128,1152]{1,0:T(8,128)(2,1)} %get-tuple-element.51.own.refs_0_, f32[128,1152]{1,0:T(8,128)} %get-tuple-element.45.total_ref, ...), custom_call_target="tpu_custom_call" | custom-call | flops 226492416 | bytes 4194304 | tf_op jit(solution)/shard_map/pallas_call | solution.py:220
  42.3 2.1 %collective-permute-start.6 = (bf16[128,1152]{1,0:T(8,128)(2,1)}, bf16[128,1152]{1,0:T(8,128)(2,1)S(1)}, u32[]{:S(2)}, u32[]{:S(2)}) collective-permute-start(bf16[128,1152]{1,0:T(8,128)(2,1)} %get-tuple-element.51.own.refs_0_), channel_id=1, source_target_pairs={{0,128},{64,192},{128,0},{192,64},{1,129},{65,193},{129,1},{193,65... | collective-permute-start | bytes 884744 | tf_op jit(solution)/shard_map/ppermute | solution.py:41
  44.4 3.5 %collective-permute-done.7.refs_4_ = bf16[128,1152]{1,0:T(8,128)(2,1)S(1)} collective-permute-done((bf16[128,1152]{1,0:T(8,128)(2,1)}, bf16[128,1152]{1,0:T(8,128)(2,1)S(1)}, u32[]{:S(2)}, u32[]{:S(2)}) %collective-permute-start.7) | collective-permute-done | bytes 294944 | tf_op jit(solution)/shard_map/ppermute | solution.py:41
  47.9 5.5 %collective-permute-start.9 = (bf16[128,1152]{1,0:T(8,128)(2,1)S(1)}, bf16[128,1152]{1,0:T(8,128)(2,1)S(1)}, u32[]{:S(2)}, u32[]{:S(2)}) collective-permute-start(bf16[128,1152]{1,0:T(8,128)(2,1)S(1)} %collective-permute-done.7.refs_4_), channel_id=1, source_target_pairs={{0,48},{16,32},{32,16},{48,0},{1,49},{17,33},{33,17},{49,1},{2,50}... | collective-permute-start | bytes 884744 | tf_op jit(solution)/shard_map/ppermute | solution.py:41
  53.5 4.4 %collective-permute-done.6.refs_3_ = bf16[128,1152]{1,0:T(8,128)(2,1)S(1)} collective-permute-done((bf16[128,1152]{1,0:T(8,128)(2,1)}, bf16[128,1152]{1,0:T(8,128)(2,1)S(1)}, u32[]{:S(2)}, u32[]{:S(2)}) %collective-permute-start.6) | collective-permute-done | bytes 294944 | tf_op jit(solution)/shard_map/ppermute | solution.py:41
  58.5 4.0 %shard_map.97.refs_0_ = f32[128,1152]{1,0:T(8,128)} custom-call(f32[1]{0:T(128)S(6)} %copy.10.heat_log, f32[1]{0:T(128)S(6)} %copy.11.shift, bf16[144,1152]{1,0:T(8,128)(2,1)} %shard_map.94.refs_0_.own, f32[128,128]{1,0:T(8,128)} %get-tuple-element.42.key.refs_3_.refs_4_, f32[2,8,128]{2,1,0:T(8,128)} %get-tuple-element.43.near_rows, ...), custom_call_target="tpu_custom_call" | custom-call | flops 377487360 | bytes 4194304 | tf_op jit(solution)/shard_map/pallas_call | solution.py:248
  63.3 3.1 %shard_map.98 = (bf16[304,128]{1,0:T(8,128)(2,1)}, bf16[304,128]{1,0:T(8,128)(2,1)}, bf16[304,128]{1,0:T(8,128)(2,1)}, bf16[304,128]{1,0:T(8,128)(2,1)}, f32[1,8,128]{2,1,0:T(8,128)}) custom-call(s32[2]{0:T(128)} %pad_add_fusion.spot, f32[1]{0:T(128)S(6)} %copy.10.heat_log, f32[1]{0:T(128)S(6)} %copy.11.shift, ...), custom_call_target="tpu_custom_call" | custom-call | flops 150994944 | bytes 4194304 | tf_op jit(solution)/shard_map/pallas_call | solution.py:313
  66.4 1.5 %collective-permute-start.10 = (bf16[304,128]{1,0:T(8,128)(2,1)}, bf16[304,128]{1,0:T(8,128)(2,1)S(1)}, u32[]{:S(2)}, u32[]{:S(2)}) collective-permute-start(bf16[304,128]{1,0:T(8,128)(2,1)} %get-tuple-element.64), channel_id=1, source_target_pairs={{0,1},{1,2},{2,3},{3,0},{4,5},{5,6},{6,7},{7,4},{8,9},{9,10},{10,1... | collective-permute-start | bytes 233480 | tf_op jit(solution)/shard_map/ppermute | solution.py:457
  67.9 1.7 %collective-permute-start.11 = (bf16[304,128]{1,0:T(8,128)(2,1)}, bf16[304,128]{1,0:T(8,128)(2,1)S(1)}, u32[]{:S(2)}, u32[]{:S(2)}) collective-permute-start(bf16[304,128]{1,0:T(8,128)(2,1)} %get-tuple-element.65), channel_id=1, source_target_pairs={{0,3},{1,0},{2,1},{3,2},{4,7},{5,4},{6,5},{7,6},{8,11},{9,8},{10,9... | collective-permute-start | bytes 233480 | tf_op jit(solution)/shard_map/ppermute | solution.py:457
  69.6 1.8 %collective-permute-start.12 = (bf16[304,128]{1,0:T(8,128)(2,1)}, bf16[304,128]{1,0:T(8,128)(2,1)S(1)}, u32[]{:S(2)}, u32[]{:S(2)}) collective-permute-start(bf16[304,128]{1,0:T(8,128)(2,1)} %get-tuple-element.71), channel_id=1, source_target_pairs={{0,2},{1,3},{2,0},{3,1},{4,6},{5,7},{6,4},{7,5},{8,10},{9,11},{10,... | collective-permute-start | bytes 233480 | tf_op jit(solution)/shard_map/ppermute | solution.py:457
  73.1 3.0 %shard_map.99 = (bf16[288,128]{1,0:T(8,128)(2,1)}, bf16[288,128]{1,0:T(8,128)(2,1)}, bf16[288,128]{1,0:T(8,128)(2,1)}, bf16[288,128]{1,0:T(8,128)(2,1)}) custom-call(s32[2]{0:T(128)} %pad_add_fusion.spot, f32[1]{0:T(128)S(6)} %copy.10.heat_log, f32[1]{0:T(128)S(6)} %copy.11.shift, bf16[144,1152]{1,0:T(8,128)(2,1)} %shard_map.94.refs_0_.own, ...), custom_call_target="tpu_custom_call" | custom-call | flops 150994944 | bytes 4194304 | tf_op jit(solution)/shard_map/pallas_call | solution.py:313
  77.5 2.9 %collective-permute-start.15 = (bf16[288,128]{1,0:T(8,128)(2,1)}, bf16[288,128]{1,0:T(8,128)(2,1)S(1)}, u32[]{:S(2)}, u32[]{:S(2)}) collective-permute-start(bf16[288,128]{1,0:T(8,128)(2,1)} %get-tuple-element.75), channel_id=1, source_target_pairs={{0,2},{1,3},{2,0},{3,1},{4,6},{5,7},{6,4},{7,5},{8,10},{9,11},{10,... | collective-permute-start | bytes 221192 | tf_op jit(solution)/shard_map/ppermute | solution.py:457
  81.8 2.0 %shard_map.100 = (f32[32,48,128]{2,1,0:T(8,128)S(1)}, bf16[32,48,128]{2,1,0:T(8,128)(2,1)S(1)}) custom-call(s32[2]{0:T(128)S(1)} %copy-done.4, bf16[512,1152]{1,0:T(8,128)(2,1)S(1)} %copy-done.1, bf16[304,128]{1,0:T(8,128)(2,1)S(1)} %copy-done.2, bf16[304,128]{1,0:T(8,128)(2,1)S(1)} %collective-permute-done.10.refs_1_, ...), custom_call_target="tpu_custom_call" | custom-call | flops 339738624 | bytes 4194304 | tf_op jit(solution)/shard_map/pallas_call | solution.py:373
  87.2 2.0 %shard_map.101 = (f32[32,48,128]{2,1,0:T(8,128)S(1)}, bf16[32,48,128]{2,1,0:T(8,128)(2,1)S(1)}) custom-call(s32[2]{0:T(128)S(1)} %copy-done.4, bf16[512,1152]{1,0:T(8,128)(2,1)S(1)} %copy-done, bf16[288,128]{1,0:T(8,128)(2,1)S(1)} %copy-done.3, bf16[288,128]{1,0:T(8,128)(2,1)S(1)} %collective-permute-done.14.refs_1_, ...), custom_call_target="tpu_custom_call" | custom-call | flops 339738624 | bytes 4194304 | tf_op jit(solution)/shard_map/pallas_call | solution.py:373
  89.3 1.7 %collective-permute-done.17.taken_txt = bf16[32,48,128]{2,1,0:T(8,128)(2,1)S(1)} collective-permute-done((bf16[32,48,128]{2,1,0:T(8,128)(2,1)S(1)}, bf16[32,48,128]{2,1,0:T(8,128)(2,1)S(1)}, u32[]{:S(2)}, u32[]{:S(2)}) %collective-permute-start.17) | collective-permute-done | bytes 393248 | tf_op jit(solution)/shard_map/ppermute | solution.py:41
  91.1 30.0 %all_to_all.5.parts = bf16[32,96,128]{2,1,0:T(8,128)(2,1)S(1)} all-to-all(bf16[32,96,128]{2,1,0:T(8,128)(2,1)S(1)} %shard_map.102), channel_id=1, replica_groups=mesh['ly'=4,'lz'=4,'lc'=2,'dz'=2,'dx'=4] {'ly','lz','dz'}, dimensions={0} | all-to-all | bytes 1572864 | tf_op jit(solution)/shard_map/all_to_all | solution.py:480
  (60 shorter events, 13.4 us)
Async XLA Ops:
  7.2 55.4 %all-gather.3.cloned.1.call-start = ((), (), s32[]{:S(2)}) async-start(), calls=%async_computation.1 | async-start | bytes 1474560 | tf_op jit(solution)/shard_map/all_gather | solution.py:435
  10.6 70.3 %all-gather.5.cloned.1.call-start = ((), (), s32[]{:S(2)}) async-start(), calls=%async_computation.2 | async-start | bytes 1474560 | tf_op jit(solution)/shard_map/all_gather | solution.py:436
  11.4 9.9 %collective-permute-start = (bf16[144,1152]{1,0:T(8,128)(2,1)}, bf16[144,1152]{1,0:T(8,128)(2,1)S(1)}, u32[]{:S(2)}, u32[]{:S(2)}) collective-permute-start(bf16[144,1152]{1,0:T(8,128)(2,1)} %shard_map.94.refs_0_.own), channel_id=1, source_target_pairs={{0,8},{8,0},{1,9},{9,1},{2,10},{10,2},{3,11},{11,3},{4,12},{12,4},... | collective-permute-start | bytes 995336 | tf_op jit(solution)/shard_map/ppermute | solution.py:41
  11.5 16.6 %collective-permute-start.1 = (bf16[144,1152]{1,0:T(8,128)(2,1)}, bf16[144,1152]{1,0:T(8,128)(2,1)S(1)}, u32[]{:S(2)}, u32[]{:S(2)}) collective-permute-start(bf16[144,1152]{1,0:T(8,128)(2,1)} %shard_map.94.refs_0_.own), channel_id=1, source_target_pairs={{0,64},{64,0},{128,192},{192,128},{1,65},{65,1},{129,193},{193,129... | collective-permute-start | bytes 995336 | tf_op jit(solution)/shard_map/ppermute | solution.py:41
  13.2 17.6 %collective-permute-start.2 = (bf16[144,1152]{1,0:T(8,128)(2,1)}, bf16[144,1152]{1,0:T(8,128)(2,1)S(1)}, u32[]{:S(2)}, u32[]{:S(2)}) collective-permute-start(bf16[144,1152]{1,0:T(8,128)(2,1)} %shard_map.94.refs_0_.own), channel_id=1, source_target_pairs={{0,16},{16,0},{32,48},{48,32},{1,17},{17,1},{33,49},{49,33},{2,18}... | collective-permute-start | bytes 995336 | tf_op jit(solution)/shard_map/ppermute | solution.py:41
  16.4 15.1 %collective-permute-start.3 = (bf16[144,1152]{1,0:T(8,128)(2,1)}, bf16[144,1152]{1,0:T(8,128)(2,1)S(1)}, u32[]{:S(2)}, u32[]{:S(2)}) collective-permute-start(bf16[144,1152]{1,0:T(8,128)(2,1)} %shard_map.94.refs_0_.own), channel_id=1, source_target_pairs={{0,128},{64,192},{128,0},{192,64},{1,129},{65,193},{129,1},{193,65... | collective-permute-start | bytes 995336 | tf_op jit(solution)/shard_map/ppermute | solution.py:41
  28.1 10.2 %copy-start.7 = (bf16[144,1152]{1,0:T(8,128)(2,1)}, bf16[144,1152]{1,0:T(8,128)(2,1)S(1)}, u32[]{:S(2)}) copy-start(bf16[144,1152]{1,0:T(8,128)(2,1)S(1)} %collective-permute-done.1.refs_0_) | copy-start | bytes 995332
  31.5 6.9 %collective-permute-start.4 = (bf16[128,1152]{1,0:T(8,128)(2,1)}, bf16[128,1152]{1,0:T(8,128)(2,1)S(1)}, u32[]{:S(2)}, u32[]{:S(2)}) collective-permute-start(bf16[128,1152]{1,0:T(8,128)(2,1)} %get-tuple-element.51.own.refs_0_), channel_id=1, source_target_pairs={{0,8},{8,0},{1,9},{9,1},{2,10},{10,2},{3,11},{11,3},{4,12},{12,4},... | collective-permute-start | bytes 884744 | tf_op jit(solution)/shard_map/ppermute | solution.py:41
  31.5 16.4 %collective-permute-start.7 = (bf16[128,1152]{1,0:T(8,128)(2,1)}, bf16[128,1152]{1,0:T(8,128)(2,1)S(1)}, u32[]{:S(2)}, u32[]{:S(2)}) collective-permute-start(bf16[128,1152]{1,0:T(8,128)(2,1)} %get-tuple-element.51.own.refs_0_), channel_id=1, source_target_pairs={{0,16},{16,0},{32,48},{48,32},{1,17},{17,1},{33,49},{49,33},{2,18}... | collective-permute-start | bytes 884744 | tf_op jit(solution)/shard_map/ppermute | solution.py:41
  34.8 27.8 %collective-permute-start.8 = (bf16[144,1152]{1,0:T(8,128)(2,1)S(1)}, bf16[144,1152]{1,0:T(8,128)(2,1)S(1)}, u32[]{:S(2)}, u32[]{:S(2)}) collective-permute-start(bf16[144,1152]{1,0:T(8,128)(2,1)S(1)} %collective-permute-done.2.refs_2_), channel_id=1, source_target_pairs={{0,48},{16,32},{32,16},{48,0},{1,49},{17,33},{33,17},{49,1},{2,50}... | collective-permute-start | bytes 995336 | tf_op jit(solution)/shard_map/ppermute | solution.py:41
  38.3 19.5 %copy-start.11 = (bf16[128,1152]{1,0:T(8,128)(2,1)}, bf16[128,1152]{1,0:T(8,128)(2,1)S(1)}, u32[]{:S(2)}) copy-start(bf16[128,1152]{1,0:T(8,128)(2,1)S(1)} %collective-permute-done.4.refs_1_) | copy-start | bytes 884740
  42.2 11.3 %collective-permute-start.5 = (bf16[128,1152]{1,0:T(8,128)(2,1)}, bf16[128,1152]{1,0:T(8,128)(2,1)S(1)}, u32[]{:S(2)}, u32[]{:S(2)}) collective-permute-start(bf16[128,1152]{1,0:T(8,128)(2,1)} %get-tuple-element.51.own.refs_0_), channel_id=1, source_target_pairs={{0,64},{64,0},{128,192},{192,128},{1,65},{65,1},{129,193},{193,129... | collective-permute-start | bytes 884744 | tf_op jit(solution)/shard_map/ppermute | solution.py:41
  42.3 15.5 %collective-permute-start.6 = (bf16[128,1152]{1,0:T(8,128)(2,1)}, bf16[128,1152]{1,0:T(8,128)(2,1)S(1)}, u32[]{:S(2)}, u32[]{:S(2)}) collective-permute-start(bf16[128,1152]{1,0:T(8,128)(2,1)} %get-tuple-element.51.own.refs_0_), channel_id=1, source_target_pairs={{0,128},{64,192},{128,0},{192,64},{1,129},{65,193},{129,1},{193,65... | collective-permute-start | bytes 884744 | tf_op jit(solution)/shard_map/ppermute | solution.py:41
  47.9 23.5 %collective-permute-start.9 = (bf16[128,1152]{1,0:T(8,128)(2,1)S(1)}, bf16[128,1152]{1,0:T(8,128)(2,1)S(1)}, u32[]{:S(2)}, u32[]{:S(2)}) collective-permute-start(bf16[128,1152]{1,0:T(8,128)(2,1)S(1)} %collective-permute-done.7.refs_4_), channel_id=1, source_target_pairs={{0,48},{16,32},{32,16},{48,0},{1,49},{17,33},{33,17},{49,1},{2,50}... | collective-permute-start | bytes 884744 | tf_op jit(solution)/shard_map/ppermute | solution.py:41
  62.5 18.4 %copy-start.4 = (s32[2]{0:T(128)S(1)}, s32[2]{0:T(128)}, u32[]{:S(2)}) copy-start(s32[2]{0:T(128)} %pad_add_fusion.spot) | copy-start | bytes 28
  62.6 18.4 %copy-start.1 = (bf16[512,1152]{1,0:T(8,128)(2,1)S(1)}, bf16[512,1152]{1,0:T(8,128)(2,1)}, u32[]{:S(2)}) copy-start(bf16[512,1152]{1,0:T(8,128)(2,1)} %all-gather.3.cloned.1.call-done.feat) | copy-start | bytes 3538948
  66.4 5.8 %collective-permute-start.10 = (bf16[304,128]{1,0:T(8,128)(2,1)}, bf16[304,128]{1,0:T(8,128)(2,1)S(1)}, u32[]{:S(2)}, u32[]{:S(2)}) collective-permute-start(bf16[304,128]{1,0:T(8,128)(2,1)} %get-tuple-element.64), channel_id=1, source_target_pairs={{0,1},{1,2},{2,3},{3,0},{4,5},{5,6},{6,7},{7,4},{8,9},{9,10},{10,1... | collective-permute-start | bytes 233480 | tf_op jit(solution)/shard_map/ppermute | solution.py:457
  67.9 5.2 %collective-permute-start.11 = (bf16[304,128]{1,0:T(8,128)(2,1)}, bf16[304,128]{1,0:T(8,128)(2,1)S(1)}, u32[]{:S(2)}, u32[]{:S(2)}) collective-permute-start(bf16[304,128]{1,0:T(8,128)(2,1)} %get-tuple-element.65), channel_id=1, source_target_pairs={{0,3},{1,0},{2,1},{3,2},{4,7},{5,4},{6,5},{7,6},{8,11},{9,8},{10,9... | collective-permute-start | bytes 233480 | tf_op jit(solution)/shard_map/ppermute | solution.py:457
  69.6 11.3 %collective-permute-start.12 = (bf16[304,128]{1,0:T(8,128)(2,1)}, bf16[304,128]{1,0:T(8,128)(2,1)S(1)}, u32[]{:S(2)}, u32[]{:S(2)}) collective-permute-start(bf16[304,128]{1,0:T(8,128)(2,1)} %get-tuple-element.71), channel_id=1, source_target_pairs={{0,2},{1,3},{2,0},{3,1},{4,6},{5,7},{6,4},{7,5},{8,10},{9,11},{10,... | collective-permute-start | bytes 233480 | tf_op jit(solution)/shard_map/ppermute | solution.py:457
  76.2 7.8 %collective-permute-start.14 = (bf16[288,128]{1,0:T(8,128)(2,1)}, bf16[288,128]{1,0:T(8,128)(2,1)S(1)}, u32[]{:S(2)}, u32[]{:S(2)}) collective-permute-start(bf16[288,128]{1,0:T(8,128)(2,1)} %get-tuple-element.74), channel_id=1, source_target_pairs={{0,1},{1,2},{2,3},{3,0},{4,5},{5,6},{6,7},{7,4},{8,9},{9,10},{10,1... | collective-permute-start | bytes 221192 | tf_op jit(solution)/shard_map/ppermute | solution.py:457
  77.5 6.4 %collective-permute-start.15 = (bf16[288,128]{1,0:T(8,128)(2,1)}, bf16[288,128]{1,0:T(8,128)(2,1)S(1)}, u32[]{:S(2)}, u32[]{:S(2)}) collective-permute-start(bf16[288,128]{1,0:T(8,128)(2,1)} %get-tuple-element.75), channel_id=1, source_target_pairs={{0,2},{1,3},{2,0},{3,1},{4,6},{5,7},{6,4},{7,5},{8,10},{9,11},{10,... | collective-permute-start | bytes 221192 | tf_op jit(solution)/shard_map/ppermute | solution.py:457
  80.5 4.6 %collective-permute-start.16 = (bf16[288,128]{1,0:T(8,128)(2,1)}, bf16[288,128]{1,0:T(8,128)(2,1)S(1)}, u32[]{:S(2)}, u32[]{:S(2)}) collective-permute-start(bf16[288,128]{1,0:T(8,128)(2,1)} %get-tuple-element.76), channel_id=1, source_target_pairs={{0,3},{1,0},{2,1},{3,2},{4,7},{5,4},{6,5},{7,6},{8,11},{9,8},{10,9... | collective-permute-start | bytes 221192 | tf_op jit(solution)/shard_map/ppermute | solution.py:457
  83.9 5.4 %collective-permute-start.13 = (bf16[32,48,128]{2,1,0:T(8,128)(2,1)S(1)}, bf16[32,48,128]{2,1,0:T(8,128)(2,1)S(1)}, u32[]{:S(2)}, u32[]{:S(2)}) collective-permute-start(bf16[32,48,128]{2,1,0:T(8,128)(2,1)S(1)} %get-tuple-element.73), channel_id=1, source_target_pairs={{0,8},{8,0},{1,9},{9,1},{2,10},{10,2},{3,11},{11,3},{4,12},{12,4},... | collective-permute-start | bytes 1179656 | tf_op jit(solution)/shard_map/ppermute | solution.py:41
  89.2 1.8 %collective-permute-start.17 = (bf16[32,48,128]{2,1,0:T(8,128)(2,1)S(1)}, bf16[32,48,128]{2,1,0:T(8,128)(2,1)S(1)}, u32[]{:S(2)}, u32[]{:S(2)}) collective-permute-start(bf16[32,48,128]{2,1,0:T(8,128)(2,1)S(1)} %get-tuple-element.78), channel_id=1, source_target_pairs={{0,8},{8,0},{1,9},{9,1},{2,10},{10,2},{3,11},{11,3},{4,12},{12,4},... | collective-permute-start | bytes 1179656 | tf_op jit(solution)/shard_map/ppermute | solution.py:41
  (11 other events, 35.7 us)
Sparse Core Ops, SparseCore 0:
  10.8 29.5 all-gather.2
  42.1 27.5 all-gather.4

commit v18 on v16

--- a/solution.py
+++ b/solution.py
@@ -376,7 +376,7 @@
         out_specs=[VMEM, VMEM],
         out_shape=[jax.ShapeDtypeStruct(shape, F32), jax.ShapeDtypeStruct(shape, BF16)],
         scratch_shapes=[pltpu.VMEM((2, *shape), F32)],
-        compiler_params=params(24),
+        compiler_params=params(24 if with_stats else 56),
         cost_estimate=cost(2 * 4 * ROWS * 2 * COLS * feat.shape[1], 4 * 2**20),
     )(spot, feat, *spreads)
 

time: 125 us -> 127 us (1.016)
  Pallas kernels: 28.4 us -> 30.2 us
    pallas_call x2, Pallas kernels: 4.03 us -> 5.85 us  [heads(): pl.pallas_call(functools.partial(head_kernel, with_stats), in_specs=[SMEM...]
    unnamed x30 -> x34, local copies, waits for them, and re-layouts: 4.38 us -> 3.98 us
  transfers between devices with their start and end apart: 20 -> 20, of which waited for: 7 -> 7; matrix products, arithmetic and copies ran while one was open for 1% -> 1% of each run, Pallas kernels for 19% -> 20%
where the time goes in v18:
time: 127 us
  starting transfers between devices  32.5 us (26%)
  Pallas kernels  30.2 us (24%)
  blocking collectives  26.6 us (21%)
  waiting for transfers between devices  17.3 us (14%)
  between operations  15.5 us (12%)
  local copies, waits for them, and re-layouts  3.98 us (3%)
    all_to_all x1, blocking collectives, body(): sums = lax.all_to_all(sums, ('ly', 'lz', 'dz'), 0, 0, tiled=True)  26.6 us
    ppermute x12, starting transfers between devices, exchange(): lax.ppermute(array, axis, [(i, i ^ apart) for i in range(lax.axis_size(ax...  22.9 us
    ppermute x12, waiting for transfers between devices, exchange(): lax.ppermute(array, axis, [(i, i ^ apart) for i in range(lax.axis_size(ax...  15.7 us
    ppermute x6, starting transfers between devices, turn(): lax.ppermute(array, axis, [(i, (i + step) % size) for i in range(size)])  9.49 us
    pallas_call x2, Pallas kernels, late(): pl.pallas_call(functools.partial(late_kernel, with_stats, ways, len(block...  6.13 us
    pallas_call x1, Pallas kernels, early(): pl.pallas_call(early_kernel, in_specs=[SMEM] * 3 + [VMEM] * 2 + [hbm] * 2...  6.04 us
    pallas_call x2, Pallas kernels, heads(): pl.pallas_call(functools.partial(head_kernel, with_stats), in_specs=[SMEM...  5.85 us
    unnamed x34, local copies, waits for them, and re-layouts  3.98 us
  transfers between devices with their start and end apart: 20, of which 7 were waited for; matrix products, arithmetic and copies ran while one was open for 1% of the time, Pallas kernels for 20%

profile of v18, /device:TPU:32, one launch (start us, length us, event | category | flops | bytes accessed | tf_op | source)
XLA Modules:
  0.0 126.8 jit_solution(7903133704074720994)
XLA Ops:
  7.2 3.4 %shard_map.94.refs_0_.own = bf16[144,1152]{1,0:T(8,128)(2,1)} custom-call(bf16[128,1152]{1,0:T(8,128)(2,1)} %bitcast.4, bf16[1152,1152]{1,0:T(8,128)(2,1)} %wt_hbm.1, s32[1,128]{1,0:T(1,128)} %key.1), custom_call_target="tpu_custom_call" | custom-call | flops 339738624 | bytes 4194304 | tf_op jit(solution)/shard_map/pallas_call | solution.py:81
  11.5 1.7 %collective-permute-start.1 = (bf16[144,1152]{1,0:T(8,128)(2,1)}, bf16[144,1152]{1,0:T(8,128)(2,1)S(1)}, u32[]{:S(2)}, u32[]{:S(2)}) collective-permute-start(bf16[144,1152]{1,0:T(8,128)(2,1)} %shard_map.94.refs_0_.own), channel_id=1, source_target_pairs={{0,64},{64,0},{128,192},{192,128},{1,65},{65,1},{129,193},{193,129... | collective-permute-start | bytes 995336 | tf_op jit(solution)/shard_map/ppermute | solution.py:41
  13.2 3.3 %collective-permute-start.2 = (bf16[144,1152]{1,0:T(8,128)(2,1)}, bf16[144,1152]{1,0:T(8,128)(2,1)S(1)}, u32[]{:S(2)}, u32[]{:S(2)}) collective-permute-start(bf16[144,1152]{1,0:T(8,128)(2,1)} %shard_map.94.refs_0_.own), channel_id=1, source_target_pairs={{0,16},{16,0},{32,48},{48,32},{1,17},{17,1},{33,49},{49,33},{2,18}... | collective-permute-start | bytes 995336 | tf_op jit(solution)/shard_map/ppermute | solution.py:41
  16.5 2.9 %collective-permute-start.3 = (bf16[144,1152]{1,0:T(8,128)(2,1)}, bf16[144,1152]{1,0:T(8,128)(2,1)S(1)}, u32[]{:S(2)}, u32[]{:S(2)}) collective-permute-start(bf16[144,1152]{1,0:T(8,128)(2,1)} %shard_map.94.refs_0_.own), channel_id=1, source_target_pairs={{0,128},{64,192},{128,0},{192,64},{1,129},{65,193},{129,1},{193,65... | collective-permute-start | bytes 995336 | tf_op jit(solution)/shard_map/ppermute | solution.py:41
  22.0 6.0 %shard_map.95 = (bf16[128,1152]{1,0:T(8,128)(2,1)}, f32[2,8,128]{2,1,0:T(8,128)}, f32[128,1152]{1,0:T(8,128)}, f32[128,1152]{1,0:T(8,128)}, f32[128,128]{1,0:T(8...) custom-call(s32[2]{0:T(128)} %pad_add_fusion.spot, ...), custom_call_target="tpu_custom_call" | custom-call | flops 377487360 | bytes 8388608 | tf_op jit(solution)/shard_map/pallas_call | solution.py:190
  28.1 2.7 %collective-permute-done.2.refs_2_ = bf16[144,1152]{1,0:T(8,128)(2,1)S(1)} collective-permute-done((bf16[144,1152]{1,0:T(8,128)(2,1)}, bf16[144,1152]{1,0:T(8,128)(2,1)S(1)}, u32[]{:S(2)}, u32[]{:S(2)}) %collective-permute-start.2) | collective-permute-done | bytes 331808 | tf_op jit(solution)/shard_map/ppermute | solution.py:41
  31.5 3.3 %collective-permute-start.7 = (bf16[128,1152]{1,0:T(8,128)(2,1)}, bf16[128,1152]{1,0:T(8,128)(2,1)S(1)}, u32[]{:S(2)}, u32[]{:S(2)}) collective-permute-start(bf16[128,1152]{1,0:T(8,128)(2,1)} %get-tuple-element.51.own.refs_0_), channel_id=1, source_target_pairs={{0,16},{16,0},{32,48},{48,32},{1,17},{17,1},{33,49},{49,33},{2,18}... | collective-permute-start | bytes 884744 | tf_op jit(solution)/shard_map/ppermute | solution.py:41
  34.8 3.6 %collective-permute-start.8 = (bf16[144,1152]{1,0:T(8,128)(2,1)S(1)}, bf16[144,1152]{1,0:T(8,128)(2,1)S(1)}, u32[]{:S(2)}, u32[]{:S(2)}) collective-permute-start(bf16[144,1152]{1,0:T(8,128)(2,1)S(1)} %collective-permute-done.2.refs_2_), channel_id=1, source_target_pairs={{0,48},{16,32},{32,16},{48,0},{1,49},{17,33},{33,17},{49,1},{2,50}... | collective-permute-start | bytes 995336 | tf_op jit(solution)/shard_map/ppermute | solution.py:41
  38.4 3.8 %shard_map.96 = (f32[128,1152]{1,0:T(8,128)}, f32[3,128,128]{2,1,0:T(8,128)}, f32[3,8,128]{2,1,0:T(8,128)}) custom-call(f32[1]{0:T(128)S(6)} %copy.10.heat_log, f32[1]{0:T(128)S(6)} %copy.11.shift, bf16[128,1152]{1,0:T(8,128)(2,1)} %get-tuple-element.51.own.refs_0_, f32[128,1152]{1,0:T(8,128)} %get-tuple-element.45.total_ref, ...), custom_call_target="tpu_custom_call" | custom-call | flops 226492416 | bytes 4194304 | tf_op jit(solution)/shard_map/pallas_call | solution.py:220
  42.3 2.1 %collective-permute-start.6 = (bf16[128,1152]{1,0:T(8,128)(2,1)}, bf16[128,1152]{1,0:T(8,128)(2,1)S(1)}, u32[]{:S(2)}, u32[]{:S(2)}) collective-permute-start(bf16[128,1152]{1,0:T(8,128)(2,1)} %get-tuple-element.51.own.refs_0_), channel_id=1, source_target_pairs={{0,128},{64,192},{128,0},{192,64},{1,129},{65,193},{129,1},{193,65... | collective-permute-start | bytes 884744 | tf_op jit(solution)/shard_map/ppermute | solution.py:41
  44.4 3.5 %collective-permute-done.7.refs_4_ = bf16[128,1152]{1,0:T(8,128)(2,1)S(1)} collective-permute-done((bf16[128,1152]{1,0:T(8,128)(2,1)}, bf16[128,1152]{1,0:T(8,128)(2,1)S(1)}, u32[]{:S(2)}, u32[]{:S(2)}) %collective-permute-start.7) | collective-permute-done | bytes 294944 | tf_op jit(solution)/shard_map/ppermute | solution.py:41
  47.9 5.5 %collective-permute-start.9 = (bf16[128,1152]{1,0:T(8,128)(2,1)S(1)}, bf16[128,1152]{1,0:T(8,128)(2,1)S(1)}, u32[]{:S(2)}, u32[]{:S(2)}) collective-permute-start(bf16[128,1152]{1,0:T(8,128)(2,1)S(1)} %collective-permute-done.7.refs_4_), channel_id=1, source_target_pairs={{0,48},{16,32},{32,16},{48,0},{1,49},{17,33},{33,17},{49,1},{2,50}... | collective-permute-start | bytes 884744 | tf_op jit(solution)/shard_map/ppermute | solution.py:41
  53.5 7.1 %collective-permute-done.8.refs_5_ = bf16[144,1152]{1,0:T(8,128)(2,1)S(1)} collective-permute-done((bf16[144,1152]{1,0:T(8,128)(2,1)S(1)}, bf16[144,1152]{1,0:T(8,128)(2,1)S(1)}, u32[]{:S(2)}, u32[]{:S(2)}) %collective-permute-start.8) | collective-permute-done | bytes 331808 | tf_op jit(solution)/shard_map/ppermute | solution.py:41
  61.3 3.1 %shard_map.98 = (bf16[304,128]{1,0:T(8,128)(2,1)}, bf16[304,128]{1,0:T(8,128)(2,1)}, bf16[304,128]{1,0:T(8,128)(2,1)}, bf16[304,128]{1,0:T(8,128)(2,1)}, f32[1,8,128]{2,1,0:T(8,128)}) custom-call(s32[2]{0:T(128)} %pad_add_fusion.spot, f32[1]{0:T(128)S(6)} %copy.10.heat_log, f32[1]{0:T(128)S(6)} %copy.11.shift, ...), custom_call_target="tpu_custom_call" | custom-call | flops 150994944 | bytes 4194304 | tf_op jit(solution)/shard_map/pallas_call | solution.py:313
  66.0 1.8 %collective-permute-start.11 = (bf16[304,128]{1,0:T(8,128)(2,1)}, bf16[304,128]{1,0:T(8,128)(2,1)S(1)}, u32[]{:S(2)}, u32[]{:S(2)}) collective-permute-start(bf16[304,128]{1,0:T(8,128)(2,1)} %get-tuple-element.65), channel_id=1, source_target_pairs={{0,3},{1,0},{2,1},{3,2},{4,7},{5,4},{6,5},{7,6},{8,11},{9,8},{10,9... | collective-permute-start | bytes 233480 | tf_op jit(solution)/shard_map/ppermute | solution.py:457
  67.8 1.8 %collective-permute-start.12 = (bf16[304,128]{1,0:T(8,128)(2,1)}, bf16[304,128]{1,0:T(8,128)(2,1)S(1)}, u32[]{:S(2)}, u32[]{:S(2)}) collective-permute-start(bf16[304,128]{1,0:T(8,128)(2,1)} %get-tuple-element.71), channel_id=1, source_target_pairs={{0,2},{1,3},{2,0},{3,1},{4,6},{5,7},{6,4},{7,5},{8,10},{9,11},{10,... | collective-permute-start | bytes 233480 | tf_op jit(solution)/shard_map/ppermute | solution.py:457
  69.6 4.0 %shard_map.97.refs_0_ = f32[128,1152]{1,0:T(8,128)} custom-call(f32[1]{0:T(128)S(6)} %copy.10.heat_log, f32[1]{0:T(128)S(6)} %copy.11.shift, bf16[144,1152]{1,0:T(8,128)(2,1)} %shard_map.94.refs_0_.own, f32[128,128]{1,0:T(8,128)} %get-tuple-element.42.key.refs_3_.refs_4_, f32[2,8,128]{2,1,0:T(8,128)} %get-tuple-element.43.near_rows, ...), custom_call_target="tpu_custom_call" | custom-call | flops 377487360 | bytes 4194304 | tf_op jit(solution)/shard_map/pallas_call | solution.py:248
  74.3 3.0 %shard_map.99 = (bf16[288,128]{1,0:T(8,128)(2,1)}, bf16[288,128]{1,0:T(8,128)(2,1)}, bf16[288,128]{1,0:T(8,128)(2,1)}, bf16[288,128]{1,0:T(8,128)(2,1)}) custom-call(s32[2]{0:T(128)} %pad_add_fusion.spot, f32[1]{0:T(128)S(6)} %copy.10.heat_log, f32[1]{0:T(128)S(6)} %copy.11.shift, bf16[144,1152]{1,0:T(8,128)(2,1)} %shard_map.94.refs_0_.own, ...), custom_call_target="tpu_custom_call" | custom-call | flops 150994944 | bytes 4194304 | tf_op jit(solution)/shard_map/pallas_call | solution.py:313
  77.9 2.0 %collective-permute-start.15 = (bf16[288,128]{1,0:T(8,128)(2,1)}, bf16[288,128]{1,0:T(8,128)(2,1)S(1)}, u32[]{:S(2)}, u32[]{:S(2)}) collective-permute-start(bf16[288,128]{1,0:T(8,128)(2,1)} %get-tuple-element.75), channel_id=1, source_target_pairs={{0,2},{1,3},{2,0},{3,1},{4,6},{5,7},{6,4},{7,5},{8,10},{9,11},{10,... | collective-permute-start | bytes 221192 | tf_op jit(solution)/shard_map/ppermute | solution.py:457
  79.9 1.7 %collective-permute-start.16 = (bf16[288,128]{1,0:T(8,128)(2,1)}, bf16[288,128]{1,0:T(8,128)(2,1)S(1)}, u32[]{:S(2)}, u32[]{:S(2)}) collective-permute-start(bf16[288,128]{1,0:T(8,128)(2,1)} %get-tuple-element.76), channel_id=1, source_target_pairs={{0,3},{1,0},{2,1},{3,2},{4,7},{5,4},{6,5},{7,6},{8,11},{9,8},{10,9... | collective-permute-start | bytes 221192 | tf_op jit(solution)/shard_map/ppermute | solution.py:457
  81.7 2.0 %shard_map.100 = (f32[32,48,128]{2,1,0:T(8,128)S(1)}, bf16[32,48,128]{2,1,0:T(8,128)(2,1)S(1)}) custom-call(s32[2]{0:T(128)S(1)} %copy-done.3, bf16[512,1152]{1,0:T(8,128)(2,1)S(1)} %copy-done, bf16[304,128]{1,0:T(8,128)(2,1)S(1)} %copy-done.2, bf16[304,128]{1,0:T(8,128)(2,1)S(1)} %collective-permute-done.10.refs_1_, ...), custom_call_target="tpu_custom_call" | custom-call | flops 339738624 | bytes 4194304 | tf_op jit(solution)/shard_map/pallas_call | solution.py:373
  85.3 3.8 %shard_map.101 = (f32[32,48,128]{2,1,0:T(8,128)}, bf16[32,48,128]{2,1,0:T(8,128)(2,1)}) custom-call(s32[2]{0:T(128)} %pad_add_fusion.spot, bf16[512,1152]{1,0:T(8,128)(2,1)} %all-gather.5.cloned.1.call-done.feat, bf16[288,128]{1,0:T(8,128)(2,1)} %get-tuple-element.67.refs_0_, bf16[288,128]{1,0:T(8,128)(2,1)} %copy-done.14, bf16[288,128]{1,0:T(8,128)(2,1)} %copy-done.15, ...), custom_call_target="tpu_custom_call" | custom-call | flops 339738624 | bytes 4194304 | tf_op jit(solution)/shard_map/pallas_call | solution.py:373
  89.4 1.7 %collective-permute-done.17.taken_txt = bf16[32,48,128]{2,1,0:T(8,128)(2,1)S(1)} collective-permute-done((bf16[32,48,128]{2,1,0:T(8,128)(2,1)}, bf16[32,48,128]{2,1,0:T(8,128)(2,1)S(1)}, u32[]{:S(2)}, u32[]{:S(2)}) %collective-permute-start.17) | collective-permute-done | bytes 393248 | tf_op jit(solution)/shard_map/ppermute | solution.py:41
  92.4 26.6 %all_to_all.5.parts = bf16[32,96,128]{2,1,0:T(8,128)(2,1)S(1)} all-to-all(bf16[32,96,128]{2,1,0:T(8,128)(2,1)S(1)} %shard_map.102), channel_id=1, replica_groups=mesh['ly'=4,'lz'=4,'lc'=2,'dz'=2,'dx'=4] {'ly','lz','dz'}, dimensions={0} | all-to-all | bytes 1572864 | tf_op jit(solution)/shard_map/all_to_all | solution.py:480
  (64 shorter events, 10.8 us)
Async XLA Ops:
  7.2 53.4 %all-gather.3.cloned.1.call-start = ((), (), s32[]{:S(2)}) async-start(), calls=%async_computation.1 | async-start | bytes 1474560 | tf_op jit(solution)/shard_map/all_gather | solution.py:435
  10.7 71.0 %all-gather.5.cloned.1.call-start = ((), (), s32[]{:S(2)}) async-start(), calls=%async_computation.2 | async-start | bytes 1474560 | tf_op jit(solution)/shard_map/all_gather | solution.py:436
  11.4 9.9 %collective-permute-start = (bf16[144,1152]{1,0:T(8,128)(2,1)}, bf16[144,1152]{1,0:T(8,128)(2,1)S(1)}, u32[]{:S(2)}, u32[]{:S(2)}) collective-permute-start(bf16[144,1152]{1,0:T(8,128)(2,1)} %shard_map.94.refs_0_.own), channel_id=1, source_target_pairs={{0,8},{8,0},{1,9},{9,1},{2,10},{10,2},{3,11},{11,3},{4,12},{12,4},... | collective-permute-start | bytes 995336 | tf_op jit(solution)/shard_map/ppermute | solution.py:41
  11.5 16.6 %collective-permute-start.1 = (bf16[144,1152]{1,0:T(8,128)(2,1)}, bf16[144,1152]{1,0:T(8,128)(2,1)S(1)}, u32[]{:S(2)}, u32[]{:S(2)}) collective-permute-start(bf16[144,1152]{1,0:T(8,128)(2,1)} %shard_map.94.refs_0_.own), channel_id=1, source_target_pairs={{0,64},{64,0},{128,192},{192,128},{1,65},{65,1},{129,193},{193,129... | collective-permute-start | bytes 995336 | tf_op jit(solution)/shard_map/ppermute | solution.py:41
  13.2 17.6 %collective-permute-start.2 = (bf16[144,1152]{1,0:T(8,128)(2,1)}, bf16[144,1152]{1,0:T(8,128)(2,1)S(1)}, u32[]{:S(2)}, u32[]{:S(2)}) collective-permute-start(bf16[144,1152]{1,0:T(8,128)(2,1)} %shard_map.94.refs_0_.own), channel_id=1, source_target_pairs={{0,16},{16,0},{32,48},{48,32},{1,17},{17,1},{33,49},{49,33},{2,18}... | collective-permute-start | bytes 995336 | tf_op jit(solution)/shard_map/ppermute | solution.py:41
  16.5 15.1 %collective-permute-start.3 = (bf16[144,1152]{1,0:T(8,128)(2,1)}, bf16[144,1152]{1,0:T(8,128)(2,1)S(1)}, u32[]{:S(2)}, u32[]{:S(2)}) collective-permute-start(bf16[144,1152]{1,0:T(8,128)(2,1)} %shard_map.94.refs_0_.own), channel_id=1, source_target_pairs={{0,128},{64,192},{128,0},{192,64},{1,129},{65,193},{129,1},{193,65... | collective-permute-start | bytes 995336 | tf_op jit(solution)/shard_map/ppermute | solution.py:41
  31.5 6.9 %collective-permute-start.4 = (bf16[128,1152]{1,0:T(8,128)(2,1)}, bf16[128,1152]{1,0:T(8,128)(2,1)S(1)}, u32[]{:S(2)}, u32[]{:S(2)}) collective-permute-start(bf16[128,1152]{1,0:T(8,128)(2,1)} %get-tuple-element.51.own.refs_0_), channel_id=1, source_target_pairs={{0,8},{8,0},{1,9},{9,1},{2,10},{10,2},{3,11},{11,3},{4,12},{12,4},... | collective-permute-start | bytes 884744 | tf_op jit(solution)/shard_map/ppermute | solution.py:41
  31.5 16.4 %collective-permute-start.7 = (bf16[128,1152]{1,0:T(8,128)(2,1)}, bf16[128,1152]{1,0:T(8,128)(2,1)S(1)}, u32[]{:S(2)}, u32[]{:S(2)}) collective-permute-start(bf16[128,1152]{1,0:T(8,128)(2,1)} %get-tuple-element.51.own.refs_0_), channel_id=1, source_target_pairs={{0,16},{16,0},{32,48},{48,32},{1,17},{17,1},{33,49},{49,33},{2,18}... | collective-permute-start | bytes 884744 | tf_op jit(solution)/shard_map/ppermute | solution.py:41
  34.8 25.7 %collective-permute-start.8 = (bf16[144,1152]{1,0:T(8,128)(2,1)S(1)}, bf16[144,1152]{1,0:T(8,128)(2,1)S(1)}, u32[]{:S(2)}, u32[]{:S(2)}) collective-permute-start(bf16[144,1152]{1,0:T(8,128)(2,1)S(1)} %collective-permute-done.2.refs_2_), channel_id=1, source_target_pairs={{0,48},{16,32},{32,16},{48,0},{1,49},{17,33},{33,17},{49,1},{2,50}... | collective-permute-start | bytes 995336 | tf_op jit(solution)/shard_map/ppermute | solution.py:41
  38.4 31.2 %copy-start.9 = (bf16[128,1152]{1,0:T(8,128)(2,1)}, bf16[128,1152]{1,0:T(8,128)(2,1)S(1)}, u32[]{:S(2)}) copy-start(bf16[128,1152]{1,0:T(8,128)(2,1)S(1)} %collective-permute-done.4.refs_1_) | copy-start | bytes 884740
  42.2 22.2 %collective-permute-start.5 = (bf16[128,1152]{1,0:T(8,128)(2,1)}, bf16[128,1152]{1,0:T(8,128)(2,1)S(1)}, u32[]{:S(2)}, u32[]{:S(2)}) collective-permute-start(bf16[128,1152]{1,0:T(8,128)(2,1)} %get-tuple-element.51.own.refs_0_), channel_id=1, source_target_pairs={{0,64},{64,0},{128,192},{192,128},{1,65},{65,1},{129,193},{193,129... | collective-permute-start | bytes 884744 | tf_op jit(solution)/shard_map/ppermute | solution.py:41
  42.3 22.1 %collective-permute-start.6 = (bf16[128,1152]{1,0:T(8,128)(2,1)}, bf16[128,1152]{1,0:T(8,128)(2,1)S(1)}, u32[]{:S(2)}, u32[]{:S(2)}) collective-permute-start(bf16[128,1152]{1,0:T(8,128)(2,1)} %get-tuple-element.51.own.refs_0_), channel_id=1, source_target_pairs={{0,128},{64,192},{128,0},{192,64},{1,129},{65,193},{129,1},{193,65... | collective-permute-start | bytes 884744 | tf_op jit(solution)/shard_map/ppermute | solution.py:41
  47.9 21.6 %copy-start.10 = (bf16[128,1152]{1,0:T(8,128)(2,1)}, bf16[128,1152]{1,0:T(8,128)(2,1)S(1)}, u32[]{:S(2)}) copy-start(bf16[128,1152]{1,0:T(8,128)(2,1)S(1)} %collective-permute-done.7.refs_4_) | copy-start | bytes 884740
  47.9 25.6 %collective-permute-start.9 = (bf16[128,1152]{1,0:T(8,128)(2,1)S(1)}, bf16[128,1152]{1,0:T(8,128)(2,1)S(1)}, u32[]{:S(2)}, u32[]{:S(2)}) collective-permute-start(bf16[128,1152]{1,0:T(8,128)(2,1)S(1)} %collective-permute-done.7.refs_4_), channel_id=1, source_target_pairs={{0,48},{16,32},{32,16},{48,0},{1,49},{17,33},{33,17},{49,1},{2,50}... | collective-permute-start | bytes 884744 | tf_op jit(solution)/shard_map/ppermute | solution.py:41
  64.4 17.3 %copy-start.2 = (bf16[304,128]{1,0:T(8,128)(2,1)S(1)}, bf16[304,128]{1,0:T(8,128)(2,1)}, u32[]{:S(2)}) copy-start(bf16[304,128]{1,0:T(8,128)(2,1)} %get-tuple-element.70.refs_0_) | copy-start | bytes 233476
  64.4 17.3 %copy-start.3 = (s32[2]{0:T(128)S(1)}, s32[2]{0:T(128)}, u32[]{:S(2)}) copy-start(s32[2]{0:T(128)} %pad_add_fusion.spot) | copy-start | bytes 28
  64.5 9.1 %collective-permute-start.10 = (bf16[304,128]{1,0:T(8,128)(2,1)}, bf16[304,128]{1,0:T(8,128)(2,1)S(1)}, u32[]{:S(2)}, u32[]{:S(2)}) collective-permute-start(bf16[304,128]{1,0:T(8,128)(2,1)} %get-tuple-element.64), channel_id=1, source_target_pairs={{0,1},{1,2},{2,3},{3,0},{4,5},{5,6},{6,7},{7,4},{8,9},{9,10},{10,1... | collective-permute-start | bytes 233480 | tf_op jit(solution)/shard_map/ppermute | solution.py:457
  66.0 7.6 %collective-permute-start.11 = (bf16[304,128]{1,0:T(8,128)(2,1)}, bf16[304,128]{1,0:T(8,128)(2,1)S(1)}, u32[]{:S(2)}, u32[]{:S(2)}) collective-permute-start(bf16[304,128]{1,0:T(8,128)(2,1)} %get-tuple-element.65), channel_id=1, source_target_pairs={{0,3},{1,0},{2,1},{3,2},{4,7},{5,4},{6,5},{7,6},{8,11},{9,8},{10,9... | collective-permute-start | bytes 233480 | tf_op jit(solution)/shard_map/ppermute | solution.py:457
  67.8 13.9 %collective-permute-start.12 = (bf16[304,128]{1,0:T(8,128)(2,1)}, bf16[304,128]{1,0:T(8,128)(2,1)S(1)}, u32[]{:S(2)}, u32[]{:S(2)}) collective-permute-start(bf16[304,128]{1,0:T(8,128)(2,1)} %get-tuple-element.71), channel_id=1, source_target_pairs={{0,2},{1,3},{2,0},{3,1},{4,6},{5,7},{6,4},{7,5},{8,10},{9,11},{10,... | collective-permute-start | bytes 233480 | tf_op jit(solution)/shard_map/ppermute | solution.py:457
  77.3 6.5 %collective-permute-start.14 = (bf16[288,128]{1,0:T(8,128)(2,1)}, bf16[288,128]{1,0:T(8,128)(2,1)S(1)}, u32[]{:S(2)}, u32[]{:S(2)}) collective-permute-start(bf16[288,128]{1,0:T(8,128)(2,1)} %get-tuple-element.74), channel_id=1, source_target_pairs={{0,1},{1,2},{2,3},{3,0},{4,5},{5,6},{6,7},{7,4},{8,9},{9,10},{10,1... | collective-permute-start | bytes 221192 | tf_op jit(solution)/shard_map/ppermute | solution.py:457
  77.9 6.1 %collective-permute-start.15 = (bf16[288,128]{1,0:T(8,128)(2,1)}, bf16[288,128]{1,0:T(8,128)(2,1)S(1)}, u32[]{:S(2)}, u32[]{:S(2)}) collective-permute-start(bf16[288,128]{1,0:T(8,128)(2,1)} %get-tuple-element.75), channel_id=1, source_target_pairs={{0,2},{1,3},{2,0},{3,1},{4,6},{5,7},{6,4},{7,5},{8,10},{9,11},{10,... | collective-permute-start | bytes 221192 | tf_op jit(solution)/shard_map/ppermute | solution.py:457
  79.9 4.8 %collective-permute-start.16 = (bf16[288,128]{1,0:T(8,128)(2,1)}, bf16[288,128]{1,0:T(8,128)(2,1)S(1)}, u32[]{:S(2)}, u32[]{:S(2)}) collective-permute-start(bf16[288,128]{1,0:T(8,128)(2,1)} %get-tuple-element.76), channel_id=1, source_target_pairs={{0,3},{1,0},{2,1},{3,2},{4,7},{5,4},{6,5},{7,6},{8,11},{9,8},{10,9... | collective-permute-start | bytes 221192 | tf_op jit(solution)/shard_map/ppermute | solution.py:457
  83.7 5.7 %collective-permute-start.13 = (bf16[32,48,128]{2,1,0:T(8,128)(2,1)S(1)}, bf16[32,48,128]{2,1,0:T(8,128)(2,1)S(1)}, u32[]{:S(2)}, u32[]{:S(2)}) collective-permute-start(bf16[32,48,128]{2,1,0:T(8,128)(2,1)S(1)} %get-tuple-element.73), channel_id=1, source_target_pairs={{0,8},{8,0},{1,9},{9,1},{2,10},{10,2},{3,11},{11,3},{4,12},{12,4},... | collective-permute-start | bytes 1179656 | tf_op jit(solution)/shard_map/ppermute | solution.py:41
  89.2 1.9 %collective-permute-start.17 = (bf16[32,48,128]{2,1,0:T(8,128)(2,1)}, bf16[32,48,128]{2,1,0:T(8,128)(2,1)S(1)}, u32[]{:S(2)}, u32[]{:S(2)}) collective-permute-start(bf16[32,48,128]{2,1,0:T(8,128)(2,1)} %get-tuple-element.78), channel_id=1, source_target_pairs={{0,8},{8,0},{1,9},{9,1},{2,10},{10,2},{3,11},{11,3},{4,12},{12,4},... | collective-permute-start | bytes 1179656 | tf_op jit(solution)/shard_map/ppermute | solution.py:41
  (13 other events, 57.9 us)
Sparse Core Ops, SparseCore 0:
  10.8 29.5 all-gather.2
  42.1 28.1 all-gather.4
